TPU v7x, 256 devices: a whole 4x4x8 slice. The times are simulated.
256 devices in a mesh: tm: 32 (over x, z_lo, core), space: 8 (over z_hi, y).
Axes of the slice: x: 4, y: 4, z: 8 (z_hi: 2, z_lo: 4; z = z_hi * 4 + z_lo), core: 2. Of those that a mesh axis runs over, the one named last changes fastest.
Arguments:
- slice_starts: float32 [32, 3, 128, 32, 128], P('tm', None, 'space'), may hold values from -6 to 6
- coriolis: float32 [32], replicated, may hold values from 0.05 to 0.2
- stratification: float32 [128, 32, 128], P('space'), may hold values from 0.25 to 1
- inverse_blocks: float32 [3, 128, 128], replicated, may hold values from 0 to 0.51153846
Outputs:
- new_starts: float32 [32, 3, 128, 32, 128], P('tm', None, 'space')
All inputs are finite; a program needn't handle non-finite values.
Results may differ from a plain program's by a relative error of at most 0.00011.
Values sent between devices are 32-bit elements; how exact they have to be, the bound alone decides.
No kernel may reach another device: no remote copies, remote signals or barrier semaphores. Data moves between devices by JAX's collectives and lax.ppermute only.
A program may use at most 64 MiB of HBM per device.

v0:
```python
import jax
import jax.numpy as jnp
from jax import lax
from jax.sharding import PartitionSpec as P

STEPS = 8


TIME_STEP = 0.5
VISCOSITY = 0.1
DIFFUSIVITY = 0.3
COARSE_STEP = 4.0
COARSE_SPACING = 4.0


def with_halo(cells, sides, width):
    for axis, dim in sides:
        count = lax.axis_size(axis)
        head = lax.slice_in_dim(cells, 0, width, axis=dim)
        tail = lax.slice_in_dim(cells, cells.shape[dim] - width, cells.shape[dim], axis=dim)
        cells = jnp.concatenate(
            [
                lax.ppermute(tail, axis, [(i, (i + 1) % count) for i in range(count)]),
                cells,
                lax.ppermute(head, axis, [((i + 1) % count, i) for i in range(count)]),
            ],
            axis=dim,
        )
    return cells


def from_behind(block, axis, distance):
    devices = range(lax.axis_size(axis))
    route = [(i - distance, i) for i in devices if i - distance in devices]
    return lax.ppermute(block, axis, route)


def passed_along(array, axis, by):
    size = lax.axis_size(axis)
    return lax.ppermute(array, axis, [(i, (i + by) % size) for i in range(size)])


def along_x(field):
    return (field[2:] - field[:-2]) * 0.5


def along_y(field):
    return (jnp.roll(field, -1, axis=1) - jnp.roll(field, 1, axis=1)) * 0.5


def lateral_laplacian(field):
    middle = field[1:-1]
    return (
        field[2:]
        + field[:-2]
        + jnp.roll(middle, -1, axis=1)
        + jnp.roll(middle, 1, axis=1)
        - 4.0 * middle
    )


def vertical_second(field):
    padded = jnp.concatenate([field[..., :1], field, field[..., -1:]], axis=-1)
    return padded[..., 2:] + padded[..., :-2] - 2.0 * field


def fine_core(padded, coriolis, stratification):
    zonal, meridional, buoyancy = (padded[0], padded[1], padded[2])
    spin = coriolis[None, :, None]
    zonal_mid = zonal[1:-1]
    meridional_mid = meridional[1:-1]
    zonal_new = zonal_mid + TIME_STEP * (
        spin * meridional_mid
        - along_x(buoyancy)
        + VISCOSITY * lateral_laplacian(zonal)
        + DIFFUSIVITY * vertical_second(zonal_mid)
    )
    meridional_new = meridional_mid + TIME_STEP * (
        -spin * zonal_new
        - along_y(buoyancy[1:-1])
        + VISCOSITY * lateral_laplacian(meridional)
        + DIFFUSIVITY * vertical_second(meridional_mid)
    )
    buoyancy_mid = buoyancy[2:-2]
    buoyancy_new = buoyancy_mid + TIME_STEP * (
        -stratification * (along_x(zonal_new) + along_y(meridional_new[1:-1]))
        + VISCOSITY * lateral_laplacian(buoyancy[1:-1])
        + DIFFUSIVITY * vertical_second(buoyancy_mid)
    )
    return jnp.stack([zonal_new[1:-1], meridional_new[1:-1], buoyancy_new])


def coarse_core(padded, spin_coarse, strat_coarse, inverse_blocks):
    zonal, meridional, buoyancy = (padded[0], padded[1], padded[2])
    spin = spin_coarse[None, :, None]
    ratio = COARSE_STEP / COARSE_SPACING
    zonal_half = zonal[1:-1] + COARSE_STEP * spin * meridional[1:-1] - ratio * along_x(buoyancy)
    meridional_half = (
        meridional[1:-1] - COARSE_STEP * spin * zonal_half - ratio * along_y(buoyancy[1:-1])
    )
    buoyancy_half = buoyancy[2:-2] - ratio * strat_coarse * (
        along_x(zonal_half) + along_y(meridional_half[1:-1])
    )
    explicit = jnp.stack([zonal_half[1:-1], meridional_half[1:-1], buoyancy_half])
    return jnp.einsum("kxyj,kij->kxyi", explicit, inverse_blocks, precision=lax.Precision.HIGHEST)


def restrict(state):
    kinds, across, along, levels = state.shape
    return state.reshape(kinds, across // 4, 4, along // 4, 4, levels).mean(axis=(2, 4))


def prolong(state):
    kinds, across, along, levels = state.shape
    expanded = jnp.broadcast_to(state[:, :, None, :, None, :], (kinds, across, 4, along, 4, levels))
    return expanded.reshape(kinds, across * 4, along * 4, levels)


def per_device(slice_starts, coriolis, stratification, inverse_blocks):
    start = slice_starts[0]
    spin_coarse = coriolis.reshape(-1, 4).mean(axis=1)
    strat_coarse = restrict(stratification[None])[0]
    first = lax.axis_index("tm") == 0
    local_coarse = restrict(start)
    fine = start
    for step in range(STEPS):
        padded = with_halo(fine, (("space", 1),), 2)
        fine = fine_core(padded, coriolis, stratification)

    def coarse_map(state):
        rimmed = with_halo(state, (("space", 1),), 2)
        return coarse_core(rimmed, spin_coarse, strat_coarse, inverse_blocks)

    start_image = coarse_map(local_coarse)
    delta = fine - prolong(start_image)
    increment_coarse = restrict(delta)

    def advance(turn, current):
        sent = from_behind(current + increment_coarse, "tm", 1)
        return coarse_map(jnp.where(first, local_coarse, sent))

    image = lax.fori_loop(0, lax.axis_size("tm") - 1, advance, start_image)
    result = passed_along(prolong(image) + delta, "tm", 1)
    return result[None]


def solution(mesh):
    in_specs = (P("tm", None, "space", None, None), P(), P("space", None, None), P())
    out_specs = P("tm", None, "space", None, None)
    return jax.shard_map(
        per_device, mesh=mesh, in_specs=in_specs, out_specs=out_specs, check_vma=False
    )
```

profile of v0, /device:TPU:26, one launch (start us, length us, event | category | flops | bytes accessed | tf_op | source)
XLA Modules:
  0.0 733.3 jit_solution(9290427516537844291)
XLA Ops:
  1.0 6.9 collective-permute-start.5
  9.4 8.1 %collective-permute-start.3 = (f32[3,2,8,128]{3,2,1,0:T(8,128)S(1)}, f32[3,2,8,128]{3,2,1,0:T(8,128)S(1)}, u32[]{:S(2)}, u32[]{:S(2)}) collective-permute-start(f32[3,2,8,128]{3,2,1,0:T(8,128)S(1)} %get-tuple-element.372), channel_id=1, source_target_pairs={{0,1},{1,2},{2,3},{3,4},{4,5},{5,6},{6,7},{7,0},{8,9},{9,10},{10,1... | collective-permute-start | bytes 73736 | tf_op jit(solution)/shard_map/ppermute | solution.py:23
  19.0 8.3 %collective-permute-done.4 = f32[3,2,8,128]{3,2,1,0:T(8,128)S(1)} collective-permute-done((f32[3,2,8,128]{3,2,1,0:T(8,128)S(1)}, f32[3,2,8,128]{3,2,1,0:T(8,128)S(1)}, u32[]{:S(2)}, u32[]{:S(2)}) %collective-permute-start.4) | collective-permute-done | bytes 24608 | tf_op jit(solution)/shard_map/ppermute | solution.py:25
  35.5 6.2 collective-permute-done.8
  44.2 8.0 %collective-permute-start.9 = (f32[3,2,32,128]{3,2,1,0:T(8,128)S(1)}, f32[3,2,32,128]{3,2,1,0:T(8,128)S(1)}, u32[]{:S(2)}, u32[]{:S(2)}) collective-permute-start(f32[3,2,32,128]{3,2,1,0:T(8,128)S(1)} %get-tuple-element.140), channel_id=1, source_target_pairs={{0,1},{1,2},{2,3},{3,4},{4,5},{5,6},{6,7},{7,0},{8,9},{9,10},{10,1... | collective-permute-start | bytes 294920 | tf_op jit(solution)/shard_map/ppermute | solution.py:23
  58.1 8.1 %collective-permute-start.11 = (f32[3,2,32,128]{3,2,1,0:T(8,128)S(1)}, f32[3,2,32,128]{3,2,1,0:T(8,128)S(1)}, u32[]{:S(2)}, u32[]{:S(2)}) collective-permute-start(f32[3,2,32,128]{3,2,1,0:T(8,128)S(1)} %get-tuple-element.136), channel_id=1, source_target_pairs={{0,1},{1,2},{2,3},{3,4},{4,5},{5,6},{6,7},{7,0},{8,9},{9,10},{10,1... | collective-permute-start | bytes 294920 | tf_op jit(solution)/shard_map/ppermute | solution.py:23
  68.5 8.5 %collective-permute-done.12 = f32[3,2,32,128]{3,2,1,0:T(8,128)S(1)} collective-permute-done((f32[3,2,32,128]{3,2,1,0:T(8,128)S(1)}, f32[3,2,32,128]{3,2,1,0:T(8,128)S(1)}, u32[]{:S(2)}, u32[]{:S(2)}) %collective-permute-start.12) | collective-permute-done | bytes 98336 | tf_op jit(solution)/shard_map/ppermute | solution.py:25
  97.2 6.3 collective-permute-done.16
  133.2 583.8 %while.10 = (s32[]{:T(128)}, f32[3,4,8,128]{3,2,1,0:T(8,128)S(1)}, pred[]{:T(512)}, f32[3,4,8,128]{3,2,1,0:T(8,128)S(1)}, f32[3,4,8,128]{3,2,1,0:T(8,128)S(1)}, ...) while((s32[]{:T(128)}, f32[3,4,8,128]{3,2,1,0:T(8,128)S(1)}, ...), condition=%wide.region_5.6_spmd, body=%wide.region_4.5_spmd.sunk | while | flops 19146760 | bytes 1843542 | solution.py:142
  135.1 6.3 collective-permute-done
  154.0 6.4 collective-permute-done
  173.1 6.2 collective-permute-done
  229.5 6.2 collective-permute-done
  286.0 6.2 collective-permute-done
  323.6 6.2 collective-permute-done
  342.4 6.2 collective-permute-done
  380.0 6.2 collective-permute-done
  436.4 6.2 collective-permute-done
  492.9 6.2 collective-permute-done
  530.5 6.2 collective-permute-done
  586.9 6.2 collective-permute-done
  643.4 6.2 collective-permute-done
  709.9 6.4 collective-permute-done.2
  718.3 14.1 %collective-permute-done.21 = f32[3,16,32,128]{3,2,1,0:T(8,128)S(1)} collective-permute-done((f32[3,16,32,128]{3,2,1,0:T(8,128)S(1)}, f32[3,16,32,128]{3,2,1,0:T(8,128)S(1)}, u32[]{:S(2)}, u32[]{:S(2)}) %collective-permute-start.21) | collective-permute-done | bytes 786464 | tf_op jit(solution)/shard_map/ppermute | solution.py:40
  (793 shorter events, 567.9 us)
Async XLA Ops:
  1.0 27.8 %collective-permute-start.5 = (f32[3,2,32,128]{3,2,1,0:T(8,128)S(1)}, f32[3,2,32,128]{3,2,1,0:T(8,128)S(1)}, u32[]{:S(2)}, u32[]{:S(2)}) collective-permute-start(f32[3,2,32,128]{3,2,1,0:T(8,128)S(1)} %get-tuple-element.146), channel_id=1, source_target_pairs={{0,1},{1,2},{2,3},{3,4},{4,5},{5,6},{6,7},{7,0},{8,9},{9,10},{10,1... | collective-permute-start | bytes 294920 | tf_op jit(solution)/shard_map/ppermute | solution.py:23
  8.0 20.8 %collective-permute-start.6 = (f32[3,2,32,128]{3,2,1,0:T(8,128)S(1)}, f32[3,2,32,128]{3,2,1,0:T(8,128)S(1)}, u32[]{:S(2)}, u32[]{:S(2)}) collective-permute-start(f32[3,2,32,128]{3,2,1,0:T(8,128)S(1)} %get-tuple-element.145), channel_id=1, source_target_pairs={{1,0},{2,1},{3,2},{4,3},{5,4},{6,5},{7,6},{0,7},{9,8},{10,9},{11,1... | collective-permute-start | bytes 294920 | tf_op jit(solution)/shard_map/ppermute | solution.py:25
  30.9 10.8 %collective-permute-start.8 = (f32[3,2,32,128]{3,2,1,0:T(8,128)S(1)}, f32[3,2,32,128]{3,2,1,0:T(8,128)S(1)}, u32[]{:S(2)}, u32[]{:S(2)}) collective-permute-start(f32[3,2,32,128]{3,2,1,0:T(8,128)S(1)} %get-tuple-element.143), channel_id=1, source_target_pairs={{1,0},{2,1},{3,2},{4,3},{5,4},{6,5},{7,6},{0,7},{9,8},{10,9},{11,1... | collective-permute-start | bytes 294920 | tf_op jit(solution)/shard_map/ppermute | solution.py:25
  44.1 11.7 %collective-permute-start.10 = (f32[3,2,32,128]{3,2,1,0:T(8,128)S(1)}, f32[3,2,32,128]{3,2,1,0:T(8,128)S(1)}, u32[]{:S(2)}, u32[]{:S(2)}) collective-permute-start(f32[3,2,32,128]{3,2,1,0:T(8,128)S(1)} %get-tuple-element.139), channel_id=1, source_target_pairs={{1,0},{2,1},{3,2},{4,3},{5,4},{6,5},{7,6},{0,7},{9,8},{10,9},{11,1... | collective-permute-start | bytes 294920 | tf_op jit(solution)/shard_map/ppermute | solution.py:25
  44.2 11.6 %collective-permute-start.9 = (f32[3,2,32,128]{3,2,1,0:T(8,128)S(1)}, f32[3,2,32,128]{3,2,1,0:T(8,128)S(1)}, u32[]{:S(2)}, u32[]{:S(2)}) collective-permute-start(f32[3,2,32,128]{3,2,1,0:T(8,128)S(1)} %get-tuple-element.140), channel_id=1, source_target_pairs={{0,1},{1,2},{2,3},{3,4},{4,5},{5,6},{6,7},{7,0},{8,9},{9,10},{10,1... | collective-permute-start | bytes 294920 | tf_op jit(solution)/shard_map/ppermute | solution.py:23
  58.1 10.4 %collective-permute-start.11 = (f32[3,2,32,128]{3,2,1,0:T(8,128)S(1)}, f32[3,2,32,128]{3,2,1,0:T(8,128)S(1)}, u32[]{:S(2)}, u32[]{:S(2)}) collective-permute-start(f32[3,2,32,128]{3,2,1,0:T(8,128)S(1)} %get-tuple-element.136), channel_id=1, source_target_pairs={{0,1},{1,2},{2,3},{3,4},{4,5},{5,6},{6,7},{7,0},{8,9},{9,10},{10,1... | collective-permute-start | bytes 294920 | tf_op jit(solution)/shard_map/ppermute | solution.py:23
  66.2 10.7 %collective-permute-start.12 = (f32[3,2,32,128]{3,2,1,0:T(8,128)S(1)}, f32[3,2,32,128]{3,2,1,0:T(8,128)S(1)}, u32[]{:S(2)}, u32[]{:S(2)}) collective-permute-start(f32[3,2,32,128]{3,2,1,0:T(8,128)S(1)} %get-tuple-element.135), channel_id=1, source_target_pairs={{1,0},{2,1},{3,2},{4,3},{5,4},{6,5},{7,6},{0,7},{9,8},{10,9},{11,1... | collective-permute-start | bytes 294920 | tf_op jit(solution)/shard_map/ppermute | solution.py:25
  79.4 10.7 %collective-permute-start.14 = (f32[3,2,32,128]{3,2,1,0:T(8,128)S(1)}, f32[3,2,32,128]{3,2,1,0:T(8,128)S(1)}, u32[]{:S(2)}, u32[]{:S(2)}) collective-permute-start(f32[3,2,32,128]{3,2,1,0:T(8,128)S(1)} %get-tuple-element.131), channel_id=1, source_target_pairs={{1,0},{2,1},{3,2},{4,3},{5,4},{6,5},{7,6},{0,7},{9,8},{10,9},{11,1... | collective-permute-start | bytes 294920 | tf_op jit(solution)/shard_map/ppermute | solution.py:25
  92.6 10.9 %collective-permute-start.16 = (f32[3,2,32,128]{3,2,1,0:T(8,128)S(1)}, f32[3,2,32,128]{3,2,1,0:T(8,128)S(1)}, u32[]{:S(2)}, u32[]{:S(2)}) collective-permute-start(f32[3,2,32,128]{3,2,1,0:T(8,128)S(1)} %get-tuple-element.127), channel_id=1, source_target_pairs={{1,0},{2,1},{3,2},{4,3},{5,4},{6,5},{7,6},{0,7},{9,8},{10,9},{11,1... | collective-permute-start | bytes 294920 | tf_op jit(solution)/shard_map/ppermute | solution.py:25
  105.9 10.7 %collective-permute-start.18 = (f32[3,2,32,128]{3,2,1,0:T(8,128)S(1)}, f32[3,2,32,128]{3,2,1,0:T(8,128)S(1)}, u32[]{:S(2)}, u32[]{:S(2)}) collective-permute-start(f32[3,2,32,128]{3,2,1,0:T(8,128)S(1)} %get-tuple-element.123), channel_id=1, source_target_pairs={{1,0},{2,1},{3,2},{4,3},{5,4},{6,5},{7,6},{0,7},{9,8},{10,9},{11,1... | collective-permute-start | bytes 294920 | tf_op jit(solution)/shard_map/ppermute | solution.py:25
  119.1 10.7 %collective-permute-start.20 = (f32[3,2,32,128]{3,2,1,0:T(8,128)S(1)}, f32[3,2,32,128]{3,2,1,0:T(8,128)S(1)}, u32[]{:S(2)}, u32[]{:S(2)}) collective-permute-start(f32[3,2,32,128]{3,2,1,0:T(8,128)S(1)} %get-tuple-element.119), channel_id=1, source_target_pairs={{1,0},{2,1},{3,2},{4,3},{5,4},{6,5},{7,6},{0,7},{9,8},{10,9},{11,1... | collective-permute-start | bytes 294920 | tf_op jit(solution)/shard_map/ppermute | solution.py:25
  141.5 9.9 %collective-permute-start.2 = (f32[3,2,8,128]{3,2,1,0:T(8,128)S(1)}, f32[3,2,8,128]{3,2,1,0:T(8,128)S(1)}, u32[]{:S(2)}, u32[]{:S(2)}) collective-permute-start(f32[3,2,8,128]{3,2,1,0:T(8,128)S(1)} %get-tuple-element.453), channel_id=1, source_target_pairs={{1,0},{2,1},{3,2},{4,3},{5,4},{6,5},{7,6},{0,7},{9,8},{10,9},{11,1... | collective-permute-start | bytes 73736 | tf_op jit(solution)/shard_map/while/body/eval_jaxpr/ppermute | solution.py:25
  160.6 9.9 %collective-permute-start.2 = (f32[3,2,8,128]{3,2,1,0:T(8,128)S(1)}, f32[3,2,8,128]{3,2,1,0:T(8,128)S(1)}, u32[]{:S(2)}, u32[]{:S(2)}) collective-permute-start(f32[3,2,8,128]{3,2,1,0:T(8,128)S(1)} %get-tuple-element.453), channel_id=1, source_target_pairs={{1,0},{2,1},{3,2},{4,3},{5,4},{6,5},{7,6},{0,7},{9,8},{10,9},{11,1... | collective-permute-start | bytes 73736 | tf_op jit(solution)/shard_map/while/body/eval_jaxpr/ppermute | solution.py:25
  198.2 9.9 %collective-permute-start.2 = (f32[3,2,8,128]{3,2,1,0:T(8,128)S(1)}, f32[3,2,8,128]{3,2,1,0:T(8,128)S(1)}, u32[]{:S(2)}, u32[]{:S(2)}) collective-permute-start(f32[3,2,8,128]{3,2,1,0:T(8,128)S(1)} %get-tuple-element.453), channel_id=1, source_target_pairs={{1,0},{2,1},{3,2},{4,3},{5,4},{6,5},{7,6},{0,7},{9,8},{10,9},{11,1... | collective-permute-start | bytes 73736 | tf_op jit(solution)/shard_map/while/body/eval_jaxpr/ppermute | solution.py:25
  217.0 9.9 %collective-permute-start.2 = (f32[3,2,8,128]{3,2,1,0:T(8,128)S(1)}, f32[3,2,8,128]{3,2,1,0:T(8,128)S(1)}, u32[]{:S(2)}, u32[]{:S(2)}) collective-permute-start(f32[3,2,8,128]{3,2,1,0:T(8,128)S(1)} %get-tuple-element.453), channel_id=1, source_target_pairs={{1,0},{2,1},{3,2},{4,3},{5,4},{6,5},{7,6},{0,7},{9,8},{10,9},{11,1... | collective-permute-start | bytes 73736 | tf_op jit(solution)/shard_map/while/body/eval_jaxpr/ppermute | solution.py:25
  254.6 9.9 %collective-permute-start.2 = (f32[3,2,8,128]{3,2,1,0:T(8,128)S(1)}, f32[3,2,8,128]{3,2,1,0:T(8,128)S(1)}, u32[]{:S(2)}, u32[]{:S(2)}) collective-permute-start(f32[3,2,8,128]{3,2,1,0:T(8,128)S(1)} %get-tuple-element.453), channel_id=1, source_target_pairs={{1,0},{2,1},{3,2},{4,3},{5,4},{6,5},{7,6},{0,7},{9,8},{10,9},{11,1... | collective-permute-start | bytes 73736 | tf_op jit(solution)/shard_map/while/body/eval_jaxpr/ppermute | solution.py:25
  292.3 9.9 %collective-permute-start.2 = (f32[3,2,8,128]{3,2,1,0:T(8,128)S(1)}, f32[3,2,8,128]{3,2,1,0:T(8,128)S(1)}, u32[]{:S(2)}, u32[]{:S(2)}) collective-permute-start(f32[3,2,8,128]{3,2,1,0:T(8,128)S(1)} %get-tuple-element.453), channel_id=1, source_target_pairs={{1,0},{2,1},{3,2},{4,3},{5,4},{6,5},{7,6},{0,7},{9,8},{10,9},{11,1... | collective-permute-start | bytes 73736 | tf_op jit(solution)/shard_map/while/body/eval_jaxpr/ppermute | solution.py:25
  311.1 9.9 %collective-permute-start.2 = (f32[3,2,8,128]{3,2,1,0:T(8,128)S(1)}, f32[3,2,8,128]{3,2,1,0:T(8,128)S(1)}, u32[]{:S(2)}, u32[]{:S(2)}) collective-permute-start(f32[3,2,8,128]{3,2,1,0:T(8,128)S(1)} %get-tuple-element.453), channel_id=1, source_target_pairs={{1,0},{2,1},{3,2},{4,3},{5,4},{6,5},{7,6},{0,7},{9,8},{10,9},{11,1... | collective-permute-start | bytes 73736 | tf_op jit(solution)/shard_map/while/body/eval_jaxpr/ppermute | solution.py:25
  348.7 9.9 %collective-permute-start.2 = (f32[3,2,8,128]{3,2,1,0:T(8,128)S(1)}, f32[3,2,8,128]{3,2,1,0:T(8,128)S(1)}, u32[]{:S(2)}, u32[]{:S(2)}) collective-permute-start(f32[3,2,8,128]{3,2,1,0:T(8,128)S(1)} %get-tuple-element.453), channel_id=1, source_target_pairs={{1,0},{2,1},{3,2},{4,3},{5,4},{6,5},{7,6},{0,7},{9,8},{10,9},{11,1... | collective-permute-start | bytes 73736 | tf_op jit(solution)/shard_map/while/body/eval_jaxpr/ppermute | solution.py:25
  367.5 9.9 %collective-permute-start.2 = (f32[3,2,8,128]{3,2,1,0:T(8,128)S(1)}, f32[3,2,8,128]{3,2,1,0:T(8,128)S(1)}, u32[]{:S(2)}, u32[]{:S(2)}) collective-permute-start(f32[3,2,8,128]{3,2,1,0:T(8,128)S(1)} %get-tuple-element.453), channel_id=1, source_target_pairs={{1,0},{2,1},{3,2},{4,3},{5,4},{6,5},{7,6},{0,7},{9,8},{10,9},{11,1... | collective-permute-start | bytes 73736 | tf_op jit(solution)/shard_map/while/body/eval_jaxpr/ppermute | solution.py:25
  405.1 9.9 %collective-permute-start.2 = (f32[3,2,8,128]{3,2,1,0:T(8,128)S(1)}, f32[3,2,8,128]{3,2,1,0:T(8,128)S(1)}, u32[]{:S(2)}, u32[]{:S(2)}) collective-permute-start(f32[3,2,8,128]{3,2,1,0:T(8,128)S(1)} %get-tuple-element.453), channel_id=1, source_target_pairs={{1,0},{2,1},{3,2},{4,3},{5,4},{6,5},{7,6},{0,7},{9,8},{10,9},{11,1... | collective-permute-start | bytes 73736 | tf_op jit(solution)/shard_map/while/body/eval_jaxpr/ppermute | solution.py:25
  442.7 9.9 %collective-permute-start.2 = (f32[3,2,8,128]{3,2,1,0:T(8,128)S(1)}, f32[3,2,8,128]{3,2,1,0:T(8,128)S(1)}, u32[]{:S(2)}, u32[]{:S(2)}) collective-permute-start(f32[3,2,8,128]{3,2,1,0:T(8,128)S(1)} %get-tuple-element.453), channel_id=1, source_target_pairs={{1,0},{2,1},{3,2},{4,3},{5,4},{6,5},{7,6},{0,7},{9,8},{10,9},{11,1... | collective-permute-start | bytes 73736 | tf_op jit(solution)/shard_map/while/body/eval_jaxpr/ppermute | solution.py:25
  706.1 10.3 %collective-permute-start.2 = (f32[3,2,8,128]{3,2,1,0:T(8,128)S(1)}, f32[3,2,8,128]{3,2,1,0:T(8,128)S(1)}, u32[]{:S(2)}, u32[]{:S(2)}) collective-permute-start(f32[3,2,8,128]{3,2,1,0:T(8,128)S(1)} %get-tuple-element.453), channel_id=1, source_target_pairs={{1,0},{2,1},{3,2},{4,3},{5,4},{6,5},{7,6},{0,7},{9,8},{10,9},{11,1... | collective-permute-start | bytes 73736 | tf_op jit(solution)/shard_map/while/body/eval_jaxpr/ppermute | solution.py:25
  718.2 14.2 %collective-permute-start.21 = (f32[3,16,32,128]{3,2,1,0:T(8,128)S(1)}, f32[3,16,32,128]{3,2,1,0:T(8,128)S(1)}, u32[]{:S(2)}, u32[]{:S(2)}) collective-permute-start(f32[3,16,32,128]{3,2,1,0:T(8,128)S(1)} %fusion.22), channel_id=1, source_target_pairs={{0,8},{8,16},{16,24},{24,32},{32,40},{40,48},{48,56},{56,64},{64,7... | collective-permute-start | bytes 2359304 | tf_op jit(solution)/shard_map/ppermute | solution.py:40
  (95 other events, 729.1 us)
where the time goes:
time: 734 us; the launch traced here: 733 us
  waiting for transfers between devices  518 us (71%)
  starting transfers between devices  166 us (23%)
  other arithmetic  20.5 us (3%)
  matrix products  12.7 us (2%)
  local copies, waits for them, and re-layouts  12.1 us (2%)
    ppermute x40, waiting for transfers between devices, with_halo(): lax.ppermute(head, axis, [((i + 1) % count, i) for i in range(count)])  241 us
    ppermute x31, waiting for transfers between devices, from_behind(): return lax.ppermute(block, axis, route)  192 us
    ppermute x40, starting transfers between devices, with_halo(): lax.ppermute(head, axis, [((i + 1) % count, i) for i in range(count)])  72.5 us
    ppermute x40, waiting for transfers between devices, with_halo(): lax.ppermute(tail, axis, [(i, (i + 1) % count) for i in range(count)])  71.1 us
    ppermute x31, starting transfers between devices, from_behind(): return lax.ppermute(block, axis, route)  59.5 us
    ppermute x40, starting transfers between devices, with_halo(): lax.ppermute(tail, axis, [(i, (i + 1) % count) for i in range(count)])  34.2 us
  transfers between devices with their start and end apart: 112, of which 109 were waited for; matrix products, arithmetic and copies ran while one was open for 0% of the time, Pallas kernels for 0%

commit v1 on v0

v1 whole, which is shorter than its diff:
```python
import jax
import jax.numpy as jnp
from jax import lax
from jax.experimental import pallas as pl
from jax.experimental.pallas import tpu as pltpu
from jax.sharding import Mesh
from jax.sharding import PartitionSpec as P

AXES = ("x", "zl", "c", "zh", "y")
SIZES = (4, 4, 2, 2, 4)
TM = ("x", "zl", "c")
SPACE = ("zh", "y")
PLANE = ("zl", "zh", "y")

VMEM = pl.BlockSpec(memory_space=pltpu.VMEM)
SMEM = pl.BlockSpec(memory_space=pltpu.SMEM)
PARAMS = pltpu.CompilerParams(vmem_limit_bytes=40 * 1024 * 1024)

HALO = 8
WIDE = 16 + 2 * HALO


def ring(size, by):
    return [(i, (i + by) % size) for i in range(size)]


def y_next(q):
    return pltpu.roll(q, q.shape[0] - 1, 0)


def y_prev(q):
    return pltpu.roll(q, 1, 0)


def fine_steps(bufs, strat, half_spin, lane_weight):
    def spread(q):
        diff = (pltpu.roll(q, 127, 1) - q) * lane_weight
        return diff - pltpu.roll(diff, 1, 1)

    for step in range(4):
        src, dst = bufs[step % 2], bufs[(step + 1) % 2]
        reach = 2 * (3 - step)
        first = HALO - reach
        count = 16 + 2 * reach

        def zonal(x, src=src):
            u = src[0, x]
            sides = src[0, x + 1] + src[0, x - 1] + (y_next(u) + y_prev(u))
            push = src[2, x + 1] - src[2, x - 1]
            return (
                (0.8 * u + spread(u))
                + (half_spin[...] * src[1, x] - 0.25 * push)
                + 0.05 * sides
            )

        def chunk(i, carry, src=src, dst=dst, first=first, zonal=zonal):
            before, here = carry
            for k in range(4):
                x = first + 4 * i + k
                after = zonal(x + 1)
                dst[0, x] = here
                v = src[1, x]
                b = src[2, x]
                b_next, b_prev = y_next(b), y_prev(b)
                v_new = (
                    (0.8 * v + spread(v))
                    - (half_spin[...] * here + 0.25 * (b_next - b_prev))
                    + 0.05 * (src[1, x + 1] + src[1, x - 1] + (y_next(v) + y_prev(v)))
                )
                dst[1, x] = v_new
                flow = (after - before) + (y_next(v_new) - y_prev(v_new))
                dst[2, x] = (
                    (0.8 * b + spread(b))
                    - strat[x] * flow
                    + 0.05 * (src[2, x + 1] + src[2, x - 1] + (b_next + b_prev))
                )
                before, here = here, after
            return before, here

        lax.fori_loop(0, count // 4, chunk, (zonal(first - 1), zonal(first)))


def lane_weights():
    lane = lax.broadcasted_iota(jnp.int32, (32, 128), 1)
    return jnp.where(lane < 127, 0.15, 0.0).astype(jnp.float32)


def fill_strat(strat, left, own, right):
    for x in range(6):
        strat[HALO - 6 + x] = 0.25 * left[x]
        strat[HALO + 16 + x] = 0.25 * right[x]
    for x in range(16):
        strat[HALO + x] = 0.25 * own[x]


def first_half_kernel(spin, left, start, right, own_strat, low, high, one, two, strat):
    for k in range(3):
        for x in range(8):
            one[k, x] = left[8 * k + x]
            one[k, 24 + x] = right[8 * k + x]
        for x in range(16):
            one[k, 8 + x] = start[k, x]
    fill_strat(strat, left.at[pl.ds(24, 6)], own_strat, right.at[pl.ds(24, 6)])
    fine_steps((one, two), strat, spin, lane_weights())
    for k in range(3):
        for x in range(8):
            low[k, x] = one[k, 8 + x]
            high[k, x] = one[k, 16 + x]


def second_half_kernel(
    spin, left, low, high, right, left_first, right_first, own_strat, next_mean, strat_tile,
    detail, payload, one, two, strat, rows,
):
    for k in range(3):
        for x in range(8):
            one[k, x] = left[k, x]
            one[k, 8 + x] = low[k, x]
            one[k, 16 + x] = high[k, x]
            one[k, 24 + x] = right[k, x]
    fill_strat(strat, left_first.at[pl.ds(24, 6)], own_strat, right_first.at[pl.ds(24, 6)])
    fine_steps((one, two), strat, spin, lane_weights())
    for k in range(3):
        for cell in range(4):
            x = HALO + 4 * cell
            slot = (4 * k + cell) % 2
            rows[slot] = (one[k, x] + one[k, x + 1]) + (one[k, x + 2] + one[k, x + 3])
            parts = [rows[slot, pl.ds(j, 8, stride=4), :] for j in range(4)]
            mean = ((parts[0] + parts[1]) + (parts[2] + parts[3])) * 0.0625
            payload[4 * k + cell] = mean - next_mean[k, cell]
            for j in range(4):
                rows[2 + slot, pl.ds(j, 8, stride=4), :] = mean
            for j in range(4):
                detail[k, 4 * cell + j] = one[k, x + j] - rows[2 + slot]
    payload[12] = strat_tile[...]


def coarse_step(state, halves, blocks, spin, strat, added=None):
    zonal, meridional = {}, {}

    def half_zonal(x):
        x = x % 32
        if x not in zonal:
            push = state[2, (x + 1) % 32] - state[2, (x - 1) % 32]
            zonal[x] = state[0, x] + spin * state[1, x] - 0.5 * push
        return zonal[x]

    def half_meridional(x):
        b = state[2, x]
        return state[1, x] - spin * half_zonal(x) - 0.5 * (y_next(b) - y_prev(b))

    def keep(k, pair, value):
        top = value.astype(jnp.bfloat16)
        rest = (value - top.astype(jnp.float32)).astype(jnp.bfloat16)
        halves[k, pl.ds(16 * pair, 16), pl.ds(0, 128)] = top
        halves[k, pl.ds(16 * pair, 16), pl.ds(128, 128)] = rest

    for pair in range(16):
        columns = [[], [], []]
        for x in (2 * pair, 2 * pair + 1):
            u = half_zonal(x)
            v = half_meridional(x)
            flow = (half_zonal(x + 1) - half_zonal(x - 1)) + (y_next(v) - y_prev(v))
            columns[0].append(u)
            columns[1].append(v)
            columns[2].append(state[2, x] - strat[x] * flow)
        for k in range(3):
            keep(k, pair, jnp.concatenate(columns[k], axis=0))
    for k in range(3):
        wide = jnp.dot(halves[k], blocks[k], preferred_element_type=jnp.float32)
        image = (wide[:, :128] + wide[:, 128:]).reshape(32, 8, 128)
        for x in range(32):
            tile = image[x]
            state[k, x] = tile if added is None else tile + added(k, x)


def chosen(mine, other, core, turn):
    run = turn // 2
    is_mine = jnp.full((8, 128), turn % 2 - core, jnp.int32) == 0

    def tile(k, x):
        place, row = 8 * run + x // 4, 4 * k + x % 4
        return jnp.where(is_mine, mine[place, row], other[place, row])

    return tile


def plane_kernel(where, spin, blocks, mine, other, end, part, strat, state, halves):
    core = where[0]
    for x in range(32):
        strat[x] = 0.5 * mine[8 * (x % 4) + x // 4, 12]
    start = chosen(mine, other, core, 0)
    for k in range(3):
        for x in range(32):
            state[k, x] = start(k, x)

    def turn(i, carry):
        coarse_step(state, halves, blocks, spin[...], strat, chosen(mine, other, core, i))
        return carry

    lax.fori_loop(1, 8, turn, 0)
    for k in range(3):
        for x in range(32):
            end[k, x] = state[k, x]
        part[k] = state[k, pl.ds(16 * core, 16)]


def final_kernel(
    where, spin, blocks, mine, other, strat, end, here, there, detail, mean, out,
    ends, state, halves, rows,
):
    core, row, turns, block = where[0], where[1], where[2], where[3]
    groups = jnp.where((row == 0) & (turns == 0), 4, row)
    for k in range(3):
        for x in range(32):
            ends[0, k, x] = end[k, x]
    for j in range(3):
        for k in range(3):
            ends[j + 1, k, pl.ds(16 * core, 16)] = here[j, k]
            ends[j + 1, k, pl.ds(16 * (1 - core), 16)] = there[j, k]

    scale = jnp.where(groups > 0, 1.0, 0.0).astype(jnp.float32)
    first = row % 4
    for k in range(3):
        for x in range(32):
            state[k, x] = ends[first, k, x] * scale

    def group(g, carry):
        def plain(i, inner):
            coarse_step(state, halves, blocks, spin[...], strat)
            return inner

        lax.fori_loop(0, 8, plain, 0)
        place = (row - g + 4) % 4
        for k in range(3):
            for x in range(32):
                state[k, x] = state[k, x] + ends[place, k, x]
        return carry

    lax.fori_loop(1, groups, group, 0)

    def turn(i, carry):
        coarse_step(state, halves, blocks, spin[...], strat, chosen(mine, other, core, i))
        return carry

    lax.fori_loop(0, turns, turn, 0)

    for k in range(3):
        for cell in range(4):
            slot = (4 * k + cell) % 2
            value = state[k, 4 * block + cell] + mean[k, cell]
            for j in range(4):
                rows[slot, pl.ds(j, 8, stride=4), :] = value
            for j in range(4):
                out[k, 4 * cell + j] = detail[k, 4 * cell + j] + rows[slot]


def call(kernel, outs, scratch, scalars=0):
    f32 = jnp.float32

    def run(*args):
        return pl.pallas_call(
            kernel,
            out_shape=[jax.ShapeDtypeStruct(shape, f32) for shape in outs],
            in_specs=[SMEM] * scalars + [VMEM] * (len(args) - scalars),
            out_specs=[VMEM] * len(outs),
            scratch_shapes=[pltpu.VMEM(shape, kind) for shape, kind in scratch],
            compiler_params=PARAMS,
        )(*args)

    return run


def restrict(state):
    kinds, across, along, levels = state.shape
    return state.reshape(kinds, across // 4, 4, along // 4, 4, levels).mean(axis=(2, 4))


def per_device(slice_starts, coriolis, stratification, inverse_blocks):
    f32, bf16 = jnp.float32, jnp.bfloat16
    start = slice_starts[0]
    fine_scratch = [((3, WIDE, 32, 128), f32)] * 2 + [((WIDE, 32, 128), f32)]
    chain_scratch = [((3, 32, 8, 128), f32), ((3, 256, 256), bf16)]

    head = jnp.concatenate([start[:, :8].reshape(24, 32, 128), stratification[:6]])
    tail = jnp.concatenate([start[:, 8:].reshape(24, 32, 128), stratification[10:]])
    left = lax.ppermute(tail, SPACE, ring(8, 1))
    right = lax.ppermute(head, SPACE, ring(8, -1))
    mean = restrict(start)
    next_mean = lax.ppermute(mean, TM, ring(32, -1))

    run, core = lax.axis_index("zl"), lax.axis_index("c")
    where = jnp.stack(
        [core, lax.axis_index("x"), 2 * run + core, lax.axis_index(SPACE)]
    ).astype(jnp.int32)
    half_spin = jnp.broadcast_to(0.5 * coriolis[:, None], (32, 128))
    coarse_spin = jnp.broadcast_to(4.0 * coriolis.reshape(8, 4).mean(axis=1)[:, None], (8, 128))
    strat_tile = lax.dynamic_index_in_dim(restrict(stratification[None])[0], run, 0, keepdims=False)
    turned = jnp.swapaxes(inverse_blocks, 1, 2)
    top = lax.reduce_precision(turned, exponent_bits=8, mantissa_bits=7)
    wide = jnp.concatenate([top, turned - top], axis=2).astype(bf16)
    blocks = jnp.concatenate([wide, wide], axis=1)

    low, high = call(first_half_kernel, [(3, 8, 32, 128)] * 2, fine_scratch)(
        half_spin, left, start, right, stratification
    )
    left_again = lax.ppermute(high, SPACE, ring(8, 1))
    right_again = lax.ppermute(low, SPACE, ring(8, -1))
    detail, payload = call(
        second_half_kernel,
        [(3, 16, 32, 128), (13, 8, 128)],
        fine_scratch + [((4, 32, 128), f32)],
    )(
        half_spin, left_again, low, high, right_again, left, right, stratification,
        next_mean, strat_tile,
    )

    mine = lax.all_to_all(jnp.broadcast_to(payload[None], (32, 13, 8, 128)), PLANE, 0, 0)
    other = lax.ppermute(mine, "c", ring(2, 1))
    detail = lax.ppermute(detail, TM, ring(32, 1))
    end, part, strat = call(
        plane_kernel, [(3, 32, 8, 128), (3, 16, 8, 128), (32, 8, 128)], chain_scratch, 1
    )(where, coarse_spin, blocks, mine, other)
    here = jnp.stack([lax.ppermute(part, "x", ring(4, by)) for by in (1, 2, 3)])
    there = lax.ppermute(here, "c", ring(2, 1))
    (out,) = call(
        final_kernel,
        [(3, 16, 32, 128)],
        [((4, 3, 32, 8, 128), f32)] + chain_scratch + [((2, 32, 128), f32)],
        1,
    )(where, coarse_spin, blocks, mine, other, strat, end, here, there, detail, mean)
    return out[None]


def solution(mesh):
    inner = Mesh(mesh.devices.reshape(SIZES), AXES)
    in_specs = (P(TM, None, SPACE, None, None), P(), P(SPACE, None, None), P())
    out_specs = P(TM, None, SPACE, None, None)
    return jax.shard_map(
        per_device, mesh=inner, in_specs=in_specs, out_specs=out_specs, check_vma=False
    )
```

time: 734 us -> 161 us (0.22)
  the two profiles are of different devices: /device:TPU:26 before, /device:TPU:24 now
where the time goes in v1:
time: 161 us; the launch traced here: 160 us
  blocking collectives  58.1 us (36%)
  waiting for transfers between devices  50.8 us (32%)
  Pallas kernels  24 us (15%)
  starting transfers between devices  20.8 us (13%)
  local copies, waits for them, and re-layouts  4.33 us (3%)
  other arithmetic  1.61 us (1%)
    all_to_all x1, blocking collectives, per_device(): lax.all_to_all(jnp.broadcast_to(payload[None], (32, 13, 8, 128)), PLANE,...  58.1 us
    pallas_call x4, Pallas kernels, run(): pl.pallas_call(kernel, out_shape=[jax.ShapeDtypeStruct(shape, f32) for sh...  24 us
    ppermute x3, waiting for transfers between devices, per_device(): here = jnp.stack([lax.ppermute(part, 'x', ring(4, by)) for by in (1, 2, 3)])  19.1 us
    ppermute x1, waiting for transfers between devices, per_device(): left = lax.ppermute(tail, SPACE, ring(8, 1))  13.1 us
    ppermute x1, waiting for transfers between devices, per_device(): right = lax.ppermute(head, SPACE, ring(8, -1))  8.49 us
    ppermute x1, waiting for transfers between devices, per_device(): next_mean = lax.ppermute(mean, TM, ring(32, -1))  7.53 us
    ppermute x1, starting transfers between devices, per_device(): next_mean = lax.ppermute(mean, TM, ring(32, -1))  7.07 us
    ppermute x1, starting transfers between devices, per_device(): left = lax.ppermute(tail, SPACE, ring(8, 1))  6.93 us
  transfers between devices with their start and end apart: 11, of which 8 were waited for; matrix products, arithmetic and copies ran while one was open for 2% of the time, Pallas kernels for 0%

profile of v1, /device:TPU:24, one launch (start us, length us, event | category | flops | bytes accessed | tf_op | source)
XLA Modules:
  0.0 159.8 jit_solution(9665156385810796097)
XLA Ops:
  0.0 1.0 fusion.3
  1.0 1.3 fusion.2
  2.3 6.9 %collective-permute-start = (f32[30,32,128]{2,1,0:T(8,128)S(1)}, f32[30,32,128]{2,1,0:T(8,128)S(1)}, u32[]{:S(2)}, u32[]{:S(2)}) collective-permute-start(f32[30,32,128]{2,1,0:T(8,128)S(1)} %pad_maximum_fusion.1), channel_id=1, source_target_pairs={{0,1},{1,2},{2,3},{3,4},{4,5},{5,6},{6,7},{7,0},{8,9},{9,10},{10,1... | collective-permute-start | bytes 1474568 | tf_op jit(solution)/shard_map/ppermute | solution.py:287
  9.4 13.1 %collective-permute-done.left.left_first = f32[30,32,128]{2,1,0:T(8,128)S(1)} collective-permute-done((f32[30,32,128]{2,1,0:T(8,128)S(1)}, f32[30,32,128]{2,1,0:T(8,128)S(1)}, u32[]{:S(2)}, u32[]{:S(2)}) %collective-permute-start) | collective-permute-done | bytes 491552 | tf_op jit(solution)/shard_map/ppermute | solution.py:287
  22.5 8.5 %collective-permute-done.1.right.right_first = f32[30,32,128]{2,1,0:T(8,128)S(1)} collective-permute-done((f32[30,32,128]{2,1,0:T(8,128)S(1)}, f32[30,32,128]{2,1,0:T(8,128)S(1)}, u32[]{:S(2)}, u32[]{:S(2)}) %collective-permute-start.1) | collective-permute-done | bytes 491552 | tf_op jit(solution)/shard_map/ppermute | solution.py:288
  31.0 5.5 %shard_map.46 = (f32[3,8,32,128]{3,2,1,0:T(8,128)S(1)}, f32[3,8,32,128]{3,2,1,0:T(8,128)S(1)}) custom-call(f32[32,128]{1,0:T(8,128)S(1)} %broadcast_in_dim.9.spin, f32[30,32,128]{2,1,0:T(8,128)S(1)} %collective-permute-done.left.left_first, f32[3,16,32,128]{3,2,1,0:T(8,128)S(1)} %bitcast.19, f32[30,32,128]{2,1,0:T(8,128)S(1)} %collective-permute-done.1.right.right_first, ...), custom_call_target="tpu_custom_call" | custom-call | tf_op jit(solution)/shard_map/pallas_call | solution.py:262
  36.8 1.9 %collective-permute-start.3 = (f32[3,8,32,128]{3,2,1,0:T(8,128)S(1)}, f32[3,8,32,128]{3,2,1,0:T(8,128)}, u32[]{:S(2)}, u32[]{:S(2)}) collective-permute-start(f32[3,8,32,128]{3,2,1,0:T(8,128)S(1)} %get-tuple-element.13.low), channel_id=1, source_target_pairs={{0,7},{1,0},{2,1},{3,2},{4,3},{5,4},{6,5},{7,6},{8,15},{9,8},{10,9... | collective-permute-start | bytes 1179656 | tf_op jit(solution)/shard_map/ppermute | solution.py:308
  38.7 0.2 reduce_sum.28
  38.9 7.1 %collective-permute-start.4 = (f32[3,4,8,128]{3,2,1,0:T(8,128)S(1)}, f32[3,4,8,128]{3,2,1,0:T(8,128)S(1)}, u32[]{:S(2)}, u32[]{:S(2)}) collective-permute-start(f32[3,4,8,128]{3,2,1,0:T(8,128)S(1)} %broadcast_multiply_fusion.mean), channel_id=1, source_target_pairs={{0,248},{8,0},{16,8},{24,16},{32,24},{40,32},{48,40},{56,48},{64,5... | collective-permute-start | bytes 147464 | tf_op jit(solution)/shard_map/ppermute | solution.py:290
  46.1 7.5 %collective-permute-done.4.next_mean = f32[3,4,8,128]{3,2,1,0:T(8,128)S(1)} collective-permute-done((f32[3,4,8,128]{3,2,1,0:T(8,128)S(1)}, f32[3,4,8,128]{3,2,1,0:T(8,128)S(1)}, u32[]{:S(2)}, u32[]{:S(2)}) %collective-permute-start.4) | collective-permute-done | bytes 49184 | tf_op jit(solution)/shard_map/ppermute | solution.py:290
  53.6 6.7 %shard_map.47 = (f32[3,16,32,128]{3,2,1,0:T(8,128)S(1)}, f32[13,8,128]{2,1,0:T(8,128)S(1)}) custom-call(f32[32,128]{1,0:T(8,128)S(1)} %broadcast_in_dim.9.spin, f32[3,8,32,128]{3,2,1,0:T(8,128)S(1)} %collective-permute-done.2.left, f32[3,8,32,128]{3,2,1,0:T(8,128)S(1)} %get-tuple-element.13.low, f32[3,8,32,128]{3,2,1,0:T(8,128)S(1)} %get-tuple-element.12.high, ...), custom_call_target="tpu_custom_call" | custom-call | tf_op jit(solution)/shard_map/pallas_call | solution.py:262
  60.5 58.1 %all_to_all.5.mine = f32[32,13,8,128]{3,2,1,0:T(8,128)S(1)} all-to-all(f32[32,13,8,128]{3,2,1,0:T(8,128)S(1)} %broadcast_in_dim.10), channel_id=1, replica_groups=mesh['x'=4,'zl'=4,'c'=2,'zh'=2,'y'=4] {'zl','zh','y'}, dimensions={0} | all-to-all | bytes 3407872 | tf_op jit(solution)/shard_map/all_to_all | solution.py:318
  118.7 1.7 %copy.6 = f32[3,128,128]{1,2,0:T(8,128)} copy(f32[3,128,128]{2,1,0:T(8,128)} %param.7) | data formatting | bytes 393216 | tf_op args[3]
  120.6 1.0 reduce-precision_convert_fusion
  121.6 0.6 collective-permute-done.5.other
  122.2 2.8 %shard_map.48 = (f32[3,32,8,128]{3,2,1,0:T(8,128)S(1)}, f32[3,16,8,128]{3,2,1,0:T(8,128)S(1)}, f32[32,8,128]{2,1,0:T(8,128)S(1)}) custom-call(s32[4]{0:T(128)S(1)} %pad_add_fusion.where, f32[8,128]{1,0:T(8,128)S(1)} %broadcast_in_dim.8.spin, bf16[3,256,256]{2,1,0:T(8,128)(2,1)S(1)} %maximum_maximum_fusion.blocks, f32[32,13,8,128]{3,2,1,0:T(8,128)S(1)} %all_to_all.5.mine, ...), custom_call_target="tpu_custom_call" | custom-call | tf_op jit(solution)/shard_map/pallas_call | solution.py:262
  125.0 2.8 %collective-permute-start.8 = (f32[3,16,8,128]{3,2,1,0:T(8,128)S(1)}, f32[3,16,8,128]{3,2,1,0:T(8,128)S(1)}, u32[]{:S(2)}, u32[]{:S(2)}) collective-permute-start(f32[3,16,8,128]{3,2,1,0:T(8,128)S(1)} %get-tuple-element.17), channel_id=1, source_target_pairs={{0,192},{64,0},{128,64},{192,128},{1,193},{65,1},{129,65},{193,129... | collective-permute-start | bytes 589832 | tf_op jit(solution)/shard_map/ppermute | solution.py:324
  127.8 0.8 collective-permute-start.7
  128.6 0.9 collective-permute-start.6
  129.5 7.0 %collective-permute-done.8 = f32[3,16,8,128]{3,2,1,0:T(8,128)S(1)} collective-permute-done((f32[3,16,8,128]{3,2,1,0:T(8,128)S(1)}, f32[3,16,8,128]{3,2,1,0:T(8,128)S(1)}, u32[]{:S(2)}, u32[]{:S(2)}) %collective-permute-start.8) | collective-permute-done | bytes 196640 | tf_op jit(solution)/shard_map/ppermute | solution.py:324
  136.5 9.0 %collective-permute-done.7 = f32[3,16,8,128]{3,2,1,0:T(8,128)S(1)} collective-permute-done((f32[3,16,8,128]{3,2,1,0:T(8,128)S(1)}, f32[3,16,8,128]{3,2,1,0:T(8,128)S(1)}, u32[]{:S(2)}, u32[]{:S(2)}) %collective-permute-start.7) | collective-permute-done | bytes 196640 | tf_op jit(solution)/shard_map/ppermute | solution.py:324
  145.6 3.0 %collective-permute-done.6 = f32[3,16,8,128]{3,2,1,0:T(8,128)S(1)} collective-permute-done((f32[3,16,8,128]{3,2,1,0:T(8,128)S(1)}, f32[3,16,8,128]{3,2,1,0:T(8,128)S(1)}, u32[]{:S(2)}, u32[]{:S(2)}) %collective-permute-start.6) | collective-permute-done | bytes 196640 | tf_op jit(solution)/shard_map/ppermute | solution.py:324
  148.8 2.0 %collective-permute-done.9.there = f32[3,3,16,8,128]{4,3,2,1,0:T(8,128)S(1)} collective-permute-done((f32[3,3,16,8,128]{4,3,2,1,0:T(8,128)S(1)}, f32[3,3,16,8,128]{4,3,2,1,0:T(8,128)S(1)}, u32[]{:S(2)}, u32[]{:S(2)}) %collective-permute-start.9) | collective-permute-done | bytes 589856 | tf_op jit(solution)/shard_map/ppermute | solution.py:325
  150.7 9.0 %shard_map.49 = f32[3,16,32,128]{3,2,1,0:T(8,128)} custom-call(s32[4]{0:T(128)S(1)} %pad_add_fusion.where, f32[8,128]{1,0:T(8,128)S(1)} %broadcast_in_dim.8.spin, bf16[3,256,256]{2,1,0:T(8,128)(2,1)S(1)} %maximum_maximum_fusion.blocks, f32[32,13,8,128]{3,2,1,0:T(8,128)S(1)} %all_to_all.5.mine, f32[32,13,8,128]{3,2,1,0:T(8,128)S(1)} %collective-permute-done.5.other, ...), custom_call_target="tpu_custom_call" | custom-call | tf_op jit(solution)/shard_map/pallas_call | solution.py:262
  (32 shorter events, 1.2 us)
Async XLA Ops:
  1.0 8.4 %copy-start.4 = (f32[32]{0:T(128)S(1)}, f32[32]{0:T(128)}, u32[]{:S(2)}) copy-start(f32[32]{0:T(128)} %param.5) | copy-start | bytes 388
  1.0 30.1 %copy-start = (f32[1,3,16,32,128]{4,3,2,1,0:T(8,128)S(1)}, f32[1,3,16,32,128]{4,3,2,1,0:T(8,128)}, u32[]{:S(2)}) copy-start(f32[1,3,16,32,128]{4,3,2,1,0:T(8,128)} %param.4) | copy-start | bytes 2359300
  1.0 30.0 %copy-start.1 = (f32[16,32,128]{2,1,0:T(8,128)S(1)}, f32[16,32,128]{2,1,0:T(8,128)}, u32[]{:S(2)}) copy-start(f32[16,32,128]{2,1,0:T(8,128)} %own_strat.3) | copy-start | bytes 786436
  2.3 20.1 %collective-permute-start = (f32[30,32,128]{2,1,0:T(8,128)S(1)}, f32[30,32,128]{2,1,0:T(8,128)S(1)}, u32[]{:S(2)}, u32[]{:S(2)}) collective-permute-start(f32[30,32,128]{2,1,0:T(8,128)S(1)} %pad_maximum_fusion.1), channel_id=1, source_target_pairs={{0,1},{1,2},{2,3},{3,4},{4,5},{5,6},{6,7},{7,0},{8,9},{9,10},{10,1... | collective-permute-start | bytes 1474568 | tf_op jit(solution)/shard_map/ppermute | solution.py:287
  9.3 21.7 %collective-permute-start.1 = (f32[30,32,128]{2,1,0:T(8,128)S(1)}, f32[30,32,128]{2,1,0:T(8,128)S(1)}, u32[]{:S(2)}, u32[]{:S(2)}) collective-permute-start(f32[30,32,128]{2,1,0:T(8,128)S(1)} %pad_maximum_fusion.2), channel_id=1, source_target_pairs={{0,7},{1,0},{2,1},{3,2},{4,3},{5,4},{6,5},{7,6},{8,15},{9,8},{10,9... | collective-permute-start | bytes 1474568 | tf_op jit(solution)/shard_map/ppermute | solution.py:288
  36.6 17.0 %collective-permute-start.2 = (f32[3,8,32,128]{3,2,1,0:T(8,128)S(1)}, f32[3,8,32,128]{3,2,1,0:T(8,128)S(1)}, u32[]{:S(2)}, u32[]{:S(2)}) collective-permute-start(f32[3,8,32,128]{3,2,1,0:T(8,128)S(1)} %get-tuple-element.12.high), channel_id=1, source_target_pairs={{0,1},{1,2},{2,3},{3,4},{4,5},{5,6},{6,7},{7,0},{8,9},{9,10},{10,1... | collective-permute-start | bytes 1179656 | tf_op jit(solution)/shard_map/ppermute | solution.py:307
  36.8 16.8 %collective-permute-start.3 = (f32[3,8,32,128]{3,2,1,0:T(8,128)S(1)}, f32[3,8,32,128]{3,2,1,0:T(8,128)}, u32[]{:S(2)}, u32[]{:S(2)}) collective-permute-start(f32[3,8,32,128]{3,2,1,0:T(8,128)S(1)} %get-tuple-element.13.low), channel_id=1, source_target_pairs={{0,7},{1,0},{2,1},{3,2},{4,3},{5,4},{6,5},{7,6},{8,15},{9,8},{10,9... | collective-permute-start | bytes 1179656 | tf_op jit(solution)/shard_map/ppermute | solution.py:308
  38.9 14.7 %collective-permute-start.4 = (f32[3,4,8,128]{3,2,1,0:T(8,128)S(1)}, f32[3,4,8,128]{3,2,1,0:T(8,128)S(1)}, u32[]{:S(2)}, u32[]{:S(2)}) collective-permute-start(f32[3,4,8,128]{3,2,1,0:T(8,128)S(1)} %broadcast_multiply_fusion.mean), channel_id=1, source_target_pairs={{0,248},{8,0},{16,8},{24,16},{32,24},{40,32},{48,40},{56,48},{64,5... | collective-permute-start | bytes 147464 | tf_op jit(solution)/shard_map/ppermute | solution.py:290
  60.3 58.2 %copy-start.2 = (f32[3,16,32,128]{3,2,1,0:T(8,128)}, f32[3,16,32,128]{3,2,1,0:T(8,128)S(1)}, u32[]{:S(2)}) copy-start(f32[3,16,32,128]{3,2,1,0:T(8,128)S(1)} %get-tuple-element.18) | copy-start | bytes 2359300
  118.5 3.6 %collective-permute-start.5 = (f32[32,13,8,128]{3,2,1,0:T(8,128)S(1)}, f32[32,13,8,128]{3,2,1,0:T(8,128)S(1)}, u32[]{:S(2)}, u32[]{:S(2)}) collective-permute-start(f32[32,13,8,128]{3,2,1,0:T(8,128)S(1)} %all_to_all.5.mine), channel_id=1, source_target_pairs={{0,8},{8,0},{1,9},{9,1},{2,10},{10,2},{3,11},{11,3},{4,12},{12,4},... | collective-permute-start | bytes 5111816 | tf_op jit(solution)/shard_map/ppermute | solution.py:319
  122.2 7.3 %copy-start.3 = (f32[3,16,32,128]{3,2,1,0:T(8,128)S(1)}, f32[3,16,32,128]{3,2,1,0:T(8,128)}, u32[]{:S(2)}) copy-start(f32[3,16,32,128]{3,2,1,0:T(8,128)} %copy-done.2) | copy-start | bytes 2359300
  125.0 11.5 %collective-permute-start.8 = (f32[3,16,8,128]{3,2,1,0:T(8,128)S(1)}, f32[3,16,8,128]{3,2,1,0:T(8,128)S(1)}, u32[]{:S(2)}, u32[]{:S(2)}) collective-permute-start(f32[3,16,8,128]{3,2,1,0:T(8,128)S(1)} %get-tuple-element.17), channel_id=1, source_target_pairs={{0,192},{64,0},{128,64},{192,128},{1,193},{65,1},{129,65},{193,129... | collective-permute-start | bytes 589832 | tf_op jit(solution)/shard_map/ppermute | solution.py:324
  127.8 17.8 %collective-permute-start.7 = (f32[3,16,8,128]{3,2,1,0:T(8,128)S(1)}, f32[3,16,8,128]{3,2,1,0:T(8,128)S(1)}, u32[]{:S(2)}, u32[]{:S(2)}) collective-permute-start(f32[3,16,8,128]{3,2,1,0:T(8,128)S(1)} %get-tuple-element.17), channel_id=1, source_target_pairs={{0,128},{64,192},{128,0},{192,64},{1,129},{65,193},{129,1},{193,65... | collective-permute-start | bytes 589832 | tf_op jit(solution)/shard_map/ppermute | solution.py:324
  128.6 20.0 %collective-permute-start.6 = (f32[3,16,8,128]{3,2,1,0:T(8,128)S(1)}, f32[3,16,8,128]{3,2,1,0:T(8,128)S(1)}, u32[]{:S(2)}, u32[]{:S(2)}) collective-permute-start(f32[3,16,8,128]{3,2,1,0:T(8,128)S(1)} %get-tuple-element.17), channel_id=1, source_target_pairs={{0,64},{64,128},{128,192},{192,0},{1,65},{65,129},{129,193},{193,1... | collective-permute-start | bytes 589832 | tf_op jit(solution)/shard_map/ppermute | solution.py:324
  129.5 19.3 %collective-permute-start.10 = (f32[3,16,32,128]{3,2,1,0:T(8,128)S(1)}, f32[3,16,32,128]{3,2,1,0:T(8,128)S(1)}, u32[]{:S(2)}, u32[]{:S(2)}) collective-permute-start(f32[3,16,32,128]{3,2,1,0:T(8,128)S(1)} %copy-done.3), channel_id=1, source_target_pairs={{0,8},{8,16},{16,24},{24,32},{32,40},{40,48},{48,56},{56,64},{64,7... | collective-permute-start | bytes 2359304 | tf_op jit(solution)/shard_map/ppermute | solution.py:320
  148.7 2.1 %collective-permute-start.9 = (f32[3,3,16,8,128]{4,3,2,1,0:T(8,128)S(1)}, f32[3,3,16,8,128]{4,3,2,1,0:T(8,128)S(1)}, u32[]{:S(2)}, u32[]{:S(2)}) collective-permute-start(f32[3,3,16,8,128]{4,3,2,1,0:T(8,128)S(1)} %pad_maximum_fusion.here), channel_id=1, source_target_pairs={{0,8},{8,0},{1,9},{9,1},{2,10},{10,2},{3,11},{11,3},{4,12},{12,4},... | collective-permute-start | bytes 1769480 | tf_op jit(solution)/shard_map/ppermute | solution.py:325

commit v2 on v1

--- a/solution.py
+++ b/solution.py
@@ -10,7 +10,6 @@
 SIZES = (4, 4, 2, 2, 4)
 TM = ("x", "zl", "c")
 SPACE = ("zh", "y")
-PLANE = ("zl", "zh", "y")
 
 VMEM = pl.BlockSpec(memory_space=pltpu.VMEM)
 SMEM = pl.BlockSpec(memory_space=pltpu.SMEM)
@@ -109,7 +108,7 @@
 
 
 def second_half_kernel(
-    spin, left, low, high, right, left_first, right_first, own_strat, next_mean, strat_tile,
+    spin, left, low, high, right, left_first, right_first, own_strat, next_mean,
     detail, payload, one, two, strat, rows,
 ):
     for k in range(3):
@@ -132,10 +131,9 @@
                 rows[2 + slot, pl.ds(j, 8, stride=4), :] = mean
             for j in range(4):
                 detail[k, 4 * cell + j] = one[k, x + j] - rows[2 + slot]
-    payload[12] = strat_tile[...]
-
-
-def coarse_step(state, halves, blocks, spin, strat, added=None):
+
+
+def coarse_step(state, halves, blocks, spin, strat):
     zonal, meridional = {}, {}
 
     def half_zonal(x):
@@ -170,32 +168,46 @@
         wide = jnp.dot(halves[k], blocks[k], preferred_element_type=jnp.float32)
         image = (wide[:, :128] + wide[:, 128:]).reshape(32, 8, 128)
         for x in range(32):
-            tile = image[x]
-            state[k, x] = tile if added is None else tile + added(k, x)
-
-
-def chosen(mine, other, core, turn):
-    run = turn // 2
-    is_mine = jnp.full((8, 128), turn % 2 - core, jnp.int32) == 0
-
-    def tile(k, x):
-        place, row = 8 * run + x // 4, 4 * k + x % 4
-        return jnp.where(is_mine, mine[place, row], other[place, row])
-
-    return tile
-
-
-def plane_kernel(where, spin, blocks, mine, other, end, part, strat, state, halves):
-    core = where[0]
-    for x in range(32):
-        strat[x] = 0.5 * mine[8 * (x % 4) + x // 4, 12]
-    start = chosen(mine, other, core, 0)
-    for k in range(3):
-        for x in range(32):
-            state[k, x] = start(k, x)
+            state[k, x] = image[x]
+
+
+def table(where, increments, mine, other):
+    for j in range(4):
+        run = (where[0] - j + 4) % 4
+        for n in range(12):
+            increments[2 * run + where[1], n] = mine[j][n]
+            increments[2 * run + 1 - where[1], n] = other[j][n]
+
+
+def add_block(state, increments, turn, block):
+    for k in range(3):
+        for cell in range(4):
+            place = 4 * block + cell
+            state[k, place] = state[k, place] + increments[turn, 4 * k + cell]
+
+
+def clear(state):
+    for k in range(3):
+        for x in range(32):
+            state[k, x] = jnp.zeros((8, 128), jnp.float32)
+
+
+def plane_kernel(where, spin, blocks, strat_mine, strat_other, *refs):
+    mine, other, (end, part, strat, state, halves, increments) = refs[:4], refs[4:8], refs[8:]
+    core, zh, y = where[1], where[3], where[4]
+    for j in range(4):
+        column = (y - j + 4) % 4
+        for cell in range(4):
+            strat[4 * (4 * zh + column) + cell] = 0.5 * strat_mine[j, cell]
+            strat[4 * (4 * (1 - zh) + column) + cell] = 0.5 * strat_other[j, cell]
+    table(where, increments, mine, other)
+    clear(state)
+    block = 4 * zh + y
+    add_block(state, increments, 0, block)
 
     def turn(i, carry):
-        coarse_step(state, halves, blocks, spin[...], strat, chosen(mine, other, core, i))
+        coarse_step(state, halves, blocks, spin[...], strat)
+        add_block(state, increments, i, block)
         return carry
 
     lax.fori_loop(1, 8, turn, 0)
@@ -205,25 +217,25 @@
         part[k] = state[k, pl.ds(16 * core, 16)]
 
 
-def final_kernel(
-    where, spin, blocks, mine, other, strat, end, here, there, detail, mean, out,
-    ends, state, halves, rows,
-):
-    core, row, turns, block = where[0], where[1], where[2], where[3]
+def chain_kernel(where, spin, blocks, strat, end, *refs):
+    mine, other, here, there = refs[:4], refs[4:8], refs[8:11], refs[11:14]
+    parts, (ends, state, halves, increments) = refs[14:18], refs[18:]
+    run, core, row, zh, y = where[0], where[1], where[2], where[3], where[4]
+    turns = 2 * run + core
     groups = jnp.where((row == 0) & (turns == 0), 4, row)
+    table(where, increments, mine, other)
     for k in range(3):
         for x in range(32):
             ends[0, k, x] = end[k, x]
     for j in range(3):
         for k in range(3):
-            ends[j + 1, k, pl.ds(16 * core, 16)] = here[j, k]
-            ends[j + 1, k, pl.ds(16 * (1 - core), 16)] = there[j, k]
+            ends[j + 1, k, pl.ds(16 * core, 16)] = here[j][k]
+            ends[j + 1, k, pl.ds(16 * (1 - core), 16)] = there[j][k]
 
     scale = jnp.where(groups > 0, 1.0, 0.0).astype(jnp.float32)
-    first = row % 4
-    for k in range(3):
-        for x in range(32):
-            state[k, x] = ends[first, k, x] * scale
+    for k in range(3):
+        for x in range(32):
+            state[k, x] = ends[row, k, x] * scale
 
     def group(g, carry):
         def plain(i, inner):
@@ -238,17 +250,30 @@
         return carry
 
     lax.fori_loop(1, groups, group, 0)
+    block = 4 * zh + y
 
     def turn(i, carry):
-        coarse_step(state, halves, blocks, spin[...], strat, chosen(mine, other, core, i))
+        coarse_step(state, halves, blocks, spin[...], strat)
+        add_block(state, increments, i, block)
         return carry
 
     lax.fori_loop(0, turns, turn, 0)
 
+    for j in range(4):
+        column = (y + j) % 4
+        for half in range(2):
+            side = zh if half == 0 else 1 - zh
+            for k in range(3):
+                for cell in range(4):
+                    parts[j][half, 4 * k + cell] = state[k, 4 * (4 * side + column) + cell]
+
+
+def final_kernel(kept, sent, detail, mean, out, rows):
     for k in range(3):
         for cell in range(4):
-            slot = (4 * k + cell) % 2
-            value = state[k, 4 * block + cell] + mean[k, cell]
+            n = 4 * k + cell
+            slot = n % 2
+            value = kept[n] + sent[n] + mean[k, cell]
             for j in range(4):
                 rows[slot, pl.ds(j, 8, stride=4), :] = value
             for j in range(4):
@@ -280,7 +305,7 @@
     f32, bf16 = jnp.float32, jnp.bfloat16
     start = slice_starts[0]
     fine_scratch = [((3, WIDE, 32, 128), f32)] * 2 + [((WIDE, 32, 128), f32)]
-    chain_scratch = [((3, 32, 8, 128), f32), ((3, 256, 256), bf16)]
+    chain_scratch = [((3, 32, 8, 128), f32), ((3, 256, 256), bf16), ((8, 12, 8, 128), f32)]
 
     head = jnp.concatenate([start[:, :8].reshape(24, 32, 128), stratification[:6]])
     tail = jnp.concatenate([start[:, 8:].reshape(24, 32, 128), stratification[10:]])
@@ -289,46 +314,53 @@
     mean = restrict(start)
     next_mean = lax.ppermute(mean, TM, ring(32, -1))
 
-    run, core = lax.axis_index("zl"), lax.axis_index("c")
-    where = jnp.stack(
-        [core, lax.axis_index("x"), 2 * run + core, lax.axis_index(SPACE)]
-    ).astype(jnp.int32)
+    where = jnp.stack([lax.axis_index(name) for name in ("zl", "c", "x", "zh", "y")]).astype(jnp.int32)
     half_spin = jnp.broadcast_to(0.5 * coriolis[:, None], (32, 128))
     coarse_spin = jnp.broadcast_to(4.0 * coriolis.reshape(8, 4).mean(axis=1)[:, None], (8, 128))
-    strat_tile = lax.dynamic_index_in_dim(restrict(stratification[None])[0], run, 0, keepdims=False)
     turned = jnp.swapaxes(inverse_blocks, 1, 2)
     top = lax.reduce_precision(turned, exponent_bits=8, mantissa_bits=7)
     wide = jnp.concatenate([top, turned - top], axis=2).astype(bf16)
     blocks = jnp.concatenate([wide, wide], axis=1)
+    own_strat = restrict(stratification[None])[0]
+    strat_mine = jnp.stack(
+        [own_strat] + [lax.ppermute(own_strat, "y", ring(4, by)) for by in (1, 2, 3)]
+    )
+    strat_other = lax.ppermute(strat_mine, "zh", ring(2, 1))
 
     low, high = call(first_half_kernel, [(3, 8, 32, 128)] * 2, fine_scratch)(
         half_spin, left, start, right, stratification
     )
     left_again = lax.ppermute(high, SPACE, ring(8, 1))
     right_again = lax.ppermute(low, SPACE, ring(8, -1))
-    detail, payload = call(
+    detail, increment = call(
         second_half_kernel,
-        [(3, 16, 32, 128), (13, 8, 128)],
+        [(3, 16, 32, 128), (12, 8, 128)],
         fine_scratch + [((4, 32, 128), f32)],
     )(
-        half_spin, left_again, low, high, right_again, left, right, stratification,
-        next_mean, strat_tile,
-    )
-
-    mine = lax.all_to_all(jnp.broadcast_to(payload[None], (32, 13, 8, 128)), PLANE, 0, 0)
-    other = lax.ppermute(mine, "c", ring(2, 1))
+        half_spin, left_again, low, high, right_again, left, right, stratification, next_mean
+    )
+
+    mine = [increment] + [lax.ppermute(increment, "zl", ring(4, by)) for by in (1, 2, 3)]
+    other = [lax.ppermute(part, "c", ring(2, 1)) for part in mine]
     detail = lax.ppermute(detail, TM, ring(32, 1))
     end, part, strat = call(
         plane_kernel, [(3, 32, 8, 128), (3, 16, 8, 128), (32, 8, 128)], chain_scratch, 1
-    )(where, coarse_spin, blocks, mine, other)
-    here = jnp.stack([lax.ppermute(part, "x", ring(4, by)) for by in (1, 2, 3)])
-    there = lax.ppermute(here, "c", ring(2, 1))
-    (out,) = call(
-        final_kernel,
-        [(3, 16, 32, 128)],
-        [((4, 3, 32, 8, 128), f32)] + chain_scratch + [((2, 32, 128), f32)],
+    )(where, coarse_spin, blocks, strat_mine, strat_other, *mine, *other)
+    here = [lax.ppermute(part, "x", ring(4, by)) for by in (1, 2, 3)]
+    there = [lax.ppermute(part, "c", ring(2, 1)) for part in here]
+    parts = call(
+        chain_kernel,
+        [(2, 12, 8, 128)] * 4,
+        [((4, 3, 32, 8, 128), f32)] + chain_scratch,
         1,
-    )(where, coarse_spin, blocks, mine, other, strat, end, here, there, detail, mean)
+    )(where, coarse_spin, blocks, strat, end, *mine, *other, *here, *there)
+    total = parts[0]
+    for by in (1, 2, 3):
+        total = total + lax.ppermute(parts[by], "y", ring(4, by))
+    sent = lax.ppermute(total[1], "zh", ring(2, 1))
+    (out,) = call(final_kernel, [(3, 16, 32, 128)], [((2, 32, 128), f32)])(
+        total[0], sent, detail, mean
+    )
     return out[None]
 
 

time: 161 us -> 125 us (0.78)
  blocking collectives: 58.1 us -> 0 us
  starting transfers between devices: 20.8 us -> 43.7 us
  waiting for transfers between devices: 50.8 us -> 54.1 us
    all_to_all x1 -> x0, blocking collectives: 58.1 us -> none  [per_device(): lax.all_to_all(jnp.broadcast_to(payload[None], (32, 13, 8, 128)), PLANE,...]
    ppermute x5 -> x21, starting transfers between devices: 4.62 us -> 31.2 us  [the longest x3 17.4 us: per_device(): lax.ppermute(increment, 'zl', ring(4, by))]
    ppermute x1, waiting for transfers between devices: 7.53 us -> 0.01 us  [per_device(): next_mean = lax.ppermute(mean, TM, ring(32, -1))]
    ppermute x1, waiting for transfers between devices: 0.01 us -> 6.03 us  [per_device(): right_again = lax.ppermute(low, SPACE, ring(8, -1))]
    ppermute x5 -> x21, waiting for transfers between devices: 21.7 us -> 26.3 us  [the longest x1 6.45 us: per_device(): sent = lax.ppermute(total[1], 'zh', ring(2, 1))]
    ppermute x1, waiting for transfers between devices: 0.01 us -> 4.48 us  [per_device(): left_again = lax.ppermute(high, SPACE, ring(8, 1))]
    ppermute x1, waiting for transfers between devices: 13.1 us -> 8.81 us  [per_device(): left = lax.ppermute(tail, SPACE, ring(8, 1))]
    ppermute x1, starting transfers between devices: 7.07 us -> 3.36 us  [per_device(): next_mean = lax.ppermute(mean, TM, ring(32, -1))]
  transfers between devices with their start and end apart: 11 -> 27, of which waited for: 8 -> 16; matrix products, arithmetic and copies ran while one was open for 2% -> 1% of each run, Pallas kernels for 0% -> 15%
where the time goes in v2:
time: 125 us
  waiting for transfers between devices  54.1 us (43%)
  starting transfers between devices  43.7 us (35%)
  Pallas kernels  22.8 us (18%)
  local copies, waits for them, and re-layouts  3.14 us (3%)
    pallas_call x5, Pallas kernels, run(): pl.pallas_call(kernel, out_shape=[jax.ShapeDtypeStruct(shape, f32) for sh...  22.8 us
    ppermute x3, starting transfers between devices, per_device(): lax.ppermute(increment, 'zl', ring(4, by))  17.4 us
    ppermute x1, waiting for transfers between devices, per_device(): left = lax.ppermute(tail, SPACE, ring(8, 1))  8.81 us
    ppermute x1, waiting for transfers between devices, per_device(): right = lax.ppermute(head, SPACE, ring(8, -1))  8.49 us
    ppermute x1, starting transfers between devices, per_device(): left = lax.ppermute(tail, SPACE, ring(8, 1))  6.93 us
    ppermute x1, waiting for transfers between devices, per_device(): sent = lax.ppermute(total[1], 'zh', ring(2, 1))  6.45 us
    ppermute x3, waiting for transfers between devices, per_device(): here = [lax.ppermute(part, 'x', ring(4, by)) for by in (1, 2, 3)]  6.04 us
    ppermute x1, waiting for transfers between devices, per_device(): right_again = lax.ppermute(low, SPACE, ring(8, -1))  6.03 us
  transfers between devices with their start and end apart: 27, of which 16 were waited for; matrix products, arithmetic and copies ran while one was open for 1% of the time, Pallas kernels for 15%

profile of v2, /device:TPU:24, one launch (start us, length us, event | category | flops | bytes accessed | tf_op | source)
XLA Modules:
  0.0 124.7 jit_solution(4389485858499778752)
XLA Ops:
  1.3 6.9 %collective-permute-start.4 = (f32[30,32,128]{2,1,0:T(8,128)S(1)}, f32[30,32,128]{2,1,0:T(8,128)S(1)}, u32[]{:S(2)}, u32[]{:S(2)}) collective-permute-start(f32[30,32,128]{2,1,0:T(8,128)S(1)} %pad_maximum_fusion), channel_id=1, source_target_pairs={{0,1},{1,2},{2,3},{3,4},{4,5},{5,6},{6,7},{7,0},{8,9},{9,10},{10,1... | collective-permute-start | bytes 1474568 | tf_op jit(solution)/shard_map/ppermute | solution.py:312
  8.6 3.4 %collective-permute-start.8 = (f32[3,4,8,128]{3,2,1,0:T(8,128)S(1)}, f32[3,4,8,128]{3,2,1,0:T(8,128)S(1)}, u32[]{:S(2)}, u32[]{:S(2)}) collective-permute-start(f32[3,4,8,128]{3,2,1,0:T(8,128)S(1)} %broadcast_multiply_fusion.mean), channel_id=1, source_target_pairs={{0,248},{8,0},{16,8},{24,16},{32,24},{40,32},{48,40},{56,48},{64,5... | collective-permute-start | bytes 147464 | tf_op jit(solution)/shard_map/ppermute | solution.py:315
  12.6 8.8 %collective-permute-done.4.left.left_first = f32[30,32,128]{2,1,0:T(8,128)S(1)} collective-permute-done((f32[30,32,128]{2,1,0:T(8,128)S(1)}, f32[30,32,128]{2,1,0:T(8,128)S(1)}, u32[]{:S(2)}, u32[]{:S(2)}) %collective-permute-start.4) | collective-permute-done | bytes 491552 | tf_op jit(solution)/shard_map/ppermute | solution.py:312
  21.4 8.5 %collective-permute-done.5.right.right_first = f32[30,32,128]{2,1,0:T(8,128)S(1)} collective-permute-done((f32[30,32,128]{2,1,0:T(8,128)S(1)}, f32[30,32,128]{2,1,0:T(8,128)S(1)}, u32[]{:S(2)}, u32[]{:S(2)}) %collective-permute-start.5) | collective-permute-done | bytes 491552 | tf_op jit(solution)/shard_map/ppermute | solution.py:313
  30.0 5.5 %shard_map.46 = (f32[3,8,32,128]{3,2,1,0:T(8,128)S(1)}, f32[3,8,32,128]{3,2,1,0:T(8,128)S(1)}) custom-call(f32[32,128]{1,0:T(8,128)S(1)} %broadcast_in_dim.7.spin, f32[30,32,128]{2,1,0:T(8,128)S(1)} %collective-permute-done.4.left.left_first, f32[3,16,32,128]{3,2,1,0:T(8,128)S(1)} %bitcast.25, f32[30,32,128]{2,1,0:T(8,128)S(1)} %collective-permute-done.5.right.right_first, ...), custom_call_target="tpu_custom_call" | custom-call | tf_op jit(solution)/shard_map/pallas_call | solution.py:287
  35.7 1.9 %collective-permute-start.7 = (f32[3,8,32,128]{3,2,1,0:T(8,128)S(1)}, f32[3,8,32,128]{3,2,1,0:T(8,128)S(1)}, u32[]{:S(2)}, u32[]{:S(2)}) collective-permute-start(f32[3,8,32,128]{3,2,1,0:T(8,128)S(1)} %get-tuple-element.17.low), channel_id=1, source_target_pairs={{0,7},{1,0},{2,1},{3,2},{4,3},{5,4},{6,5},{7,6},{8,15},{9,8},{10,9... | collective-permute-start | bytes 1179656 | tf_op jit(solution)/shard_map/ppermute | solution.py:334
  37.7 3.2 %collective-permute-start = (f32[4,8,128]{2,1,0:T(8,128)S(1)}, f32[4,8,128]{2,1,0:T(8,128)S(1)}, u32[]{:S(2)}, u32[]{:S(2)}) collective-permute-start(f32[4,8,128]{2,1,0:T(8,128)S(1)} %get-tuple-element.36), channel_id=1, source_target_pairs={{0,1},{1,2},{2,3},{3,0},{4,5},{5,6},{6,7},{7,4},{8,9},{9,10},{10,1... | collective-permute-start | bytes 49160 | tf_op jit(solution)/shard_map/ppermute | solution.py:326
  41.2 4.5 %collective-permute-done.6.left = f32[3,8,32,128]{3,2,1,0:T(8,128)S(1)} collective-permute-done((f32[3,8,32,128]{3,2,1,0:T(8,128)S(1)}, f32[3,8,32,128]{3,2,1,0:T(8,128)S(1)}, u32[]{:S(2)}, u32[]{:S(2)}) %collective-permute-start.6) | collective-permute-done | bytes 393248 | tf_op jit(solution)/shard_map/ppermute | solution.py:333
  45.6 6.0 %collective-permute-done.7.right = f32[3,8,32,128]{3,2,1,0:T(8,128)S(1)} collective-permute-done((f32[3,8,32,128]{3,2,1,0:T(8,128)S(1)}, f32[3,8,32,128]{3,2,1,0:T(8,128)S(1)}, u32[]{:S(2)}, u32[]{:S(2)}) %collective-permute-start.7) | collective-permute-done | bytes 393248 | tf_op jit(solution)/shard_map/ppermute | solution.py:334
  51.7 5.6 %shard_map.47 = (f32[3,16,32,128]{3,2,1,0:T(8,128)S(1)}, f32[12,8,128]{2,1,0:T(8,128)S(1)}) custom-call(f32[32,128]{1,0:T(8,128)S(1)} %broadcast_in_dim.7.spin, f32[3,8,32,128]{3,2,1,0:T(8,128)S(1)} %collective-permute-done.6.left, f32[3,8,32,128]{3,2,1,0:T(8,128)S(1)} %get-tuple-element.17.low, f32[3,8,32,128]{3,2,1,0:T(8,128)S(1)} %get-tuple-element.16.high, ...), custom_call_target="tpu_custom_call" | custom-call | tf_op jit(solution)/shard_map/pallas_call | solution.py:287
  58.2 15.0 %collective-permute-start.9 = (f32[12,8,128]{2,1,0:T(8,128)S(1)}, f32[12,8,128]{2,1,0:T(8,128)S(1)}, u32[]{:S(2)}, u32[]{:S(2)}) collective-permute-start(f32[12,8,128]{2,1,0:T(8,128)S(1)} %get-tuple-element.18.refs_0_), channel_id=1, source_target_pairs={{0,16},{16,32},{32,48},{48,0},{1,17},{17,33},{33,49},{49,1},{2,18}... | collective-permute-start | bytes 147464 | tf_op jit(solution)/shard_map/ppermute | solution.py:343
  73.2 1.8 %collective-permute-start.10 = (f32[12,8,128]{2,1,0:T(8,128)S(1)}, f32[12,8,128]{2,1,0:T(8,128)S(1)}, u32[]{:S(2)}, u32[]{:S(2)}) collective-permute-start(f32[12,8,128]{2,1,0:T(8,128)S(1)} %get-tuple-element.18.refs_0_), channel_id=1, source_target_pairs={{0,32},{16,48},{32,0},{48,16},{1,33},{17,49},{33,1},{49,17},{2,34}... | collective-permute-start | bytes 147464 | tf_op jit(solution)/shard_map/ppermute | solution.py:343
  77.2 2.4 %collective-permute-done.10.refs_2_ = f32[12,8,128]{2,1,0:T(8,128)S(1)} collective-permute-done((f32[12,8,128]{2,1,0:T(8,128)S(1)}, f32[12,8,128]{2,1,0:T(8,128)S(1)}, u32[]{:S(2)}, u32[]{:S(2)}) %collective-permute-start.10) | collective-permute-done | bytes 49184 | tf_op jit(solution)/shard_map/ppermute | solution.py:343
  80.9 2.9 %collective-permute-done.3.strat_other = f32[4,4,8,128]{3,2,1,0:T(8,128)S(1)} collective-permute-done((f32[4,4,8,128]{3,2,1,0:T(8,128)S(1)}, f32[4,4,8,128]{3,2,1,0:T(8,128)S(1)}, u32[]{:S(2)}, u32[]{:S(2)}) %collective-permute-start.3) | collective-permute-done | bytes 65568 | tf_op jit(solution)/shard_map/ppermute | solution.py:328
  84.0 2.8 %shard_map.48 = (f32[3,32,8,128]{3,2,1,0:T(8,128)S(1)}, f32[3,16,8,128]{3,2,1,0:T(8,128)S(1)}, f32[32,8,128]{2,1,0:T(8,128)S(1)}) custom-call(s32[5]{0:T(128)S(1)} %stack.35.where, f32[8,128]{1,0:T(8,128)S(1)} %broadcast_in_dim.6.spin, bf16[3,256,256]{2,1,0:T(8,128)(2,1)S(1)} %maximum_maximum_fusion.blocks, ...), custom_call_target="tpu_custom_call" | custom-call | tf_op jit(solution)/shard_map/pallas_call | solution.py:287
  88.3 2.7 %collective-permute-start.17 = (f32[3,16,8,128]{3,2,1,0:T(8,128)S(1)}, f32[3,16,8,128]{3,2,1,0:T(8,128)S(1)}, u32[]{:S(2)}, u32[]{:S(2)}) collective-permute-start(f32[3,16,8,128]{3,2,1,0:T(8,128)S(1)} %get-tuple-element.21), channel_id=1, source_target_pairs={{0,128},{64,192},{128,0},{192,64},{1,129},{65,193},{129,1},{193,65... | collective-permute-start | bytes 589832 | tf_op jit(solution)/shard_map/ppermute | solution.py:349
  92.5 3.2 %collective-permute-done.16.refs_8_ = f32[3,16,8,128]{3,2,1,0:T(8,128)S(1)} collective-permute-done((f32[3,16,8,128]{3,2,1,0:T(8,128)S(1)}, f32[3,16,8,128]{3,2,1,0:T(8,128)S(1)}, u32[]{:S(2)}, u32[]{:S(2)}) %collective-permute-start.16) | collective-permute-done | bytes 196640 | tf_op jit(solution)/shard_map/ppermute | solution.py:349
  95.7 2.9 %collective-permute-done.17.refs_9_ = f32[3,16,8,128]{3,2,1,0:T(8,128)S(1)} collective-permute-done((f32[3,16,8,128]{3,2,1,0:T(8,128)S(1)}, f32[3,16,8,128]{3,2,1,0:T(8,128)S(1)}, u32[]{:S(2)}, u32[]{:S(2)}) %collective-permute-start.17) | collective-permute-done | bytes 196640 | tf_op jit(solution)/shard_map/ppermute | solution.py:349
  100.2 7.9 %shard_map.49 = (f32[2,12,8,128]{3,2,1,0:T(8,128)S(1)}, f32[2,12,8,128]{3,2,1,0:T(8,128)S(1)}, f32[2,12,8,128]{3,2,1,0:T(8,128)S(1)}, f32[2,12,8,128]{3,2,1,0:T(8,128)S(1)}) custom-call(s32[5]{0:T(128)S(1)} %stack.35.where, f32[8,128]{1,0:T(8,128)S(1)} %broadcast_in_dim.6.spin, bf16[3,256,256]{2,1,0:T(8,128)(2,1)S(1)} %maximum_maximum_fusion.blocks, ...), custom_call_target="tpu_custom_call" | custom-call | tf_op jit(solution)/shard_map/pallas_call | solution.py:287
  108.4 1.9 %collective-permute-start.24 = (f32[2,12,8,128]{3,2,1,0:T(8,128)S(1)}, f32[2,12,8,128]{3,2,1,0:T(8,128)S(1)}, u32[]{:S(2)}, u32[]{:S(2)}) collective-permute-start(f32[2,12,8,128]{3,2,1,0:T(8,128)S(1)} %get-tuple-element.25), channel_id=1, source_target_pairs={{0,3},{1,0},{2,1},{3,2},{4,7},{5,4},{6,5},{7,6},{8,11},{9,8},{10,9... | collective-permute-start | bytes 294920 | tf_op jit(solution)/shard_map/ppermute | solution.py:359
  110.3 2.6 %collective-permute-done.22 = f32[2,12,8,128]{3,2,1,0:T(8,128)S(1)} collective-permute-done((f32[2,12,8,128]{3,2,1,0:T(8,128)S(1)}, f32[2,12,8,128]{3,2,1,0:T(8,128)S(1)}, u32[]{:S(2)}, u32[]{:S(2)}) %collective-permute-start.22) | collective-permute-done | bytes 98336 | tf_op jit(solution)/shard_map/ppermute | solution.py:359
  112.9 1.6 %collective-permute-done.23 = f32[2,12,8,128]{3,2,1,0:T(8,128)S(1)} collective-permute-done((f32[2,12,8,128]{3,2,1,0:T(8,128)S(1)}, f32[2,12,8,128]{3,2,1,0:T(8,128)S(1)}, u32[]{:S(2)}, u32[]{:S(2)}) %collective-permute-start.23) | collective-permute-done | bytes 98336 | tf_op jit(solution)/shard_map/ppermute | solution.py:359
  115.6 1.6 %collective-permute-start.25 = (f32[12,8,128]{2,1,0:T(8,128)S(1)}, f32[12,8,128]{2,1,0:T(8,128)S(1)}, u32[]{:S(2)}, u32[]{:S(2)}) collective-permute-start(f32[12,8,128]{2,1,0:T(8,128)S(1)} %get-tuple-element.33), channel_id=1, source_target_pairs={{0,4},{4,0},{1,5},{5,1},{2,6},{6,2},{3,7},{7,3},{8,12},{12,8},{9,1... | collective-permute-start | bytes 147464 | tf_op jit(solution)/shard_map/ppermute | solution.py:360
  117.2 6.4 %collective-permute-done.25.sent = f32[12,8,128]{2,1,0:T(8,128)S(1)} collective-permute-done((f32[12,8,128]{2,1,0:T(8,128)S(1)}, f32[12,8,128]{2,1,0:T(8,128)S(1)}, u32[]{:S(2)}, u32[]{:S(2)}) %collective-permute-start.25) | collective-permute-done | bytes 49184 | tf_op jit(solution)/shard_map/ppermute | solution.py:360
  (67 shorter events, 14.3 us)
Async XLA Ops:
  1.3 20.1 %collective-permute-start.4 = (f32[30,32,128]{2,1,0:T(8,128)S(1)}, f32[30,32,128]{2,1,0:T(8,128)S(1)}, u32[]{:S(2)}, u32[]{:S(2)}) collective-permute-start(f32[30,32,128]{2,1,0:T(8,128)S(1)} %pad_maximum_fusion), channel_id=1, source_target_pairs={{0,1},{1,2},{2,3},{3,4},{4,5},{5,6},{6,7},{7,0},{8,9},{9,10},{10,1... | collective-permute-start | bytes 1474568 | tf_op jit(solution)/shard_map/ppermute | solution.py:312
  8.3 21.7 %collective-permute-start.5 = (f32[30,32,128]{2,1,0:T(8,128)S(1)}, f32[30,32,128]{2,1,0:T(8,128)S(1)}, u32[]{:S(2)}, u32[]{:S(2)}) collective-permute-start(f32[30,32,128]{2,1,0:T(8,128)S(1)} %pad_maximum_fusion.1), channel_id=1, source_target_pairs={{0,7},{1,0},{2,1},{3,2},{4,3},{5,4},{6,5},{7,6},{8,15},{9,8},{10,9... | collective-permute-start | bytes 1474568 | tf_op jit(solution)/shard_map/ppermute | solution.py:313
  8.6 32.4 %collective-permute-start.8 = (f32[3,4,8,128]{3,2,1,0:T(8,128)S(1)}, f32[3,4,8,128]{3,2,1,0:T(8,128)S(1)}, u32[]{:S(2)}, u32[]{:S(2)}) collective-permute-start(f32[3,4,8,128]{3,2,1,0:T(8,128)S(1)} %broadcast_multiply_fusion.mean), channel_id=1, source_target_pairs={{0,248},{8,0},{16,8},{24,16},{32,24},{40,32},{48,40},{56,48},{64,5... | collective-permute-start | bytes 147464 | tf_op jit(solution)/shard_map/ppermute | solution.py:315
  35.5 10.1 %collective-permute-start.6 = (f32[3,8,32,128]{3,2,1,0:T(8,128)S(1)}, f32[3,8,32,128]{3,2,1,0:T(8,128)S(1)}, u32[]{:S(2)}, u32[]{:S(2)}) collective-permute-start(f32[3,8,32,128]{3,2,1,0:T(8,128)S(1)} %get-tuple-element.16.high), channel_id=1, source_target_pairs={{0,1},{1,2},{2,3},{3,4},{4,5},{5,6},{6,7},{7,0},{8,9},{9,10},{10,1... | collective-permute-start | bytes 1179656 | tf_op jit(solution)/shard_map/ppermute | solution.py:333
  35.7 15.9 %collective-permute-start.7 = (f32[3,8,32,128]{3,2,1,0:T(8,128)S(1)}, f32[3,8,32,128]{3,2,1,0:T(8,128)S(1)}, u32[]{:S(2)}, u32[]{:S(2)}) collective-permute-start(f32[3,8,32,128]{3,2,1,0:T(8,128)S(1)} %get-tuple-element.17.low), channel_id=1, source_target_pairs={{0,7},{1,0},{2,1},{3,2},{4,3},{5,4},{6,5},{7,6},{8,15},{9,8},{10,9... | collective-permute-start | bytes 1179656 | tf_op jit(solution)/shard_map/ppermute | solution.py:334
  37.6 37.4 %collective-permute-start.2 = (f32[4,8,128]{2,1,0:T(8,128)S(1)}, f32[4,8,128]{2,1,0:T(8,128)S(1)}, u32[]{:S(2)}, u32[]{:S(2)}) collective-permute-start(f32[4,8,128]{2,1,0:T(8,128)S(1)} %get-tuple-element.36), channel_id=1, source_target_pairs={{0,3},{1,0},{2,1},{3,2},{4,7},{5,4},{6,5},{7,6},{8,11},{9,8},{10,9... | collective-permute-start | bytes 49160 | tf_op jit(solution)/shard_map/ppermute | solution.py:326
  37.7 37.9 %collective-permute-start = (f32[4,8,128]{2,1,0:T(8,128)S(1)}, f32[4,8,128]{2,1,0:T(8,128)S(1)}, u32[]{:S(2)}, u32[]{:S(2)}) collective-permute-start(f32[4,8,128]{2,1,0:T(8,128)S(1)} %get-tuple-element.36), channel_id=1, source_target_pairs={{0,1},{1,2},{2,3},{3,0},{4,5},{5,6},{6,7},{7,4},{8,9},{9,10},{10,1... | collective-permute-start | bytes 49160 | tf_op jit(solution)/shard_map/ppermute | solution.py:326
  41.0 34.6 %collective-permute-start.1 = (f32[4,8,128]{2,1,0:T(8,128)S(1)}, f32[4,8,128]{2,1,0:T(8,128)S(1)}, u32[]{:S(2)}, u32[]{:S(2)}) collective-permute-start(f32[4,8,128]{2,1,0:T(8,128)S(1)} %get-tuple-element.36), channel_id=1, source_target_pairs={{0,2},{1,3},{2,0},{3,1},{4,6},{5,7},{6,4},{7,5},{8,10},{9,11},{10,... | collective-permute-start | bytes 49160 | tf_op jit(solution)/shard_map/ppermute | solution.py:326
  58.2 19.0 %collective-permute-start.9 = (f32[12,8,128]{2,1,0:T(8,128)S(1)}, f32[12,8,128]{2,1,0:T(8,128)S(1)}, u32[]{:S(2)}, u32[]{:S(2)}) collective-permute-start(f32[12,8,128]{2,1,0:T(8,128)S(1)} %get-tuple-element.18.refs_0_), channel_id=1, source_target_pairs={{0,16},{16,32},{32,48},{48,0},{1,17},{17,33},{33,49},{49,1},{2,18}... | collective-permute-start | bytes 147464 | tf_op jit(solution)/shard_map/ppermute | solution.py:343
  73.2 6.3 %collective-permute-start.10 = (f32[12,8,128]{2,1,0:T(8,128)S(1)}, f32[12,8,128]{2,1,0:T(8,128)S(1)}, u32[]{:S(2)}, u32[]{:S(2)}) collective-permute-start(f32[12,8,128]{2,1,0:T(8,128)S(1)} %get-tuple-element.18.refs_0_), channel_id=1, source_target_pairs={{0,32},{16,48},{32,0},{48,16},{1,33},{17,49},{33,1},{49,17},{2,34}... | collective-permute-start | bytes 147464 | tf_op jit(solution)/shard_map/ppermute | solution.py:343
  75.1 5.5 %collective-permute-start.11 = (f32[12,8,128]{2,1,0:T(8,128)S(1)}, f32[12,8,128]{2,1,0:T(8,128)S(1)}, u32[]{:S(2)}, u32[]{:S(2)}) collective-permute-start(f32[12,8,128]{2,1,0:T(8,128)S(1)} %get-tuple-element.18.refs_0_), channel_id=1, source_target_pairs={{0,48},{16,0},{32,16},{48,32},{1,49},{17,1},{33,17},{49,33},{2,50}... | collective-permute-start | bytes 147464 | tf_op jit(solution)/shard_map/ppermute | solution.py:343
  75.6 8.3 %collective-permute-start.3 = (f32[4,4,8,128]{3,2,1,0:T(8,128)S(1)}, f32[4,4,8,128]{3,2,1,0:T(8,128)S(1)}, u32[]{:S(2)}, u32[]{:S(2)}) collective-permute-start(f32[4,4,8,128]{3,2,1,0:T(8,128)S(1)} %pad_maximum_fusion.2.strat_mine), channel_id=1, source_target_pairs={{0,4},{4,0},{1,5},{5,1},{2,6},{6,2},{3,7},{7,3},{8,12},{12,8},{9,1... | collective-permute-start | bytes 196616 | tf_op jit(solution)/shard_map/ppermute | solution.py:328
  76.1 7.8 %collective-permute-start.12 = (f32[12,8,128]{2,1,0:T(8,128)S(1)}, f32[12,8,128]{2,1,0:T(8,128)S(1)}, u32[]{:S(2)}, u32[]{:S(2)}) collective-permute-start(f32[12,8,128]{2,1,0:T(8,128)S(1)} %get-tuple-element.18.refs_0_), channel_id=1, source_target_pairs={{0,8},{8,0},{1,9},{9,1},{2,10},{10,2},{3,11},{11,3},{4,12},{12,4},... | collective-permute-start | bytes 147464 | tf_op jit(solution)/shard_map/ppermute | solution.py:344
  77.2 6.7 %collective-permute-start.13 = (f32[12,8,128]{2,1,0:T(8,128)S(1)}, f32[12,8,128]{2,1,0:T(8,128)S(1)}, u32[]{:S(2)}, u32[]{:S(2)}) collective-permute-start(f32[12,8,128]{2,1,0:T(8,128)S(1)} %collective-permute-done.9.refs_1_), channel_id=1, source_target_pairs={{0,8},{8,0},{1,9},{9,1},{2,10},{10,2},{3,11},{11,3},{4,12},{12,4},... | collective-permute-start | bytes 147464 | tf_op jit(solution)/shard_map/ppermute | solution.py:344
  79.5 4.4 %collective-permute-start.14 = (f32[12,8,128]{2,1,0:T(8,128)S(1)}, f32[12,8,128]{2,1,0:T(8,128)S(1)}, u32[]{:S(2)}, u32[]{:S(2)}) collective-permute-start(f32[12,8,128]{2,1,0:T(8,128)S(1)} %collective-permute-done.10.refs_2_), channel_id=1, source_target_pairs={{0,8},{8,0},{1,9},{9,1},{2,10},{10,2},{3,11},{11,3},{4,12},{12,4},... | collective-permute-start | bytes 147464 | tf_op jit(solution)/shard_map/ppermute | solution.py:344
  86.7 8.9 %collective-permute-start.16 = (f32[3,16,8,128]{3,2,1,0:T(8,128)S(1)}, f32[3,16,8,128]{3,2,1,0:T(8,128)S(1)}, u32[]{:S(2)}, u32[]{:S(2)}) collective-permute-start(f32[3,16,8,128]{3,2,1,0:T(8,128)S(1)} %get-tuple-element.21), channel_id=1, source_target_pairs={{0,64},{64,128},{128,192},{192,0},{1,65},{65,129},{129,193},{193,1... | collective-permute-start | bytes 589832 | tf_op jit(solution)/shard_map/ppermute | solution.py:349
  88.3 10.2 %collective-permute-start.17 = (f32[3,16,8,128]{3,2,1,0:T(8,128)S(1)}, f32[3,16,8,128]{3,2,1,0:T(8,128)S(1)}, u32[]{:S(2)}, u32[]{:S(2)}) collective-permute-start(f32[3,16,8,128]{3,2,1,0:T(8,128)S(1)} %get-tuple-element.21), channel_id=1, source_target_pairs={{0,128},{64,192},{128,0},{192,64},{1,129},{65,193},{129,1},{193,65... | collective-permute-start | bytes 589832 | tf_op jit(solution)/shard_map/ppermute | solution.py:349
  91.0 7.5 %collective-permute-start.18 = (f32[3,16,8,128]{3,2,1,0:T(8,128)S(1)}, f32[3,16,8,128]{3,2,1,0:T(8,128)S(1)}, u32[]{:S(2)}, u32[]{:S(2)}) collective-permute-start(f32[3,16,8,128]{3,2,1,0:T(8,128)S(1)} %get-tuple-element.21), channel_id=1, source_target_pairs={{0,192},{64,0},{128,64},{192,128},{1,193},{65,1},{129,65},{193,129... | collective-permute-start | bytes 589832 | tf_op jit(solution)/shard_map/ppermute | solution.py:349
  95.7 3.5 %collective-permute-start.19 = (f32[3,16,8,128]{3,2,1,0:T(8,128)S(1)}, f32[3,16,8,128]{3,2,1,0:T(8,128)S(1)}, u32[]{:S(2)}, u32[]{:S(2)}) collective-permute-start(f32[3,16,8,128]{3,2,1,0:T(8,128)S(1)} %collective-permute-done.16.refs_8_), channel_id=1, source_target_pairs={{0,8},{8,0},{1,9},{9,1},{2,10},{10,2},{3,11},{11,3},{4,12},{12,4},... | collective-permute-start | bytes 589832 | tf_op jit(solution)/shard_map/ppermute | solution.py:350
  99.0 24.7 %collective-permute-start.26 = (f32[3,16,32,128]{3,2,1,0:T(8,128)S(1)}, f32[3,16,32,128]{3,2,1,0:T(8,128)S(1)}, u32[]{:S(2)}, u32[]{:S(2)}) collective-permute-start(f32[3,16,32,128]{3,2,1,0:T(8,128)S(1)} %copy-done.3), channel_id=1, source_target_pairs={{0,8},{8,16},{16,24},{24,32},{32,40},{40,48},{48,56},{56,64},{64,7... | collective-permute-start | bytes 2359304 | tf_op jit(solution)/shard_map/ppermute | solution.py:345
  108.2 4.7 %collective-permute-start.22 = (f32[2,12,8,128]{3,2,1,0:T(8,128)S(1)}, f32[2,12,8,128]{3,2,1,0:T(8,128)S(1)}, u32[]{:S(2)}, u32[]{:S(2)}) collective-permute-start(f32[2,12,8,128]{3,2,1,0:T(8,128)S(1)} %get-tuple-element.23), channel_id=1, source_target_pairs={{0,1},{1,2},{2,3},{3,0},{4,5},{5,6},{6,7},{7,4},{8,9},{9,10},{10,1... | collective-permute-start | bytes 294920 | tf_op jit(solution)/shard_map/ppermute | solution.py:359
  108.3 6.2 %collective-permute-start.23 = (f32[2,12,8,128]{3,2,1,0:T(8,128)S(1)}, f32[2,12,8,128]{3,2,1,0:T(8,128)S(1)}, u32[]{:S(2)}, u32[]{:S(2)}) collective-permute-start(f32[2,12,8,128]{3,2,1,0:T(8,128)S(1)} %get-tuple-element.24), channel_id=1, source_target_pairs={{0,2},{1,3},{2,0},{3,1},{4,6},{5,7},{6,4},{7,5},{8,10},{9,11},{10,... | collective-permute-start | bytes 294920 | tf_op jit(solution)/shard_map/ppermute | solution.py:359
  108.4 7.2 %collective-permute-start.24 = (f32[2,12,8,128]{3,2,1,0:T(8,128)S(1)}, f32[2,12,8,128]{3,2,1,0:T(8,128)S(1)}, u32[]{:S(2)}, u32[]{:S(2)}) collective-permute-start(f32[2,12,8,128]{3,2,1,0:T(8,128)S(1)} %get-tuple-element.25), channel_id=1, source_target_pairs={{0,3},{1,0},{2,1},{3,2},{4,7},{5,4},{6,5},{7,6},{8,11},{9,8},{10,9... | collective-permute-start | bytes 294920 | tf_op jit(solution)/shard_map/ppermute | solution.py:359
  115.6 8.1 %collective-permute-start.25 = (f32[12,8,128]{2,1,0:T(8,128)S(1)}, f32[12,8,128]{2,1,0:T(8,128)S(1)}, u32[]{:S(2)}, u32[]{:S(2)}) collective-permute-start(f32[12,8,128]{2,1,0:T(8,128)S(1)} %get-tuple-element.33), channel_id=1, source_target_pairs={{0,4},{4,0},{1,5},{5,1},{2,6},{6,2},{3,7},{7,3},{8,12},{12,8},{9,1... | collective-permute-start | bytes 147464 | tf_op jit(solution)/shard_map/ppermute | solution.py:360
  (9 other events, 45.6 us)

commit v3 on v2

--- a/solution.py
+++ b/solution.py
@@ -1,3 +1,5 @@
+import itertools
+
 import jax
 import jax.numpy as jnp
 from jax import lax
@@ -92,32 +94,52 @@
         strat[HALO + x] = 0.25 * own[x]
 
 
-def first_half_kernel(spin, left, start, right, own_strat, low, high, one, two, strat):
-    for k in range(3):
-        for x in range(8):
-            one[k, x] = left[8 * k + x]
-            one[k, 24 + x] = right[8 * k + x]
+def fill_state(buf, left, own, right):
+    for k in range(3):
         for x in range(16):
-            one[k, 8 + x] = start[k, x]
-    fill_strat(strat, left.at[pl.ds(24, 6)], own_strat, right.at[pl.ds(24, 6)])
+            buf[k, HALO + x] = own[k, x]
+    for x in range(8):
+        buf[0, x] = left[x]
+        buf[2, x] = left[15 + x]
+        buf[0, 24 + x] = right[x]
+        buf[2, 24 + x] = right[15 + x]
+    for x in range(7):
+        buf[1, 1 + x] = left[8 + x]
+        buf[1, 24 + x] = right[8 + x]
+
+
+def first_half_kernel(
+    spin, y, c0, c1, c2, c3, left_strat, right_strat, own_strat, start, left, right,
+    middle, low, high, columns, one, two, strat,
+):
+    fill_state(one, left, start, right)
+    fill_strat(strat, left_strat, own_strat, right_strat)
+    for j, cells in enumerate((c0, c1, c2, c3)):
+        columns[(y[0] - j + 4) % 4] = cells[...]
     fine_steps((one, two), strat, spin, lane_weights())
     for k in range(3):
-        for x in range(8):
-            low[k, x] = one[k, 8 + x]
-            high[k, x] = one[k, 16 + x]
+        for x in range(16):
+            middle[k, x] = one[k, HALO + x]
+    for x in range(8):
+        low[x] = one[0, 8 + x]
+        low[15 + x] = one[2, 8 + x]
+        high[x] = one[0, 16 + x]
+        high[15 + x] = one[2, 16 + x]
+    for x in range(7):
+        low[8 + x] = one[1, 8 + x]
+        high[8 + x] = one[1, 17 + x]
 
 
 def second_half_kernel(
-    spin, left, low, high, right, left_first, right_first, own_strat, next_mean,
-    detail, payload, one, two, strat, rows,
+    spin, zh, near, far, next_mean, left_strat, right_strat, own_strat, middle, left, right,
+    detail, increment, coarse_strat, one, two, strat, rows,
 ):
-    for k in range(3):
-        for x in range(8):
-            one[k, x] = left[k, x]
-            one[k, 8 + x] = low[k, x]
-            one[k, 16 + x] = high[k, x]
-            one[k, 24 + x] = right[k, x]
-    fill_strat(strat, left_first.at[pl.ds(24, 6)], own_strat, right_first.at[pl.ds(24, 6)])
+    fill_state(one, left, middle, right)
+    fill_strat(strat, left_strat, own_strat, right_strat)
+    for column in range(4):
+        for cell in range(4):
+            coarse_strat[16 * zh[0] + 4 * column + cell] = 0.5 * near[column, cell]
+            coarse_strat[16 * (1 - zh[0]) + 4 * column + cell] = 0.5 * far[column, cell]
     fine_steps((one, two), strat, spin, lane_weights())
     for k in range(3):
         for cell in range(4):
@@ -126,7 +148,7 @@
             rows[slot] = (one[k, x] + one[k, x + 1]) + (one[k, x + 2] + one[k, x + 3])
             parts = [rows[slot, pl.ds(j, 8, stride=4), :] for j in range(4)]
             mean = ((parts[0] + parts[1]) + (parts[2] + parts[3])) * 0.0625
-            payload[4 * k + cell] = mean - next_mean[k, cell]
+            increment[4 * k + cell] = mean - next_mean[k, cell]
             for j in range(4):
                 rows[2 + slot, pl.ds(j, 8, stride=4), :] = mean
             for j in range(4):
@@ -192,14 +214,17 @@
             state[k, x] = jnp.zeros((8, 128), jnp.float32)
 
 
-def plane_kernel(where, spin, blocks, strat_mine, strat_other, *refs):
-    mine, other, (end, part, strat, state, halves, increments) = refs[:4], refs[4:8], refs[8:]
+def steps(count, state, halves, blocks, spin, strat):
+    def step(i, carry):
+        coarse_step(state, halves, blocks, spin[...], strat)
+        return carry
+
+    lax.fori_loop(0, count, step, 0)
+
+
+def plane_kernel(where, spin, blocks, strat, *refs):
+    mine, other, (state, part, halves, increments) = refs[:4], refs[4:8], refs[8:]
     core, zh, y = where[1], where[3], where[4]
-    for j in range(4):
-        column = (y - j + 4) % 4
-        for cell in range(4):
-            strat[4 * (4 * zh + column) + cell] = 0.5 * strat_mine[j, cell]
-            strat[4 * (4 * (1 - zh) + column) + cell] = 0.5 * strat_other[j, cell]
     table(where, increments, mine, other)
     clear(state)
     block = 4 * zh + y
@@ -212,44 +237,45 @@
 
     lax.fori_loop(1, 8, turn, 0)
     for k in range(3):
+        part[k] = state[k, pl.ds(16 * core, 16)]
+
+
+def power_kernel(where, spin, blocks, strat, before, *refs):
+    state, part, halves = refs[-3:]
+    for k in range(3):
         for x in range(32):
-            end[k, x] = state[k, x]
-        part[k] = state[k, pl.ds(16 * core, 16)]
-
-
-def chain_kernel(where, spin, blocks, strat, end, *refs):
-    mine, other, here, there = refs[:4], refs[4:8], refs[8:11], refs[11:14]
-    parts, (ends, state, halves, increments) = refs[14:18], refs[18:]
+            state[k, x] = before[k, x]
+    steps(8, state, halves, blocks, spin, strat)
+    for k in range(3):
+        part[k] = state[k, pl.ds(16 * where[1], 16)]
+
+
+def chain_kernel(where, spin, blocks, strat, last, *refs):
+    mine, other, here, there = refs[:4], refs[4:8], refs[10:7:-1], refs[13:10:-1]
+    parts, (state, halves, increments) = refs[14:18], refs[18:]
     run, core, row, zh, y = where[0], where[1], where[2], where[3], where[4]
     turns = 2 * run + core
-    groups = jnp.where((row == 0) & (turns == 0), 4, row)
+    closing = (row == 0) & (turns == 0)
     table(where, increments, mine, other)
-    for k in range(3):
-        for x in range(32):
-            ends[0, k, x] = end[k, x]
-    for j in range(3):
-        for k in range(3):
-            ends[j + 1, k, pl.ds(16 * core, 16)] = here[j][k]
-            ends[j + 1, k, pl.ds(16 * (1 - core), 16)] = there[j][k]
-
-    scale = jnp.where(groups > 0, 1.0, 0.0).astype(jnp.float32)
-    for k in range(3):
-        for x in range(32):
-            state[k, x] = ends[row, k, x] * scale
-
-    def group(g, carry):
-        def plain(i, inner):
-            coarse_step(state, halves, blocks, spin[...], strat)
-            return inner
-
-        lax.fori_loop(0, 8, plain, 0)
-        place = (row - g + 4) % 4
+    clear(state)
+
+    @pl.when(closing)
+    def _():
         for k in range(3):
             for x in range(32):
-                state[k, x] = state[k, x] + ends[place, k, x]
-        return carry
-
-    lax.fori_loop(1, groups, group, 0)
+                state[k, x] = last[k, x]
+        steps(8, state, halves, blocks, spin, strat)
+
+    for j in range(3):
+
+        @pl.when(closing | (row > j))
+        def _(j=j):
+            for k in range(3):
+                for x in range(16):
+                    near, far = 16 * core + x, 16 * (1 - core) + x
+                    state[k, near] = state[k, near] + here[j][k, x]
+                    state[k, far] = state[k, far] + there[j][k, x]
+
     block = 4 * zh + y
 
     def turn(i, carry):
@@ -280,14 +306,15 @@
                 out[k, 4 * cell + j] = detail[k, 4 * cell + j] + rows[slot]
 
 
-def call(kernel, outs, scratch, scalars=0):
+def call(kernel, outs, scratch, cost=0):
     f32 = jnp.float32
 
     def run(*args):
         return pl.pallas_call(
             kernel,
             out_shape=[jax.ShapeDtypeStruct(shape, f32) for shape in outs],
-            in_specs=[SMEM] * scalars + [VMEM] * (len(args) - scalars),
+            in_specs=[SMEM if arg.dtype == jnp.int32 else VMEM for arg in args],
+            cost_estimate=pl.CostEstimate(flops=cost, bytes_accessed=cost // 256, transcendentals=0),
             out_specs=[VMEM] * len(outs),
             scratch_shapes=[pltpu.VMEM(shape, kind) for shape, kind in scratch],
             compiler_params=PARAMS,
@@ -301,59 +328,77 @@
     return state.reshape(kinds, across // 4, 4, along // 4, 4, levels).mean(axis=(2, 4))
 
 
+def strat_sources(by):
+    pairs = []
+    for x, zl, c, zh, y in itertools.product(*map(range, SIZES)):
+        from_zh, from_y = divmod((4 * zh + y + by) % 8, 4)
+        from_zl = zl if from_zh == zh else 3 - zl
+        source = (((x * 4 + from_zl) * 2 + c) * 2 + from_zh) * 4 + from_y
+        pairs.append((source, (((x * 4 + zl) * 2 + c) * 2 + zh) * 4 + y))
+    return pairs
+
+
 def per_device(slice_starts, coriolis, stratification, inverse_blocks):
     f32, bf16 = jnp.float32, jnp.bfloat16
     start = slice_starts[0]
     fine_scratch = [((3, WIDE, 32, 128), f32)] * 2 + [((WIDE, 32, 128), f32)]
-    chain_scratch = [((3, 32, 8, 128), f32), ((3, 256, 256), bf16), ((8, 12, 8, 128), f32)]
-
-    head = jnp.concatenate([start[:, :8].reshape(24, 32, 128), stratification[:6]])
-    tail = jnp.concatenate([start[:, 8:].reshape(24, 32, 128), stratification[10:]])
+    halves, state = ((3, 256, 256), bf16), ((3, 32, 8, 128), f32)
+    increments = ((8, 12, 8, 128), f32)
+
+    head = jnp.concatenate([start[0, :8], start[1, :7], start[2, :8]])
+    tail = jnp.concatenate([start[0, 8:], start[1, 9:], start[2, 8:]])
     left = lax.ppermute(tail, SPACE, ring(8, 1))
     right = lax.ppermute(head, SPACE, ring(8, -1))
+    left_strat = lax.ppermute(stratification[10:], AXES, strat_sources(-1))
+    right_strat = lax.ppermute(stratification[:6], AXES, strat_sources(1))
     mean = restrict(start)
     next_mean = lax.ppermute(mean, TM, ring(32, -1))
-
-    where = jnp.stack([lax.axis_index(name) for name in ("zl", "c", "x", "zh", "y")]).astype(jnp.int32)
+    own_strat = restrict(stratification[None])[0]
+    strat_parts = [own_strat] + [lax.ppermute(own_strat, "y", ring(4, by)) for by in (1, 2, 3)]
+
+    spots = [lax.axis_index(name).astype(jnp.int32) for name in ("zl", "c", "x", "zh", "y")]
+    where = jnp.stack(spots)
     half_spin = jnp.broadcast_to(0.5 * coriolis[:, None], (32, 128))
     coarse_spin = jnp.broadcast_to(4.0 * coriolis.reshape(8, 4).mean(axis=1)[:, None], (8, 128))
     turned = jnp.swapaxes(inverse_blocks, 1, 2)
     top = lax.reduce_precision(turned, exponent_bits=8, mantissa_bits=7)
     wide = jnp.concatenate([top, turned - top], axis=2).astype(bf16)
     blocks = jnp.concatenate([wide, wide], axis=1)
-    own_strat = restrict(stratification[None])[0]
-    strat_mine = jnp.stack(
-        [own_strat] + [lax.ppermute(own_strat, "y", ring(4, by)) for by in (1, 2, 3)]
-    )
-    strat_other = lax.ppermute(strat_mine, "zh", ring(2, 1))
-
-    low, high = call(first_half_kernel, [(3, 8, 32, 128)] * 2, fine_scratch)(
-        half_spin, left, start, right, stratification
+
+    middle, low, high, near = call(
+        first_half_kernel,
+        [(3, 16, 32, 128), (23, 32, 128), (23, 32, 128), (4, 4, 8, 128)],
+        fine_scratch,
+    )(
+        half_spin, spots[4][None], *strat_parts, left_strat, right_strat, stratification,
+        start, left, right,
     )
     left_again = lax.ppermute(high, SPACE, ring(8, 1))
     right_again = lax.ppermute(low, SPACE, ring(8, -1))
-    detail, increment = call(
+    far = lax.ppermute(near, "zh", ring(2, 1))
+    detail, increment, strat = call(
         second_half_kernel,
-        [(3, 16, 32, 128), (12, 8, 128)],
+        [(3, 16, 32, 128), (12, 8, 128), (32, 8, 128)],
         fine_scratch + [((4, 32, 128), f32)],
     )(
-        half_spin, left_again, low, high, right_again, left, right, stratification, next_mean
+        half_spin, spots[3][None], near, far, next_mean, left_strat, right_strat,
+        stratification, middle, left_again, right_again,
     )
 
     mine = [increment] + [lax.ppermute(increment, "zl", ring(4, by)) for by in (1, 2, 3)]
     other = [lax.ppermute(part, "c", ring(2, 1)) for part in mine]
     detail = lax.ppermute(detail, TM, ring(32, 1))
-    end, part, strat = call(
-        plane_kernel, [(3, 32, 8, 128), (3, 16, 8, 128), (32, 8, 128)], chain_scratch, 1
-    )(where, coarse_spin, blocks, strat_mine, strat_other, *mine, *other)
-    here = [lax.ppermute(part, "x", ring(4, by)) for by in (1, 2, 3)]
+    common = (where, coarse_spin, blocks, strat)
+    pair = [state[0], (3, 16, 8, 128)]
+    end, part = call(plane_kernel, pair, [halves, increments])(*common, *mine, *other)
+    here = [lax.ppermute(part, "x", ring(4, 1))]
+    for by in (2, 3):
+        end, part = call(power_kernel, pair, [halves], 10**9)(*common, end, *here[: by - 2])
+        here.append(lax.ppermute(part, "x", ring(4, by)))
     there = [lax.ppermute(part, "c", ring(2, 1)) for part in here]
-    parts = call(
-        chain_kernel,
-        [(2, 12, 8, 128)] * 4,
-        [((4, 3, 32, 8, 128), f32)] + chain_scratch,
-        1,
-    )(where, coarse_spin, blocks, strat, end, *mine, *other, *here, *there)
+    parts = call(chain_kernel, [(2, 12, 8, 128)] * 4, [state, halves, increments])(
+        *common, end, *mine, *other, *here[::-1], *there[::-1]
+    )
     total = parts[0]
     for by in (1, 2, 3):
         total = total + lax.ppermute(parts[by], "y", ring(4, by))

time: 125 us -> 132 us (1.056)
  waiting for transfers between devices: 54.1 us -> 60.9 us
  starting transfers between devices: 43.7 us -> 39.3 us
  Pallas kernels: 22.8 us -> 25.3 us
  local copies, waits for them, and re-layouts: 3.14 us -> 4.93 us
    ppermute x4 -> x6, waiting for transfers between devices: 8.97 us -> 27.5 us  [the longest x1 19.5 us: per_device(): right_strat = lax.ppermute(stratification[:6], AXES, strat_sources(1))]
    ppermute x3, starting transfers between devices: 17.4 us -> 3.01 us  [per_device(): lax.ppermute(increment, 'zl', ring(4, by))]
    ppermute x1, waiting for transfers between devices: 0.01 us -> 12.1 us  [per_device(): next_mean = lax.ppermute(mean, TM, ring(32, -1))]
    ppermute x1, waiting for transfers between devices: 8.81 us -> 0.01 us  [per_device(): left = lax.ppermute(tail, SPACE, ring(8, 1))]
    ppermute x1, waiting for transfers between devices: 8.49 us -> 0.01 us  [per_device(): right = lax.ppermute(head, SPACE, ring(8, -1))]
    ppermute x4 -> x6, starting transfers between devices: 6.21 us -> 13.5 us  [the longest x1 5.94 us: per_device(): left_strat = lax.ppermute(stratification[10:], AXES, strat_sources(-1))]
    ppermute x1, waiting for transfers between devices: 4.48 us -> 0.01 us  [per_device(): left_again = lax.ppermute(high, SPACE, ring(8, 1))]
    pallas_call x5 -> x7, Pallas kernels: 22.8 us -> 25.3 us  [run(): pl.pallas_call(kernel, out_shape=[jax.ShapeDtypeStruct(shape, f32) for sh...]
  transfers between devices with their start and end apart: 27 -> 29, of which waited for: 16 -> 15; matrix products, arithmetic and copies ran while one was open for 1% -> 2% of each run, Pallas kernels for 15% -> 7%
where the time goes in v3:
time: 132 us
  waiting for transfers between devices  60.9 us (46%)
  starting transfers between devices  39.3 us (30%)
  Pallas kernels  25.3 us (19%)
  local copies, waits for them, and re-layouts  4.93 us (4%)
  other arithmetic  1.52 us (1%)
    pallas_call x7, Pallas kernels, run(): pl.pallas_call(kernel, out_shape=[jax.ShapeDtypeStruct(shape, f32) for sh...  25.3 us
    ppermute x1, waiting for transfers between devices, per_device(): right_strat = lax.ppermute(stratification[:6], AXES, strat_sources(1))  19.5 us
    ppermute x1, waiting for transfers between devices, per_device(): next_mean = lax.ppermute(mean, TM, ring(32, -1))  12.1 us
    ppermute x1, starting transfers between devices, per_device(): left = lax.ppermute(tail, SPACE, ring(8, 1))  7.67 us
    ppermute x3, waiting for transfers between devices, per_device(): total = total + lax.ppermute(parts[by], 'y', ring(4, by))  6.09 us
    ppermute x1, starting transfers between devices, per_device(): left_strat = lax.ppermute(stratification[10:], AXES, strat_sources(-1))  5.94 us
    ppermute x1, waiting for transfers between devices, per_device(): sent = lax.ppermute(total[1], 'zh', ring(2, 1))  5.25 us
    ppermute x3, waiting for transfers between devices, per_device(): lax.ppermute(increment, 'zl', ring(4, by))  5.18 us
  transfers between devices with their start and end apart: 29, of which 15 were waited for; matrix products, arithmetic and copies ran while one was open for 2% of the time, Pallas kernels for 7%

profile of v3, /device:TPU:24, one launch (start us, length us, event | category | flops | bytes accessed | tf_op | source)
XLA Modules:
  0.0 132.1 jit_solution(13394761486704554538)
XLA Ops:
  1.9 2.7 %collective-permute-start.1 = (f32[4,8,128]{2,1,0:T(8,128)S(1)}, f32[4,8,128]{2,1,0:T(8,128)S(1)}, u32[]{:S(2)}, u32[]{:S(2)}) collective-permute-start(f32[4,8,128]{2,1,0:T(8,128)S(1)} %broadcast_multiply_fusion.1.c0), channel_id=1, source_target_pairs={{0,2},{1,3},{2,0},{3,1},{4,6},{5,7},{6,4},{7,5},{8,10},{9,11},{10,... | collective-permute-start | bytes 49160 | tf_op jit(solution)/shard_map/ppermute | solution.py:357
  7.1 7.7 %collective-permute-start.5 = (f32[23,32,128]{2,1,0:T(8,128)S(1)}, f32[23,32,128]{2,1,0:T(8,128)S(1)}, u32[]{:S(2)}, u32[]{:S(2)}) collective-permute-start(f32[23,32,128]{2,1,0:T(8,128)S(1)} %pad_maximum_fusion), channel_id=1, source_target_pairs={{0,1},{1,2},{2,3},{3,4},{4,5},{5,6},{6,7},{7,0},{8,9},{9,10},{10,1... | collective-permute-start | bytes 1130504 | tf_op jit(solution)/shard_map/ppermute | solution.py:350
  15.9 5.9 %collective-permute-start.3 = (f32[6,32,128]{2,1,0:T(8,128)S(1)}, f32[6,32,128]{2,1,0:T(8,128)S(1)}, u32[]{:S(2)}, u32[]{:S(2)}) collective-permute-start(f32[6,32,128]{2,1,0:T(8,128)S(1)} %get-tuple-element.46), channel_id=1, source_target_pairs={{55,0},{0,1},{1,2},{2,3},{51,4},{4,5},{5,6},{6,7},{63,8},{8,9},{9,... | collective-permute-start | bytes 294920 | tf_op jit(solution)/shard_map/ppermute | solution.py:352
  21.9 19.5 %collective-permute-done.4.right_strat = f32[6,32,128]{2,1,0:T(8,128)S(1)} collective-permute-done((f32[6,32,128]{2,1,0:T(8,128)S(1)}, f32[6,32,128]{2,1,0:T(8,128)S(1)}, u32[]{:S(2)}, u32[]{:S(2)}) %collective-permute-start.4) | collective-permute-done | bytes 98336 | tf_op jit(solution)/shard_map/ppermute | solution.py:353
  41.5 6.3 %shard_map.46 = (f32[3,16,32,128]{3,2,1,0:T(8,128)S(1)}, f32[23,32,128]{2,1,0:T(8,128)S(1)}, f32[23,32,128]{2,1,0:T(8,128)}, f32[4,4,8,128]{3,2,1,0:T(8,128)S(1)}) custom-call(f32[32,128]{1,0:T(8,128)S(1)} %broadcast_in_dim.7.spin, s32[1]{0:T(128)} %bitcast.4.y, f32[4,8,128]{2,1,0:T(8,128)S(1)} %broadcast_multiply_fusion.1.c0, ...), custom_call_target="tpu_custom_call" | custom-call | tf_op jit(solution)/shard_map/pallas_call | solution.py:313
  51.0 2.2 %collective-permute-start.8 = (f32[3,4,8,128]{3,2,1,0:T(8,128)S(1)}, f32[3,4,8,128]{3,2,1,0:T(8,128)S(1)}, u32[]{:S(2)}, u32[]{:S(2)}) collective-permute-start(f32[3,4,8,128]{3,2,1,0:T(8,128)S(1)} %broadcast_multiply_fusion.mean), channel_id=1, source_target_pairs={{0,248},{8,0},{16,8},{24,16},{32,24},{40,32},{48,40},{56,48},{64,5... | collective-permute-start | bytes 147464 | tf_op jit(solution)/shard_map/ppermute | solution.py:355
  53.3 12.1 %collective-permute-done.8.next_mean = f32[3,4,8,128]{3,2,1,0:T(8,128)S(1)} collective-permute-done((f32[3,4,8,128]{3,2,1,0:T(8,128)S(1)}, f32[3,4,8,128]{3,2,1,0:T(8,128)S(1)}, u32[]{:S(2)}, u32[]{:S(2)}) %collective-permute-start.8) | collective-permute-done | bytes 49184 | tf_op jit(solution)/shard_map/ppermute | solution.py:355
  65.5 3.2 %collective-permute-done.7.far = f32[4,4,8,128]{3,2,1,0:T(8,128)S(1)} collective-permute-done((f32[4,4,8,128]{3,2,1,0:T(8,128)S(1)}, f32[4,4,8,128]{3,2,1,0:T(8,128)S(1)}, u32[]{:S(2)}, u32[]{:S(2)}) %collective-permute-start.7) | collective-permute-done | bytes 65568 | tf_op jit(solution)/shard_map/ppermute | solution.py:378
  68.7 3.5 %collective-permute-done.10.right = f32[23,32,128]{2,1,0:T(8,128)S(1)} collective-permute-done((f32[23,32,128]{2,1,0:T(8,128)S(1)}, f32[23,32,128]{2,1,0:T(8,128)S(1)}, u32[]{:S(2)}, u32[]{:S(2)}) %collective-permute-start.10) | collective-permute-done | bytes 376864 | tf_op jit(solution)/shard_map/ppermute | solution.py:377
  72.3 5.6 %shard_map.47 = (f32[3,16,32,128]{3,2,1,0:T(8,128)S(1)}, f32[12,8,128]{2,1,0:T(8,128)S(1)}, f32[32,8,128]{2,1,0:T(8,128)S(1)}) custom-call(f32[32,128]{1,0:T(8,128)S(1)} %broadcast_in_dim.7.spin, s32[1]{0:T(128)} %bitcast.3.zh, f32[4,4,8,128]{3,2,1,0:T(8,128)S(1)} %get-tuple-element.22.near, f32[4,4,8,128]{3,2,1,0:T(8,128)S(1)} %collective-permute-done.7.far, ...), custom_call_target="tpu_custom_call" | custom-call | tf_op jit(solution)/shard_map/pallas_call | solution.py:313
  78.8 2.4 %collective-permute-start.13 = (f32[12,8,128]{2,1,0:T(8,128)S(1)}, f32[12,8,128]{2,1,0:T(8,128)S(1)}, u32[]{:S(2)}, u32[]{:S(2)}) collective-permute-start(f32[12,8,128]{2,1,0:T(8,128)S(1)} %get-tuple-element.27.refs_0_), channel_id=1, source_target_pairs={{0,48},{16,0},{32,16},{48,32},{1,49},{17,1},{33,17},{49,33},{2,50}... | collective-permute-start | bytes 147464 | tf_op jit(solution)/shard_map/ppermute | solution.py:388
  83.4 2.8 %collective-permute-done.12.refs_2_ = f32[12,8,128]{2,1,0:T(8,128)S(1)} collective-permute-done((f32[12,8,128]{2,1,0:T(8,128)S(1)}, f32[12,8,128]{2,1,0:T(8,128)S(1)}, u32[]{:S(2)}, u32[]{:S(2)}) %collective-permute-start.12) | collective-permute-done | bytes 49184 | tf_op jit(solution)/shard_map/ppermute | solution.py:388
  88.5 2.8 %shard_map.48 = (f32[3,32,8,128]{3,2,1,0:T(8,128)S(1)}, f32[3,16,8,128]{3,2,1,0:T(8,128)S(1)}) custom-call(s32[5]{0:T(128)S(1)} %stack.23.where, f32[8,128]{1,0:T(8,128)S(1)} %broadcast_in_dim.6.spin, bf16[3,256,256]{2,1,0:T(8,128)(2,1)S(1)} %maximum_maximum_fusion.blocks, f32[32,8,128]{2,1,0:T(8,128)S(1)} %get-tuple-element.26.strat, ...), custom_call_target="tpu_custom_call" | custom-call | tf_op jit(solution)/shard_map/pallas_call | solution.py:313
  91.3 1.6 %collective-permute-start.18 = (f32[3,16,8,128]{3,2,1,0:T(8,128)S(1)}, f32[3,16,8,128]{3,2,1,0:T(8,128)S(1)}, u32[]{:S(2)}, u32[]{:S(2)}) collective-permute-start(f32[3,16,8,128]{3,2,1,0:T(8,128)S(1)} %get-tuple-element.30), channel_id=1, source_target_pairs={{0,64},{64,128},{128,192},{192,0},{1,65},{65,129},{129,193},{193,1... | collective-permute-start | bytes 589832 | tf_op jit(solution)/shard_map/ppermute | solution.py:394
  92.9 3.0 %shard_map.49 = (f32[3,32,8,128]{3,2,1,0:T(8,128)S(1)}, f32[3,16,8,128]{3,2,1,0:T(8,128)S(1)}) custom-call(s32[5]{0:T(128)S(1)} %stack.23.where, f32[8,128]{1,0:T(8,128)S(1)} %broadcast_in_dim.6.spin, bf16[3,256,256]{2,1,0:T(8,128)(2,1)S(1)} %maximum_maximum_fusion.blocks, f32[32,8,128]{2,1,0:T(8,128)S(1)} %get-tuple-element.26.strat, ...), custom_call_target="tpu_custom_call" | custom-call | flops 1000000000 | bytes 3906250 | tf_op jit(solution)/shard_map/pallas_call | solution.py:313
  95.9 2.8 %collective-permute-start.20 = (f32[3,16,8,128]{3,2,1,0:T(8,128)S(1)}, f32[3,16,8,128]{3,2,1,0:T(8,128)S(1)}, u32[]{:S(2)}, u32[]{:S(2)}) collective-permute-start(f32[3,16,8,128]{3,2,1,0:T(8,128)S(1)} %get-tuple-element.33), channel_id=1, source_target_pairs={{0,128},{64,192},{128,0},{192,64},{1,129},{65,193},{129,1},{193,65... | collective-permute-start | bytes 589832 | tf_op jit(solution)/shard_map/ppermute | solution.py:397
  99.7 3.0 %shard_map.50 = (f32[3,32,8,128]{3,2,1,0:T(8,128)S(1)}, f32[3,16,8,128]{3,2,1,0:T(8,128)S(1)}) custom-call(s32[5]{0:T(128)S(1)} %stack.23.where, f32[8,128]{1,0:T(8,128)S(1)} %broadcast_in_dim.6.spin, bf16[3,256,256]{2,1,0:T(8,128)(2,1)S(1)} %maximum_maximum_fusion.blocks, f32[32,8,128]{2,1,0:T(8,128)S(1)} %get-tuple-element.26.strat, ...), custom_call_target="tpu_custom_call" | custom-call | flops 1000000000 | bytes 3906250 | tf_op jit(solution)/shard_map/pallas_call | solution.py:313
  102.7 2.1 %collective-permute-start.19 = (f32[3,16,8,128]{3,2,1,0:T(8,128)S(1)}, f32[3,16,8,128]{3,2,1,0:T(8,128)S(1)}, u32[]{:S(2)}, u32[]{:S(2)}) collective-permute-start(f32[3,16,8,128]{3,2,1,0:T(8,128)S(1)} %get-tuple-element.32), channel_id=1, source_target_pairs={{0,192},{64,0},{128,64},{192,128},{1,193},{65,1},{129,65},{193,129... | collective-permute-start | bytes 589832 | tf_op jit(solution)/shard_map/ppermute | solution.py:397
  105.4 3.7 %collective-permute-done.19.refs_8_ = f32[3,16,8,128]{3,2,1,0:T(8,128)S(1)} collective-permute-done((f32[3,16,8,128]{3,2,1,0:T(8,128)S(1)}, f32[3,16,8,128]{3,2,1,0:T(8,128)S(1)}, u32[]{:S(2)}, u32[]{:S(2)}) %collective-permute-start.19) | collective-permute-done | bytes 196640 | tf_op jit(solution)/shard_map/ppermute | solution.py:397
  110.5 3.6 %shard_map.51 = (f32[2,12,8,128]{3,2,1,0:T(8,128)S(1)}, f32[2,12,8,128]{3,2,1,0:T(8,128)S(1)}, f32[2,12,8,128]{3,2,1,0:T(8,128)S(1)}, f32[2,12,8,128]{3,2,1,0:T(8,128)S(1)}) custom-call(s32[5]{0:T(128)S(1)} %stack.23.where, f32[8,128]{1,0:T(8,128)S(1)} %broadcast_in_dim.6.spin, bf16[3,256,256]{2,1,0:T(8,128)(2,1)S(1)} %maximum_maximum_fusion.blocks, ...), custom_call_target="tpu_custom_call" | custom-call | tf_op jit(solution)/shard_map/pallas_call | solution.py:313
  116.4 2.4 %collective-permute-done.24 = f32[2,12,8,128]{3,2,1,0:T(8,128)S(1)} collective-permute-done((f32[2,12,8,128]{3,2,1,0:T(8,128)S(1)}, f32[2,12,8,128]{3,2,1,0:T(8,128)S(1)}, u32[]{:S(2)}, u32[]{:S(2)}) %collective-permute-start.24) | collective-permute-done | bytes 98336 | tf_op jit(solution)/shard_map/ppermute | solution.py:404
  118.8 2.9 %collective-permute-done.25 = f32[2,12,8,128]{3,2,1,0:T(8,128)S(1)} collective-permute-done((f32[2,12,8,128]{3,2,1,0:T(8,128)S(1)}, f32[2,12,8,128]{3,2,1,0:T(8,128)S(1)}, u32[]{:S(2)}, u32[]{:S(2)}) %collective-permute-start.25) | collective-permute-done | bytes 98336 | tf_op jit(solution)/shard_map/ppermute | solution.py:404
  122.6 3.4 %collective-permute-start.27 = (f32[12,8,128]{2,1,0:T(8,128)S(1)}, f32[12,8,128]{2,1,0:T(8,128)S(1)}, u32[]{:S(2)}, u32[]{:S(2)}) collective-permute-start(f32[12,8,128]{2,1,0:T(8,128)S(1)} %get-tuple-element.49), channel_id=1, source_target_pairs={{0,4},{4,0},{1,5},{5,1},{2,6},{6,2},{3,7},{7,3},{8,12},{12,8},{9,1... | collective-permute-start | bytes 147464 | tf_op jit(solution)/shard_map/ppermute | solution.py:405
  125.9 5.2 %collective-permute-done.27.sent = f32[12,8,128]{2,1,0:T(8,128)S(1)} collective-permute-done((f32[12,8,128]{2,1,0:T(8,128)S(1)}, f32[12,8,128]{2,1,0:T(8,128)S(1)}, u32[]{:S(2)}, u32[]{:S(2)}) %collective-permute-start.27) | collective-permute-done | bytes 49184 | tf_op jit(solution)/shard_map/ppermute | solution.py:405
  (75 shorter events, 21.2 us)
Async XLA Ops:
  1.0 14.8 %collective-permute-start.2 = (f32[4,8,128]{2,1,0:T(8,128)S(1)}, f32[4,8,128]{2,1,0:T(8,128)S(1)}, u32[]{:S(2)}, u32[]{:S(2)}) collective-permute-start(f32[4,8,128]{2,1,0:T(8,128)S(1)} %broadcast_multiply_fusion.1.c0), channel_id=1, source_target_pairs={{0,3},{1,0},{2,1},{3,2},{4,7},{5,4},{6,5},{7,6},{8,11},{9,8},{10,9... | collective-permute-start | bytes 49160 | tf_op jit(solution)/shard_map/ppermute | solution.py:357
  1.9 14.0 %collective-permute-start.1 = (f32[4,8,128]{2,1,0:T(8,128)S(1)}, f32[4,8,128]{2,1,0:T(8,128)S(1)}, u32[]{:S(2)}, u32[]{:S(2)}) collective-permute-start(f32[4,8,128]{2,1,0:T(8,128)S(1)} %broadcast_multiply_fusion.1.c0), channel_id=1, source_target_pairs={{0,2},{1,3},{2,0},{3,1},{4,6},{5,7},{6,4},{7,5},{8,10},{9,11},{10,... | collective-permute-start | bytes 49160 | tf_op jit(solution)/shard_map/ppermute | solution.py:357
  4.5 17.3 %collective-permute-start = (f32[4,8,128]{2,1,0:T(8,128)S(1)}, f32[4,8,128]{2,1,0:T(8,128)S(1)}, u32[]{:S(2)}, u32[]{:S(2)}) collective-permute-start(f32[4,8,128]{2,1,0:T(8,128)S(1)} %broadcast_multiply_fusion.1.c0), channel_id=1, source_target_pairs={{0,1},{1,2},{2,3},{3,0},{4,5},{5,6},{6,7},{7,4},{8,9},{9,10},{10,1... | collective-permute-start | bytes 49160 | tf_op jit(solution)/shard_map/ppermute | solution.py:357
  7.1 34.3 %collective-permute-start.5 = (f32[23,32,128]{2,1,0:T(8,128)S(1)}, f32[23,32,128]{2,1,0:T(8,128)S(1)}, u32[]{:S(2)}, u32[]{:S(2)}) collective-permute-start(f32[23,32,128]{2,1,0:T(8,128)S(1)} %pad_maximum_fusion), channel_id=1, source_target_pairs={{0,1},{1,2},{2,3},{3,4},{4,5},{5,6},{6,7},{7,0},{8,9},{9,10},{10,1... | collective-permute-start | bytes 1130504 | tf_op jit(solution)/shard_map/ppermute | solution.py:350
  14.8 26.6 %collective-permute-start.6 = (f32[23,32,128]{2,1,0:T(8,128)S(1)}, f32[23,32,128]{2,1,0:T(8,128)S(1)}, u32[]{:S(2)}, u32[]{:S(2)}) collective-permute-start(f32[23,32,128]{2,1,0:T(8,128)S(1)} %pad_maximum_fusion.1), channel_id=1, source_target_pairs={{0,7},{1,0},{2,1},{3,2},{4,3},{5,4},{6,5},{7,6},{8,15},{9,8},{10,9... | collective-permute-start | bytes 1130504 | tf_op jit(solution)/shard_map/ppermute | solution.py:351
  15.8 25.6 %collective-permute-start.4 = (f32[6,32,128]{2,1,0:T(8,128)S(1)}, f32[6,32,128]{2,1,0:T(8,128)S(1)}, u32[]{:S(2)}, u32[]{:S(2)}) collective-permute-start(f32[6,32,128]{2,1,0:T(8,128)S(1)} %get-tuple-element.45), channel_id=1, source_target_pairs={{1,0},{2,1},{3,2},{52,3},{5,4},{6,5},{7,6},{48,7},{9,8},{10,9},{11... | collective-permute-start | bytes 294920 | tf_op jit(solution)/shard_map/ppermute | solution.py:353
  15.9 25.5 %collective-permute-start.3 = (f32[6,32,128]{2,1,0:T(8,128)S(1)}, f32[6,32,128]{2,1,0:T(8,128)S(1)}, u32[]{:S(2)}, u32[]{:S(2)}) collective-permute-start(f32[6,32,128]{2,1,0:T(8,128)S(1)} %get-tuple-element.46), channel_id=1, source_target_pairs={{55,0},{0,1},{1,2},{2,3},{51,4},{4,5},{5,6},{6,7},{63,8},{8,9},{9,... | collective-permute-start | bytes 294920 | tf_op jit(solution)/shard_map/ppermute | solution.py:352
  47.8 21.0 %collective-permute-start.9 = (f32[23,32,128]{2,1,0:T(8,128)}, f32[23,32,128]{2,1,0:T(8,128)S(1)}, u32[]{:S(2)}, u32[]{:S(2)}) collective-permute-start(f32[23,32,128]{2,1,0:T(8,128)} %get-tuple-element.24), channel_id=1, source_target_pairs={{0,1},{1,2},{2,3},{3,4},{4,5},{5,6},{6,7},{7,0},{8,9},{9,10},{10,1... | collective-permute-start | bytes 1130504 | tf_op jit(solution)/shard_map/ppermute | solution.py:376
  48.6 23.7 %collective-permute-start.10 = (f32[23,32,128]{2,1,0:T(8,128)S(1)}, f32[23,32,128]{2,1,0:T(8,128)S(1)}, u32[]{:S(2)}, u32[]{:S(2)}) collective-permute-start(f32[23,32,128]{2,1,0:T(8,128)S(1)} %get-tuple-element.25), channel_id=1, source_target_pairs={{0,7},{1,0},{2,1},{3,2},{4,3},{5,4},{6,5},{7,6},{8,15},{9,8},{10,9... | collective-permute-start | bytes 1130504 | tf_op jit(solution)/shard_map/ppermute | solution.py:377
  50.0 18.7 %collective-permute-start.7 = (f32[4,4,8,128]{3,2,1,0:T(8,128)S(1)}, f32[4,4,8,128]{3,2,1,0:T(8,128)S(1)}, u32[]{:S(2)}, u32[]{:S(2)}) collective-permute-start(f32[4,4,8,128]{3,2,1,0:T(8,128)S(1)} %get-tuple-element.22.near), channel_id=1, source_target_pairs={{0,4},{4,0},{1,5},{5,1},{2,6},{6,2},{3,7},{7,3},{8,12},{12,8},{9,1... | collective-permute-start | bytes 196616 | tf_op jit(solution)/shard_map/ppermute | solution.py:378
  51.0 14.5 %collective-permute-start.8 = (f32[3,4,8,128]{3,2,1,0:T(8,128)S(1)}, f32[3,4,8,128]{3,2,1,0:T(8,128)S(1)}, u32[]{:S(2)}, u32[]{:S(2)}) collective-permute-start(f32[3,4,8,128]{3,2,1,0:T(8,128)S(1)} %broadcast_multiply_fusion.mean), channel_id=1, source_target_pairs={{0,248},{8,0},{16,8},{24,16},{32,24},{40,32},{48,40},{56,48},{64,5... | collective-permute-start | bytes 147464 | tf_op jit(solution)/shard_map/ppermute | solution.py:355
  81.3 5.0 %collective-permute-start.12 = (f32[12,8,128]{2,1,0:T(8,128)S(1)}, f32[12,8,128]{2,1,0:T(8,128)S(1)}, u32[]{:S(2)}, u32[]{:S(2)}) collective-permute-start(f32[12,8,128]{2,1,0:T(8,128)S(1)} %get-tuple-element.27.refs_0_), channel_id=1, source_target_pairs={{0,32},{16,48},{32,0},{48,16},{1,33},{17,49},{33,1},{49,17},{2,34}... | collective-permute-start | bytes 147464 | tf_op jit(solution)/shard_map/ppermute | solution.py:388
  81.3 5.9 %collective-permute-start.11 = (f32[12,8,128]{2,1,0:T(8,128)S(1)}, f32[12,8,128]{2,1,0:T(8,128)S(1)}, u32[]{:S(2)}, u32[]{:S(2)}) collective-permute-start(f32[12,8,128]{2,1,0:T(8,128)S(1)} %get-tuple-element.27.refs_0_), channel_id=1, source_target_pairs={{0,16},{16,32},{32,48},{48,0},{1,17},{17,33},{33,49},{49,1},{2,18}... | collective-permute-start | bytes 147464 | tf_op jit(solution)/shard_map/ppermute | solution.py:388
  81.9 6.3 %collective-permute-start.14 = (f32[12,8,128]{2,1,0:T(8,128)S(1)}, f32[12,8,128]{2,1,0:T(8,128)S(1)}, u32[]{:S(2)}, u32[]{:S(2)}) collective-permute-start(f32[12,8,128]{2,1,0:T(8,128)S(1)} %get-tuple-element.27.refs_0_), channel_id=1, source_target_pairs={{0,8},{8,0},{1,9},{9,1},{2,10},{10,2},{3,11},{11,3},{4,12},{12,4},... | collective-permute-start | bytes 147464 | tf_op jit(solution)/shard_map/ppermute | solution.py:389
  83.4 4.7 %collective-permute-start.17 = (f32[12,8,128]{2,1,0:T(8,128)S(1)}, f32[12,8,128]{2,1,0:T(8,128)S(1)}, u32[]{:S(2)}, u32[]{:S(2)}) collective-permute-start(f32[12,8,128]{2,1,0:T(8,128)S(1)} %collective-permute-done.13.refs_3_), channel_id=1, source_target_pairs={{0,8},{8,0},{1,9},{9,1},{2,10},{10,2},{3,11},{11,3},{4,12},{12,4},... | collective-permute-start | bytes 147464 | tf_op jit(solution)/shard_map/ppermute | solution.py:389
  91.3 8.4 %collective-permute-start.18 = (f32[3,16,8,128]{3,2,1,0:T(8,128)S(1)}, f32[3,16,8,128]{3,2,1,0:T(8,128)S(1)}, u32[]{:S(2)}, u32[]{:S(2)}) collective-permute-start(f32[3,16,8,128]{3,2,1,0:T(8,128)S(1)} %get-tuple-element.30), channel_id=1, source_target_pairs={{0,64},{64,128},{128,192},{192,0},{1,65},{65,129},{129,193},{193,1... | collective-permute-start | bytes 589832 | tf_op jit(solution)/shard_map/ppermute | solution.py:394
  95.9 9.0 %collective-permute-start.20 = (f32[3,16,8,128]{3,2,1,0:T(8,128)S(1)}, f32[3,16,8,128]{3,2,1,0:T(8,128)S(1)}, u32[]{:S(2)}, u32[]{:S(2)}) collective-permute-start(f32[3,16,8,128]{3,2,1,0:T(8,128)S(1)} %get-tuple-element.33), channel_id=1, source_target_pairs={{0,128},{64,192},{128,0},{192,64},{1,129},{65,193},{129,1},{193,65... | collective-permute-start | bytes 589832 | tf_op jit(solution)/shard_map/ppermute | solution.py:397
  102.7 6.3 %collective-permute-start.19 = (f32[3,16,8,128]{3,2,1,0:T(8,128)S(1)}, f32[3,16,8,128]{3,2,1,0:T(8,128)S(1)}, u32[]{:S(2)}, u32[]{:S(2)}) collective-permute-start(f32[3,16,8,128]{3,2,1,0:T(8,128)S(1)} %get-tuple-element.32), channel_id=1, source_target_pairs={{0,192},{64,0},{128,64},{192,128},{1,193},{65,1},{129,65},{193,129... | collective-permute-start | bytes 589832 | tf_op jit(solution)/shard_map/ppermute | solution.py:397
  104.8 4.7 %collective-permute-start.23 = (f32[3,16,8,128]{3,2,1,0:T(8,128)S(1)}, f32[3,16,8,128]{3,2,1,0:T(8,128)S(1)}, u32[]{:S(2)}, u32[]{:S(2)}) collective-permute-start(f32[3,16,8,128]{3,2,1,0:T(8,128)S(1)} %collective-permute-done.18.refs_0_.refs_10_), channel_id=1, source_target_pairs={{0,8},{8,0},{1,9},{9,1},{2,10},{10,2},{3,11},{11,3},{4,12},{12,4},... | collective-permute-start | bytes 589832 | tf_op jit(solution)/shard_map/ppermute | solution.py:398
  104.9 4.7 %collective-permute-start.22 = (f32[3,16,8,128]{3,2,1,0:T(8,128)S(1)}, f32[3,16,8,128]{3,2,1,0:T(8,128)S(1)}, u32[]{:S(2)}, u32[]{:S(2)}) collective-permute-start(f32[3,16,8,128]{3,2,1,0:T(8,128)S(1)} %collective-permute-done.20.refs_9_), channel_id=1, source_target_pairs={{0,8},{8,0},{1,9},{9,1},{2,10},{10,2},{3,11},{11,3},{4,12},{12,4},... | collective-permute-start | bytes 589832 | tf_op jit(solution)/shard_map/ppermute | solution.py:398
  109.0 16.9 %collective-permute-start.28 = (f32[3,16,32,128]{3,2,1,0:T(8,128)S(1)}, f32[3,16,32,128]{3,2,1,0:T(8,128)S(1)}, u32[]{:S(2)}, u32[]{:S(2)}) collective-permute-start(f32[3,16,32,128]{3,2,1,0:T(8,128)S(1)} %copy-done.3), channel_id=1, source_target_pairs={{0,8},{8,16},{16,24},{24,32},{32,40},{40,48},{48,56},{56,64},{64,7... | collective-permute-start | bytes 2359304 | tf_op jit(solution)/shard_map/ppermute | solution.py:390
  115.5 6.2 %collective-permute-start.25 = (f32[2,12,8,128]{3,2,1,0:T(8,128)S(1)}, f32[2,12,8,128]{3,2,1,0:T(8,128)S(1)}, u32[]{:S(2)}, u32[]{:S(2)}) collective-permute-start(f32[2,12,8,128]{3,2,1,0:T(8,128)S(1)} %get-tuple-element.36), channel_id=1, source_target_pairs={{0,2},{1,3},{2,0},{3,1},{4,6},{5,7},{6,4},{7,5},{8,10},{9,11},{10,... | collective-permute-start | bytes 294920 | tf_op jit(solution)/shard_map/ppermute | solution.py:404
  115.5 7.0 %collective-permute-start.26 = (f32[2,12,8,128]{3,2,1,0:T(8,128)S(1)}, f32[2,12,8,128]{3,2,1,0:T(8,128)S(1)}, u32[]{:S(2)}, u32[]{:S(2)}) collective-permute-start(f32[2,12,8,128]{3,2,1,0:T(8,128)S(1)} %get-tuple-element.37), channel_id=1, source_target_pairs={{0,3},{1,0},{2,1},{3,2},{4,7},{5,4},{6,5},{7,6},{8,11},{9,8},{10,9... | collective-permute-start | bytes 294920 | tf_op jit(solution)/shard_map/ppermute | solution.py:404
  122.6 8.6 %collective-permute-start.27 = (f32[12,8,128]{2,1,0:T(8,128)S(1)}, f32[12,8,128]{2,1,0:T(8,128)S(1)}, u32[]{:S(2)}, u32[]{:S(2)}) collective-permute-start(f32[12,8,128]{2,1,0:T(8,128)S(1)} %get-tuple-element.49), channel_id=1, source_target_pairs={{0,4},{4,0},{1,5},{5,1},{2,6},{6,2},{3,7},{7,3},{8,12},{12,8},{9,1... | collective-permute-start | bytes 147464 | tf_op jit(solution)/shard_map/ppermute | solution.py:405
  (12 other events, 69.6 us)

commit v4 on v3

--- a/solution.py
+++ b/solution.py
@@ -1,5 +1,3 @@
-import itertools
-
 import jax
 import jax.numpy as jnp
 from jax import lax
@@ -17,8 +15,11 @@
 SMEM = pl.BlockSpec(memory_space=pltpu.SMEM)
 PARAMS = pltpu.CompilerParams(vmem_limit_bytes=40 * 1024 * 1024)
 
-HALO = 8
+STEPS = 8
+HALO = 16
 WIDE = 16 + 2 * HALO
+COST = 10**10
+UNROLL = (11, 20, 18, 16, 14, 12, 10, 16)
 
 
 def ring(size, by):
@@ -33,121 +34,102 @@
     return pltpu.roll(q, 1, 0)
 
 
-def fine_steps(bufs, strat, half_spin, lane_weight):
-    def spread(q):
-        diff = (pltpu.roll(q, 127, 1) - q) * lane_weight
-        return diff - pltpu.roll(diff, 1, 1)
-
-    for step in range(4):
+def fine_steps(bufs, strat, half_spin, weights):
+    here_weight, up_weight, down_weight = weights
+
+    def vertical(q):
+        above, below = pltpu.roll(q, 127, 1), pltpu.roll(q, 1, 1)
+        return here_weight[...] * q + (up_weight[...] * above + down_weight[...] * below)
+
+    for step in range(STEPS):
         src, dst = bufs[step % 2], bufs[(step + 1) % 2]
-        reach = 2 * (3 - step)
+        reach = 2 * (STEPS - 1 - step)
         first = HALO - reach
         count = 16 + 2 * reach
+        unroll = UNROLL[step]
 
         def zonal(x, src=src):
             u = src[0, x]
             sides = src[0, x + 1] + src[0, x - 1] + (y_next(u) + y_prev(u))
             push = src[2, x + 1] - src[2, x - 1]
-            return (
-                (0.8 * u + spread(u))
-                + (half_spin[...] * src[1, x] - 0.25 * push)
-                + 0.05 * sides
-            )
-
-        def chunk(i, carry, src=src, dst=dst, first=first, zonal=zonal):
+            return vertical(u) + (half_spin[...] * src[1, x] - 0.25 * push) + 0.05 * sides
+
+        def chunk(i, carry, src=src, dst=dst, first=first, unroll=unroll, zonal=zonal):
             before, here = carry
-            for k in range(4):
-                x = first + 4 * i + k
+            for k in range(unroll):
+                x = first + unroll * i + k
                 after = zonal(x + 1)
                 dst[0, x] = here
                 v = src[1, x]
                 b = src[2, x]
                 b_next, b_prev = y_next(b), y_prev(b)
                 v_new = (
-                    (0.8 * v + spread(v))
+                    vertical(v)
                     - (half_spin[...] * here + 0.25 * (b_next - b_prev))
                     + 0.05 * (src[1, x + 1] + src[1, x - 1] + (y_next(v) + y_prev(v)))
                 )
                 dst[1, x] = v_new
                 flow = (after - before) + (y_next(v_new) - y_prev(v_new))
                 dst[2, x] = (
-                    (0.8 * b + spread(b))
+                    vertical(b)
                     - strat[x] * flow
                     + 0.05 * (src[2, x + 1] + src[2, x - 1] + (b_next + b_prev))
                 )
                 before, here = here, after
             return before, here
 
-        lax.fori_loop(0, count // 4, chunk, (zonal(first - 1), zonal(first)))
-
-
-def lane_weights():
+        lax.fori_loop(0, count // unroll, chunk, (zonal(first - 1), zonal(first)))
+
+
+def block_means(rows, cells):
+    rows[...] = (cells[0] + cells[1]) + (cells[2] + cells[3])
+    parts = [rows[pl.ds(j, 8, stride=4), :] for j in range(4)]
+    return ((parts[0] + parts[1]) + (parts[2] + parts[3])) * 0.0625
+
+
+def means_kernel(start, strat, mean, own_strat, rows):
+    for k in range(3):
+        for cell in range(4):
+            cells = [start[k, 4 * cell + j] for j in range(4)]
+            mean[k, cell] = block_means(rows.at[cell % 2], cells)
+    for cell in range(4):
+        cells = [strat[4 * cell + j] for j in range(4)]
+        own_strat[cell] = block_means(rows.at[cell % 2], cells)
+
+
+def fine_kernel(
+    spin, place, near, far, blocks, next_mean, own, left, right,
+    detail, increment, coarse_strat, one, two, strat, rows, weights,
+):
+    del blocks
+    for k in range(3):
+        for x in range(16):
+            one[k, x] = left[16 * k + x]
+            one[k, 16 + x] = own[16 * k + x]
+            one[k, 32 + x] = right[16 * k + x]
+    for x in range(16):
+        strat[x] = 0.25 * left[48 + x]
+        strat[16 + x] = 0.25 * own[48 + x]
+        strat[32 + x] = 0.25 * right[48 + x]
+    zh, y = place[0], place[1]
+    for j in range(4):
+        column = (y - j + 4) % 4
+        for cell in range(4):
+            mine, other = 4 * zh + column, 4 * (1 - zh) + column
+            coarse_strat[4 * mine + cell] = 0.5 * near[j, cell]
+            coarse_strat[4 * other + cell] = 0.5 * far[j, cell]
     lane = lax.broadcasted_iota(jnp.int32, (32, 128), 1)
-    return jnp.where(lane < 127, 0.15, 0.0).astype(jnp.float32)
-
-
-def fill_strat(strat, left, own, right):
-    for x in range(6):
-        strat[HALO - 6 + x] = 0.25 * left[x]
-        strat[HALO + 16 + x] = 0.25 * right[x]
-    for x in range(16):
-        strat[HALO + x] = 0.25 * own[x]
-
-
-def fill_state(buf, left, own, right):
-    for k in range(3):
-        for x in range(16):
-            buf[k, HALO + x] = own[k, x]
-    for x in range(8):
-        buf[0, x] = left[x]
-        buf[2, x] = left[15 + x]
-        buf[0, 24 + x] = right[x]
-        buf[2, 24 + x] = right[15 + x]
-    for x in range(7):
-        buf[1, 1 + x] = left[8 + x]
-        buf[1, 24 + x] = right[8 + x]
-
-
-def first_half_kernel(
-    spin, y, c0, c1, c2, c3, left_strat, right_strat, own_strat, start, left, right,
-    middle, low, high, columns, one, two, strat,
-):
-    fill_state(one, left, start, right)
-    fill_strat(strat, left_strat, own_strat, right_strat)
-    for j, cells in enumerate((c0, c1, c2, c3)):
-        columns[(y[0] - j + 4) % 4] = cells[...]
-    fine_steps((one, two), strat, spin, lane_weights())
-    for k in range(3):
-        for x in range(16):
-            middle[k, x] = one[k, HALO + x]
-    for x in range(8):
-        low[x] = one[0, 8 + x]
-        low[15 + x] = one[2, 8 + x]
-        high[x] = one[0, 16 + x]
-        high[15 + x] = one[2, 16 + x]
-    for x in range(7):
-        low[8 + x] = one[1, 8 + x]
-        high[8 + x] = one[1, 17 + x]
-
-
-def second_half_kernel(
-    spin, zh, near, far, next_mean, left_strat, right_strat, own_strat, middle, left, right,
-    detail, increment, coarse_strat, one, two, strat, rows,
-):
-    fill_state(one, left, middle, right)
-    fill_strat(strat, left_strat, own_strat, right_strat)
-    for column in range(4):
-        for cell in range(4):
-            coarse_strat[16 * zh[0] + 4 * column + cell] = 0.5 * near[column, cell]
-            coarse_strat[16 * (1 - zh[0]) + 4 * column + cell] = 0.5 * far[column, cell]
-    fine_steps((one, two), strat, spin, lane_weights())
+    up = jnp.where(lane < 127, 0.15, 0.0).astype(jnp.float32)
+    down = jnp.where(lane > 0, 0.15, 0.0).astype(jnp.float32)
+    weights[0] = 0.8 - up - down
+    weights[1] = up
+    weights[2] = down
+    fine_steps((one, two), strat, spin, [weights.at[n] for n in range(3)])
     for k in range(3):
         for cell in range(4):
             x = HALO + 4 * cell
             slot = (4 * k + cell) % 2
-            rows[slot] = (one[k, x] + one[k, x + 1]) + (one[k, x + 2] + one[k, x + 3])
-            parts = [rows[slot, pl.ds(j, 8, stride=4), :] for j in range(4)]
-            mean = ((parts[0] + parts[1]) + (parts[2] + parts[3])) * 0.0625
+            mean = block_means(rows.at[slot], [one[k, x + j] for j in range(4)])
             increment[4 * k + cell] = mean - next_mean[k, cell]
             for j in range(4):
                 rows[2 + slot, pl.ds(j, 8, stride=4), :] = mean
@@ -194,8 +176,10 @@
 
 
 def table(where, increments, mine, other):
-    for j in range(4):
-        run = (where[0] - j + 4) % 4
+    zl = where[0]
+    low = zl % 2
+    beside = zl + 1 - 2 * low
+    for j, run in enumerate((zl, beside, (zl + 2) % 4, (beside + 2) % 4)):
         for n in range(12):
             increments[2 * run + where[1], n] = mine[j][n]
             increments[2 * run + 1 - where[1], n] = other[j][n]
@@ -323,38 +307,29 @@
     return run
 
 
-def restrict(state):
-    kinds, across, along, levels = state.shape
-    return state.reshape(kinds, across // 4, 4, along // 4, 4, levels).mean(axis=(2, 4))
-
-
-def strat_sources(by):
-    pairs = []
-    for x, zl, c, zh, y in itertools.product(*map(range, SIZES)):
-        from_zh, from_y = divmod((4 * zh + y + by) % 8, 4)
-        from_zl = zl if from_zh == zh else 3 - zl
-        source = (((x * 4 + from_zl) * 2 + c) * 2 + from_zh) * 4 + from_y
-        pairs.append((source, (((x * 4 + zl) * 2 + c) * 2 + zh) * 4 + y))
-    return pairs
+def swapped(by):
+    return [(i, i ^ by) for i in range(4)]
+
+
+def gathered(part, axis):
+    return jnp.stack([part] + [lax.ppermute(part, axis, ring(4, by)) for by in (1, 2, 3)])
 
 
 def per_device(slice_starts, coriolis, stratification, inverse_blocks):
     f32, bf16 = jnp.float32, jnp.bfloat16
     start = slice_starts[0]
-    fine_scratch = [((3, WIDE, 32, 128), f32)] * 2 + [((WIDE, 32, 128), f32)]
     halves, state = ((3, 256, 256), bf16), ((3, 32, 8, 128), f32)
     increments = ((8, 12, 8, 128), f32)
 
-    head = jnp.concatenate([start[0, :8], start[1, :7], start[2, :8]])
-    tail = jnp.concatenate([start[0, 8:], start[1, 9:], start[2, 8:]])
-    left = lax.ppermute(tail, SPACE, ring(8, 1))
-    right = lax.ppermute(head, SPACE, ring(8, -1))
-    left_strat = lax.ppermute(stratification[10:], AXES, strat_sources(-1))
-    right_strat = lax.ppermute(stratification[:6], AXES, strat_sources(1))
-    mean = restrict(start)
+    own = jnp.concatenate([start.reshape(48, 32, 128), stratification])
+    left = lax.ppermute(own, SPACE, ring(8, 1))
+    right = lax.ppermute(own, SPACE, ring(8, -1))
+    mean, own_strat = call(
+        means_kernel, [(3, 4, 8, 128), (4, 8, 128)], [((2, 32, 128), f32)], COST
+    )(start, stratification)
+    near = gathered(own_strat, "y")
+    far = lax.ppermute(near, "zh", ring(2, 1))
     next_mean = lax.ppermute(mean, TM, ring(32, -1))
-    own_strat = restrict(stratification[None])[0]
-    strat_parts = [own_strat] + [lax.ppermute(own_strat, "y", ring(4, by)) for by in (1, 2, 3)]
 
     spots = [lax.axis_index(name).astype(jnp.int32) for name in ("zl", "c", "x", "zh", "y")]
     where = jnp.stack(spots)
@@ -365,27 +340,18 @@
     wide = jnp.concatenate([top, turned - top], axis=2).astype(bf16)
     blocks = jnp.concatenate([wide, wide], axis=1)
 
-    middle, low, high, near = call(
-        first_half_kernel,
-        [(3, 16, 32, 128), (23, 32, 128), (23, 32, 128), (4, 4, 8, 128)],
-        fine_scratch,
+    detail, increment, strat = call(
+        fine_kernel,
+        [(3, 16, 32, 128), (12, 8, 128), (32, 8, 128)],
+        [((3, WIDE, 32, 128), f32)] * 2
+        + [((WIDE, 32, 128), f32), ((4, 32, 128), f32), ((3, 32, 128), f32)],
     )(
-        half_spin, spots[4][None], *strat_parts, left_strat, right_strat, stratification,
-        start, left, right,
+        half_spin, where[3:], near, far, blocks, next_mean, own, left, right
     )
-    left_again = lax.ppermute(high, SPACE, ring(8, 1))
-    right_again = lax.ppermute(low, SPACE, ring(8, -1))
-    far = lax.ppermute(near, "zh", ring(2, 1))
-    detail, increment, strat = call(
-        second_half_kernel,
-        [(3, 16, 32, 128), (12, 8, 128), (32, 8, 128)],
-        fine_scratch + [((4, 32, 128), f32)],
-    )(
-        half_spin, spots[3][None], near, far, next_mean, left_strat, right_strat,
-        stratification, middle, left_again, right_again,
-    )
-
-    mine = [increment] + [lax.ppermute(increment, "zl", ring(4, by)) for by in (1, 2, 3)]
+
+    beside = lax.ppermute(increment, "zl", swapped(1))
+    mine = [increment, beside]
+    mine += [lax.ppermute(part, "zl", swapped(2)) for part in (increment, beside)]
     other = [lax.ppermute(part, "c", ring(2, 1)) for part in mine]
     detail = lax.ppermute(detail, TM, ring(32, 1))
     common = (where, coarse_spin, blocks, strat)
@@ -393,7 +359,7 @@
     end, part = call(plane_kernel, pair, [halves, increments])(*common, *mine, *other)
     here = [lax.ppermute(part, "x", ring(4, 1))]
     for by in (2, 3):
-        end, part = call(power_kernel, pair, [halves], 10**9)(*common, end, *here[: by - 2])
+        end, part = call(power_kernel, pair, [halves], COST)(*common, end, *here[: by - 2])
         here.append(lax.ppermute(part, "x", ring(4, by)))
     there = [lax.ppermute(part, "c", ring(2, 1)) for part in here]
     parts = call(chain_kernel, [(2, 12, 8, 128)] * 4, [state, halves, increments])(

time: 132 us -> 132 us (level)
  waiting for transfers between devices: 60.9 us -> 49.2 us
  starting transfers between devices: 39.3 us -> 50.1 us
  other arithmetic: 1.52 us -> 2.92 us
    ppermute x12 -> x8, starting transfers between devices: 22.8 us -> 33.5 us  [the longest x1 16.8 us: per_device(): beside = lax.ppermute(increment, 'zl', swapped(1))]
    ppermute x1, waiting for transfers between devices: 12.1 us -> 4.24 us  [per_device(): next_mean = lax.ppermute(mean, TM, ring(32, -1))]
    ppermute x12 -> x8, waiting for transfers between devices: 28.3 us -> 23.2 us  [the longest x3 16.5 us: gathered(): lax.ppermute(part, axis, ring(4, by))]
    ppermute x1, starting transfers between devices: 3.36 us -> 0.86 us  [per_device(): sent = lax.ppermute(total[1], 'zh', ring(2, 1))]
    ppermute x1, waiting for transfers between devices: 5.25 us -> 7.52 us  [per_device(): sent = lax.ppermute(total[1], 'zh', ring(2, 1))]
    squeeze x2 -> x0, local copies, waits for them, and re-layouts: 2.1 us -> none  [per_device(): head = jnp.concatenate([start[0, :8], start[1, :7], start[2, :8]])]
    unnamed x15 -> x25, local copies, waits for them, and re-layouts: 2.5 us -> 3.51 us
  transfers between devices with their start and end apart: 29 -> 25, of which waited for: 15 -> 14; matrix products, arithmetic and copies ran while one was open for 2% -> 2% of each run, Pallas kernels for 7% -> 8%
where the time goes in v4:
time: 132 us; the launch traced here: 131 us
  starting transfers between devices  50.1 us (38%)
  waiting for transfers between devices  49.2 us (37%)
  Pallas kernels  25.1 us (19%)
  local copies, waits for them, and re-layouts  3.82 us (3%)
  other arithmetic  2.92 us (2%)
    pallas_call x7, Pallas kernels, run(): pl.pallas_call(kernel, out_shape=[jax.ShapeDtypeStruct(shape, f32) for sh...  25.1 us
    ppermute x1, starting transfers between devices, per_device(): beside = lax.ppermute(increment, 'zl', swapped(1))  16.8 us
    ppermute x3, waiting for transfers between devices, gathered(): lax.ppermute(part, axis, ring(4, by))  16.5 us
    ppermute x1, waiting for transfers between devices, per_device(): sent = lax.ppermute(total[1], 'zh', ring(2, 1))  7.52 us
    ppermute x1, starting transfers between devices, per_device(): left = lax.ppermute(own, SPACE, ring(8, 1))  6.93 us
    ppermute x3, waiting for transfers between devices, per_device(): total = total + lax.ppermute(parts[by], 'y', ring(4, by))  5.92 us
    ppermute x2, starting transfers between devices, per_device(): lax.ppermute(part, 'zl', swapped(2))  5.16 us
    ppermute x2, starting transfers between devices, per_device(): here.append(lax.ppermute(part, 'x', ring(4, by)))  4.97 us
  transfers between devices with their start and end apart: 25, of which 14 were waited for; matrix products, arithmetic and copies ran while one was open for 2% of the time, Pallas kernels for 8%

profile of v4, /device:TPU:24, one launch (start us, length us, event | category | flops | bytes accessed | tf_op | source)
XLA Modules:
  0.0 131.3 jit_solution(15269148205960455123)
XLA Ops:
  1.4 6.9 %collective-permute-start.5 = (f32[64,32,128]{2,1,0:T(8,128)S(1)}, f32[64,32,128]{2,1,0:T(8,128)S(1)}, u32[]{:S(2)}, u32[]{:S(2)}) collective-permute-start(f32[64,32,128]{2,1,0:T(8,128)S(1)} %pad_maximum_fusion.own), channel_id=1, source_target_pairs={{0,1},{1,2},{2,3},{3,4},{4,5},{5,6},{6,7},{7,0},{8,9},{9,10},{10,1... | collective-permute-start | bytes 3145736 | tf_op jit(solution)/shard_map/ppermute | solution.py:325
  8.5 3.2 %collective-permute-start = (f32[4,8,128]{2,1,0:T(8,128)S(1)}, f32[4,8,128]{2,1,0:T(8,128)}, u32[]{:S(2)}, u32[]{:S(2)}) collective-permute-start(f32[4,8,128]{2,1,0:T(8,128)S(1)} %get-tuple-element.20), channel_id=1, source_target_pairs={{0,1},{1,2},{2,3},{3,0},{4,5},{5,6},{6,7},{7,4},{8,9},{9,10},{10,1... | collective-permute-start | bytes 49160 | tf_op jit(solution)/shard_map/ppermute | solution.py:315
  14.8 16.5 %collective-permute-done.2 = f32[4,8,128]{2,1,0:T(8,128)} collective-permute-done((f32[4,8,128]{2,1,0:T(8,128)S(1)}, f32[4,8,128]{2,1,0:T(8,128)}, u32[]{:S(2)}, u32[]{:S(2)}) %collective-permute-start.2) | collective-permute-done | bytes 16416 | tf_op jit(solution)/shard_map/ppermute | solution.py:315
  31.3 2.5 %collective-permute-start.4 = (f32[3,4,8,128]{3,2,1,0:T(8,128)}, f32[3,4,8,128]{3,2,1,0:T(8,128)S(1)}, u32[]{:S(2)}, u32[]{:S(2)}) collective-permute-start(f32[3,4,8,128]{3,2,1,0:T(8,128)} %copy-done.5), channel_id=1, source_target_pairs={{0,248},{8,0},{16,8},{24,16},{32,24},{40,32},{48,40},{56,48},{64,5... | collective-permute-start | bytes 147464 | tf_op jit(solution)/shard_map/ppermute | solution.py:332
  34.5 2.0 %collective-permute-start.3 = (f32[4,4,8,128]{3,2,1,0:T(8,128)S(1)}, f32[4,4,8,128]{3,2,1,0:T(8,128)S(1)}, u32[]{:S(2)}, u32[]{:S(2)}) collective-permute-start(f32[4,4,8,128]{3,2,1,0:T(8,128)S(1)} %pad_maximum_fusion.1.near), channel_id=1, source_target_pairs={{0,4},{4,0},{1,5},{5,1},{2,6},{6,2},{3,7},{7,3},{8,12},{12,8},{9,1... | collective-permute-start | bytes 196616 | tf_op jit(solution)/shard_map/ppermute | solution.py:331
  36.6 4.2 %collective-permute-done.4.next_mean = f32[3,4,8,128]{3,2,1,0:T(8,128)S(1)} collective-permute-done((f32[3,4,8,128]{3,2,1,0:T(8,128)}, f32[3,4,8,128]{3,2,1,0:T(8,128)S(1)}, u32[]{:S(2)}, u32[]{:S(2)}) %collective-permute-start.4) | collective-permute-done | bytes 49184 | tf_op jit(solution)/shard_map/ppermute | solution.py:332
  40.8 2.0 %collective-permute-done.3.far = f32[4,4,8,128]{3,2,1,0:T(8,128)S(1)} collective-permute-done((f32[4,4,8,128]{3,2,1,0:T(8,128)S(1)}, f32[4,4,8,128]{3,2,1,0:T(8,128)S(1)}, u32[]{:S(2)}, u32[]{:S(2)}) %collective-permute-start.3) | collective-permute-done | bytes 65568 | tf_op jit(solution)/shard_map/ppermute | solution.py:331
  42.8 4.4 %collective-permute-done.6.right = f32[64,32,128]{2,1,0:T(8,128)S(1)} collective-permute-done((f32[64,32,128]{2,1,0:T(8,128)S(1)}, f32[64,32,128]{2,1,0:T(8,128)S(1)}, u32[]{:S(2)}, u32[]{:S(2)}) %collective-permute-start.6) | collective-permute-done | bytes 1048608 | tf_op jit(solution)/shard_map/ppermute | solution.py:326
  47.3 11.2 %shard_map.47 = (f32[3,16,32,128]{3,2,1,0:T(8,128)S(1)}, f32[12,8,128]{2,1,0:T(8,128)}, f32[32,8,128]{2,1,0:T(8,128)S(1)}) custom-call(f32[32,128]{1,0:T(8,128)S(1)} %broadcast_in_dim.7.spin, s32[2]{0:T(128)S(1)} %pad_add_fusion.place, f32[4,4,8,128]{3,2,1,0:T(8,128)S(1)} %pad_maximum_fusion.1.near, f32[4,4,8,128]{3,2,1,0:T(8,128)S(1)} %collective-permute-done.3.far, ...), custom_call_target="tpu_custom_call" | custom-call | tf_op jit(solution)/shard_map/pallas_call | solution.py:297
  60.1 16.8 %collective-permute-start.7 = (f32[12,8,128]{2,1,0:T(8,128)}, f32[12,8,128]{2,1,0:T(8,128)S(1)}, u32[]{:S(2)}, u32[]{:S(2)}) collective-permute-start(f32[12,8,128]{2,1,0:T(8,128)} %get-tuple-element.23.refs_0_), channel_id=1, source_target_pairs={{0,16},{16,0},{32,48},{48,32},{1,17},{17,1},{33,49},{49,33},{2,18}... | collective-permute-start | bytes 147464 | tf_op jit(solution)/shard_map/ppermute | solution.py:352
  76.8 1.6 %collective-permute-start.8 = (f32[12,8,128]{2,1,0:T(8,128)}, f32[12,8,128]{2,1,0:T(8,128)S(1)}, u32[]{:S(2)}, u32[]{:S(2)}) collective-permute-start(f32[12,8,128]{2,1,0:T(8,128)} %get-tuple-element.23.refs_0_), channel_id=1, source_target_pairs={{0,32},{16,48},{32,0},{48,16},{1,33},{17,49},{33,1},{49,17},{2,34}... | collective-permute-start | bytes 147464 | tf_op jit(solution)/shard_map/ppermute | solution.py:354
  79.1 3.6 %collective-permute-start.9 = (f32[12,8,128]{2,1,0:T(8,128)S(1)}, f32[12,8,128]{2,1,0:T(8,128)S(1)}, u32[]{:S(2)}, u32[]{:S(2)}) collective-permute-start(f32[12,8,128]{2,1,0:T(8,128)S(1)} %collective-permute-done.7.refs_1_), channel_id=1, source_target_pairs={{0,32},{16,48},{32,0},{48,16},{1,33},{17,49},{33,1},{49,17},{2,34}... | collective-permute-start | bytes 147464 | tf_op jit(solution)/shard_map/ppermute | solution.py:354
  87.0 3.0 %shard_map.48 = (f32[3,32,8,128]{3,2,1,0:T(8,128)S(1)}, f32[3,16,8,128]{3,2,1,0:T(8,128)S(1)}) custom-call(s32[5]{0:T(128)S(1)} %stack.40.where, f32[8,128]{1,0:T(8,128)S(1)} %broadcast_in_dim.6.spin, bf16[3,256,256]{2,1,0:T(8,128)(2,1)S(1)} %maximum_maximum_fusion.blocks, f32[32,8,128]{2,1,0:T(8,128)S(1)} %copy-done.2, ...), custom_call_target="tpu_custom_call" | custom-call | tf_op jit(solution)/shard_map/pallas_call | solution.py:297
  90.0 1.6 %collective-permute-start.14 = (f32[3,16,8,128]{3,2,1,0:T(8,128)S(1)}, f32[3,16,8,128]{3,2,1,0:T(8,128)S(1)}, u32[]{:S(2)}, u32[]{:S(2)}) collective-permute-start(f32[3,16,8,128]{3,2,1,0:T(8,128)S(1)} %get-tuple-element.26), channel_id=1, source_target_pairs={{0,64},{64,128},{128,192},{192,0},{1,65},{65,129},{129,193},{193,1... | collective-permute-start | bytes 589832 | tf_op jit(solution)/shard_map/ppermute | solution.py:360
  91.5 3.0 %shard_map.49 = (f32[3,32,8,128]{3,2,1,0:T(8,128)S(1)}, f32[3,16,8,128]{3,2,1,0:T(8,128)S(1)}) custom-call(s32[5]{0:T(128)S(1)} %stack.40.where, f32[8,128]{1,0:T(8,128)S(1)} %broadcast_in_dim.6.spin, bf16[3,256,256]{2,1,0:T(8,128)(2,1)S(1)} %maximum_maximum_fusion.blocks, f32[32,8,128]{2,1,0:T(8,128)S(1)} %copy-done.3, ...), custom_call_target="tpu_custom_call" | custom-call | flops 10000000000 | bytes 39062500 | tf_op jit(solution)/shard_map/pallas_call | solution.py:297
  94.5 2.8 %collective-permute-start.16 = (f32[3,16,8,128]{3,2,1,0:T(8,128)S(1)}, f32[3,16,8,128]{3,2,1,0:T(8,128)S(1)}, u32[]{:S(2)}, u32[]{:S(2)}) collective-permute-start(f32[3,16,8,128]{3,2,1,0:T(8,128)S(1)} %get-tuple-element.29), channel_id=1, source_target_pairs={{0,128},{64,192},{128,0},{192,64},{1,129},{65,193},{129,1},{193,65... | collective-permute-start | bytes 589832 | tf_op jit(solution)/shard_map/ppermute | solution.py:363
  98.2 3.0 %shard_map.50 = (f32[3,32,8,128]{3,2,1,0:T(8,128)S(1)}, f32[3,16,8,128]{3,2,1,0:T(8,128)S(1)}) custom-call(s32[5]{0:T(128)S(1)} %stack.40.where, f32[8,128]{1,0:T(8,128)S(1)} %broadcast_in_dim.6.spin, bf16[3,256,256]{2,1,0:T(8,128)(2,1)S(1)} %maximum_maximum_fusion.blocks, f32[32,8,128]{2,1,0:T(8,128)S(1)} %copy-done.3, ...), custom_call_target="tpu_custom_call" | custom-call | flops 10000000000 | bytes 39062500 | tf_op jit(solution)/shard_map/pallas_call | solution.py:297
  101.2 2.1 %collective-permute-start.15 = (f32[3,16,8,128]{3,2,1,0:T(8,128)S(1)}, f32[3,16,8,128]{3,2,1,0:T(8,128)S(1)}, u32[]{:S(2)}, u32[]{:S(2)}) collective-permute-start(f32[3,16,8,128]{3,2,1,0:T(8,128)S(1)} %get-tuple-element.28), channel_id=1, source_target_pairs={{0,192},{64,0},{128,64},{192,128},{1,193},{65,1},{129,65},{193,129... | collective-permute-start | bytes 589832 | tf_op jit(solution)/shard_map/ppermute | solution.py:363
  103.9 3.6 %collective-permute-done.15.refs_8_ = f32[3,16,8,128]{3,2,1,0:T(8,128)S(1)} collective-permute-done((f32[3,16,8,128]{3,2,1,0:T(8,128)S(1)}, f32[3,16,8,128]{3,2,1,0:T(8,128)S(1)}, u32[]{:S(2)}, u32[]{:S(2)}) %collective-permute-start.15) | collective-permute-done | bytes 196640 | tf_op jit(solution)/shard_map/ppermute | solution.py:363
  108.9 3.9 %shard_map.51 = (f32[2,12,8,128]{3,2,1,0:T(8,128)S(1)}, f32[2,12,8,128]{3,2,1,0:T(8,128)S(1)}, f32[2,12,8,128]{3,2,1,0:T(8,128)S(1)}, f32[2,12,8,128]{3,2,1,0:T(8,128)S(1)}) custom-call(s32[5]{0:T(128)S(1)} %stack.40.where, f32[8,128]{1,0:T(8,128)S(1)} %broadcast_in_dim.6.spin, bf16[3,256,256]{2,1,0:T(8,128)(2,1)S(1)} %maximum_maximum_fusion.blocks, ...), custom_call_target="tpu_custom_call" | custom-call | tf_op jit(solution)/shard_map/pallas_call | solution.py:297
  112.8 2.2 %collective-permute-start.20 = (f32[2,12,8,128]{3,2,1,0:T(8,128)S(1)}, f32[2,12,8,128]{3,2,1,0:T(8,128)S(1)}, u32[]{:S(2)}, u32[]{:S(2)}) collective-permute-start(f32[2,12,8,128]{3,2,1,0:T(8,128)S(1)} %get-tuple-element.31), channel_id=1, source_target_pairs={{0,1},{1,2},{2,3},{3,0},{4,5},{5,6},{6,7},{7,4},{8,9},{9,10},{10,1... | collective-permute-start | bytes 294920 | tf_op jit(solution)/shard_map/ppermute | solution.py:370
  115.9 2.3 %collective-permute-done.20 = f32[2,12,8,128]{3,2,1,0:T(8,128)S(1)} collective-permute-done((f32[2,12,8,128]{3,2,1,0:T(8,128)S(1)}, f32[2,12,8,128]{3,2,1,0:T(8,128)S(1)}, u32[]{:S(2)}, u32[]{:S(2)}) %collective-permute-start.20) | collective-permute-done | bytes 98336 | tf_op jit(solution)/shard_map/ppermute | solution.py:370
  118.2 3.0 %collective-permute-done.21 = f32[2,12,8,128]{3,2,1,0:T(8,128)S(1)} collective-permute-done((f32[2,12,8,128]{3,2,1,0:T(8,128)S(1)}, f32[2,12,8,128]{3,2,1,0:T(8,128)S(1)}, u32[]{:S(2)}, u32[]{:S(2)}) %collective-permute-start.21) | collective-permute-done | bytes 98336 | tf_op jit(solution)/shard_map/ppermute | solution.py:370
  122.8 7.5 %collective-permute-done.23.sent = f32[12,8,128]{2,1,0:T(8,128)S(1)} collective-permute-done((f32[12,8,128]{2,1,0:T(8,128)S(1)}, f32[12,8,128]{2,1,0:T(8,128)S(1)}, u32[]{:S(2)}, u32[]{:S(2)}) %collective-permute-start.23) | collective-permute-done | bytes 49184 | tf_op jit(solution)/shard_map/ppermute | solution.py:371
  (71 shorter events, 18.3 us)
Async XLA Ops:
  1.4 41.4 %collective-permute-start.5 = (f32[64,32,128]{2,1,0:T(8,128)S(1)}, f32[64,32,128]{2,1,0:T(8,128)S(1)}, u32[]{:S(2)}, u32[]{:S(2)}) collective-permute-start(f32[64,32,128]{2,1,0:T(8,128)S(1)} %pad_maximum_fusion.own), channel_id=1, source_target_pairs={{0,1},{1,2},{2,3},{3,4},{4,5},{5,6},{6,7},{7,0},{8,9},{9,10},{10,1... | collective-permute-start | bytes 3145736 | tf_op jit(solution)/shard_map/ppermute | solution.py:325
  8.3 38.9 %collective-permute-start.6 = (f32[64,32,128]{2,1,0:T(8,128)S(1)}, f32[64,32,128]{2,1,0:T(8,128)S(1)}, u32[]{:S(2)}, u32[]{:S(2)}) collective-permute-start(f32[64,32,128]{2,1,0:T(8,128)S(1)} %pad_maximum_fusion.own), channel_id=1, source_target_pairs={{0,7},{1,0},{2,1},{3,2},{4,3},{5,4},{6,5},{7,6},{8,15},{9,8},{10,9... | collective-permute-start | bytes 3145736 | tf_op jit(solution)/shard_map/ppermute | solution.py:326
  8.4 22.8 %collective-permute-start.2 = (f32[4,8,128]{2,1,0:T(8,128)S(1)}, f32[4,8,128]{2,1,0:T(8,128)}, u32[]{:S(2)}, u32[]{:S(2)}) collective-permute-start(f32[4,8,128]{2,1,0:T(8,128)S(1)} %get-tuple-element.20), channel_id=1, source_target_pairs={{0,3},{1,0},{2,1},{3,2},{4,7},{5,4},{6,5},{7,6},{8,11},{9,8},{10,9... | collective-permute-start | bytes 49160 | tf_op jit(solution)/shard_map/ppermute | solution.py:315
  8.5 25.3 %collective-permute-start = (f32[4,8,128]{2,1,0:T(8,128)S(1)}, f32[4,8,128]{2,1,0:T(8,128)}, u32[]{:S(2)}, u32[]{:S(2)}) collective-permute-start(f32[4,8,128]{2,1,0:T(8,128)S(1)} %get-tuple-element.20), channel_id=1, source_target_pairs={{0,1},{1,2},{2,3},{3,0},{4,5},{5,6},{6,7},{7,4},{8,9},{9,10},{10,1... | collective-permute-start | bytes 49160 | tf_op jit(solution)/shard_map/ppermute | solution.py:315
  11.7 22.0 %collective-permute-start.1 = (f32[4,8,128]{2,1,0:T(8,128)S(1)}, f32[4,8,128]{2,1,0:T(8,128)}, u32[]{:S(2)}, u32[]{:S(2)}) collective-permute-start(f32[4,8,128]{2,1,0:T(8,128)S(1)} %get-tuple-element.20), channel_id=1, source_target_pairs={{0,2},{1,3},{2,0},{3,1},{4,6},{5,7},{6,4},{7,5},{8,10},{9,11},{10,... | collective-permute-start | bytes 49160 | tf_op jit(solution)/shard_map/ppermute | solution.py:315
  31.3 9.6 %collective-permute-start.4 = (f32[3,4,8,128]{3,2,1,0:T(8,128)}, f32[3,4,8,128]{3,2,1,0:T(8,128)S(1)}, u32[]{:S(2)}, u32[]{:S(2)}) collective-permute-start(f32[3,4,8,128]{3,2,1,0:T(8,128)} %copy-done.5), channel_id=1, source_target_pairs={{0,248},{8,0},{16,8},{24,16},{32,24},{40,32},{48,40},{56,48},{64,5... | collective-permute-start | bytes 147464 | tf_op jit(solution)/shard_map/ppermute | solution.py:332
  34.5 8.3 %collective-permute-start.3 = (f32[4,4,8,128]{3,2,1,0:T(8,128)S(1)}, f32[4,4,8,128]{3,2,1,0:T(8,128)S(1)}, u32[]{:S(2)}, u32[]{:S(2)}) collective-permute-start(f32[4,4,8,128]{3,2,1,0:T(8,128)S(1)} %pad_maximum_fusion.1.near), channel_id=1, source_target_pairs={{0,4},{4,0},{1,5},{5,1},{2,6},{6,2},{3,7},{7,3},{8,12},{12,8},{9,1... | collective-permute-start | bytes 196616 | tf_op jit(solution)/shard_map/ppermute | solution.py:331
  60.1 19.0 %collective-permute-start.7 = (f32[12,8,128]{2,1,0:T(8,128)}, f32[12,8,128]{2,1,0:T(8,128)S(1)}, u32[]{:S(2)}, u32[]{:S(2)}) collective-permute-start(f32[12,8,128]{2,1,0:T(8,128)} %get-tuple-element.23.refs_0_), channel_id=1, source_target_pairs={{0,16},{16,0},{32,48},{48,32},{1,17},{17,1},{33,49},{49,33},{2,18}... | collective-permute-start | bytes 147464 | tf_op jit(solution)/shard_map/ppermute | solution.py:352
  76.8 6.4 %collective-permute-start.8 = (f32[12,8,128]{2,1,0:T(8,128)}, f32[12,8,128]{2,1,0:T(8,128)S(1)}, u32[]{:S(2)}, u32[]{:S(2)}) collective-permute-start(f32[12,8,128]{2,1,0:T(8,128)} %get-tuple-element.23.refs_0_), channel_id=1, source_target_pairs={{0,32},{16,48},{32,0},{48,16},{1,33},{17,49},{33,1},{49,17},{2,34}... | collective-permute-start | bytes 147464 | tf_op jit(solution)/shard_map/ppermute | solution.py:354
  79.1 5.7 %collective-permute-start.9 = (f32[12,8,128]{2,1,0:T(8,128)S(1)}, f32[12,8,128]{2,1,0:T(8,128)S(1)}, u32[]{:S(2)}, u32[]{:S(2)}) collective-permute-start(f32[12,8,128]{2,1,0:T(8,128)S(1)} %collective-permute-done.7.refs_1_), channel_id=1, source_target_pairs={{0,32},{16,48},{32,0},{48,16},{1,33},{17,49},{33,1},{49,17},{2,34}... | collective-permute-start | bytes 147464 | tf_op jit(solution)/shard_map/ppermute | solution.py:354
  82.7 2.4 %collective-permute-start.10 = (f32[12,8,128]{2,1,0:T(8,128)}, f32[12,8,128]{2,1,0:T(8,128)S(1)}, u32[]{:S(2)}, u32[]{:S(2)}) collective-permute-start(f32[12,8,128]{2,1,0:T(8,128)} %get-tuple-element.23.refs_0_), channel_id=1, source_target_pairs={{0,8},{8,0},{1,9},{9,1},{2,10},{10,2},{3,11},{11,3},{4,12},{12,4},... | collective-permute-start | bytes 147464 | tf_op jit(solution)/shard_map/ppermute | solution.py:355
  82.7 2.4 %collective-permute-start.11 = (f32[12,8,128]{2,1,0:T(8,128)S(1)}, f32[12,8,128]{2,1,0:T(8,128)S(1)}, u32[]{:S(2)}, u32[]{:S(2)}) collective-permute-start(f32[12,8,128]{2,1,0:T(8,128)S(1)} %collective-permute-done.7.refs_1_), channel_id=1, source_target_pairs={{0,8},{8,0},{1,9},{9,1},{2,10},{10,2},{3,11},{11,3},{4,12},{12,4},... | collective-permute-start | bytes 147464 | tf_op jit(solution)/shard_map/ppermute | solution.py:355
  83.2 1.9 %collective-permute-start.12 = (f32[12,8,128]{2,1,0:T(8,128)S(1)}, f32[12,8,128]{2,1,0:T(8,128)S(1)}, u32[]{:S(2)}, u32[]{:S(2)}) collective-permute-start(f32[12,8,128]{2,1,0:T(8,128)S(1)} %collective-permute-done.8.refs_2_), channel_id=1, source_target_pairs={{0,8},{8,0},{1,9},{9,1},{2,10},{10,2},{3,11},{11,3},{4,12},{12,4},... | collective-permute-start | bytes 147464 | tf_op jit(solution)/shard_map/ppermute | solution.py:355
  90.0 8.3 %collective-permute-start.14 = (f32[3,16,8,128]{3,2,1,0:T(8,128)S(1)}, f32[3,16,8,128]{3,2,1,0:T(8,128)S(1)}, u32[]{:S(2)}, u32[]{:S(2)}) collective-permute-start(f32[3,16,8,128]{3,2,1,0:T(8,128)S(1)} %get-tuple-element.26), channel_id=1, source_target_pairs={{0,64},{64,128},{128,192},{192,0},{1,65},{65,129},{129,193},{193,1... | collective-permute-start | bytes 589832 | tf_op jit(solution)/shard_map/ppermute | solution.py:360
  94.5 8.9 %collective-permute-start.16 = (f32[3,16,8,128]{3,2,1,0:T(8,128)S(1)}, f32[3,16,8,128]{3,2,1,0:T(8,128)S(1)}, u32[]{:S(2)}, u32[]{:S(2)}) collective-permute-start(f32[3,16,8,128]{3,2,1,0:T(8,128)S(1)} %get-tuple-element.29), channel_id=1, source_target_pairs={{0,128},{64,192},{128,0},{192,64},{1,129},{65,193},{129,1},{193,65... | collective-permute-start | bytes 589832 | tf_op jit(solution)/shard_map/ppermute | solution.py:363
  101.2 6.2 %collective-permute-start.15 = (f32[3,16,8,128]{3,2,1,0:T(8,128)S(1)}, f32[3,16,8,128]{3,2,1,0:T(8,128)S(1)}, u32[]{:S(2)}, u32[]{:S(2)}) collective-permute-start(f32[3,16,8,128]{3,2,1,0:T(8,128)S(1)} %get-tuple-element.28), channel_id=1, source_target_pairs={{0,192},{64,0},{128,64},{192,128},{1,193},{65,1},{129,65},{193,129... | collective-permute-start | bytes 589832 | tf_op jit(solution)/shard_map/ppermute | solution.py:363
  103.4 4.6 %collective-permute-start.19 = (f32[3,16,8,128]{3,2,1,0:T(8,128)S(1)}, f32[3,16,8,128]{3,2,1,0:T(8,128)S(1)}, u32[]{:S(2)}, u32[]{:S(2)}) collective-permute-start(f32[3,16,8,128]{3,2,1,0:T(8,128)S(1)} %collective-permute-done.14.refs_0_.refs_10_), channel_id=1, source_target_pairs={{0,8},{8,0},{1,9},{9,1},{2,10},{10,2},{3,11},{11,3},{4,12},{12,4},... | collective-permute-start | bytes 589832 | tf_op jit(solution)/shard_map/ppermute | solution.py:364
  103.4 4.6 %collective-permute-start.18 = (f32[3,16,8,128]{3,2,1,0:T(8,128)S(1)}, f32[3,16,8,128]{3,2,1,0:T(8,128)S(1)}, u32[]{:S(2)}, u32[]{:S(2)}) collective-permute-start(f32[3,16,8,128]{3,2,1,0:T(8,128)S(1)} %collective-permute-done.16.refs_9_), channel_id=1, source_target_pairs={{0,8},{8,0},{1,9},{9,1},{2,10},{10,2},{3,11},{11,3},{4,12},{12,4},... | collective-permute-start | bytes 589832 | tf_op jit(solution)/shard_map/ppermute | solution.py:364
  107.5 1.4 %collective-permute-start.17 = (f32[3,16,8,128]{3,2,1,0:T(8,128)S(1)}, f32[3,16,8,128]{3,2,1,0:T(8,128)S(1)}, u32[]{:S(2)}, u32[]{:S(2)}) collective-permute-start(f32[3,16,8,128]{3,2,1,0:T(8,128)S(1)} %collective-permute-done.15.refs_8_), channel_id=1, source_target_pairs={{0,8},{8,0},{1,9},{9,1},{2,10},{10,2},{3,11},{11,3},{4,12},{12,4},... | collective-permute-start | bytes 589832 | tf_op jit(solution)/shard_map/ppermute | solution.py:364
  107.5 15.3 %collective-permute-start.24 = (f32[3,16,32,128]{3,2,1,0:T(8,128)S(1)}, f32[3,16,32,128]{3,2,1,0:T(8,128)S(1)}, u32[]{:S(2)}, u32[]{:S(2)}) collective-permute-start(f32[3,16,32,128]{3,2,1,0:T(8,128)S(1)} %copy-done.8), channel_id=1, source_target_pairs={{0,8},{8,16},{16,24},{24,32},{32,40},{40,48},{48,56},{56,64},{64,7... | collective-permute-start | bytes 2359304 | tf_op jit(solution)/shard_map/ppermute | solution.py:356
  112.8 5.4 %collective-permute-start.20 = (f32[2,12,8,128]{3,2,1,0:T(8,128)S(1)}, f32[2,12,8,128]{3,2,1,0:T(8,128)S(1)}, u32[]{:S(2)}, u32[]{:S(2)}) collective-permute-start(f32[2,12,8,128]{3,2,1,0:T(8,128)S(1)} %get-tuple-element.31), channel_id=1, source_target_pairs={{0,1},{1,2},{2,3},{3,0},{4,5},{5,6},{6,7},{7,4},{8,9},{9,10},{10,1... | collective-permute-start | bytes 294920 | tf_op jit(solution)/shard_map/ppermute | solution.py:370
  115.0 6.2 %collective-permute-start.21 = (f32[2,12,8,128]{3,2,1,0:T(8,128)S(1)}, f32[2,12,8,128]{3,2,1,0:T(8,128)S(1)}, u32[]{:S(2)}, u32[]{:S(2)}) collective-permute-start(f32[2,12,8,128]{3,2,1,0:T(8,128)S(1)} %get-tuple-element.32), channel_id=1, source_target_pairs={{0,2},{1,3},{2,0},{3,1},{4,6},{5,7},{6,4},{7,5},{8,10},{9,11},{10,... | collective-permute-start | bytes 294920 | tf_op jit(solution)/shard_map/ppermute | solution.py:370
  115.0 6.9 %collective-permute-start.22 = (f32[2,12,8,128]{3,2,1,0:T(8,128)S(1)}, f32[2,12,8,128]{3,2,1,0:T(8,128)S(1)}, u32[]{:S(2)}, u32[]{:S(2)}) collective-permute-start(f32[2,12,8,128]{3,2,1,0:T(8,128)S(1)} %get-tuple-element.33), channel_id=1, source_target_pairs={{0,3},{1,0},{2,1},{3,2},{4,7},{5,4},{6,5},{7,6},{8,11},{9,8},{10,9... | collective-permute-start | bytes 294920 | tf_op jit(solution)/shard_map/ppermute | solution.py:370
  121.9 8.4 %collective-permute-start.23 = (f32[12,8,128]{2,1,0:T(8,128)S(1)}, f32[12,8,128]{2,1,0:T(8,128)S(1)}, u32[]{:S(2)}, u32[]{:S(2)}) collective-permute-start(f32[12,8,128]{2,1,0:T(8,128)S(1)} %get-tuple-element.37), channel_id=1, source_target_pairs={{0,4},{4,0},{1,5},{5,1},{2,6},{6,2},{3,7},{7,3},{8,12},{12,8},{9,1... | collective-permute-start | bytes 147464 | tf_op jit(solution)/shard_map/ppermute | solution.py:371
  (13 other events, 89.5 us)

commit v5 on v4

--- a/solution.py
+++ b/solution.py
@@ -19,6 +19,7 @@
 HALO = 16
 WIDE = 16 + 2 * HALO
 COST = 10**10
+DIRECT = 40
 UNROLL = (11, 20, 18, 16, 14, 12, 10, 16)
 
 
@@ -34,7 +35,7 @@
     return pltpu.roll(q, 1, 0)
 
 
-def fine_steps(bufs, strat, half_spin, weights):
+def fine_steps(bufs, out, strat, half_spin, weights):
     here_weight, up_weight, down_weight = weights
 
     def vertical(q):
@@ -46,6 +47,9 @@
         reach = 2 * (STEPS - 1 - step)
         first = HALO - reach
         count = 16 + 2 * reach
+        back = 0
+        if reach == 0:
+            dst, back = out, HALO
         unroll = UNROLL[step]
 
         def zonal(x, src=src):
@@ -54,12 +58,12 @@
             push = src[2, x + 1] - src[2, x - 1]
             return vertical(u) + (half_spin[...] * src[1, x] - 0.25 * push) + 0.05 * sides
 
-        def chunk(i, carry, src=src, dst=dst, first=first, unroll=unroll, zonal=zonal):
+        def chunk(i, carry, src=src, dst=dst, first=first, unroll=unroll, zonal=zonal, back=back):
             before, here = carry
             for k in range(unroll):
                 x = first + unroll * i + k
                 after = zonal(x + 1)
-                dst[0, x] = here
+                dst[0, x - back] = here
                 v = src[1, x]
                 b = src[2, x]
                 b_next, b_prev = y_next(b), y_prev(b)
@@ -68,9 +72,9 @@
                     - (half_spin[...] * here + 0.25 * (b_next - b_prev))
                     + 0.05 * (src[1, x + 1] + src[1, x - 1] + (y_next(v) + y_prev(v)))
                 )
-                dst[1, x] = v_new
+                dst[1, x - back] = v_new
                 flow = (after - before) + (y_next(v_new) - y_prev(v_new))
-                dst[2, x] = (
+                dst[2, x - back] = (
                     vertical(b)
                     - strat[x] * flow
                     + 0.05 * (src[2, x + 1] + src[2, x - 1] + (b_next + b_prev))
@@ -98,43 +102,49 @@
 
 
 def fine_kernel(
-    spin, place, near, far, blocks, next_mean, own, left, right,
-    detail, increment, coarse_strat, one, two, strat, rows, weights,
+    spin, blocks, start, own_strat, left, right, left_near, right_near, left_far, right_far,
+    out, one, two, strat, weights,
 ):
     del blocks
     for k in range(3):
         for x in range(16):
-            one[k, x] = left[16 * k + x]
-            one[k, 16 + x] = own[16 * k + x]
-            one[k, 32 + x] = right[16 * k + x]
+            one[k, 16 + x] = start[k, x]
     for x in range(16):
-        strat[x] = 0.25 * left[48 + x]
-        strat[16 + x] = 0.25 * own[48 + x]
-        strat[32 + x] = 0.25 * right[48 + x]
-    zh, y = place[0], place[1]
-    for j in range(4):
-        column = (y - j + 4) % 4
-        for cell in range(4):
-            mine, other = 4 * zh + column, 4 * (1 - zh) + column
-            coarse_strat[4 * mine + cell] = 0.5 * near[j, cell]
-            coarse_strat[4 * other + cell] = 0.5 * far[j, cell]
+        strat[16 + x] = 0.25 * own_strat[x]
+    for at, direct, near, far in ((0, left, left_near, left_far), (32, right, right_near, right_far)):
+        for x in range(DIRECT):
+            one[x // 16, at + x % 16] = direct[x]
+        for x in range(64 - DIRECT):
+            value = near[x] + far[x]
+            if DIRECT + x < 48:
+                one[2, at + DIRECT + x - 32] = value
+            else:
+                strat[at + DIRECT + x - 48] = 0.25 * value
     lane = lax.broadcasted_iota(jnp.int32, (32, 128), 1)
     up = jnp.where(lane < 127, 0.15, 0.0).astype(jnp.float32)
     down = jnp.where(lane > 0, 0.15, 0.0).astype(jnp.float32)
     weights[0] = 0.8 - up - down
     weights[1] = up
     weights[2] = down
-    fine_steps((one, two), strat, spin, [weights.at[n] for n in range(3)])
-    for k in range(3):
+    fine_steps((one, two), out, strat, spin, [weights.at[n] for n in range(3)])
+
+
+def split_kernel(place, fine, next_mean, strat_near, strat_far, detail, increment, strat, rows):
+    zh, y = place[0], place[1]
+    for j in range(4):
+        column = (y - j + 4) % 4
         for cell in range(4):
-            x = HALO + 4 * cell
+            strat[4 * (4 * zh + column) + cell] = 0.5 * strat_near[j, cell]
+            strat[4 * (4 * (1 - zh) + column) + cell] = 0.5 * strat_far[j, cell]
+    for k in range(3):
+        for cell in range(4):
             slot = (4 * k + cell) % 2
-            mean = block_means(rows.at[slot], [one[k, x + j] for j in range(4)])
+            mean = block_means(rows.at[slot], [fine[k, 4 * cell + j] for j in range(4)])
             increment[4 * k + cell] = mean - next_mean[k, cell]
             for j in range(4):
                 rows[2 + slot, pl.ds(j, 8, stride=4), :] = mean
             for j in range(4):
-                detail[k, 4 * cell + j] = one[k, x + j] - rows[2 + slot]
+                detail[k, 4 * cell + j] = fine[k, 4 * cell + j] - rows[2 + slot]
 
 
 def coarse_step(state, halves, blocks, spin, strat):
@@ -321,9 +331,14 @@
     halves, state = ((3, 256, 256), bf16), ((3, 32, 8, 128), f32)
     increments = ((8, 12, 8, 128), f32)
 
-    own = jnp.concatenate([start.reshape(48, 32, 128), stratification])
-    left = lax.ppermute(own, SPACE, ring(8, 1))
-    right = lax.ppermute(own, SPACE, ring(8, -1))
+    layers = start.reshape(48, 32, 128)
+    rest = jnp.concatenate([layers[DIRECT:], stratification])
+    left_near = lax.ppermute(rest, SPACE, [(s, s + 1) for s in range(8) if s % 4 != 3])
+    right_near = lax.ppermute(rest, SPACE, [(s, s - 1) for s in range(8) if s % 4 != 0])
+    left = lax.ppermute(layers[:DIRECT], SPACE, ring(8, 1))
+    right = lax.ppermute(layers[:DIRECT], SPACE, ring(8, -1))
+    left_far = lax.ppermute(right_near, SPACE, [(2, 4), (6, 0)])
+    right_far = lax.ppermute(left_near, SPACE, [(1, 7), (5, 3)])
     mean, own_strat = call(
         means_kernel, [(3, 4, 8, 128), (4, 8, 128)], [((2, 32, 128), f32)], COST
     )(start, stratification)
@@ -340,22 +355,26 @@
     wide = jnp.concatenate([top, turned - top], axis=2).astype(bf16)
     blocks = jnp.concatenate([wide, wide], axis=1)
 
+    (fine,) = call(
+        fine_kernel,
+        [(3, 16, 32, 128)],
+        [((3, WIDE, 32, 128), f32)] * 2 + [((WIDE, 32, 128), f32), ((3, 32, 128), f32)],
+        COST,
+    )(
+        half_spin, blocks, start, stratification,
+        left, right, left_near, right_near, left_far, right_far,
+    )
     detail, increment, strat = call(
-        fine_kernel,
-        [(3, 16, 32, 128), (12, 8, 128), (32, 8, 128)],
-        [((3, WIDE, 32, 128), f32)] * 2
-        + [((WIDE, 32, 128), f32), ((4, 32, 128), f32), ((3, 32, 128), f32)],
-    )(
-        half_spin, where[3:], near, far, blocks, next_mean, own, left, right
-    )
+        split_kernel, [(3, 16, 32, 128), (12, 8, 128), (32, 8, 128)], [((4, 32, 128), f32)]
+    )(where[3:], fine, next_mean, near, far)
 
     beside = lax.ppermute(increment, "zl", swapped(1))
     mine = [increment, beside]
     mine += [lax.ppermute(part, "zl", swapped(2)) for part in (increment, beside)]
     other = [lax.ppermute(part, "c", ring(2, 1)) for part in mine]
     detail = lax.ppermute(detail, TM, ring(32, 1))
+    pair = [state[0], (3, 16, 8, 128)]
     common = (where, coarse_spin, blocks, strat)
-    pair = [state[0], (3, 16, 8, 128)]
     end, part = call(plane_kernel, pair, [halves, increments])(*common, *mine, *other)
     here = [lax.ppermute(part, "x", ring(4, 1))]
     for by in (2, 3):

time: 132 us -> 130 us (0.985)
  waiting for transfers between devices: 49.2 us -> 44.8 us
  starting transfers between devices: 50.1 us -> 53.5 us
    ppermute x1, starting transfers between devices: 16.8 us -> 0.09 us  [per_device(): beside = lax.ppermute(increment, 'zl', swapped(1))]
    ppermute x2 -> x6, starting transfers between devices: 6.93 us -> 16.3 us  [the longest x1 9.48 us: per_device(): left = lax.ppermute(layers[:DIRECT], SPACE, ring(8, 1))]
    ppermute x3, starting transfers between devices: 4.68 us -> 9.62 us  [gathered(): lax.ppermute(part, axis, ring(4, by))]
    ppermute x1, starting transfers between devices: 1.96 us -> 6.72 us  [per_device(): far = lax.ppermute(near, 'zh', ring(2, 1))]
    ppermute x3, waiting for transfers between devices: 16.5 us -> 21.2 us  [gathered(): lax.ppermute(part, axis, ring(4, by))]
    ppermute x2 -> x6, waiting for transfers between devices: 4.43 us -> 0.05 us  [the longest x1 0.03 us: per_device(): lax.ppermute(rest, SPACE, [(s, s + 1) for s in range(8) if s % 4 != 3])]
    ppermute x1, waiting for transfers between devices: 4.24 us -> 0.01 us  [per_device(): next_mean = lax.ppermute(mean, TM, ring(32, -1))]
    ppermute x2, starting transfers between devices: 5.16 us -> 9.33 us  [per_device(): lax.ppermute(part, 'zl', swapped(2))]
  transfers between devices with their start and end apart: 25 -> 29, of which waited for: 14 -> 14; matrix products, arithmetic and copies ran while one was open for 2% -> 1% of each run, Pallas kernels for 8% -> 16%
where the time goes in v5:
time: 130 us; the launch traced here: 129 us
  starting transfers between devices  53.5 us (41%)
  waiting for transfers between devices  44.8 us (34%)
  Pallas kernels  24.9 us (19%)
  local copies, waits for them, and re-layouts  3.06 us (2%)
  other arithmetic  2.03 us (2%)
    pallas_call x8, Pallas kernels, run(): pl.pallas_call(kernel, out_shape=[jax.ShapeDtypeStruct(shape, f32) for sh...  24.9 us
    ppermute x3, waiting for transfers between devices, gathered(): lax.ppermute(part, axis, ring(4, by))  21.2 us
    ppermute x3, starting transfers between devices, gathered(): lax.ppermute(part, axis, ring(4, by))  9.62 us
    ppermute x1, starting transfers between devices, per_device(): left = lax.ppermute(layers[:DIRECT], SPACE, ring(8, 1))  9.48 us
    ppermute x2, starting transfers between devices, per_device(): lax.ppermute(part, 'zl', swapped(2))  9.33 us
    ppermute x1, starting transfers between devices, per_device(): far = lax.ppermute(near, 'zh', ring(2, 1))  6.72 us
    ppermute x1, waiting for transfers between devices, per_device(): sent = lax.ppermute(total[1], 'zh', ring(2, 1))  5.81 us
    ppermute x3, waiting for transfers between devices, per_device(): total = total + lax.ppermute(parts[by], 'y', ring(4, by))  5.69 us
  transfers between devices with their start and end apart: 29, of which 14 were waited for; matrix products, arithmetic and copies ran while one was open for 1% of the time, Pallas kernels for 16%

profile of v5, /device:TPU:24, one launch (start us, length us, event | category | flops | bytes accessed | tf_op | source)
XLA Modules:
  0.0 128.6 jit_solution(4678522385061811955)
XLA Ops:
  1.0 1.7 %pad_maximum_fusion = f32[24,32,128]{2,1,0:T(8,128)} fusion(f32[16,32,128]{2,1,0:T(8,128)} %strat.1, f32[8,32,128]{2,1,0:T(8,128)S(1)} %slice.20), kind=kLoop, calls=%fused_computation.1 | loop fusion | flops 98304 | bytes 786432 | tf_op jit(solution)/shard_map/concatenate | solution.py:335
  2.7 2.8 %collective-permute-start.3 = (f32[24,32,128]{2,1,0:T(8,128)}, f32[24,32,128]{2,1,0:T(8,128)S(1)}, u32[]{:S(2)}, u32[]{:S(2)}) collective-permute-start(f32[24,32,128]{2,1,0:T(8,128)} %pad_maximum_fusion), channel_id=1, source_target_pairs={{1,0},{2,1},{3,2},{5,4},{6,5},{7,6},{9,8},{10,9},{11,10},{13,12},{... | collective-permute-start | bytes 1179656 | tf_op jit(solution)/shard_map/ppermute | solution.py:337
  7.7 9.5 %collective-permute-start = (f32[40,32,128]{2,1,0:T(8,128)}, f32[40,32,128]{2,1,0:T(8,128)S(1)}, u32[]{:S(2)}, u32[]{:S(2)}) collective-permute-start(f32[40,32,128]{2,1,0:T(8,128)} %slice.19), channel_id=1, source_target_pairs={{0,1},{1,2},{2,3},{3,4},{4,5},{5,6},{6,7},{7,0},{8,9},{9,10},{10,1... | collective-permute-start | bytes 1966088 | tf_op jit(solution)/shard_map/ppermute | solution.py:338
  21.1 10.1 %collective-permute-done.8 = f32[4,8,128]{2,1,0:T(8,128)S(1)} collective-permute-done((f32[4,8,128]{2,1,0:T(8,128)S(1)}, f32[4,8,128]{2,1,0:T(8,128)S(1)}, u32[]{:S(2)}, u32[]{:S(2)}) %collective-permute-start.8) | collective-permute-done | bytes 16416 | tf_op jit(solution)/shard_map/ppermute | solution.py:325
  31.2 9.5 %collective-permute-start.9 = (f32[4,8,128]{2,1,0:T(8,128)S(1)}, f32[4,8,128]{2,1,0:T(8,128)S(1)}, u32[]{:S(2)}, u32[]{:S(2)}) collective-permute-start(f32[4,8,128]{2,1,0:T(8,128)S(1)} %get-tuple-element.21), channel_id=1, source_target_pairs={{0,3},{1,0},{2,1},{3,2},{4,7},{5,4},{6,5},{7,6},{8,11},{9,8},{10,9... | collective-permute-start | bytes 49160 | tf_op jit(solution)/shard_map/ppermute | solution.py:325
  40.8 7.4 %collective-permute-done.9 = f32[4,8,128]{2,1,0:T(8,128)S(1)} collective-permute-done((f32[4,8,128]{2,1,0:T(8,128)S(1)}, f32[4,8,128]{2,1,0:T(8,128)S(1)}, u32[]{:S(2)}, u32[]{:S(2)}) %collective-permute-start.9) | collective-permute-done | bytes 16416 | tf_op jit(solution)/shard_map/ppermute | solution.py:325
  48.2 3.7 %collective-permute-done.7 = f32[4,8,128]{2,1,0:T(8,128)S(1)} collective-permute-done((f32[4,8,128]{2,1,0:T(8,128)S(1)}, f32[4,8,128]{2,1,0:T(8,128)S(1)}, u32[]{:S(2)}, u32[]{:S(2)}) %collective-permute-start.7) | collective-permute-done | bytes 16416 | tf_op jit(solution)/shard_map/ppermute | solution.py:325
  53.4 6.7 %collective-permute-start.10 = (f32[4,4,8,128]{3,2,1,0:T(8,128)S(1)}, f32[4,4,8,128]{3,2,1,0:T(8,128)S(1)}, u32[]{:S(2)}, u32[]{:S(2)}) collective-permute-start(f32[4,4,8,128]{3,2,1,0:T(8,128)S(1)} %pad_maximum_fusion.1.strat_near), channel_id=1, source_target_pairs={{0,4},{4,0},{1,5},{5,1},{2,6},{6,2},{3,7},{7,3},{8,12},{12,8},{9,1... | collective-permute-start | bytes 196616 | tf_op jit(solution)/shard_map/ppermute | solution.py:346
  60.2 11.1 %shard_map.46.fine = f32[3,16,32,128]{3,2,1,0:T(8,128)S(1)} custom-call(f32[32,128]{1,0:T(8,128)S(1)} %broadcast_in_dim.7.spin, bf16[3,256,256]{2,1,0:T(8,128)(2,1)S(1)} %maximum_maximum_fusion.blocks, f32[3,16,32,128]{3,2,1,0:T(8,128)S(1)} %bitcast.22, f32[16,32,128]{2,1,0:T(8,128)S(1)} %copy-done.1, f32[40,32,128]{2,1,0:T(8,128)S(1)} %collective-permute-done.left, ...), custom_call_target="tpu_custom_call" | custom-call | flops 10000000000 | bytes 39062500 | tf_op jit(solution)/shard_map/pallas_call | solution.py:307
  72.1 5.5 %collective-permute-start.12 = (f32[12,8,128]{2,1,0:T(8,128)S(1)}, f32[12,8,128]{2,1,0:T(8,128)S(1)}, u32[]{:S(2)}, u32[]{:S(2)}) collective-permute-start(f32[12,8,128]{2,1,0:T(8,128)S(1)} %get-tuple-element.23.refs_0_), channel_id=1, source_target_pairs={{0,32},{16,48},{32,0},{48,16},{1,33},{17,49},{33,1},{49,17},{2,34}... | collective-permute-start | bytes 147464 | tf_op jit(solution)/shard_map/ppermute | solution.py:373
  77.5 3.9 %collective-permute-start.13 = (f32[12,8,128]{2,1,0:T(8,128)S(1)}, f32[12,8,128]{2,1,0:T(8,128)S(1)}, u32[]{:S(2)}, u32[]{:S(2)}) collective-permute-start(f32[12,8,128]{2,1,0:T(8,128)S(1)} %collective-permute-done.11.refs_1_), channel_id=1, source_target_pairs={{0,32},{16,48},{32,0},{48,16},{1,33},{17,49},{33,1},{49,17},{2,34}... | collective-permute-start | bytes 147464 | tf_op jit(solution)/shard_map/ppermute | solution.py:373
  81.9 2.1 %collective-permute-done.13.refs_3_ = f32[12,8,128]{2,1,0:T(8,128)S(1)} collective-permute-done((f32[12,8,128]{2,1,0:T(8,128)S(1)}, f32[12,8,128]{2,1,0:T(8,128)S(1)}, u32[]{:S(2)}, u32[]{:S(2)}) %collective-permute-start.13) | collective-permute-done | bytes 49184 | tf_op jit(solution)/shard_map/ppermute | solution.py:373
  85.3 2.7 %shard_map.49 = (f32[3,32,8,128]{3,2,1,0:T(8,128)S(1)}, f32[3,16,8,128]{3,2,1,0:T(8,128)S(1)}) custom-call(s32[5]{0:T(128)S(1)} %stack.40.where, f32[8,128]{1,0:T(8,128)S(1)} %broadcast_in_dim.6.spin, bf16[3,256,256]{2,1,0:T(8,128)(2,1)S(1)} %maximum_maximum_fusion.blocks, f32[32,8,128]{2,1,0:T(8,128)S(1)} %get-tuple-element.22.strat, ...), custom_call_target="tpu_custom_call" | custom-call | tf_op jit(solution)/shard_map/pallas_call | solution.py:307
  88.9 3.0 %shard_map.50 = (f32[3,32,8,128]{3,2,1,0:T(8,128)S(1)}, f32[3,16,8,128]{3,2,1,0:T(8,128)S(1)}) custom-call(s32[5]{0:T(128)S(1)} %stack.40.where, f32[8,128]{1,0:T(8,128)S(1)} %broadcast_in_dim.6.spin, bf16[3,256,256]{2,1,0:T(8,128)(2,1)S(1)} %maximum_maximum_fusion.blocks, f32[32,8,128]{2,1,0:T(8,128)S(1)} %get-tuple-element.22.strat, ...), custom_call_target="tpu_custom_call" | custom-call | flops 10000000000 | bytes 39062500 | tf_op jit(solution)/shard_map/pallas_call | solution.py:307
  91.9 2.8 %collective-permute-start.20 = (f32[3,16,8,128]{3,2,1,0:T(8,128)S(1)}, f32[3,16,8,128]{3,2,1,0:T(8,128)S(1)}, u32[]{:S(2)}, u32[]{:S(2)}) collective-permute-start(f32[3,16,8,128]{3,2,1,0:T(8,128)S(1)} %get-tuple-element.29), channel_id=1, source_target_pairs={{0,128},{64,192},{128,0},{192,64},{1,129},{65,193},{129,1},{193,65... | collective-permute-start | bytes 589832 | tf_op jit(solution)/shard_map/ppermute | solution.py:382
  94.7 1.6 %collective-permute-done.18.refs_0_.refs_10_ = f32[3,16,8,128]{3,2,1,0:T(8,128)S(1)} collective-permute-done((f32[3,16,8,128]{3,2,1,0:T(8,128)S(1)}, f32[3,16,8,128]{3,2,1,0:T(8,128)S(1)}, u32[]{:S(2)}, u32[]{:S(2)}) %collective-permute-start.18) | collective-permute-done | bytes 196640 | tf_op jit(solution)/shard_map/ppermute | solution.py:379
  96.4 2.9 %shard_map.51 = (f32[3,32,8,128]{3,2,1,0:T(8,128)S(1)}, f32[3,16,8,128]{3,2,1,0:T(8,128)S(1)}) custom-call(s32[5]{0:T(128)S(1)} %stack.40.where, f32[8,128]{1,0:T(8,128)S(1)} %broadcast_in_dim.6.spin, bf16[3,256,256]{2,1,0:T(8,128)(2,1)S(1)} %maximum_maximum_fusion.blocks, f32[32,8,128]{2,1,0:T(8,128)S(1)} %get-tuple-element.22.strat, ...), custom_call_target="tpu_custom_call" | custom-call | flops 10000000000 | bytes 39062500 | tf_op jit(solution)/shard_map/pallas_call | solution.py:307
  101.2 4.1 %collective-permute-done.19.refs_8_ = f32[3,16,8,128]{3,2,1,0:T(8,128)S(1)} collective-permute-done((f32[3,16,8,128]{3,2,1,0:T(8,128)S(1)}, f32[3,16,8,128]{3,2,1,0:T(8,128)S(1)}, u32[]{:S(2)}, u32[]{:S(2)}) %collective-permute-start.19) | collective-permute-done | bytes 196640 | tf_op jit(solution)/shard_map/ppermute | solution.py:382
  106.7 3.6 %shard_map.52 = (f32[2,12,8,128]{3,2,1,0:T(8,128)S(1)}, f32[2,12,8,128]{3,2,1,0:T(8,128)S(1)}, f32[2,12,8,128]{3,2,1,0:T(8,128)S(1)}, f32[2,12,8,128]{3,2,1,0:T(8,128)S(1)}) custom-call(s32[5]{0:T(128)S(1)} %stack.40.where, f32[8,128]{1,0:T(8,128)S(1)} %broadcast_in_dim.6.spin, bf16[3,256,256]{2,1,0:T(8,128)(2,1)S(1)} %maximum_maximum_fusion.blocks, ...), custom_call_target="tpu_custom_call" | custom-call | tf_op jit(solution)/shard_map/pallas_call | solution.py:307
  111.1 2.5 %collective-permute-start.25 = (f32[2,12,8,128]{3,2,1,0:T(8,128)S(1)}, f32[2,12,8,128]{3,2,1,0:T(8,128)S(1)}, u32[]{:S(2)}, u32[]{:S(2)}) collective-permute-start(f32[2,12,8,128]{3,2,1,0:T(8,128)S(1)} %get-tuple-element.32), channel_id=1, source_target_pairs={{0,2},{1,3},{2,0},{3,1},{4,6},{5,7},{6,4},{7,5},{8,10},{9,11},{10,... | collective-permute-start | bytes 294920 | tf_op jit(solution)/shard_map/ppermute | solution.py:389
  115.1 2.1 %collective-permute-done.25 = f32[2,12,8,128]{3,2,1,0:T(8,128)S(1)} collective-permute-done((f32[2,12,8,128]{3,2,1,0:T(8,128)S(1)}, f32[2,12,8,128]{3,2,1,0:T(8,128)S(1)}, u32[]{:S(2)}, u32[]{:S(2)}) %collective-permute-start.25) | collective-permute-done | bytes 98336 | tf_op jit(solution)/shard_map/ppermute | solution.py:389
  117.2 2.2 %collective-permute-done.26 = f32[2,12,8,128]{3,2,1,0:T(8,128)S(1)} collective-permute-done((f32[2,12,8,128]{3,2,1,0:T(8,128)S(1)}, f32[2,12,8,128]{3,2,1,0:T(8,128)S(1)}, u32[]{:S(2)}, u32[]{:S(2)}) %collective-permute-start.26) | collective-permute-done | bytes 98336 | tf_op jit(solution)/shard_map/ppermute | solution.py:389
  119.6 2.2 %collective-permute-done.28.detail = f32[3,16,32,128]{3,2,1,0:T(8,128)S(1)} collective-permute-done((f32[3,16,32,128]{3,2,1,0:T(8,128)S(1)}, f32[3,16,32,128]{3,2,1,0:T(8,128)S(1)}, u32[]{:S(2)}, u32[]{:S(2)}) %collective-permute-start.28) | collective-permute-done | bytes 786464 | tf_op jit(solution)/shard_map/ppermute | solution.py:375
  121.8 5.8 %collective-permute-done.27.sent = f32[12,8,128]{2,1,0:T(8,128)S(1)} collective-permute-done((f32[12,8,128]{2,1,0:T(8,128)S(1)}, f32[12,8,128]{2,1,0:T(8,128)S(1)}, u32[]{:S(2)}, u32[]{:S(2)}) %collective-permute-start.27) | collective-permute-done | bytes 49184 | tf_op jit(solution)/shard_map/ppermute | solution.py:390
  (66 shorter events, 18.8 us)
Async XLA Ops:
  2.7 15.6 %collective-permute-start.3 = (f32[24,32,128]{2,1,0:T(8,128)}, f32[24,32,128]{2,1,0:T(8,128)S(1)}, u32[]{:S(2)}, u32[]{:S(2)}) collective-permute-start(f32[24,32,128]{2,1,0:T(8,128)} %pad_maximum_fusion), channel_id=1, source_target_pairs={{1,0},{2,1},{3,2},{5,4},{6,5},{7,6},{9,8},{10,9},{11,10},{13,12},{... | collective-permute-start | bytes 1179656 | tf_op jit(solution)/shard_map/ppermute | solution.py:337
  5.5 14.2 %collective-permute-start.2 = (f32[24,32,128]{2,1,0:T(8,128)}, f32[24,32,128]{2,1,0:T(8,128)}, u32[]{:S(2)}, u32[]{:S(2)}) collective-permute-start(f32[24,32,128]{2,1,0:T(8,128)} %pad_maximum_fusion), channel_id=1, source_target_pairs={{0,1},{1,2},{2,3},{4,5},{5,6},{6,7},{8,9},{9,10},{10,11},{12,13},{... | collective-permute-start | bytes 1179656 | tf_op jit(solution)/shard_map/ppermute | solution.py:336
  7.7 45.7 %collective-permute-start = (f32[40,32,128]{2,1,0:T(8,128)}, f32[40,32,128]{2,1,0:T(8,128)S(1)}, u32[]{:S(2)}, u32[]{:S(2)}) collective-permute-start(f32[40,32,128]{2,1,0:T(8,128)} %slice.19), channel_id=1, source_target_pairs={{0,1},{1,2},{2,3},{3,4},{4,5},{5,6},{6,7},{7,0},{8,9},{9,10},{10,1... | collective-permute-start | bytes 1966088 | tf_op jit(solution)/shard_map/ppermute | solution.py:338
  17.2 42.9 %collective-permute-start.1 = (f32[40,32,128]{2,1,0:T(8,128)}, f32[40,32,128]{2,1,0:T(8,128)S(1)}, u32[]{:S(2)}, u32[]{:S(2)}) collective-permute-start(f32[40,32,128]{2,1,0:T(8,128)} %slice.19), channel_id=1, source_target_pairs={{0,7},{1,0},{2,1},{3,2},{4,3},{5,4},{6,5},{7,6},{8,15},{9,8},{10,9... | collective-permute-start | bytes 1966088 | tf_op jit(solution)/shard_map/ppermute | solution.py:339
  17.3 13.9 %collective-permute-start.8 = (f32[4,8,128]{2,1,0:T(8,128)S(1)}, f32[4,8,128]{2,1,0:T(8,128)S(1)}, u32[]{:S(2)}, u32[]{:S(2)}) collective-permute-start(f32[4,8,128]{2,1,0:T(8,128)S(1)} %get-tuple-element.21), channel_id=1, source_target_pairs={{0,2},{1,3},{2,0},{3,1},{4,6},{5,7},{6,4},{7,5},{8,10},{9,11},{10,... | collective-permute-start | bytes 49160 | tf_op jit(solution)/shard_map/ppermute | solution.py:325
  18.3 41.8 %collective-permute-start.4 = (f32[24,32,128]{2,1,0:T(8,128)S(1)}, f32[24,32,128]{2,1,0:T(8,128)}, u32[]{:S(2)}, u32[]{:S(2)}) collective-permute-start(f32[24,32,128]{2,1,0:T(8,128)S(1)} %collective-permute-done.3.right_near), channel_id=1, source_target_pairs={{2,4},{6,0},{10,12},{14,8},{18,20},{22,16},{26,28},{30,24},{34,36}... | collective-permute-start | bytes 1179656 | tf_op jit(solution)/shard_map/ppermute | solution.py:340
  19.8 40.3 %collective-permute-start.5 = (f32[24,32,128]{2,1,0:T(8,128)}, f32[24,32,128]{2,1,0:T(8,128)}, u32[]{:S(2)}, u32[]{:S(2)}) collective-permute-start(f32[24,32,128]{2,1,0:T(8,128)} %collective-permute-done.2.left_near), channel_id=1, source_target_pairs={{1,7},{5,3},{9,15},{13,11},{17,23},{21,19},{25,31},{29,27},{33,39}... | collective-permute-start | bytes 1179656 | tf_op jit(solution)/shard_map/ppermute | solution.py:341
  31.2 16.9 %collective-permute-start.9 = (f32[4,8,128]{2,1,0:T(8,128)S(1)}, f32[4,8,128]{2,1,0:T(8,128)S(1)}, u32[]{:S(2)}, u32[]{:S(2)}) collective-permute-start(f32[4,8,128]{2,1,0:T(8,128)S(1)} %get-tuple-element.21), channel_id=1, source_target_pairs={{0,3},{1,0},{2,1},{3,2},{4,7},{5,4},{6,5},{7,6},{8,11},{9,8},{10,9... | collective-permute-start | bytes 49160 | tf_op jit(solution)/shard_map/ppermute | solution.py:325
  48.2 3.7 %collective-permute-start.7 = (f32[4,8,128]{2,1,0:T(8,128)S(1)}, f32[4,8,128]{2,1,0:T(8,128)S(1)}, u32[]{:S(2)}, u32[]{:S(2)}) collective-permute-start(f32[4,8,128]{2,1,0:T(8,128)S(1)} %get-tuple-element.21), channel_id=1, source_target_pairs={{0,1},{1,2},{2,3},{3,0},{4,5},{5,6},{6,7},{7,4},{8,9},{9,10},{10,1... | collective-permute-start | bytes 49160 | tf_op jit(solution)/shard_map/ppermute | solution.py:325
  51.9 19.3 %collective-permute-start.6 = (f32[3,4,8,128]{3,2,1,0:T(8,128)S(1)}, f32[3,4,8,128]{3,2,1,0:T(8,128)S(1)}, u32[]{:S(2)}, u32[]{:S(2)}) collective-permute-start(f32[3,4,8,128]{3,2,1,0:T(8,128)S(1)} %get-tuple-element.20.mean), channel_id=1, source_target_pairs={{0,248},{8,0},{16,8},{24,16},{32,24},{40,32},{48,40},{56,48},{64,5... | collective-permute-start | bytes 147464 | tf_op jit(solution)/shard_map/ppermute | solution.py:347
  53.4 17.9 %collective-permute-start.10 = (f32[4,4,8,128]{3,2,1,0:T(8,128)S(1)}, f32[4,4,8,128]{3,2,1,0:T(8,128)S(1)}, u32[]{:S(2)}, u32[]{:S(2)}) collective-permute-start(f32[4,4,8,128]{3,2,1,0:T(8,128)S(1)} %pad_maximum_fusion.1.strat_near), channel_id=1, source_target_pairs={{0,4},{4,0},{1,5},{5,1},{2,6},{6,2},{3,7},{7,3},{8,12},{12,8},{9,1... | collective-permute-start | bytes 196616 | tf_op jit(solution)/shard_map/ppermute | solution.py:346
  72.0 5.6 %collective-permute-start.11 = (f32[12,8,128]{2,1,0:T(8,128)S(1)}, f32[12,8,128]{2,1,0:T(8,128)S(1)}, u32[]{:S(2)}, u32[]{:S(2)}) collective-permute-start(f32[12,8,128]{2,1,0:T(8,128)S(1)} %get-tuple-element.23.refs_0_), channel_id=1, source_target_pairs={{0,16},{16,0},{32,48},{48,32},{1,17},{17,1},{33,49},{49,33},{2,18}... | collective-permute-start | bytes 147464 | tf_op jit(solution)/shard_map/ppermute | solution.py:371
  72.1 9.9 %collective-permute-start.12 = (f32[12,8,128]{2,1,0:T(8,128)S(1)}, f32[12,8,128]{2,1,0:T(8,128)S(1)}, u32[]{:S(2)}, u32[]{:S(2)}) collective-permute-start(f32[12,8,128]{2,1,0:T(8,128)S(1)} %get-tuple-element.23.refs_0_), channel_id=1, source_target_pairs={{0,32},{16,48},{32,0},{48,16},{1,33},{17,49},{33,1},{49,17},{2,34}... | collective-permute-start | bytes 147464 | tf_op jit(solution)/shard_map/ppermute | solution.py:373
  77.5 6.5 %collective-permute-start.13 = (f32[12,8,128]{2,1,0:T(8,128)S(1)}, f32[12,8,128]{2,1,0:T(8,128)S(1)}, u32[]{:S(2)}, u32[]{:S(2)}) collective-permute-start(f32[12,8,128]{2,1,0:T(8,128)S(1)} %collective-permute-done.11.refs_1_), channel_id=1, source_target_pairs={{0,32},{16,48},{32,0},{48,16},{1,33},{17,49},{33,1},{49,17},{2,34}... | collective-permute-start | bytes 147464 | tf_op jit(solution)/shard_map/ppermute | solution.py:373
  88.0 8.4 %collective-permute-start.18 = (f32[3,16,8,128]{3,2,1,0:T(8,128)S(1)}, f32[3,16,8,128]{3,2,1,0:T(8,128)S(1)}, u32[]{:S(2)}, u32[]{:S(2)}) collective-permute-start(f32[3,16,8,128]{3,2,1,0:T(8,128)S(1)} %get-tuple-element.26), channel_id=1, source_target_pairs={{0,64},{64,128},{128,192},{192,0},{1,65},{65,129},{129,193},{193,1... | collective-permute-start | bytes 589832 | tf_op jit(solution)/shard_map/ppermute | solution.py:379
  91.9 8.9 %collective-permute-start.20 = (f32[3,16,8,128]{3,2,1,0:T(8,128)S(1)}, f32[3,16,8,128]{3,2,1,0:T(8,128)S(1)}, u32[]{:S(2)}, u32[]{:S(2)}) collective-permute-start(f32[3,16,8,128]{3,2,1,0:T(8,128)S(1)} %get-tuple-element.29), channel_id=1, source_target_pairs={{0,128},{64,192},{128,0},{192,64},{1,129},{65,193},{129,1},{193,65... | collective-permute-start | bytes 589832 | tf_op jit(solution)/shard_map/ppermute | solution.py:382
  99.2 6.1 %collective-permute-start.19 = (f32[3,16,8,128]{3,2,1,0:T(8,128)S(1)}, f32[3,16,8,128]{3,2,1,0:T(8,128)S(1)}, u32[]{:S(2)}, u32[]{:S(2)}) collective-permute-start(f32[3,16,8,128]{3,2,1,0:T(8,128)S(1)} %get-tuple-element.28), channel_id=1, source_target_pairs={{0,192},{64,0},{128,64},{192,128},{1,193},{65,1},{129,65},{193,129... | collective-permute-start | bytes 589832 | tf_op jit(solution)/shard_map/ppermute | solution.py:382
  100.6 5.2 %collective-permute-start.23 = (f32[3,16,8,128]{3,2,1,0:T(8,128)S(1)}, f32[3,16,8,128]{3,2,1,0:T(8,128)S(1)}, u32[]{:S(2)}, u32[]{:S(2)}) collective-permute-start(f32[3,16,8,128]{3,2,1,0:T(8,128)S(1)} %collective-permute-done.18.refs_0_.refs_10_), channel_id=1, source_target_pairs={{0,8},{8,0},{1,9},{9,1},{2,10},{10,2},{3,11},{11,3},{4,12},{12,4},... | collective-permute-start | bytes 589832 | tf_op jit(solution)/shard_map/ppermute | solution.py:383
  100.8 5.0 %collective-permute-start.22 = (f32[3,16,8,128]{3,2,1,0:T(8,128)S(1)}, f32[3,16,8,128]{3,2,1,0:T(8,128)S(1)}, u32[]{:S(2)}, u32[]{:S(2)}) collective-permute-start(f32[3,16,8,128]{3,2,1,0:T(8,128)S(1)} %collective-permute-done.20.refs_9_), channel_id=1, source_target_pairs={{0,8},{8,0},{1,9},{9,1},{2,10},{10,2},{3,11},{11,3},{4,12},{12,4},... | collective-permute-start | bytes 589832 | tf_op jit(solution)/shard_map/ppermute | solution.py:383
  105.3 16.5 %collective-permute-start.28 = (f32[3,16,32,128]{3,2,1,0:T(8,128)S(1)}, f32[3,16,32,128]{3,2,1,0:T(8,128)S(1)}, u32[]{:S(2)}, u32[]{:S(2)}) collective-permute-start(f32[3,16,32,128]{3,2,1,0:T(8,128)S(1)} %get-tuple-element.34), channel_id=1, source_target_pairs={{0,8},{8,16},{16,24},{24,32},{32,40},{40,48},{48,56},{56,64},{64,7... | collective-permute-start | bytes 2359304 | tf_op jit(solution)/shard_map/ppermute | solution.py:375
  110.4 4.7 %collective-permute-start.24 = (f32[2,12,8,128]{3,2,1,0:T(8,128)S(1)}, f32[2,12,8,128]{3,2,1,0:T(8,128)S(1)}, u32[]{:S(2)}, u32[]{:S(2)}) collective-permute-start(f32[2,12,8,128]{3,2,1,0:T(8,128)S(1)} %get-tuple-element.31), channel_id=1, source_target_pairs={{0,1},{1,2},{2,3},{3,0},{4,5},{5,6},{6,7},{7,4},{8,9},{9,10},{10,1... | collective-permute-start | bytes 294920 | tf_op jit(solution)/shard_map/ppermute | solution.py:389
  111.1 6.1 %collective-permute-start.25 = (f32[2,12,8,128]{3,2,1,0:T(8,128)S(1)}, f32[2,12,8,128]{3,2,1,0:T(8,128)S(1)}, u32[]{:S(2)}, u32[]{:S(2)}) collective-permute-start(f32[2,12,8,128]{3,2,1,0:T(8,128)S(1)} %get-tuple-element.32), channel_id=1, source_target_pairs={{0,2},{1,3},{2,0},{3,1},{4,6},{5,7},{6,4},{7,5},{8,10},{9,11},{10,... | collective-permute-start | bytes 294920 | tf_op jit(solution)/shard_map/ppermute | solution.py:389
  113.6 5.8 %collective-permute-start.26 = (f32[2,12,8,128]{3,2,1,0:T(8,128)S(1)}, f32[2,12,8,128]{3,2,1,0:T(8,128)S(1)}, u32[]{:S(2)}, u32[]{:S(2)}) collective-permute-start(f32[2,12,8,128]{3,2,1,0:T(8,128)S(1)} %get-tuple-element.33), channel_id=1, source_target_pairs={{0,3},{1,0},{2,1},{3,2},{4,7},{5,4},{6,5},{7,6},{8,11},{9,8},{10,9... | collective-permute-start | bytes 294920 | tf_op jit(solution)/shard_map/ppermute | solution.py:389
  119.5 8.1 %collective-permute-start.27 = (f32[12,8,128]{2,1,0:T(8,128)S(1)}, f32[12,8,128]{2,1,0:T(8,128)S(1)}, u32[]{:S(2)}, u32[]{:S(2)}) collective-permute-start(f32[12,8,128]{2,1,0:T(8,128)S(1)} %get-tuple-element.37), channel_id=1, source_target_pairs={{0,4},{4,0},{1,5},{5,1},{2,6},{6,2},{3,7},{7,3},{8,12},{12,8},{9,1... | collective-permute-start | bytes 147464 | tf_op jit(solution)/shard_map/ppermute | solution.py:390
  (9 other events, 35.9 us)

commit v6 on v5

--- a/solution.py
+++ b/solution.py
@@ -19,7 +19,6 @@
 HALO = 16
 WIDE = 16 + 2 * HALO
 COST = 10**10
-DIRECT = 40
 UNROLL = (11, 20, 18, 16, 14, 12, 10, 16)
 
 
@@ -91,35 +90,44 @@
     return ((parts[0] + parts[1]) + (parts[2] + parts[3])) * 0.0625
 
 
-def means_kernel(start, strat, mean, own_strat, rows):
+def means_kernel(start, mean, rows):
     for k in range(3):
         for cell in range(4):
             cells = [start[k, 4 * cell + j] for j in range(4)]
             mean[k, cell] = block_means(rows.at[cell % 2], cells)
-    for cell in range(4):
-        cells = [strat[4 * cell + j] for j in range(4)]
-        own_strat[cell] = block_means(rows.at[cell % 2], cells)
+
+
+def strat_means_kernel(left, own, right, means, rows):
+    for n, block in enumerate((left, own, right)):
+        for cell in range(4):
+            cells = [block[4 * cell + j] for j in range(4)]
+            means[n, cell] = block_means(rows.at[cell % 2], cells)
+
+
+def columns_kernel(place, own, partner, columns):
+    y = place[1]
+    for middle, means in ((y, own), ((y + 2) % 4, partner)):
+        for n in range(3):
+
+            @pl.when((middle + n >= 1) & (middle + n <= 4))
+            def _(middle=middle, means=means, n=n):
+                columns[middle + n - 1] = means[n]
 
 
 def fine_kernel(
-    spin, blocks, start, own_strat, left, right, left_near, right_near, left_far, right_far,
+    spin, blocks, own_strat, left_near, right_near, left_far, right_far, start, left, right,
     out, one, two, strat, weights,
 ):
     del blocks
     for k in range(3):
         for x in range(16):
+            one[k, x] = left[k, x]
             one[k, 16 + x] = start[k, x]
+            one[k, 32 + x] = right[k, x]
     for x in range(16):
+        strat[x] = 0.25 * (left_near[x] + left_far[x])
         strat[16 + x] = 0.25 * own_strat[x]
-    for at, direct, near, far in ((0, left, left_near, left_far), (32, right, right_near, right_far)):
-        for x in range(DIRECT):
-            one[x // 16, at + x % 16] = direct[x]
-        for x in range(64 - DIRECT):
-            value = near[x] + far[x]
-            if DIRECT + x < 48:
-                one[2, at + DIRECT + x - 32] = value
-            else:
-                strat[at + DIRECT + x - 48] = 0.25 * value
+        strat[32 + x] = 0.25 * (right_near[x] + right_far[x])
     lane = lax.broadcasted_iota(jnp.int32, (32, 128), 1)
     up = jnp.where(lane < 127, 0.15, 0.0).astype(jnp.float32)
     down = jnp.where(lane > 0, 0.15, 0.0).astype(jnp.float32)
@@ -130,12 +138,11 @@
 
 
 def split_kernel(place, fine, next_mean, strat_near, strat_far, detail, increment, strat, rows):
-    zh, y = place[0], place[1]
-    for j in range(4):
-        column = (y - j + 4) % 4
-        for cell in range(4):
-            strat[4 * (4 * zh + column) + cell] = 0.5 * strat_near[j, cell]
-            strat[4 * (4 * (1 - zh) + column) + cell] = 0.5 * strat_far[j, cell]
+    zh = place[0]
+    for column in range(4):
+        for cell in range(4):
+            strat[16 * zh + 4 * column + cell] = 0.5 * strat_near[column, cell]
+            strat[16 * (1 - zh) + 4 * column + cell] = 0.5 * strat_far[column, cell]
     for k in range(3):
         for cell in range(4):
             slot = (4 * k + cell) % 2
@@ -234,42 +241,34 @@
         part[k] = state[k, pl.ds(16 * core, 16)]
 
 
-def power_kernel(where, spin, blocks, strat, before, *refs):
-    state, part, halves = refs[-3:]
-    for k in range(3):
-        for x in range(32):
-            state[k, x] = before[k, x]
-    steps(8, state, halves, blocks, spin, strat)
-    for k in range(3):
-        part[k] = state[k, pl.ds(16 * where[1], 16)]
-
-
-def chain_kernel(where, spin, blocks, strat, last, *refs):
-    mine, other, here, there = refs[:4], refs[4:8], refs[10:7:-1], refs[13:10:-1]
-    parts, (state, halves, increments) = refs[14:18], refs[18:]
+def chain_kernel(where, spin, blocks, strat, end, *refs):
+    mine, other, here, there = refs[:4], refs[4:8], refs[8:11], refs[11:14]
+    parts, (ends, state, halves, increments) = refs[14:18], refs[18:]
     run, core, row, zh, y = where[0], where[1], where[2], where[3], where[4]
     turns = 2 * run + core
-    closing = (row == 0) & (turns == 0)
+    groups = jnp.where((row == 0) & (turns == 0), 4, row)
     table(where, increments, mine, other)
+    for k in range(3):
+        for x in range(32):
+            ends[0, k, x] = end[k, x]
+    for j in range(3):
+        for k in range(3):
+            ends[j + 1, k, pl.ds(16 * core, 16)] = here[j][k]
+            ends[j + 1, k, pl.ds(16 * (1 - core), 16)] = there[j][k]
     clear(state)
 
-    @pl.when(closing)
-    def _():
+    def group(g, carry):
+        @pl.when(g > 0)
+        def _():
+            steps(8, state, halves, blocks, spin, strat)
+
+        place = (row - g + 4) % 4
         for k in range(3):
             for x in range(32):
-                state[k, x] = last[k, x]
-        steps(8, state, halves, blocks, spin, strat)
-
-    for j in range(3):
-
-        @pl.when(closing | (row > j))
-        def _(j=j):
-            for k in range(3):
-                for x in range(16):
-                    near, far = 16 * core + x, 16 * (1 - core) + x
-                    state[k, near] = state[k, near] + here[j][k, x]
-                    state[k, far] = state[k, far] + there[j][k, x]
-
+                state[k, x] = state[k, x] + ends[place, k, x]
+        return carry
+
+    lax.fori_loop(0, groups, group, 0)
     block = 4 * zh + y
 
     def turn(i, carry):
@@ -321,33 +320,29 @@
     return [(i, i ^ by) for i in range(4)]
 
 
-def gathered(part, axis):
-    return jnp.stack([part] + [lax.ppermute(part, axis, ring(4, by)) for by in (1, 2, 3)])
-
-
 def per_device(slice_starts, coriolis, stratification, inverse_blocks):
     f32, bf16 = jnp.float32, jnp.bfloat16
     start = slice_starts[0]
     halves, state = ((3, 256, 256), bf16), ((3, 32, 8, 128), f32)
     increments = ((8, 12, 8, 128), f32)
 
-    layers = start.reshape(48, 32, 128)
-    rest = jnp.concatenate([layers[DIRECT:], stratification])
-    left_near = lax.ppermute(rest, SPACE, [(s, s + 1) for s in range(8) if s % 4 != 3])
-    right_near = lax.ppermute(rest, SPACE, [(s, s - 1) for s in range(8) if s % 4 != 0])
-    left = lax.ppermute(layers[:DIRECT], SPACE, ring(8, 1))
-    right = lax.ppermute(layers[:DIRECT], SPACE, ring(8, -1))
+    left = lax.ppermute(start, SPACE, ring(8, 1))
+    right = lax.ppermute(start, SPACE, ring(8, -1))
+    left_near = lax.ppermute(stratification, SPACE, [(s, s + 1) for s in range(8) if s % 4 != 3])
+    right_near = lax.ppermute(stratification, SPACE, [(s, s - 1) for s in range(8) if s % 4 != 0])
     left_far = lax.ppermute(right_near, SPACE, [(2, 4), (6, 0)])
     right_far = lax.ppermute(left_near, SPACE, [(1, 7), (5, 3)])
-    mean, own_strat = call(
-        means_kernel, [(3, 4, 8, 128), (4, 8, 128)], [((2, 32, 128), f32)], COST
-    )(start, stratification)
-    near = gathered(own_strat, "y")
-    far = lax.ppermute(near, "zh", ring(2, 1))
+    (mean,) = call(means_kernel, [(3, 4, 8, 128)], [((2, 32, 128), f32)], COST)(start)
     next_mean = lax.ppermute(mean, TM, ring(32, -1))
 
     spots = [lax.axis_index(name).astype(jnp.int32) for name in ("zl", "c", "x", "zh", "y")]
     where = jnp.stack(spots)
+    (three,) = call(strat_means_kernel, [(3, 4, 8, 128)], [((2, 32, 128), f32)])(
+        left_near, stratification, right_near
+    )
+    partner = lax.ppermute(three, "y", swapped(2))
+    (near,) = call(columns_kernel, [(4, 4, 8, 128)], [])(where[3:], three, partner)
+    far = lax.ppermute(near, "zh", ring(2, 1))
     half_spin = jnp.broadcast_to(0.5 * coriolis[:, None], (32, 128))
     coarse_spin = jnp.broadcast_to(4.0 * coriolis.reshape(8, 4).mean(axis=1)[:, None], (8, 128))
     turned = jnp.swapaxes(inverse_blocks, 1, 2)
@@ -361,8 +356,8 @@
         [((3, WIDE, 32, 128), f32)] * 2 + [((WIDE, 32, 128), f32), ((3, 32, 128), f32)],
         COST,
     )(
-        half_spin, blocks, start, stratification,
-        left, right, left_near, right_near, left_far, right_far,
+        half_spin, blocks, stratification,
+        left_near, right_near, left_far, right_far, start, left, right,
     )
     detail, increment, strat = call(
         split_kernel, [(3, 16, 32, 128), (12, 8, 128), (32, 8, 128)], [((4, 32, 128), f32)]
@@ -376,14 +371,11 @@
     pair = [state[0], (3, 16, 8, 128)]
     common = (where, coarse_spin, blocks, strat)
     end, part = call(plane_kernel, pair, [halves, increments])(*common, *mine, *other)
-    here = [lax.ppermute(part, "x", ring(4, 1))]
-    for by in (2, 3):
-        end, part = call(power_kernel, pair, [halves], COST)(*common, end, *here[: by - 2])
-        here.append(lax.ppermute(part, "x", ring(4, by)))
+    here = [lax.ppermute(part, "x", ring(4, by)) for by in (1, 2, 3)]
     there = [lax.ppermute(part, "c", ring(2, 1)) for part in here]
-    parts = call(chain_kernel, [(2, 12, 8, 128)] * 4, [state, halves, increments])(
-        *common, end, *mine, *other, *here[::-1], *there[::-1]
-    )
+    parts = call(
+        chain_kernel, [(2, 12, 8, 128)] * 4, [((4, 3, 32, 8, 128), f32), state, halves, increments]
+    )(*common, end, *mine, *other, *here, *there)
     total = parts[0]
     for by in (1, 2, 3):
         total = total + lax.ppermute(parts[by], "y", ring(4, by))

time: 130 us -> 122 us (0.938)
  waiting for transfers between devices: 44.8 us -> 36.1 us
  starting transfers between devices: 53.5 us -> 58.1 us
  Pallas kernels: 24.9 us -> 23 us
  other arithmetic: 2.03 us -> 0.29 us
    ppermute x10 -> x8, waiting for transfers between devices: 27.1 us -> 19.1 us  [the longest x1 11.4 us: per_device(): partner = lax.ppermute(three, 'y', swapped(2))]
    ppermute x1, starting transfers between devices: 0.09 us -> 6.18 us  [per_device(): beside = lax.ppermute(increment, 'zl', swapped(1))]
    unnamed x9 -> x11, local copies, waits for them, and re-layouts: 0.88 us -> 3.09 us
    ppermute x1, waiting for transfers between devices: 2.17 us -> 0.01 us  [per_device(): detail = lax.ppermute(detail, TM, ring(32, 1))]
    ppermute x1, starting transfers between devices: 6.72 us -> 4.58 us  [per_device(): far = lax.ppermute(near, 'zh', ring(2, 1))]
    ppermute x1, waiting for transfers between devices: 5.81 us -> 7.86 us  [per_device(): sent = lax.ppermute(total[1], 'zh', ring(2, 1))]
    pallas_call x8, Pallas kernels: 24.9 us -> 23 us  [run(): pl.pallas_call(kernel, out_shape=[jax.ShapeDtypeStruct(shape, f32) for sh...]
    ppermute x1, starting transfers between devices: 1.46 us -> 3.37 us  [per_device(): next_mean = lax.ppermute(mean, TM, ring(32, -1))]
  transfers between devices with their start and end apart: 29 -> 27, of which waited for: 14 -> 11; matrix products, arithmetic and copies ran while one was open for 1% -> 1% of each run, Pallas kernels for 16% -> 15%
where the time goes in v6:
time: 122 us; the launch traced here: 121 us
  starting transfers between devices  58.1 us (48%)
  waiting for transfers between devices  36.1 us (30%)
  Pallas kernels  23 us (19%)
  local copies, waits for them, and re-layouts  3.4 us (3%)
    pallas_call x8, Pallas kernels, run(): pl.pallas_call(kernel, out_shape=[jax.ShapeDtypeStruct(shape, f32) for sh...  23 us
    ppermute x1, waiting for transfers between devices, per_device(): partner = lax.ppermute(three, 'y', swapped(2))  11.4 us
    ppermute x2, starting transfers between devices, per_device(): lax.ppermute(part, 'zl', swapped(2))  10.3 us
    ppermute x1, starting transfers between devices, per_device(): partner = lax.ppermute(three, 'y', swapped(2))  9.71 us
    ppermute x1, waiting for transfers between devices, per_device(): sent = lax.ppermute(total[1], 'zh', ring(2, 1))  7.86 us
    ppermute x3, waiting for transfers between devices, per_device(): here = [lax.ppermute(part, 'x', ring(4, by)) for by in (1, 2, 3)]  7.72 us
    ppermute x1, starting transfers between devices, per_device(): beside = lax.ppermute(increment, 'zl', swapped(1))  6.18 us
    ppermute x1, starting transfers between devices, per_device(): left = lax.ppermute(start, SPACE, ring(8, 1))  5.86 us
  transfers between devices with their start and end apart: 27, of which 11 were waited for; matrix products, arithmetic and copies ran while one was open for 1% of the time, Pallas kernels for 15%

profile of v6, /device:TPU:24, one launch (start us, length us, event | category | flops | bytes accessed | tf_op | source)
XLA Modules:
  0.0 121.1 jit_solution(10613757279067624018)
XLA Ops:
  0.0 1.3 %collective-permute-start = (f32[16,32,128]{2,1,0:T(8,128)}, f32[16,32,128]{2,1,0:T(8,128)S(1)}, u32[]{:S(2)}, u32[]{:S(2)}) collective-permute-start(f32[16,32,128]{2,1,0:T(8,128)} %own.1), channel_id=1, source_target_pairs={{0,1},{1,2},{2,3},{4,5},{5,6},{6,7},{8,9},{9,10},{10,11},{12,13},{... | collective-permute-start | bytes 786440 | tf_op jit(solution)/shard_map/ppermute | solution.py:331
  1.3 4.6 %collective-permute-start.1 = (f32[16,32,128]{2,1,0:T(8,128)}, f32[16,32,128]{2,1,0:T(8,128)S(1)}, u32[]{:S(2)}, u32[]{:S(2)}) collective-permute-start(f32[16,32,128]{2,1,0:T(8,128)} %own.1), channel_id=1, source_target_pairs={{1,0},{2,1},{3,2},{5,4},{6,5},{7,6},{9,8},{10,9},{11,10},{13,12},{... | collective-permute-start | bytes 786440 | tf_op jit(solution)/shard_map/ppermute | solution.py:332
  5.9 5.9 %collective-permute-start.4 = (f32[3,16,32,128]{3,2,1,0:T(8,128)}, f32[3,16,32,128]{3,2,1,0:T(8,128)S(1)}, u32[]{:S(2)}, u32[]{:S(2)}) collective-permute-start(f32[3,16,32,128]{3,2,1,0:T(8,128)} %bitcast.14), channel_id=1, source_target_pairs={{0,1},{1,2},{2,3},{3,4},{4,5},{5,6},{6,7},{7,0},{8,9},{9,10},{10,1... | collective-permute-start | bytes 2359304 | tf_op jit(solution)/shard_map/ppermute | solution.py:329
  11.7 1.2 copy-done.1
  14.7 1.3 %collective-permute-start.3 = (f32[16,32,128]{2,1,0:T(8,128)S(1)}, f32[16,32,128]{2,1,0:T(8,128)S(1)}, u32[]{:S(2)}, u32[]{:S(2)}) collective-permute-start(f32[16,32,128]{2,1,0:T(8,128)S(1)} %collective-permute-done.left_near.left), channel_id=1, source_target_pairs={{1,7},{5,3},{9,15},{13,11},{17,23},{21,19},{25,31},{29,27},{33,39}... | collective-permute-start | bytes 786440 | tf_op jit(solution)/shard_map/ppermute | solution.py:334
  17.1 9.7 %collective-permute-start.7 = (f32[3,4,8,128]{3,2,1,0:T(8,128)S(1)}, f32[3,4,8,128]{3,2,1,0:T(8,128)S(1)}, u32[]{:S(2)}, u32[]{:S(2)}) collective-permute-start(f32[3,4,8,128]{3,2,1,0:T(8,128)S(1)} %shard_map.48.own), channel_id=1, source_target_pairs={{0,2},{1,3},{2,0},{3,1},{4,6},{5,7},{6,4},{7,5},{8,10},{9,11},{10,... | collective-permute-start | bytes 147464 | tf_op jit(solution)/shard_map/ppermute | solution.py:343
  26.9 11.4 %collective-permute-done.7.partner = f32[3,4,8,128]{3,2,1,0:T(8,128)S(1)} collective-permute-done((f32[3,4,8,128]{3,2,1,0:T(8,128)S(1)}, f32[3,4,8,128]{3,2,1,0:T(8,128)S(1)}, u32[]{:S(2)}, u32[]{:S(2)}) %collective-permute-start.7) | collective-permute-done | bytes 49184 | tf_op jit(solution)/shard_map/ppermute | solution.py:343
  38.2 3.4 %collective-permute-start.6 = (f32[3,4,8,128]{3,2,1,0:T(8,128)S(1)}, f32[3,4,8,128]{3,2,1,0:T(8,128)S(1)}, u32[]{:S(2)}, u32[]{:S(2)}) collective-permute-start(f32[3,4,8,128]{3,2,1,0:T(8,128)S(1)} %shard_map.47.mean), channel_id=1, source_target_pairs={{0,248},{8,0},{16,8},{24,16},{32,24},{40,32},{48,40},{56,48},{64,5... | collective-permute-start | bytes 147464 | tf_op jit(solution)/shard_map/ppermute | solution.py:336
  42.2 4.6 %collective-permute-start.8 = (f32[4,4,8,128]{3,2,1,0:T(8,128)S(1)}, f32[4,4,8,128]{3,2,1,0:T(8,128)S(1)}, u32[]{:S(2)}, u32[]{:S(2)}) collective-permute-start(f32[4,4,8,128]{3,2,1,0:T(8,128)S(1)} %shard_map.49.strat_near), channel_id=1, source_target_pairs={{0,4},{4,0},{1,5},{5,1},{2,6},{6,2},{3,7},{7,3},{8,12},{12,8},{9,1... | collective-permute-start | bytes 196616 | tf_op jit(solution)/shard_map/ppermute | solution.py:345
  46.9 10.0 %shard_map.46.fine = f32[3,16,32,128]{3,2,1,0:T(8,128)S(1)} custom-call(f32[32,128]{1,0:T(8,128)S(1)} %broadcast_in_dim.7.spin, bf16[3,256,256]{2,1,0:T(8,128)(2,1)S(1)} %maximum_maximum_fusion.blocks, f32[16,32,128]{2,1,0:T(8,128)S(1)} %copy-done, f32[16,32,128]{2,1,0:T(8,128)S(1)} %collective-permute-done.left_near.left, ...), custom_call_target="tpu_custom_call" | custom-call | flops 10000000000 | bytes 39062500 | tf_op jit(solution)/shard_map/pallas_call | solution.py:306
  57.6 6.2 %collective-permute-start.9 = (f32[12,8,128]{2,1,0:T(8,128)S(1)}, f32[12,8,128]{2,1,0:T(8,128)S(1)}, u32[]{:S(2)}, u32[]{:S(2)}) collective-permute-start(f32[12,8,128]{2,1,0:T(8,128)S(1)} %get-tuple-element.15.refs_0_), channel_id=1, source_target_pairs={{0,16},{16,0},{32,48},{48,32},{1,17},{17,1},{33,49},{49,33},{2,18}... | collective-permute-start | bytes 147464 | tf_op jit(solution)/shard_map/ppermute | solution.py:366
  63.8 8.2 %collective-permute-start.10 = (f32[12,8,128]{2,1,0:T(8,128)S(1)}, f32[12,8,128]{2,1,0:T(8,128)S(1)}, u32[]{:S(2)}, u32[]{:S(2)}) collective-permute-start(f32[12,8,128]{2,1,0:T(8,128)S(1)} %get-tuple-element.15.refs_0_), channel_id=1, source_target_pairs={{0,32},{16,48},{32,0},{48,16},{1,33},{17,49},{33,1},{49,17},{2,34}... | collective-permute-start | bytes 147464 | tf_op jit(solution)/shard_map/ppermute | solution.py:368
  72.0 2.1 %collective-permute-start.11 = (f32[12,8,128]{2,1,0:T(8,128)S(1)}, f32[12,8,128]{2,1,0:T(8,128)S(1)}, u32[]{:S(2)}, u32[]{:S(2)}) collective-permute-start(f32[12,8,128]{2,1,0:T(8,128)S(1)} %collective-permute-done.9.refs_1_), channel_id=1, source_target_pairs={{0,32},{16,48},{32,0},{48,16},{1,33},{17,49},{33,1},{49,17},{2,34}... | collective-permute-start | bytes 147464 | tf_op jit(solution)/shard_map/ppermute | solution.py:368
  75.6 1.4 %collective-permute-done.11.refs_3_ = f32[12,8,128]{2,1,0:T(8,128)S(1)} collective-permute-done((f32[12,8,128]{2,1,0:T(8,128)S(1)}, f32[12,8,128]{2,1,0:T(8,128)S(1)}, u32[]{:S(2)}, u32[]{:S(2)}) %collective-permute-start.11) | collective-permute-done | bytes 49184 | tf_op jit(solution)/shard_map/ppermute | solution.py:368
  78.3 2.7 %shard_map.51 = (f32[3,32,8,128]{3,2,1,0:T(8,128)S(1)}, f32[3,16,8,128]{3,2,1,0:T(8,128)S(1)}) custom-call(s32[5]{0:T(128)S(1)} %stack.25.where, f32[8,128]{1,0:T(8,128)S(1)} %broadcast_in_dim.6.spin, bf16[3,256,256]{2,1,0:T(8,128)(2,1)S(1)} %maximum_maximum_fusion.blocks, f32[32,8,128]{2,1,0:T(8,128)S(1)} %get-tuple-element.14.strat, ...), custom_call_target="tpu_custom_call" | custom-call | tf_op jit(solution)/shard_map/pallas_call | solution.py:306
  81.0 1.6 %collective-permute-start.16 = (f32[3,16,8,128]{3,2,1,0:T(8,128)S(1)}, f32[3,16,8,128]{3,2,1,0:T(8,128)S(1)}, u32[]{:S(2)}, u32[]{:S(2)}) collective-permute-start(f32[3,16,8,128]{3,2,1,0:T(8,128)S(1)} %get-tuple-element.17), channel_id=1, source_target_pairs={{0,64},{64,128},{128,192},{192,0},{1,65},{65,129},{129,193},{193,1... | collective-permute-start | bytes 589832 | tf_op jit(solution)/shard_map/ppermute | solution.py:374
  82.5 2.7 %collective-permute-start.17 = (f32[3,16,8,128]{3,2,1,0:T(8,128)S(1)}, f32[3,16,8,128]{3,2,1,0:T(8,128)S(1)}, u32[]{:S(2)}, u32[]{:S(2)}) collective-permute-start(f32[3,16,8,128]{3,2,1,0:T(8,128)S(1)} %get-tuple-element.17), channel_id=1, source_target_pairs={{0,128},{64,192},{128,0},{192,64},{1,129},{65,193},{129,1},{193,65... | collective-permute-start | bytes 589832 | tf_op jit(solution)/shard_map/ppermute | solution.py:374
  85.3 1.4 %collective-permute-start.18 = (f32[3,16,8,128]{3,2,1,0:T(8,128)S(1)}, f32[3,16,8,128]{3,2,1,0:T(8,128)S(1)}, u32[]{:S(2)}, u32[]{:S(2)}) collective-permute-start(f32[3,16,8,128]{3,2,1,0:T(8,128)S(1)} %get-tuple-element.17), channel_id=1, source_target_pairs={{0,192},{64,0},{128,64},{192,128},{1,193},{65,1},{129,65},{193,129... | collective-permute-start | bytes 589832 | tf_op jit(solution)/shard_map/ppermute | solution.py:374
  86.7 2.5 %collective-permute-done.16.refs_8_ = f32[3,16,8,128]{3,2,1,0:T(8,128)S(1)} collective-permute-done((f32[3,16,8,128]{3,2,1,0:T(8,128)S(1)}, f32[3,16,8,128]{3,2,1,0:T(8,128)S(1)}, u32[]{:S(2)}, u32[]{:S(2)}) %collective-permute-start.16) | collective-permute-done | bytes 196640 | tf_op jit(solution)/shard_map/ppermute | solution.py:374
  89.2 5.2 %collective-permute-done.17.refs_9_ = f32[3,16,8,128]{3,2,1,0:T(8,128)S(1)} collective-permute-done((f32[3,16,8,128]{3,2,1,0:T(8,128)S(1)}, f32[3,16,8,128]{3,2,1,0:T(8,128)S(1)}, u32[]{:S(2)}, u32[]{:S(2)}) %collective-permute-start.17) | collective-permute-done | bytes 196640 | tf_op jit(solution)/shard_map/ppermute | solution.py:374
  96.1 8.0 %shard_map.52 = (f32[2,12,8,128]{3,2,1,0:T(8,128)S(1)}, f32[2,12,8,128]{3,2,1,0:T(8,128)S(1)}, f32[2,12,8,128]{3,2,1,0:T(8,128)S(1)}, f32[2,12,8,128]{3,2,1,0:T(8,128)S(1)}) custom-call(s32[5]{0:T(128)S(1)} %stack.25.where, f32[8,128]{1,0:T(8,128)S(1)} %broadcast_in_dim.6.spin, bf16[3,256,256]{2,1,0:T(8,128)(2,1)S(1)} %maximum_maximum_fusion.blocks, ...), custom_call_target="tpu_custom_call" | custom-call | tf_op jit(solution)/shard_map/pallas_call | solution.py:306
  104.3 3.1 %collective-permute-start.22 = (f32[2,12,8,128]{3,2,1,0:T(8,128)S(1)}, f32[2,12,8,128]{3,2,1,0:T(8,128)S(1)}, u32[]{:S(2)}, u32[]{:S(2)}) collective-permute-start(f32[2,12,8,128]{3,2,1,0:T(8,128)S(1)} %get-tuple-element.19), channel_id=1, source_target_pairs={{0,1},{1,2},{2,3},{3,0},{4,5},{5,6},{6,7},{7,4},{8,9},{9,10},{10,1... | collective-permute-start | bytes 294920 | tf_op jit(solution)/shard_map/ppermute | solution.py:381
  107.5 3.6 %collective-permute-done.24 = f32[2,12,8,128]{3,2,1,0:T(8,128)S(1)} collective-permute-done((f32[2,12,8,128]{3,2,1,0:T(8,128)S(1)}, f32[2,12,8,128]{3,2,1,0:T(8,128)S(1)}, u32[]{:S(2)}, u32[]{:S(2)}) %collective-permute-start.24) | collective-permute-done | bytes 98336 | tf_op jit(solution)/shard_map/ppermute | solution.py:381
  112.3 7.9 %collective-permute-done.25.sent = f32[12,8,128]{2,1,0:T(8,128)S(1)} collective-permute-done((f32[12,8,128]{2,1,0:T(8,128)S(1)}, f32[12,8,128]{2,1,0:T(8,128)S(1)}, u32[]{:S(2)}, u32[]{:S(2)}) %collective-permute-start.25) | collective-permute-done | bytes 49184 | tf_op jit(solution)/shard_map/ppermute | solution.py:382
  (60 shorter events, 11.1 us)
Async XLA Ops:
  0.0 14.7 %collective-permute-start = (f32[16,32,128]{2,1,0:T(8,128)}, f32[16,32,128]{2,1,0:T(8,128)S(1)}, u32[]{:S(2)}, u32[]{:S(2)}) collective-permute-start(f32[16,32,128]{2,1,0:T(8,128)} %own.1), channel_id=1, source_target_pairs={{0,1},{1,2},{2,3},{4,5},{5,6},{6,7},{8,9},{9,10},{10,11},{12,13},{... | collective-permute-start | bytes 786440 | tf_op jit(solution)/shard_map/ppermute | solution.py:331
  1.3 12.7 %collective-permute-start.1 = (f32[16,32,128]{2,1,0:T(8,128)}, f32[16,32,128]{2,1,0:T(8,128)S(1)}, u32[]{:S(2)}, u32[]{:S(2)}) collective-permute-start(f32[16,32,128]{2,1,0:T(8,128)} %own.1), channel_id=1, source_target_pairs={{1,0},{2,1},{3,2},{5,4},{6,5},{7,6},{9,8},{10,9},{11,10},{13,12},{... | collective-permute-start | bytes 786440 | tf_op jit(solution)/shard_map/ppermute | solution.py:332
  5.9 40.9 %collective-permute-start.4 = (f32[3,16,32,128]{3,2,1,0:T(8,128)}, f32[3,16,32,128]{3,2,1,0:T(8,128)S(1)}, u32[]{:S(2)}, u32[]{:S(2)}) collective-permute-start(f32[3,16,32,128]{3,2,1,0:T(8,128)} %bitcast.14), channel_id=1, source_target_pairs={{0,1},{1,2},{2,3},{3,4},{4,5},{5,6},{6,7},{7,0},{8,9},{9,10},{10,1... | collective-permute-start | bytes 2359304 | tf_op jit(solution)/shard_map/ppermute | solution.py:329
  11.7 35.1 %collective-permute-start.5 = (f32[3,16,32,128]{3,2,1,0:T(8,128)}, f32[3,16,32,128]{3,2,1,0:T(8,128)S(1)}, u32[]{:S(2)}, u32[]{:S(2)}) collective-permute-start(f32[3,16,32,128]{3,2,1,0:T(8,128)} %bitcast.15), channel_id=1, source_target_pairs={{0,7},{1,0},{2,1},{3,2},{4,3},{5,4},{6,5},{7,6},{8,15},{9,8},{10,9... | collective-permute-start | bytes 2359304 | tf_op jit(solution)/shard_map/ppermute | solution.py:330
  14.0 28.2 %collective-permute-start.2 = (f32[16,32,128]{2,1,0:T(8,128)S(1)}, f32[16,32,128]{2,1,0:T(8,128)S(1)}, u32[]{:S(2)}, u32[]{:S(2)}) collective-permute-start(f32[16,32,128]{2,1,0:T(8,128)S(1)} %collective-permute-done.1.right_near.right), channel_id=1, source_target_pairs={{2,4},{6,0},{10,12},{14,8},{18,20},{22,16},{26,28},{30,24},{34,36}... | collective-permute-start | bytes 786440 | tf_op jit(solution)/shard_map/ppermute | solution.py:333
  14.7 32.1 %collective-permute-start.3 = (f32[16,32,128]{2,1,0:T(8,128)S(1)}, f32[16,32,128]{2,1,0:T(8,128)S(1)}, u32[]{:S(2)}, u32[]{:S(2)}) collective-permute-start(f32[16,32,128]{2,1,0:T(8,128)S(1)} %collective-permute-done.left_near.left), channel_id=1, source_target_pairs={{1,7},{5,3},{9,15},{13,11},{17,23},{21,19},{25,31},{29,27},{33,39}... | collective-permute-start | bytes 786440 | tf_op jit(solution)/shard_map/ppermute | solution.py:334
  17.1 21.2 %collective-permute-start.7 = (f32[3,4,8,128]{3,2,1,0:T(8,128)S(1)}, f32[3,4,8,128]{3,2,1,0:T(8,128)S(1)}, u32[]{:S(2)}, u32[]{:S(2)}) collective-permute-start(f32[3,4,8,128]{3,2,1,0:T(8,128)S(1)} %shard_map.48.own), channel_id=1, source_target_pairs={{0,2},{1,3},{2,0},{3,1},{4,6},{5,7},{6,4},{7,5},{8,10},{9,11},{10,... | collective-permute-start | bytes 147464 | tf_op jit(solution)/shard_map/ppermute | solution.py:343
  38.2 18.6 %collective-permute-start.6 = (f32[3,4,8,128]{3,2,1,0:T(8,128)S(1)}, f32[3,4,8,128]{3,2,1,0:T(8,128)S(1)}, u32[]{:S(2)}, u32[]{:S(2)}) collective-permute-start(f32[3,4,8,128]{3,2,1,0:T(8,128)S(1)} %shard_map.47.mean), channel_id=1, source_target_pairs={{0,248},{8,0},{16,8},{24,16},{32,24},{40,32},{48,40},{56,48},{64,5... | collective-permute-start | bytes 147464 | tf_op jit(solution)/shard_map/ppermute | solution.py:336
  42.2 14.7 %collective-permute-start.8 = (f32[4,4,8,128]{3,2,1,0:T(8,128)S(1)}, f32[4,4,8,128]{3,2,1,0:T(8,128)S(1)}, u32[]{:S(2)}, u32[]{:S(2)}) collective-permute-start(f32[4,4,8,128]{3,2,1,0:T(8,128)S(1)} %shard_map.49.strat_near), channel_id=1, source_target_pairs={{0,4},{4,0},{1,5},{5,1},{2,6},{6,2},{3,7},{7,3},{8,12},{12,8},{9,1... | collective-permute-start | bytes 196616 | tf_op jit(solution)/shard_map/ppermute | solution.py:345
  57.6 14.4 %collective-permute-start.9 = (f32[12,8,128]{2,1,0:T(8,128)S(1)}, f32[12,8,128]{2,1,0:T(8,128)S(1)}, u32[]{:S(2)}, u32[]{:S(2)}) collective-permute-start(f32[12,8,128]{2,1,0:T(8,128)S(1)} %get-tuple-element.15.refs_0_), channel_id=1, source_target_pairs={{0,16},{16,0},{32,48},{48,32},{1,17},{17,1},{33,49},{49,33},{2,18}... | collective-permute-start | bytes 147464 | tf_op jit(solution)/shard_map/ppermute | solution.py:366
  63.8 11.8 %collective-permute-start.10 = (f32[12,8,128]{2,1,0:T(8,128)S(1)}, f32[12,8,128]{2,1,0:T(8,128)S(1)}, u32[]{:S(2)}, u32[]{:S(2)}) collective-permute-start(f32[12,8,128]{2,1,0:T(8,128)S(1)} %get-tuple-element.15.refs_0_), channel_id=1, source_target_pairs={{0,32},{16,48},{32,0},{48,16},{1,33},{17,49},{33,1},{49,17},{2,34}... | collective-permute-start | bytes 147464 | tf_op jit(solution)/shard_map/ppermute | solution.py:368
  72.0 5.0 %collective-permute-start.11 = (f32[12,8,128]{2,1,0:T(8,128)S(1)}, f32[12,8,128]{2,1,0:T(8,128)S(1)}, u32[]{:S(2)}, u32[]{:S(2)}) collective-permute-start(f32[12,8,128]{2,1,0:T(8,128)S(1)} %collective-permute-done.9.refs_1_), channel_id=1, source_target_pairs={{0,32},{16,48},{32,0},{48,16},{1,33},{17,49},{33,1},{49,17},{2,34}... | collective-permute-start | bytes 147464 | tf_op jit(solution)/shard_map/ppermute | solution.py:368
  74.1 3.2 %collective-permute-start.12 = (f32[12,8,128]{2,1,0:T(8,128)S(1)}, f32[12,8,128]{2,1,0:T(8,128)S(1)}, u32[]{:S(2)}, u32[]{:S(2)}) collective-permute-start(f32[12,8,128]{2,1,0:T(8,128)S(1)} %get-tuple-element.15.refs_0_), channel_id=1, source_target_pairs={{0,8},{8,0},{1,9},{9,1},{2,10},{10,2},{3,11},{11,3},{4,12},{12,4},... | collective-permute-start | bytes 147464 | tf_op jit(solution)/shard_map/ppermute | solution.py:369
  74.1 3.2 %collective-permute-start.13 = (f32[12,8,128]{2,1,0:T(8,128)S(1)}, f32[12,8,128]{2,1,0:T(8,128)S(1)}, u32[]{:S(2)}, u32[]{:S(2)}) collective-permute-start(f32[12,8,128]{2,1,0:T(8,128)S(1)} %collective-permute-done.9.refs_1_), channel_id=1, source_target_pairs={{0,8},{8,0},{1,9},{9,1},{2,10},{10,2},{3,11},{11,3},{4,12},{12,4},... | collective-permute-start | bytes 147464 | tf_op jit(solution)/shard_map/ppermute | solution.py:369
  81.0 8.3 %collective-permute-start.16 = (f32[3,16,8,128]{3,2,1,0:T(8,128)S(1)}, f32[3,16,8,128]{3,2,1,0:T(8,128)S(1)}, u32[]{:S(2)}, u32[]{:S(2)}) collective-permute-start(f32[3,16,8,128]{3,2,1,0:T(8,128)S(1)} %get-tuple-element.17), channel_id=1, source_target_pairs={{0,64},{64,128},{128,192},{192,0},{1,65},{65,129},{129,193},{193,1... | collective-permute-start | bytes 589832 | tf_op jit(solution)/shard_map/ppermute | solution.py:374
  82.5 11.9 %collective-permute-start.17 = (f32[3,16,8,128]{3,2,1,0:T(8,128)S(1)}, f32[3,16,8,128]{3,2,1,0:T(8,128)S(1)}, u32[]{:S(2)}, u32[]{:S(2)}) collective-permute-start(f32[3,16,8,128]{3,2,1,0:T(8,128)S(1)} %get-tuple-element.17), channel_id=1, source_target_pairs={{0,128},{64,192},{128,0},{192,64},{1,129},{65,193},{129,1},{193,65... | collective-permute-start | bytes 589832 | tf_op jit(solution)/shard_map/ppermute | solution.py:374
  85.3 9.2 %collective-permute-start.18 = (f32[3,16,8,128]{3,2,1,0:T(8,128)S(1)}, f32[3,16,8,128]{3,2,1,0:T(8,128)S(1)}, u32[]{:S(2)}, u32[]{:S(2)}) collective-permute-start(f32[3,16,8,128]{3,2,1,0:T(8,128)S(1)} %get-tuple-element.17), channel_id=1, source_target_pairs={{0,192},{64,0},{128,64},{192,128},{1,193},{65,1},{129,65},{193,129... | collective-permute-start | bytes 589832 | tf_op jit(solution)/shard_map/ppermute | solution.py:374
  89.2 5.7 %collective-permute-start.19 = (f32[3,16,8,128]{3,2,1,0:T(8,128)S(1)}, f32[3,16,8,128]{3,2,1,0:T(8,128)S(1)}, u32[]{:S(2)}, u32[]{:S(2)}) collective-permute-start(f32[3,16,8,128]{3,2,1,0:T(8,128)S(1)} %collective-permute-done.16.refs_8_), channel_id=1, source_target_pairs={{0,8},{8,0},{1,9},{9,1},{2,10},{10,2},{3,11},{11,3},{4,12},{12,4},... | collective-permute-start | bytes 589832 | tf_op jit(solution)/shard_map/ppermute | solution.py:375
  94.4 1.7 %collective-permute-start.21 = (f32[3,16,8,128]{3,2,1,0:T(8,128)S(1)}, f32[3,16,8,128]{3,2,1,0:T(8,128)S(1)}, u32[]{:S(2)}, u32[]{:S(2)}) collective-permute-start(f32[3,16,8,128]{3,2,1,0:T(8,128)S(1)} %collective-permute-done.18.refs_10_), channel_id=1, source_target_pairs={{0,8},{8,0},{1,9},{9,1},{2,10},{10,2},{3,11},{11,3},{4,12},{12,4},... | collective-permute-start | bytes 589832 | tf_op jit(solution)/shard_map/ppermute | solution.py:375
  94.9 25.2 %collective-permute-start.26 = (f32[3,16,32,128]{3,2,1,0:T(8,128)S(1)}, f32[3,16,32,128]{3,2,1,0:T(8,128)S(1)}, u32[]{:S(2)}, u32[]{:S(2)}) collective-permute-start(f32[3,16,32,128]{3,2,1,0:T(8,128)S(1)} %get-tuple-element.22), channel_id=1, source_target_pairs={{0,8},{8,16},{16,24},{24,32},{32,40},{40,48},{48,56},{56,64},{64,7... | collective-permute-start | bytes 2359304 | tf_op jit(solution)/shard_map/ppermute | solution.py:370
  104.2 7.0 %collective-permute-start.24 = (f32[2,12,8,128]{3,2,1,0:T(8,128)S(1)}, f32[2,12,8,128]{3,2,1,0:T(8,128)S(1)}, u32[]{:S(2)}, u32[]{:S(2)}) collective-permute-start(f32[2,12,8,128]{3,2,1,0:T(8,128)S(1)} %get-tuple-element.21), channel_id=1, source_target_pairs={{0,3},{1,0},{2,1},{3,2},{4,7},{5,4},{6,5},{7,6},{8,11},{9,8},{10,9... | collective-permute-start | bytes 294920 | tf_op jit(solution)/shard_map/ppermute | solution.py:381
  104.2 6.9 %collective-permute-start.23 = (f32[2,12,8,128]{3,2,1,0:T(8,128)S(1)}, f32[2,12,8,128]{3,2,1,0:T(8,128)S(1)}, u32[]{:S(2)}, u32[]{:S(2)}) collective-permute-start(f32[2,12,8,128]{3,2,1,0:T(8,128)S(1)} %get-tuple-element.20), channel_id=1, source_target_pairs={{0,2},{1,3},{2,0},{3,1},{4,6},{5,7},{6,4},{7,5},{8,10},{9,11},{10,... | collective-permute-start | bytes 294920 | tf_op jit(solution)/shard_map/ppermute | solution.py:381
  104.3 7.7 %collective-permute-start.22 = (f32[2,12,8,128]{3,2,1,0:T(8,128)S(1)}, f32[2,12,8,128]{3,2,1,0:T(8,128)S(1)}, u32[]{:S(2)}, u32[]{:S(2)}) collective-permute-start(f32[2,12,8,128]{3,2,1,0:T(8,128)S(1)} %get-tuple-element.19), channel_id=1, source_target_pairs={{0,1},{1,2},{2,3},{3,0},{4,5},{5,6},{6,7},{7,4},{8,9},{9,10},{10,1... | collective-permute-start | bytes 294920 | tf_op jit(solution)/shard_map/ppermute | solution.py:381
  112.1 8.1 %collective-permute-start.25 = (f32[12,8,128]{2,1,0:T(8,128)S(1)}, f32[12,8,128]{2,1,0:T(8,128)S(1)}, u32[]{:S(2)}, u32[]{:S(2)}) collective-permute-start(f32[12,8,128]{2,1,0:T(8,128)S(1)} %get-tuple-element.25), channel_id=1, source_target_pairs={{0,4},{4,0},{1,5},{5,1},{2,6},{6,2},{3,7},{7,3},{8,12},{12,8},{9,1... | collective-permute-start | bytes 147464 | tf_op jit(solution)/shard_map/ppermute | solution.py:382
  (8 other events, 40.3 us)

commit v7 on v6

--- a/solution.py
+++ b/solution.py
@@ -19,6 +19,7 @@
 HALO = 16
 WIDE = 16 + 2 * HALO
 COST = 10**10
+DIRECT = 36
 UNROLL = (11, 20, 18, 16, 14, 12, 10, 16)
 
 
@@ -97,10 +98,22 @@
             mean[k, cell] = block_means(rows.at[cell % 2], cells)
 
 
+def pack_kernel(layers, strat, direct, rest, sems):
+    copies = [
+        pltpu.make_async_copy(layers.at[pl.ds(DIRECT, 48 - DIRECT)], rest.at[pl.ds(0, 48 - DIRECT)], sems.at[0]),
+        pltpu.make_async_copy(strat, rest.at[pl.ds(48 - DIRECT, 16)], sems.at[1]),
+        pltpu.make_async_copy(layers.at[pl.ds(0, DIRECT)], direct, sems.at[2]),
+    ]
+    for copy in copies:
+        copy.start()
+    for copy in copies:
+        copy.wait()
+
+
 def strat_means_kernel(left, own, right, means, rows):
-    for n, block in enumerate((left, own, right)):
-        for cell in range(4):
-            cells = [block[4 * cell + j] for j in range(4)]
+    for n, (block, at) in enumerate(((left, 48 - DIRECT), (own, 0), (right, 48 - DIRECT))):
+        for cell in range(4):
+            cells = [block[at + 4 * cell + j] for j in range(4)]
             means[n, cell] = block_means(rows.at[cell % 2], cells)
 
 
@@ -121,13 +134,18 @@
     del blocks
     for k in range(3):
         for x in range(16):
-            one[k, x] = left[k, x]
             one[k, 16 + x] = start[k, x]
-            one[k, 32 + x] = right[k, x]
     for x in range(16):
-        strat[x] = 0.25 * (left_near[x] + left_far[x])
         strat[16 + x] = 0.25 * own_strat[x]
-        strat[32 + x] = 0.25 * (right_near[x] + right_far[x])
+    for at, direct, near, far in ((0, left, left_near, left_far), (32, right, right_near, right_far)):
+        for n in range(DIRECT):
+            one[n // 16, at + n % 16] = direct[n]
+        for n in range(64 - DIRECT):
+            value = near[n] + far[n]
+            if DIRECT + n < 48:
+                one[2, at + DIRECT + n - 32] = value
+            else:
+                strat[at + DIRECT + n - 48] = 0.25 * value
     lane = lax.broadcasted_iota(jnp.int32, (32, 128), 1)
     up = jnp.where(lane < 127, 0.15, 0.0).astype(jnp.float32)
     down = jnp.where(lane > 0, 0.15, 0.0).astype(jnp.float32)
@@ -320,16 +338,34 @@
     return [(i, i ^ by) for i in range(4)]
 
 
+def plane_pairs(by):
+    return [
+        (4 * x + zl, (4 * (x + by) + zl) % 16)
+        for x in range(4)
+        for zl in range(4)
+        if x + by < 4 or (x + by == 4 and zl == 0)
+    ]
+
+
 def per_device(slice_starts, coriolis, stratification, inverse_blocks):
     f32, bf16 = jnp.float32, jnp.bfloat16
     start = slice_starts[0]
     halves, state = ((3, 256, 256), bf16), ((3, 32, 8, 128), f32)
     increments = ((8, 12, 8, 128), f32)
 
-    left = lax.ppermute(start, SPACE, ring(8, 1))
-    right = lax.ppermute(start, SPACE, ring(8, -1))
-    left_near = lax.ppermute(stratification, SPACE, [(s, s + 1) for s in range(8) if s % 4 != 3])
-    right_near = lax.ppermute(stratification, SPACE, [(s, s - 1) for s in range(8) if s % 4 != 0])
+    anywhere = pl.BlockSpec(memory_space=pl.ANY)
+    direct, rest = pl.pallas_call(
+        pack_kernel,
+        out_shape=[jax.ShapeDtypeStruct((n, 32, 128), f32) for n in (DIRECT, 64 - DIRECT)],
+        in_specs=[anywhere] * 2,
+        out_specs=[anywhere] * 2,
+        scratch_shapes=[pltpu.SemaphoreType.DMA((3,))],
+        compiler_params=pltpu.CompilerParams(vmem_limit_bytes=60 * 1024 * 1024),
+    )(start.reshape(48, 32, 128), stratification)
+    left_near = lax.ppermute(rest, SPACE, [(s, s + 1) for s in range(8) if s % 4 != 3])
+    right_near = lax.ppermute(rest, SPACE, [(s, s - 1) for s in range(8) if s % 4 != 0])
+    left = lax.ppermute(direct, SPACE, ring(8, 1))
+    right = lax.ppermute(direct, SPACE, ring(8, -1))
     left_far = lax.ppermute(right_near, SPACE, [(2, 4), (6, 0)])
     right_far = lax.ppermute(left_near, SPACE, [(1, 7), (5, 3)])
     (mean,) = call(means_kernel, [(3, 4, 8, 128)], [((2, 32, 128), f32)], COST)(start)
@@ -371,7 +407,7 @@
     pair = [state[0], (3, 16, 8, 128)]
     common = (where, coarse_spin, blocks, strat)
     end, part = call(plane_kernel, pair, [halves, increments])(*common, *mine, *other)
-    here = [lax.ppermute(part, "x", ring(4, by)) for by in (1, 2, 3)]
+    here = [lax.ppermute(part, ("x", "zl"), plane_pairs(by)) for by in (1, 2, 3)]
     there = [lax.ppermute(part, "c", ring(2, 1)) for part in here]
     parts = call(
         chain_kernel, [(2, 12, 8, 128)] * 4, [((4, 3, 32, 8, 128), f32), state, halves, increments]

time: 122 us -> 159 us (1.30)
  Pallas kernels: 23 us -> 55.9 us
  waiting for transfers between devices: 36.1 us -> 43.2 us
  starting transfers between devices: 58.1 us -> 55.5 us
    pallas_call x0 -> x1, Pallas kernels: none -> 32.9 us  [per_device(): pl.pallas_call(pack_kernel, out_shape=[jax.ShapeDtypeStruct((n, 32, 128),...]
    ppermute x1, starting transfers between devices: 6.18 us -> 0.09 us  [per_device(): beside = lax.ppermute(increment, 'zl', swapped(1))]
    ppermute x1, waiting for transfers between devices: 11.4 us -> 16 us  [per_device(): partner = lax.ppermute(three, 'y', swapped(2))]
    ppermute x7, starting transfers between devices: 17.4 us -> 21.7 us  [the longest x3 9.96 us: per_device(): lax.ppermute(part, ('x', 'zl'), plane_pairs(by))]
    ppermute x7, waiting for transfers between devices: 7.73 us -> 11 us  [the longest x3 6.77 us: per_device(): lax.ppermute(part, ('x', 'zl'), plane_pairs(by))]
    ppermute x1, starting transfers between devices: 4.58 us -> 2.28 us  [per_device(): far = lax.ppermute(near, 'zh', ring(2, 1))]
  transfers between devices with their start and end apart: 27 -> 27, of which waited for: 11 -> 11; matrix products, arithmetic and copies ran while one was open for 1% -> 0% of each run, Pallas kernels for 15% -> 12%
where the time goes in v7:
time: 159 us; the launch traced here: 157 us
  Pallas kernels  55.9 us (35%)
  starting transfers between devices  55.5 us (35%)
  waiting for transfers between devices  43.2 us (27%)
  local copies, waits for them, and re-layouts  2.2 us (1%)
    pallas_call x1, Pallas kernels, per_device(): pl.pallas_call(pack_kernel, out_shape=[jax.ShapeDtypeStruct((n, 32, 128),...  32.9 us
    pallas_call x8, Pallas kernels, run(): pl.pallas_call(kernel, out_shape=[jax.ShapeDtypeStruct(shape, f32) for sh...  23 us
    ppermute x1, waiting for transfers between devices, per_device(): partner = lax.ppermute(three, 'y', swapped(2))  16 us
    ppermute x2, starting transfers between devices, per_device(): lax.ppermute(part, 'zl', swapped(2))  11.1 us
    ppermute x1, starting transfers between devices, per_device(): partner = lax.ppermute(three, 'y', swapped(2))  10.9 us
    ppermute x3, starting transfers between devices, per_device(): lax.ppermute(part, ('x', 'zl'), plane_pairs(by))  9.96 us
    ppermute x1, waiting for transfers between devices, per_device(): sent = lax.ppermute(total[1], 'zh', ring(2, 1))  7.73 us
    ppermute x3, waiting for transfers between devices, per_device(): lax.ppermute(part, ('x', 'zl'), plane_pairs(by))  6.77 us
  transfers between devices with their start and end apart: 27, of which 11 were waited for; matrix products, arithmetic and copies ran while one was open for 0% of the time, Pallas kernels for 12%

profile of v7, /device:TPU:24, one launch (start us, length us, event | category | flops | bytes accessed | tf_op | source)
XLA Modules:
  0.0 157.4 jit_solution(719371487728575639)
XLA Ops:
  0.0 32.9 %shard_map.46 = (f32[36,32,128]{2,1,0:T(8,128)}, f32[28,32,128]{2,1,0:T(8,128)}) custom-call(f32[48,32,128]{2,1,0:T(8,128)} %bitcast.15, f32[16,32,128]{2,1,0:T(8,128)} %own.1), custom_call_target="tpu_custom_call" | custom-call | tf_op jit(solution)/shard_map/pallas_call | solution.py:357
  32.9 1.3 collective-permute-start
  34.2 4.6 %collective-permute-start.1 = (f32[28,32,128]{2,1,0:T(8,128)}, f32[28,32,128]{2,1,0:T(8,128)S(1)}, u32[]{:S(2)}, u32[]{:S(2)}) collective-permute-start(f32[28,32,128]{2,1,0:T(8,128)} %get-tuple-element.16), channel_id=1, source_target_pairs={{1,0},{2,1},{3,2},{5,4},{6,5},{7,6},{9,8},{10,9},{11,10},{13,12},{... | collective-permute-start | bytes 1376264 | tf_op jit(solution)/shard_map/ppermute | solution.py:366
  38.8 5.9 %collective-permute-start.4 = (f32[36,32,128]{2,1,0:T(8,128)}, f32[36,32,128]{2,1,0:T(8,128)S(1)}, u32[]{:S(2)}, u32[]{:S(2)}) collective-permute-start(f32[36,32,128]{2,1,0:T(8,128)} %get-tuple-element.17), channel_id=1, source_target_pairs={{0,1},{1,2},{2,3},{3,4},{4,5},{5,6},{6,7},{7,0},{8,9},{9,10},{10,1... | collective-permute-start | bytes 1769480 | tf_op jit(solution)/shard_map/ppermute | solution.py:367
  45.7 4.3 %collective-permute-done.1.right_near.right = f32[28,32,128]{2,1,0:T(8,128)S(1)} collective-permute-done((f32[28,32,128]{2,1,0:T(8,128)}, f32[28,32,128]{2,1,0:T(8,128)S(1)}, u32[]{:S(2)}, u32[]{:S(2)}) %collective-permute-start.1) | collective-permute-done | bytes 458784 | tf_op jit(solution)/shard_map/ppermute | solution.py:366
  50.7 1.3 collective-permute-start.3
  53.0 10.9 %collective-permute-start.7 = (f32[3,4,8,128]{3,2,1,0:T(8,128)S(1)}, f32[3,4,8,128]{3,2,1,0:T(8,128)S(1)}, u32[]{:S(2)}, u32[]{:S(2)}) collective-permute-start(f32[3,4,8,128]{3,2,1,0:T(8,128)S(1)} %shard_map.49.own), channel_id=1, source_target_pairs={{0,2},{1,3},{2,0},{3,1},{4,6},{5,7},{6,4},{7,5},{8,10},{9,11},{10,... | collective-permute-start | bytes 147464 | tf_op jit(solution)/shard_map/ppermute | solution.py:379
  64.0 16.0 %collective-permute-done.7.partner = f32[3,4,8,128]{3,2,1,0:T(8,128)S(1)} collective-permute-done((f32[3,4,8,128]{3,2,1,0:T(8,128)S(1)}, f32[3,4,8,128]{3,2,1,0:T(8,128)S(1)}, u32[]{:S(2)}, u32[]{:S(2)}) %collective-permute-start.7) | collective-permute-done | bytes 49184 | tf_op jit(solution)/shard_map/ppermute | solution.py:379
  80.0 2.7 %collective-permute-start.6 = (f32[3,4,8,128]{3,2,1,0:T(8,128)S(1)}, f32[3,4,8,128]{3,2,1,0:T(8,128)S(1)}, u32[]{:S(2)}, u32[]{:S(2)}) collective-permute-start(f32[3,4,8,128]{3,2,1,0:T(8,128)S(1)} %shard_map.48.mean), channel_id=1, source_target_pairs={{0,248},{8,0},{16,8},{24,16},{32,24},{40,32},{48,40},{56,48},{64,5... | collective-permute-start | bytes 147464 | tf_op jit(solution)/shard_map/ppermute | solution.py:372
  83.3 2.3 %collective-permute-start.8 = (f32[4,4,8,128]{3,2,1,0:T(8,128)S(1)}, f32[4,4,8,128]{3,2,1,0:T(8,128)S(1)}, u32[]{:S(2)}, u32[]{:S(2)}) collective-permute-start(f32[4,4,8,128]{3,2,1,0:T(8,128)S(1)} %shard_map.50.strat_near), channel_id=1, source_target_pairs={{0,4},{4,0},{1,5},{5,1},{2,6},{6,2},{3,7},{7,3},{8,12},{12,8},{9,1... | collective-permute-start | bytes 196616 | tf_op jit(solution)/shard_map/ppermute | solution.py:381
  85.6 10.0 %shard_map.47.fine = f32[3,16,32,128]{3,2,1,0:T(8,128)S(1)} custom-call(f32[32,128]{1,0:T(8,128)S(1)} %broadcast_in_dim.7.spin, bf16[3,256,256]{2,1,0:T(8,128)(2,1)S(1)} %maximum_maximum_fusion.blocks, f32[16,32,128]{2,1,0:T(8,128)S(1)} %copy-done, f32[28,32,128]{2,1,0:T(8,128)S(1)} %collective-permute-done.left_near.left, ...), custom_call_target="tpu_custom_call" | custom-call | flops 10000000000 | bytes 39062500 | tf_op jit(solution)/shard_map/pallas_call | solution.py:324
  96.5 7.2 %collective-permute-start.10 = (f32[12,8,128]{2,1,0:T(8,128)S(1)}, f32[12,8,128]{2,1,0:T(8,128)S(1)}, u32[]{:S(2)}, u32[]{:S(2)}) collective-permute-start(f32[12,8,128]{2,1,0:T(8,128)S(1)} %get-tuple-element.19.refs_0_), channel_id=1, source_target_pairs={{0,32},{16,48},{32,0},{48,16},{1,33},{17,49},{33,1},{49,17},{2,34}... | collective-permute-start | bytes 147464 | tf_op jit(solution)/shard_map/ppermute | solution.py:404
  103.6 4.0 %collective-permute-start.11 = (f32[12,8,128]{2,1,0:T(8,128)S(1)}, f32[12,8,128]{2,1,0:T(8,128)S(1)}, u32[]{:S(2)}, u32[]{:S(2)}) collective-permute-start(f32[12,8,128]{2,1,0:T(8,128)S(1)} %collective-permute-done.9.refs_1_), channel_id=1, source_target_pairs={{0,32},{16,48},{32,0},{48,16},{1,33},{17,49},{33,1},{49,17},{2,34}... | collective-permute-start | bytes 147464 | tf_op jit(solution)/shard_map/ppermute | solution.py:404
  108.1 2.1 %collective-permute-done.11.refs_3_ = f32[12,8,128]{2,1,0:T(8,128)S(1)} collective-permute-done((f32[12,8,128]{2,1,0:T(8,128)S(1)}, f32[12,8,128]{2,1,0:T(8,128)S(1)}, u32[]{:S(2)}, u32[]{:S(2)}) %collective-permute-start.11) | collective-permute-done | bytes 49184 | tf_op jit(solution)/shard_map/ppermute | solution.py:404
  111.5 2.7 %shard_map.52 = (f32[3,32,8,128]{3,2,1,0:T(8,128)S(1)}, f32[3,16,8,128]{3,2,1,0:T(8,128)S(1)}) custom-call(s32[5]{0:T(128)S(1)} %stack.25.where, f32[8,128]{1,0:T(8,128)S(1)} %broadcast_in_dim.6.spin, bf16[3,256,256]{2,1,0:T(8,128)(2,1)S(1)} %maximum_maximum_fusion.blocks, f32[32,8,128]{2,1,0:T(8,128)S(1)} %get-tuple-element.18.strat, ...), custom_call_target="tpu_custom_call" | custom-call | tf_op jit(solution)/shard_map/pallas_call | solution.py:324
  114.2 3.4 %collective-permute-start.16 = (f32[3,16,8,128]{3,2,1,0:T(8,128)S(1)}, f32[3,16,8,128]{3,2,1,0:T(8,128)S(1)}, u32[]{:S(2)}, u32[]{:S(2)}) collective-permute-start(f32[3,16,8,128]{3,2,1,0:T(8,128)S(1)} %get-tuple-element.21), channel_id=1, source_target_pairs={{0,64},{16,80},{32,96},{48,112},{64,128},{80,144},{96,160},{112,17... | collective-permute-start | bytes 589832 | tf_op jit(solution)/shard_map/ppermute | solution.py:410
  117.6 4.6 %collective-permute-start.17 = (f32[3,16,8,128]{3,2,1,0:T(8,128)S(1)}, f32[3,16,8,128]{3,2,1,0:T(8,128)S(1)}, u32[]{:S(2)}, u32[]{:S(2)}) collective-permute-start(f32[3,16,8,128]{3,2,1,0:T(8,128)S(1)} %get-tuple-element.21), channel_id=1, source_target_pairs={{0,128},{16,144},{32,160},{48,176},{64,192},{80,208},{96,224},{112... | collective-permute-start | bytes 589832 | tf_op jit(solution)/shard_map/ppermute | solution.py:410
  122.2 1.9 %collective-permute-start.18 = (f32[3,16,8,128]{3,2,1,0:T(8,128)S(1)}, f32[3,16,8,128]{3,2,1,0:T(8,128)S(1)}, u32[]{:S(2)}, u32[]{:S(2)}) collective-permute-start(f32[3,16,8,128]{3,2,1,0:T(8,128)S(1)} %get-tuple-element.21), channel_id=1, source_target_pairs={{0,192},{16,208},{32,224},{48,240},{64,0},{1,193},{17,209},{33,225... | collective-permute-start | bytes 589832 | tf_op jit(solution)/shard_map/ppermute | solution.py:410
  124.3 5.2 %collective-permute-done.17.refs_9_ = f32[3,16,8,128]{3,2,1,0:T(8,128)S(1)} collective-permute-done((f32[3,16,8,128]{3,2,1,0:T(8,128)S(1)}, f32[3,16,8,128]{3,2,1,0:T(8,128)S(1)}, u32[]{:S(2)}, u32[]{:S(2)}) %collective-permute-start.17) | collective-permute-done | bytes 196640 | tf_op jit(solution)/shard_map/ppermute | solution.py:410
  129.5 1.5 collective-permute-done.18.refs_10_
  132.4 8.0 %shard_map.53 = (f32[2,12,8,128]{3,2,1,0:T(8,128)S(1)}, f32[2,12,8,128]{3,2,1,0:T(8,128)S(1)}, f32[2,12,8,128]{3,2,1,0:T(8,128)S(1)}, f32[2,12,8,128]{3,2,1,0:T(8,128)S(1)}) custom-call(s32[5]{0:T(128)S(1)} %stack.25.where, f32[8,128]{1,0:T(8,128)S(1)} %broadcast_in_dim.6.spin, bf16[3,256,256]{2,1,0:T(8,128)(2,1)S(1)} %maximum_maximum_fusion.blocks, ...), custom_call_target="tpu_custom_call" | custom-call | tf_op jit(solution)/shard_map/pallas_call | solution.py:324
  140.6 3.1 %collective-permute-start.22 = (f32[2,12,8,128]{3,2,1,0:T(8,128)S(1)}, f32[2,12,8,128]{3,2,1,0:T(8,128)S(1)}, u32[]{:S(2)}, u32[]{:S(2)}) collective-permute-start(f32[2,12,8,128]{3,2,1,0:T(8,128)S(1)} %get-tuple-element.23), channel_id=1, source_target_pairs={{0,1},{1,2},{2,3},{3,0},{4,5},{5,6},{6,7},{7,4},{8,9},{9,10},{10,1... | collective-permute-start | bytes 294920 | tf_op jit(solution)/shard_map/ppermute | solution.py:417
  143.7 3.6 %collective-permute-done.24 = f32[2,12,8,128]{3,2,1,0:T(8,128)S(1)} collective-permute-done((f32[2,12,8,128]{3,2,1,0:T(8,128)S(1)}, f32[2,12,8,128]{3,2,1,0:T(8,128)S(1)}, u32[]{:S(2)}, u32[]{:S(2)}) %collective-permute-start.24) | collective-permute-done | bytes 98336 | tf_op jit(solution)/shard_map/ppermute | solution.py:417
  148.7 7.7 %collective-permute-done.25.sent = f32[12,8,128]{2,1,0:T(8,128)S(1)} collective-permute-done((f32[12,8,128]{2,1,0:T(8,128)S(1)}, f32[12,8,128]{2,1,0:T(8,128)S(1)}, u32[]{:S(2)}, u32[]{:S(2)}) %collective-permute-start.25) | collective-permute-done | bytes 49184 | tf_op jit(solution)/shard_map/ppermute | solution.py:418
  (59 shorter events, 10.1 us)
Async XLA Ops:
  32.9 17.8 %collective-permute-start = (f32[28,32,128]{2,1,0:T(8,128)}, f32[28,32,128]{2,1,0:T(8,128)S(1)}, u32[]{:S(2)}, u32[]{:S(2)}) collective-permute-start(f32[28,32,128]{2,1,0:T(8,128)} %get-tuple-element.16), channel_id=1, source_target_pairs={{0,1},{1,2},{2,3},{4,5},{5,6},{6,7},{8,9},{9,10},{10,11},{12,13},{... | collective-permute-start | bytes 1376264 | tf_op jit(solution)/shard_map/ppermute | solution.py:365
  34.2 15.8 %collective-permute-start.1 = (f32[28,32,128]{2,1,0:T(8,128)}, f32[28,32,128]{2,1,0:T(8,128)S(1)}, u32[]{:S(2)}, u32[]{:S(2)}) collective-permute-start(f32[28,32,128]{2,1,0:T(8,128)} %get-tuple-element.16), channel_id=1, source_target_pairs={{1,0},{2,1},{3,2},{5,4},{6,5},{7,6},{9,8},{10,9},{11,10},{13,12},{... | collective-permute-start | bytes 1376264 | tf_op jit(solution)/shard_map/ppermute | solution.py:366
  38.8 44.5 %collective-permute-start.4 = (f32[36,32,128]{2,1,0:T(8,128)}, f32[36,32,128]{2,1,0:T(8,128)S(1)}, u32[]{:S(2)}, u32[]{:S(2)}) collective-permute-start(f32[36,32,128]{2,1,0:T(8,128)} %get-tuple-element.17), channel_id=1, source_target_pairs={{0,1},{1,2},{2,3},{3,4},{4,5},{5,6},{6,7},{7,0},{8,9},{9,10},{10,1... | collective-permute-start | bytes 1769480 | tf_op jit(solution)/shard_map/ppermute | solution.py:367
  44.6 40.9 %collective-permute-start.5 = (f32[36,32,128]{2,1,0:T(8,128)}, f32[36,32,128]{2,1,0:T(8,128)S(1)}, u32[]{:S(2)}, u32[]{:S(2)}) collective-permute-start(f32[36,32,128]{2,1,0:T(8,128)} %get-tuple-element.17), channel_id=1, source_target_pairs={{0,7},{1,0},{2,1},{3,2},{4,3},{5,4},{6,5},{7,6},{8,15},{9,8},{10,9... | collective-permute-start | bytes 1769480 | tf_op jit(solution)/shard_map/ppermute | solution.py:368
  50.0 35.5 %collective-permute-start.2 = (f32[28,32,128]{2,1,0:T(8,128)S(1)}, f32[28,32,128]{2,1,0:T(8,128)S(1)}, u32[]{:S(2)}, u32[]{:S(2)}) collective-permute-start(f32[28,32,128]{2,1,0:T(8,128)S(1)} %collective-permute-done.1.right_near.right), channel_id=1, source_target_pairs={{2,4},{6,0},{10,12},{14,8},{18,20},{22,16},{26,28},{30,24},{34,36}... | collective-permute-start | bytes 1376264 | tf_op jit(solution)/shard_map/ppermute | solution.py:369
  50.7 34.9 %collective-permute-start.3 = (f32[28,32,128]{2,1,0:T(8,128)S(1)}, f32[28,32,128]{2,1,0:T(8,128)S(1)}, u32[]{:S(2)}, u32[]{:S(2)}) collective-permute-start(f32[28,32,128]{2,1,0:T(8,128)S(1)} %collective-permute-done.left_near.left), channel_id=1, source_target_pairs={{1,7},{5,3},{9,15},{13,11},{17,23},{21,19},{25,31},{29,27},{33,39}... | collective-permute-start | bytes 1376264 | tf_op jit(solution)/shard_map/ppermute | solution.py:370
  53.0 26.9 %collective-permute-start.7 = (f32[3,4,8,128]{3,2,1,0:T(8,128)S(1)}, f32[3,4,8,128]{3,2,1,0:T(8,128)S(1)}, u32[]{:S(2)}, u32[]{:S(2)}) collective-permute-start(f32[3,4,8,128]{3,2,1,0:T(8,128)S(1)} %shard_map.49.own), channel_id=1, source_target_pairs={{0,2},{1,3},{2,0},{3,1},{4,6},{5,7},{6,4},{7,5},{8,10},{9,11},{10,... | collective-permute-start | bytes 147464 | tf_op jit(solution)/shard_map/ppermute | solution.py:379
  80.0 15.7 %collective-permute-start.6 = (f32[3,4,8,128]{3,2,1,0:T(8,128)S(1)}, f32[3,4,8,128]{3,2,1,0:T(8,128)S(1)}, u32[]{:S(2)}, u32[]{:S(2)}) collective-permute-start(f32[3,4,8,128]{3,2,1,0:T(8,128)S(1)} %shard_map.48.mean), channel_id=1, source_target_pairs={{0,248},{8,0},{16,8},{24,16},{32,24},{40,32},{48,40},{56,48},{64,5... | collective-permute-start | bytes 147464 | tf_op jit(solution)/shard_map/ppermute | solution.py:372
  83.3 12.4 %collective-permute-start.8 = (f32[4,4,8,128]{3,2,1,0:T(8,128)S(1)}, f32[4,4,8,128]{3,2,1,0:T(8,128)S(1)}, u32[]{:S(2)}, u32[]{:S(2)}) collective-permute-start(f32[4,4,8,128]{3,2,1,0:T(8,128)S(1)} %shard_map.50.strat_near), channel_id=1, source_target_pairs={{0,4},{4,0},{1,5},{5,1},{2,6},{6,2},{3,7},{7,3},{8,12},{12,8},{9,1... | collective-permute-start | bytes 196616 | tf_op jit(solution)/shard_map/ppermute | solution.py:381
  96.4 7.3 %collective-permute-start.9 = (f32[12,8,128]{2,1,0:T(8,128)S(1)}, f32[12,8,128]{2,1,0:T(8,128)S(1)}, u32[]{:S(2)}, u32[]{:S(2)}) collective-permute-start(f32[12,8,128]{2,1,0:T(8,128)S(1)} %get-tuple-element.19.refs_0_), channel_id=1, source_target_pairs={{0,16},{16,0},{32,48},{48,32},{1,17},{17,1},{33,49},{49,33},{2,18}... | collective-permute-start | bytes 147464 | tf_op jit(solution)/shard_map/ppermute | solution.py:402
  96.5 11.7 %collective-permute-start.10 = (f32[12,8,128]{2,1,0:T(8,128)S(1)}, f32[12,8,128]{2,1,0:T(8,128)S(1)}, u32[]{:S(2)}, u32[]{:S(2)}) collective-permute-start(f32[12,8,128]{2,1,0:T(8,128)S(1)} %get-tuple-element.19.refs_0_), channel_id=1, source_target_pairs={{0,32},{16,48},{32,0},{48,16},{1,33},{17,49},{33,1},{49,17},{2,34}... | collective-permute-start | bytes 147464 | tf_op jit(solution)/shard_map/ppermute | solution.py:404
  103.6 6.6 %collective-permute-start.11 = (f32[12,8,128]{2,1,0:T(8,128)S(1)}, f32[12,8,128]{2,1,0:T(8,128)S(1)}, u32[]{:S(2)}, u32[]{:S(2)}) collective-permute-start(f32[12,8,128]{2,1,0:T(8,128)S(1)} %collective-permute-done.9.refs_1_), channel_id=1, source_target_pairs={{0,32},{16,48},{32,0},{48,16},{1,33},{17,49},{33,1},{49,17},{2,34}... | collective-permute-start | bytes 147464 | tf_op jit(solution)/shard_map/ppermute | solution.py:404
  107.6 2.9 %collective-permute-start.12 = (f32[12,8,128]{2,1,0:T(8,128)S(1)}, f32[12,8,128]{2,1,0:T(8,128)S(1)}, u32[]{:S(2)}, u32[]{:S(2)}) collective-permute-start(f32[12,8,128]{2,1,0:T(8,128)S(1)} %get-tuple-element.19.refs_0_), channel_id=1, source_target_pairs={{0,8},{8,0},{1,9},{9,1},{2,10},{10,2},{3,11},{11,3},{4,12},{12,4},... | collective-permute-start | bytes 147464 | tf_op jit(solution)/shard_map/ppermute | solution.py:405
  107.6 2.9 %collective-permute-start.13 = (f32[12,8,128]{2,1,0:T(8,128)S(1)}, f32[12,8,128]{2,1,0:T(8,128)S(1)}, u32[]{:S(2)}, u32[]{:S(2)}) collective-permute-start(f32[12,8,128]{2,1,0:T(8,128)S(1)} %collective-permute-done.9.refs_1_), channel_id=1, source_target_pairs={{0,8},{8,0},{1,9},{9,1},{2,10},{10,2},{3,11},{11,3},{4,12},{12,4},... | collective-permute-start | bytes 147464 | tf_op jit(solution)/shard_map/ppermute | solution.py:405
  108.1 2.4 %collective-permute-start.14 = (f32[12,8,128]{2,1,0:T(8,128)S(1)}, f32[12,8,128]{2,1,0:T(8,128)S(1)}, u32[]{:S(2)}, u32[]{:S(2)}) collective-permute-start(f32[12,8,128]{2,1,0:T(8,128)S(1)} %collective-permute-done.10.refs_2_), channel_id=1, source_target_pairs={{0,8},{8,0},{1,9},{9,1},{2,10},{10,2},{3,11},{11,3},{4,12},{12,4},... | collective-permute-start | bytes 147464 | tf_op jit(solution)/shard_map/ppermute | solution.py:405
  114.2 10.1 %collective-permute-start.16 = (f32[3,16,8,128]{3,2,1,0:T(8,128)S(1)}, f32[3,16,8,128]{3,2,1,0:T(8,128)S(1)}, u32[]{:S(2)}, u32[]{:S(2)}) collective-permute-start(f32[3,16,8,128]{3,2,1,0:T(8,128)S(1)} %get-tuple-element.21), channel_id=1, source_target_pairs={{0,64},{16,80},{32,96},{48,112},{64,128},{80,144},{96,160},{112,17... | collective-permute-start | bytes 589832 | tf_op jit(solution)/shard_map/ppermute | solution.py:410
  117.6 11.9 %collective-permute-start.17 = (f32[3,16,8,128]{3,2,1,0:T(8,128)S(1)}, f32[3,16,8,128]{3,2,1,0:T(8,128)S(1)}, u32[]{:S(2)}, u32[]{:S(2)}) collective-permute-start(f32[3,16,8,128]{3,2,1,0:T(8,128)S(1)} %get-tuple-element.21), channel_id=1, source_target_pairs={{0,128},{16,144},{32,160},{48,176},{64,192},{80,208},{96,224},{112... | collective-permute-start | bytes 589832 | tf_op jit(solution)/shard_map/ppermute | solution.py:410
  122.2 8.7 %collective-permute-start.18 = (f32[3,16,8,128]{3,2,1,0:T(8,128)S(1)}, f32[3,16,8,128]{3,2,1,0:T(8,128)S(1)}, u32[]{:S(2)}, u32[]{:S(2)}) collective-permute-start(f32[3,16,8,128]{3,2,1,0:T(8,128)S(1)} %get-tuple-element.21), channel_id=1, source_target_pairs={{0,192},{16,208},{32,224},{48,240},{64,0},{1,193},{17,209},{33,225... | collective-permute-start | bytes 589832 | tf_op jit(solution)/shard_map/ppermute | solution.py:410
  124.3 7.2 %collective-permute-start.19 = (f32[3,16,8,128]{3,2,1,0:T(8,128)S(1)}, f32[3,16,8,128]{3,2,1,0:T(8,128)S(1)}, u32[]{:S(2)}, u32[]{:S(2)}) collective-permute-start(f32[3,16,8,128]{3,2,1,0:T(8,128)S(1)} %collective-permute-done.16.refs_8_), channel_id=1, source_target_pairs={{0,8},{8,0},{1,9},{9,1},{2,10},{10,2},{3,11},{11,3},{4,12},{12,4},... | collective-permute-start | bytes 589832 | tf_op jit(solution)/shard_map/ppermute | solution.py:411
  131.0 25.4 %collective-permute-start.26 = (f32[3,16,32,128]{3,2,1,0:T(8,128)S(1)}, f32[3,16,32,128]{3,2,1,0:T(8,128)S(1)}, u32[]{:S(2)}, u32[]{:S(2)}) collective-permute-start(f32[3,16,32,128]{3,2,1,0:T(8,128)S(1)} %get-tuple-element.26), channel_id=1, source_target_pairs={{0,8},{8,16},{16,24},{24,32},{32,40},{40,48},{48,56},{56,64},{64,7... | collective-permute-start | bytes 2359304 | tf_op jit(solution)/shard_map/ppermute | solution.py:406
  140.4 7.0 %collective-permute-start.24 = (f32[2,12,8,128]{3,2,1,0:T(8,128)S(1)}, f32[2,12,8,128]{3,2,1,0:T(8,128)S(1)}, u32[]{:S(2)}, u32[]{:S(2)}) collective-permute-start(f32[2,12,8,128]{3,2,1,0:T(8,128)S(1)} %get-tuple-element.25), channel_id=1, source_target_pairs={{0,3},{1,0},{2,1},{3,2},{4,7},{5,4},{6,5},{7,6},{8,11},{9,8},{10,9... | collective-permute-start | bytes 294920 | tf_op jit(solution)/shard_map/ppermute | solution.py:417
  140.5 6.9 %collective-permute-start.23 = (f32[2,12,8,128]{3,2,1,0:T(8,128)S(1)}, f32[2,12,8,128]{3,2,1,0:T(8,128)S(1)}, u32[]{:S(2)}, u32[]{:S(2)}) collective-permute-start(f32[2,12,8,128]{3,2,1,0:T(8,128)S(1)} %get-tuple-element.24), channel_id=1, source_target_pairs={{0,2},{1,3},{2,0},{3,1},{4,6},{5,7},{6,4},{7,5},{8,10},{9,11},{10,... | collective-permute-start | bytes 294920 | tf_op jit(solution)/shard_map/ppermute | solution.py:417
  140.6 7.7 %collective-permute-start.22 = (f32[2,12,8,128]{3,2,1,0:T(8,128)S(1)}, f32[2,12,8,128]{3,2,1,0:T(8,128)S(1)}, u32[]{:S(2)}, u32[]{:S(2)}) collective-permute-start(f32[2,12,8,128]{3,2,1,0:T(8,128)S(1)} %get-tuple-element.23), channel_id=1, source_target_pairs={{0,1},{1,2},{2,3},{3,0},{4,5},{5,6},{6,7},{7,4},{8,9},{9,10},{10,1... | collective-permute-start | bytes 294920 | tf_op jit(solution)/shard_map/ppermute | solution.py:417
  148.3 8.1 %collective-permute-start.25 = (f32[12,8,128]{2,1,0:T(8,128)S(1)}, f32[12,8,128]{2,1,0:T(8,128)S(1)}, u32[]{:S(2)}, u32[]{:S(2)}) collective-permute-start(f32[12,8,128]{2,1,0:T(8,128)S(1)} %get-tuple-element.29), channel_id=1, source_target_pairs={{0,4},{4,0},{1,5},{5,1},{2,6},{6,2},{3,7},{7,3},{8,12},{12,8},{9,1... | collective-permute-start | bytes 147464 | tf_op jit(solution)/shard_map/ppermute | solution.py:418
  (7 other events, 51.9 us)

commit v8 on v6

--- a/solution.py
+++ b/solution.py
@@ -97,8 +97,8 @@
             mean[k, cell] = block_means(rows.at[cell % 2], cells)
 
 
-def strat_means_kernel(left, own, right, means, rows):
-    for n, block in enumerate((left, own, right)):
+def strat_means_kernel(even, own, odd, means, rows):
+    for n, block in enumerate((even, own, odd)):
         for cell in range(4):
             cells = [block[4 * cell + j] for j in range(4)]
             means[n, cell] = block_means(rows.at[cell % 2], cells)
@@ -106,28 +106,31 @@
 
 def columns_kernel(place, own, partner, columns):
     y = place[1]
-    for middle, means in ((y, own), ((y + 2) % 4, partner)):
-        for n in range(3):
-
-            @pl.when((middle + n >= 1) & (middle + n <= 4))
-            def _(middle=middle, means=means, n=n):
-                columns[middle + n - 1] = means[n]
+    for column, means in ((y, own), ((y + 2) % 4, partner)):
+        columns[column + 1 - 2 * (column % 2)] = means[0]
+        columns[column] = means[1]
+
+        @pl.when((column == 1) | (column == 2))
+        def _(column=column, means=means):
+            columns[3 - column] = means[2]
 
 
 def fine_kernel(
-    spin, blocks, own_strat, left_near, right_near, left_far, right_far, start, left, right,
+    spin, blocks, place, own_strat, even_strat, odd_strat, hopped_strat, start, odd, even,
     out, one, two, strat, weights,
 ):
     del blocks
+    at_odd = 32 * (place[1] % 2)
+    at_even = 32 - at_odd
     for k in range(3):
         for x in range(16):
-            one[k, x] = left[k, x]
             one[k, 16 + x] = start[k, x]
-            one[k, 32 + x] = right[k, x]
+            one[k, at_even + x] = even[k, x]
+            one[k, at_odd + x] = odd[k, x]
     for x in range(16):
-        strat[x] = 0.25 * (left_near[x] + left_far[x])
         strat[16 + x] = 0.25 * own_strat[x]
-        strat[32 + x] = 0.25 * (right_near[x] + right_far[x])
+        strat[at_even + x] = 0.25 * even_strat[x]
+        strat[at_odd + x] = 0.25 * (odd_strat[x] + hopped_strat[x])
     lane = lax.broadcasted_iota(jnp.int32, (32, 128), 1)
     up = jnp.where(lane < 127, 0.15, 0.0).astype(jnp.float32)
     down = jnp.where(lane > 0, 0.15, 0.0).astype(jnp.float32)
@@ -250,11 +253,12 @@
     table(where, increments, mine, other)
     for k in range(3):
         for x in range(32):
-            ends[0, k, x] = end[k, x]
+            ends[row, k, x] = end[k, x]
     for j in range(3):
+        plane = row ^ (j + 1)
         for k in range(3):
-            ends[j + 1, k, pl.ds(16 * core, 16)] = here[j][k]
-            ends[j + 1, k, pl.ds(16 * (1 - core), 16)] = there[j][k]
+            ends[plane, k, pl.ds(16 * core, 16)] = here[j][k]
+            ends[plane, k, pl.ds(16 * (1 - core), 16)] = there[j][k]
     clear(state)
 
     def group(g, carry):
@@ -262,10 +266,9 @@
         def _():
             steps(8, state, halves, blocks, spin, strat)
 
-        place = (row - g + 4) % 4
         for k in range(3):
             for x in range(32):
-                state[k, x] = state[k, x] + ends[place, k, x]
+                state[k, x] = state[k, x] + ends[g, k, x]
         return carry
 
     lax.fori_loop(0, groups, group, 0)
@@ -279,7 +282,7 @@
     lax.fori_loop(0, turns, turn, 0)
 
     for j in range(4):
-        column = (y + j) % 4
+        column = y ^ j
         for half in range(2):
             side = zh if half == 0 else 1 - zh
             for k in range(3):
@@ -326,19 +329,21 @@
     halves, state = ((3, 256, 256), bf16), ((3, 32, 8, 128), f32)
     increments = ((8, 12, 8, 128), f32)
 
-    left = lax.ppermute(start, SPACE, ring(8, 1))
-    right = lax.ppermute(start, SPACE, ring(8, -1))
-    left_near = lax.ppermute(stratification, SPACE, [(s, s + 1) for s in range(8) if s % 4 != 3])
-    right_near = lax.ppermute(stratification, SPACE, [(s, s - 1) for s in range(8) if s % 4 != 0])
-    left_far = lax.ppermute(right_near, SPACE, [(2, 4), (6, 0)])
-    right_far = lax.ppermute(left_near, SPACE, [(1, 7), (5, 3)])
+    even_edges = [(s, s ^ 1) for s in range(8)]
+    odd_edges = [(s, (s + 1 if s % 2 else s - 1) % 8) for s in range(8)]
+    odd = lax.ppermute(start, SPACE, odd_edges)
+    even = lax.ppermute(start, SPACE, even_edges)
+    even_strat = lax.ppermute(stratification, SPACE, even_edges)
+    odd_strat = lax.ppermute(stratification, SPACE, [(1, 2), (2, 1), (5, 6), (6, 5)])
+    relayed = lax.ppermute(even_strat, SPACE, [(1, 5), (5, 1), (2, 6), (6, 2)])
+    hopped_strat = lax.ppermute(relayed, SPACE, [(1, 3), (5, 7), (2, 0), (6, 4)])
     (mean,) = call(means_kernel, [(3, 4, 8, 128)], [((2, 32, 128), f32)], COST)(start)
     next_mean = lax.ppermute(mean, TM, ring(32, -1))
 
     spots = [lax.axis_index(name).astype(jnp.int32) for name in ("zl", "c", "x", "zh", "y")]
     where = jnp.stack(spots)
     (three,) = call(strat_means_kernel, [(3, 4, 8, 128)], [((2, 32, 128), f32)])(
-        left_near, stratification, right_near
+        even_strat, stratification, odd_strat
     )
     partner = lax.ppermute(three, "y", swapped(2))
     (near,) = call(columns_kernel, [(4, 4, 8, 128)], [])(where[3:], three, partner)
@@ -356,8 +361,8 @@
         [((3, WIDE, 32, 128), f32)] * 2 + [((WIDE, 32, 128), f32), ((3, 32, 128), f32)],
         COST,
     )(
-        half_spin, blocks, stratification,
-        left_near, right_near, left_far, right_far, start, left, right,
+        half_spin, blocks, where[3:], stratification, even_strat, odd_strat, hopped_strat,
+        start, odd, even,
     )
     detail, increment, strat = call(
         split_kernel, [(3, 16, 32, 128), (12, 8, 128), (32, 8, 128)], [((4, 32, 128), f32)]
@@ -371,14 +376,14 @@
     pair = [state[0], (3, 16, 8, 128)]
     common = (where, coarse_spin, blocks, strat)
     end, part = call(plane_kernel, pair, [halves, increments])(*common, *mine, *other)
-    here = [lax.ppermute(part, "x", ring(4, by)) for by in (1, 2, 3)]
+    here = [lax.ppermute(part, "x", swapped(by)) for by in (1, 2, 3)]
     there = [lax.ppermute(part, "c", ring(2, 1)) for part in here]
     parts = call(
         chain_kernel, [(2, 12, 8, 128)] * 4, [((4, 3, 32, 8, 128), f32), state, halves, increments]
     )(*common, end, *mine, *other, *here, *there)
     total = parts[0]
     for by in (1, 2, 3):
-        total = total + lax.ppermute(parts[by], "y", ring(4, by))
+        total = total + lax.ppermute(parts[by], "y", swapped(by))
     sent = lax.ppermute(total[1], "zh", ring(2, 1))
     (out,) = call(final_kernel, [(3, 16, 32, 128)], [((2, 32, 128), f32)])(
         total[0], sent, detail, mean

time: 122 us -> 123 us (level)
  starting transfers between devices: 58.1 us -> 61.6 us
  waiting for transfers between devices: 36.1 us -> 34.7 us
    ppermute x12, waiting for transfers between devices: 12.3 us -> 21.2 us  [the longest x3 11.3 us: per_device(): here = [lax.ppermute(part, 'x', swapped(by)) for by in (1, 2, 3)]]
    ppermute x1, waiting for transfers between devices: 11.4 us -> 3.8 us  [per_device(): partner = lax.ppermute(three, 'y', swapped(2))]
    ppermute x1, starting transfers between devices: 6.18 us -> 0.15 us  [per_device(): beside = lax.ppermute(increment, 'zl', swapped(1))]
    ppermute x1, starting transfers between devices: 9.71 us -> 14.8 us  [per_device(): partner = lax.ppermute(three, 'y', swapped(2))]
    ppermute x2, starting transfers between devices: 10.3 us -> 13 us  [per_device(): lax.ppermute(part, 'zl', swapped(2))]
    ppermute x1, waiting for transfers between devices: 7.86 us -> 5.74 us  [per_device(): sent = lax.ppermute(total[1], 'zh', ring(2, 1))]
    ppermute x1, starting transfers between devices: 0.22 us -> 2.35 us  [per_device(): sent = lax.ppermute(total[1], 'zh', ring(2, 1))]
    ppermute x12, starting transfers between devices: 22.7 us -> 20.6 us  [the longest x1 7.68 us: per_device(): odd = lax.ppermute(start, SPACE, odd_edges)]
  transfers between devices with their start and end apart: 27 -> 27, of which waited for: 11 -> 11; matrix products, arithmetic and copies ran while one was open for 1% -> 1% of each run, Pallas kernels for 15% -> 16%
where the time goes in v8:
time: 123 us
  starting transfers between devices  61.6 us (50%)
  waiting for transfers between devices  34.7 us (28%)
  Pallas kernels  23.4 us (19%)
  local copies, waits for them, and re-layouts  2.46 us (2%)
    pallas_call x8, Pallas kernels, run(): pl.pallas_call(kernel, out_shape=[jax.ShapeDtypeStruct(shape, f32) for sh...  23.4 us
    ppermute x1, starting transfers between devices, per_device(): partner = lax.ppermute(three, 'y', swapped(2))  14.8 us
    ppermute x2, starting transfers between devices, per_device(): lax.ppermute(part, 'zl', swapped(2))  13 us
    ppermute x3, waiting for transfers between devices, per_device(): here = [lax.ppermute(part, 'x', swapped(by)) for by in (1, 2, 3)]  11.3 us
    ppermute x1, starting transfers between devices, per_device(): odd = lax.ppermute(start, SPACE, odd_edges)  7.68 us
    ppermute x1, waiting for transfers between devices, per_device(): sent = lax.ppermute(total[1], 'zh', ring(2, 1))  5.74 us
    ppermute x3, waiting for transfers between devices, per_device(): total = total + lax.ppermute(parts[by], 'y', swapped(by))  5.27 us
    ppermute x1, starting transfers between devices, per_device(): far = lax.ppermute(near, 'zh', ring(2, 1))  5.13 us
  transfers between devices with their start and end apart: 27, of which 11 were waited for; matrix products, arithmetic and copies ran while one was open for 1% of the time, Pallas kernels for 16%

profile of v8, /device:TPU:24, one launch (start us, length us, event | category | flops | bytes accessed | tf_op | source)
XLA Modules:
  0.0 122.7 jit_solution(10746829328124412050)
XLA Ops:
  0.7 7.7 %collective-permute-start.4 = (f32[3,16,32,128]{3,2,1,0:T(8,128)}, f32[3,16,32,128]{3,2,1,0:T(8,128)S(1)}, u32[]{:S(2)}, u32[]{:S(2)}) collective-permute-start(f32[3,16,32,128]{3,2,1,0:T(8,128)} %bitcast.14), channel_id=1, source_target_pairs={{0,7},{1,2},{2,1},{3,4},{4,3},{5,6},{6,5},{7,0},{8,15},{9,10},{10,... | collective-permute-start | bytes 2359304 | tf_op jit(solution)/shard_map/ppermute | solution.py:334
  9.8 1.1 copy-done.1
  11.0 4.6 %collective-permute-start.6 = (f32[3,4,8,128]{3,2,1,0:T(8,128)S(1)}, f32[3,4,8,128]{3,2,1,0:T(8,128)S(1)}, u32[]{:S(2)}, u32[]{:S(2)}) collective-permute-start(f32[3,4,8,128]{3,2,1,0:T(8,128)S(1)} %shard_map.47.mean), channel_id=1, source_target_pairs={{0,248},{8,0},{16,8},{24,16},{32,24},{40,32},{48,40},{56,48},{64,5... | collective-permute-start | bytes 147464 | tf_op jit(solution)/shard_map/ppermute | solution.py:341
  15.8 1.3 %collective-permute-start.3 = (f32[16,32,128]{2,1,0:T(8,128)S(1)}, f32[16,32,128]{2,1,0:T(8,128)S(1)}, u32[]{:S(2)}, u32[]{:S(2)}) collective-permute-start(f32[16,32,128]{2,1,0:T(8,128)S(1)} %collective-permute-done.2), channel_id=1, source_target_pairs={{1,3},{5,7},{2,0},{6,4},{9,11},{13,15},{10,8},{14,12},{17,19},{21,... | collective-permute-start | bytes 786440 | tf_op jit(solution)/shard_map/ppermute | solution.py:339
  18.1 14.8 %collective-permute-start.7 = (f32[3,4,8,128]{3,2,1,0:T(8,128)S(1)}, f32[3,4,8,128]{3,2,1,0:T(8,128)S(1)}, u32[]{:S(2)}, u32[]{:S(2)}) collective-permute-start(f32[3,4,8,128]{3,2,1,0:T(8,128)S(1)} %shard_map.48.own), channel_id=1, source_target_pairs={{0,2},{1,3},{2,0},{3,1},{4,6},{5,7},{6,4},{7,5},{8,10},{9,11},{10,... | collective-permute-start | bytes 147464 | tf_op jit(solution)/shard_map/ppermute | solution.py:348
  33.0 3.8 %collective-permute-done.7.partner = f32[3,4,8,128]{3,2,1,0:T(8,128)S(1)} collective-permute-done((f32[3,4,8,128]{3,2,1,0:T(8,128)S(1)}, f32[3,4,8,128]{3,2,1,0:T(8,128)S(1)}, u32[]{:S(2)}, u32[]{:S(2)}) %collective-permute-start.7) | collective-permute-done | bytes 49184 | tf_op jit(solution)/shard_map/ppermute | solution.py:348
  37.4 5.1 %collective-permute-start.8 = (f32[4,4,8,128]{3,2,1,0:T(8,128)S(1)}, f32[4,4,8,128]{3,2,1,0:T(8,128)S(1)}, u32[]{:S(2)}, u32[]{:S(2)}) collective-permute-start(f32[4,4,8,128]{3,2,1,0:T(8,128)S(1)} %shard_map.49.strat_near), channel_id=1, source_target_pairs={{0,4},{4,0},{1,5},{5,1},{2,6},{6,2},{3,7},{7,3},{8,12},{12,8},{9,1... | collective-permute-start | bytes 196616 | tf_op jit(solution)/shard_map/ppermute | solution.py:350
  42.5 4.6 %collective-permute-done.4.odd = f32[3,16,32,128]{3,2,1,0:T(8,128)S(1)} collective-permute-done((f32[3,16,32,128]{3,2,1,0:T(8,128)}, f32[3,16,32,128]{3,2,1,0:T(8,128)S(1)}, u32[]{:S(2)}, u32[]{:S(2)}) %collective-permute-start.4) | collective-permute-done | bytes 786464 | tf_op jit(solution)/shard_map/ppermute | solution.py:334
  47.2 10.4 %shard_map.46.fine = f32[3,16,32,128]{3,2,1,0:T(8,128)S(1)} custom-call(f32[32,128]{1,0:T(8,128)S(1)} %broadcast_in_dim.7.spin, bf16[3,256,256]{2,1,0:T(8,128)(2,1)S(1)} %maximum_maximum_fusion.blocks, s32[2]{0:T(128)S(1)} %pad_add_fusion.place, f32[16,32,128]{2,1,0:T(8,128)S(1)} %copy-done, f32[16,32,128]{2,1,0:T(8,128)S(1)} %collective-permute-done.even_strat.even, ...), custom_call_target="tpu_custom_call" | custom-call | flops 10000000000 | bytes 39062500 | tf_op jit(solution)/shard_map/pallas_call | solution.py:309
  58.5 9.0 %collective-permute-start.10 = (f32[12,8,128]{2,1,0:T(8,128)S(1)}, f32[12,8,128]{2,1,0:T(8,128)S(1)}, u32[]{:S(2)}, u32[]{:S(2)}) collective-permute-start(f32[12,8,128]{2,1,0:T(8,128)S(1)} %get-tuple-element.15.refs_0_), channel_id=1, source_target_pairs={{0,32},{16,48},{32,0},{48,16},{1,33},{17,49},{33,1},{49,17},{2,34}... | collective-permute-start | bytes 147464 | tf_op jit(solution)/shard_map/ppermute | solution.py:373
  67.5 4.0 %collective-permute-start.11 = (f32[12,8,128]{2,1,0:T(8,128)S(1)}, f32[12,8,128]{2,1,0:T(8,128)S(1)}, u32[]{:S(2)}, u32[]{:S(2)}) collective-permute-start(f32[12,8,128]{2,1,0:T(8,128)S(1)} %collective-permute-done.9.refs_1_), channel_id=1, source_target_pairs={{0,32},{16,48},{32,0},{48,16},{1,33},{17,49},{33,1},{49,17},{2,34}... | collective-permute-start | bytes 147464 | tf_op jit(solution)/shard_map/ppermute | solution.py:373
  72.0 2.1 %collective-permute-done.11.refs_3_ = f32[12,8,128]{2,1,0:T(8,128)S(1)} collective-permute-done((f32[12,8,128]{2,1,0:T(8,128)S(1)}, f32[12,8,128]{2,1,0:T(8,128)S(1)}, u32[]{:S(2)}, u32[]{:S(2)}) %collective-permute-start.11) | collective-permute-done | bytes 49184 | tf_op jit(solution)/shard_map/ppermute | solution.py:373
  75.3 2.7 %shard_map.51 = (f32[3,32,8,128]{3,2,1,0:T(8,128)S(1)}, f32[3,16,8,128]{3,2,1,0:T(8,128)S(1)}) custom-call(s32[5]{0:T(128)S(1)} %stack.25.where, f32[8,128]{1,0:T(8,128)S(1)} %broadcast_in_dim.6.spin, bf16[3,256,256]{2,1,0:T(8,128)(2,1)S(1)} %maximum_maximum_fusion.blocks, f32[32,8,128]{2,1,0:T(8,128)S(1)} %get-tuple-element.14.strat, ...), custom_call_target="tpu_custom_call" | custom-call | tf_op jit(solution)/shard_map/pallas_call | solution.py:309
  78.0 1.6 %collective-permute-start.16 = (f32[3,16,8,128]{3,2,1,0:T(8,128)S(1)}, f32[3,16,8,128]{3,2,1,0:T(8,128)S(1)}, u32[]{:S(2)}, u32[]{:S(2)}) collective-permute-start(f32[3,16,8,128]{3,2,1,0:T(8,128)S(1)} %get-tuple-element.17), channel_id=1, source_target_pairs={{0,64},{64,0},{128,192},{192,128},{1,65},{65,1},{129,193},{193,129... | collective-permute-start | bytes 589832 | tf_op jit(solution)/shard_map/ppermute | solution.py:379
  79.6 2.7 %collective-permute-start.17 = (f32[3,16,8,128]{3,2,1,0:T(8,128)S(1)}, f32[3,16,8,128]{3,2,1,0:T(8,128)S(1)}, u32[]{:S(2)}, u32[]{:S(2)}) collective-permute-start(f32[3,16,8,128]{3,2,1,0:T(8,128)S(1)} %get-tuple-element.17), channel_id=1, source_target_pairs={{0,128},{64,192},{128,0},{192,64},{1,129},{65,193},{129,1},{193,65... | collective-permute-start | bytes 589832 | tf_op jit(solution)/shard_map/ppermute | solution.py:379
  82.8 3.0 %collective-permute-done.16.refs_8_ = f32[3,16,8,128]{3,2,1,0:T(8,128)S(1)} collective-permute-done((f32[3,16,8,128]{3,2,1,0:T(8,128)S(1)}, f32[3,16,8,128]{3,2,1,0:T(8,128)S(1)}, u32[]{:S(2)}, u32[]{:S(2)}) %collective-permute-start.16) | collective-permute-done | bytes 196640 | tf_op jit(solution)/shard_map/ppermute | solution.py:379
  85.8 5.7 %collective-permute-done.17.refs_9_ = f32[3,16,8,128]{3,2,1,0:T(8,128)S(1)} collective-permute-done((f32[3,16,8,128]{3,2,1,0:T(8,128)S(1)}, f32[3,16,8,128]{3,2,1,0:T(8,128)S(1)}, u32[]{:S(2)}, u32[]{:S(2)}) %collective-permute-start.17) | collective-permute-done | bytes 196640 | tf_op jit(solution)/shard_map/ppermute | solution.py:379
  91.6 2.6 %collective-permute-done.18.refs_10_ = f32[3,16,8,128]{3,2,1,0:T(8,128)S(1)} collective-permute-done((f32[3,16,8,128]{3,2,1,0:T(8,128)S(1)}, f32[3,16,8,128]{3,2,1,0:T(8,128)S(1)}, u32[]{:S(2)}, u32[]{:S(2)}) %collective-permute-start.18) | collective-permute-done | bytes 196640 | tf_op jit(solution)/shard_map/ppermute | solution.py:379
  95.6 8.0 %shard_map.52 = (f32[2,12,8,128]{3,2,1,0:T(8,128)S(1)}, f32[2,12,8,128]{3,2,1,0:T(8,128)S(1)}, f32[2,12,8,128]{3,2,1,0:T(8,128)S(1)}, f32[2,12,8,128]{3,2,1,0:T(8,128)S(1)}) custom-call(s32[5]{0:T(128)S(1)} %stack.25.where, f32[8,128]{1,0:T(8,128)S(1)} %broadcast_in_dim.6.spin, bf16[3,256,256]{2,1,0:T(8,128)(2,1)S(1)} %maximum_maximum_fusion.blocks, ...), custom_call_target="tpu_custom_call" | custom-call | tf_op jit(solution)/shard_map/pallas_call | solution.py:309
  103.7 4.1 %collective-permute-start.23 = (f32[2,12,8,128]{3,2,1,0:T(8,128)S(1)}, f32[2,12,8,128]{3,2,1,0:T(8,128)S(1)}, u32[]{:S(2)}, u32[]{:S(2)}) collective-permute-start(f32[2,12,8,128]{3,2,1,0:T(8,128)S(1)} %get-tuple-element.20), channel_id=1, source_target_pairs={{0,2},{1,3},{2,0},{3,1},{4,6},{5,7},{6,4},{7,5},{8,10},{9,11},{10,... | collective-permute-start | bytes 294920 | tf_op jit(solution)/shard_map/ppermute | solution.py:386
  108.4 3.1 %collective-permute-done.23 = f32[2,12,8,128]{3,2,1,0:T(8,128)S(1)} collective-permute-done((f32[2,12,8,128]{3,2,1,0:T(8,128)S(1)}, f32[2,12,8,128]{3,2,1,0:T(8,128)S(1)}, u32[]{:S(2)}, u32[]{:S(2)}) %collective-permute-start.23) | collective-permute-done | bytes 98336 | tf_op jit(solution)/shard_map/ppermute | solution.py:386
  111.5 2.2 %collective-permute-done.24 = f32[2,12,8,128]{3,2,1,0:T(8,128)S(1)} collective-permute-done((f32[2,12,8,128]{3,2,1,0:T(8,128)S(1)}, f32[2,12,8,128]{3,2,1,0:T(8,128)S(1)}, u32[]{:S(2)}, u32[]{:S(2)}) %collective-permute-start.24) | collective-permute-done | bytes 98336 | tf_op jit(solution)/shard_map/ppermute | solution.py:386
  113.7 2.3 %collective-permute-start.25 = (f32[12,8,128]{2,1,0:T(8,128)S(1)}, f32[12,8,128]{2,1,0:T(8,128)S(1)}, u32[]{:S(2)}, u32[]{:S(2)}) collective-permute-start(f32[12,8,128]{2,1,0:T(8,128)S(1)} %get-tuple-element.25), channel_id=1, source_target_pairs={{0,4},{4,0},{1,5},{5,1},{2,6},{6,2},{3,7},{7,3},{8,12},{12,8},{9,1... | collective-permute-start | bytes 147464 | tf_op jit(solution)/shard_map/ppermute | solution.py:387
  116.0 5.7 %collective-permute-done.25.sent = f32[12,8,128]{2,1,0:T(8,128)S(1)} collective-permute-done((f32[12,8,128]{2,1,0:T(8,128)S(1)}, f32[12,8,128]{2,1,0:T(8,128)S(1)}, u32[]{:S(2)}, u32[]{:S(2)}) %collective-permute-start.25) | collective-permute-done | bytes 49184 | tf_op jit(solution)/shard_map/ppermute | solution.py:387
  (60 shorter events, 10.3 us)
Async XLA Ops:
  0.0 9.1 %collective-permute-start = (f32[16,32,128]{2,1,0:T(8,128)}, f32[16,32,128]{2,1,0:T(8,128)S(1)}, u32[]{:S(2)}, u32[]{:S(2)}) collective-permute-start(f32[16,32,128]{2,1,0:T(8,128)} %own.1), channel_id=1, source_target_pairs={{0,1},{1,0},{2,3},{3,2},{4,5},{5,4},{6,7},{7,6},{8,9},{9,8},{10,11... | collective-permute-start | bytes 786440 | tf_op jit(solution)/shard_map/ppermute | solution.py:336
  0.7 46.4 %collective-permute-start.4 = (f32[3,16,32,128]{3,2,1,0:T(8,128)}, f32[3,16,32,128]{3,2,1,0:T(8,128)S(1)}, u32[]{:S(2)}, u32[]{:S(2)}) collective-permute-start(f32[3,16,32,128]{3,2,1,0:T(8,128)} %bitcast.14), channel_id=1, source_target_pairs={{0,7},{1,2},{2,1},{3,4},{4,3},{5,6},{6,5},{7,0},{8,15},{9,10},{10,... | collective-permute-start | bytes 2359304 | tf_op jit(solution)/shard_map/ppermute | solution.py:334
  8.4 38.7 %collective-permute-start.5 = (f32[3,16,32,128]{3,2,1,0:T(8,128)}, f32[3,16,32,128]{3,2,1,0:T(8,128)S(1)}, u32[]{:S(2)}, u32[]{:S(2)}) collective-permute-start(f32[3,16,32,128]{3,2,1,0:T(8,128)} %bitcast.15), channel_id=1, source_target_pairs={{0,1},{1,0},{2,3},{3,2},{4,5},{5,4},{6,7},{7,6},{8,9},{9,8},{10,11... | collective-permute-start | bytes 2359304 | tf_op jit(solution)/shard_map/ppermute | solution.py:335
  8.4 8.8 %collective-permute-start.1 = (f32[16,32,128]{2,1,0:T(8,128)}, f32[16,32,128]{2,1,0:T(8,128)S(1)}, u32[]{:S(2)}, u32[]{:S(2)}) collective-permute-start(f32[16,32,128]{2,1,0:T(8,128)} %own.1), channel_id=1, source_target_pairs={{1,2},{2,1},{5,6},{6,5},{9,10},{10,9},{13,14},{14,13},{17,18},{18,... | collective-permute-start | bytes 786440 | tf_op jit(solution)/shard_map/ppermute | solution.py:337
  9.1 6.7 %collective-permute-start.2 = (f32[16,32,128]{2,1,0:T(8,128)S(1)}, f32[16,32,128]{2,1,0:T(8,128)S(1)}, u32[]{:S(2)}, u32[]{:S(2)}) collective-permute-start(f32[16,32,128]{2,1,0:T(8,128)S(1)} %collective-permute-done.even_strat.even), channel_id=1, source_target_pairs={{1,5},{5,1},{2,6},{6,2},{9,13},{13,9},{10,14},{14,10},{17,21},{21,... | collective-permute-start | bytes 786440 | tf_op jit(solution)/shard_map/ppermute | solution.py:338
  11.0 46.6 %collective-permute-start.6 = (f32[3,4,8,128]{3,2,1,0:T(8,128)S(1)}, f32[3,4,8,128]{3,2,1,0:T(8,128)S(1)}, u32[]{:S(2)}, u32[]{:S(2)}) collective-permute-start(f32[3,4,8,128]{3,2,1,0:T(8,128)S(1)} %shard_map.47.mean), channel_id=1, source_target_pairs={{0,248},{8,0},{16,8},{24,16},{32,24},{40,32},{48,40},{56,48},{64,5... | collective-permute-start | bytes 147464 | tf_op jit(solution)/shard_map/ppermute | solution.py:341
  15.8 26.7 %collective-permute-start.3 = (f32[16,32,128]{2,1,0:T(8,128)S(1)}, f32[16,32,128]{2,1,0:T(8,128)S(1)}, u32[]{:S(2)}, u32[]{:S(2)}) collective-permute-start(f32[16,32,128]{2,1,0:T(8,128)S(1)} %collective-permute-done.2), channel_id=1, source_target_pairs={{1,3},{5,7},{2,0},{6,4},{9,11},{13,15},{10,8},{14,12},{17,19},{21,... | collective-permute-start | bytes 786440 | tf_op jit(solution)/shard_map/ppermute | solution.py:339
  18.1 18.6 %collective-permute-start.7 = (f32[3,4,8,128]{3,2,1,0:T(8,128)S(1)}, f32[3,4,8,128]{3,2,1,0:T(8,128)S(1)}, u32[]{:S(2)}, u32[]{:S(2)}) collective-permute-start(f32[3,4,8,128]{3,2,1,0:T(8,128)S(1)} %shard_map.48.own), channel_id=1, source_target_pairs={{0,2},{1,3},{2,0},{3,1},{4,6},{5,7},{6,4},{7,5},{8,10},{9,11},{10,... | collective-permute-start | bytes 147464 | tf_op jit(solution)/shard_map/ppermute | solution.py:348
  37.4 20.2 %collective-permute-start.8 = (f32[4,4,8,128]{3,2,1,0:T(8,128)S(1)}, f32[4,4,8,128]{3,2,1,0:T(8,128)S(1)}, u32[]{:S(2)}, u32[]{:S(2)}) collective-permute-start(f32[4,4,8,128]{3,2,1,0:T(8,128)S(1)} %shard_map.49.strat_near), channel_id=1, source_target_pairs={{0,4},{4,0},{1,5},{5,1},{2,6},{6,2},{3,7},{7,3},{8,12},{12,8},{9,1... | collective-permute-start | bytes 196616 | tf_op jit(solution)/shard_map/ppermute | solution.py:350
  58.3 9.2 %collective-permute-start.9 = (f32[12,8,128]{2,1,0:T(8,128)S(1)}, f32[12,8,128]{2,1,0:T(8,128)S(1)}, u32[]{:S(2)}, u32[]{:S(2)}) collective-permute-start(f32[12,8,128]{2,1,0:T(8,128)S(1)} %get-tuple-element.15.refs_0_), channel_id=1, source_target_pairs={{0,16},{16,0},{32,48},{48,32},{1,17},{17,1},{33,49},{49,33},{2,18}... | collective-permute-start | bytes 147464 | tf_op jit(solution)/shard_map/ppermute | solution.py:371
  58.5 13.5 %collective-permute-start.10 = (f32[12,8,128]{2,1,0:T(8,128)S(1)}, f32[12,8,128]{2,1,0:T(8,128)S(1)}, u32[]{:S(2)}, u32[]{:S(2)}) collective-permute-start(f32[12,8,128]{2,1,0:T(8,128)S(1)} %get-tuple-element.15.refs_0_), channel_id=1, source_target_pairs={{0,32},{16,48},{32,0},{48,16},{1,33},{17,49},{33,1},{49,17},{2,34}... | collective-permute-start | bytes 147464 | tf_op jit(solution)/shard_map/ppermute | solution.py:373
  67.5 6.6 %collective-permute-start.11 = (f32[12,8,128]{2,1,0:T(8,128)S(1)}, f32[12,8,128]{2,1,0:T(8,128)S(1)}, u32[]{:S(2)}, u32[]{:S(2)}) collective-permute-start(f32[12,8,128]{2,1,0:T(8,128)S(1)} %collective-permute-done.9.refs_1_), channel_id=1, source_target_pairs={{0,32},{16,48},{32,0},{48,16},{1,33},{17,49},{33,1},{49,17},{2,34}... | collective-permute-start | bytes 147464 | tf_op jit(solution)/shard_map/ppermute | solution.py:373
  71.4 2.9 %collective-permute-start.12 = (f32[12,8,128]{2,1,0:T(8,128)S(1)}, f32[12,8,128]{2,1,0:T(8,128)S(1)}, u32[]{:S(2)}, u32[]{:S(2)}) collective-permute-start(f32[12,8,128]{2,1,0:T(8,128)S(1)} %get-tuple-element.15.refs_0_), channel_id=1, source_target_pairs={{0,8},{8,0},{1,9},{9,1},{2,10},{10,2},{3,11},{11,3},{4,12},{12,4},... | collective-permute-start | bytes 147464 | tf_op jit(solution)/shard_map/ppermute | solution.py:374
  71.5 2.9 %collective-permute-start.13 = (f32[12,8,128]{2,1,0:T(8,128)S(1)}, f32[12,8,128]{2,1,0:T(8,128)S(1)}, u32[]{:S(2)}, u32[]{:S(2)}) collective-permute-start(f32[12,8,128]{2,1,0:T(8,128)S(1)} %collective-permute-done.9.refs_1_), channel_id=1, source_target_pairs={{0,8},{8,0},{1,9},{9,1},{2,10},{10,2},{3,11},{11,3},{4,12},{12,4},... | collective-permute-start | bytes 147464 | tf_op jit(solution)/shard_map/ppermute | solution.py:374
  78.0 7.8 %collective-permute-start.16 = (f32[3,16,8,128]{3,2,1,0:T(8,128)S(1)}, f32[3,16,8,128]{3,2,1,0:T(8,128)S(1)}, u32[]{:S(2)}, u32[]{:S(2)}) collective-permute-start(f32[3,16,8,128]{3,2,1,0:T(8,128)S(1)} %get-tuple-element.17), channel_id=1, source_target_pairs={{0,64},{64,0},{128,192},{192,128},{1,65},{65,1},{129,193},{193,129... | collective-permute-start | bytes 589832 | tf_op jit(solution)/shard_map/ppermute | solution.py:379
  79.6 12.0 %collective-permute-start.17 = (f32[3,16,8,128]{3,2,1,0:T(8,128)S(1)}, f32[3,16,8,128]{3,2,1,0:T(8,128)S(1)}, u32[]{:S(2)}, u32[]{:S(2)}) collective-permute-start(f32[3,16,8,128]{3,2,1,0:T(8,128)S(1)} %get-tuple-element.17), channel_id=1, source_target_pairs={{0,128},{64,192},{128,0},{192,64},{1,129},{65,193},{129,1},{193,65... | collective-permute-start | bytes 589832 | tf_op jit(solution)/shard_map/ppermute | solution.py:379
  82.3 11.8 %collective-permute-start.18 = (f32[3,16,8,128]{3,2,1,0:T(8,128)S(1)}, f32[3,16,8,128]{3,2,1,0:T(8,128)S(1)}, u32[]{:S(2)}, u32[]{:S(2)}) collective-permute-start(f32[3,16,8,128]{3,2,1,0:T(8,128)S(1)} %get-tuple-element.17), channel_id=1, source_target_pairs={{0,192},{64,128},{128,64},{192,0},{1,193},{65,129},{129,65},{193,1... | collective-permute-start | bytes 589832 | tf_op jit(solution)/shard_map/ppermute | solution.py:379
  85.8 8.8 %collective-permute-start.19 = (f32[3,16,8,128]{3,2,1,0:T(8,128)S(1)}, f32[3,16,8,128]{3,2,1,0:T(8,128)S(1)}, u32[]{:S(2)}, u32[]{:S(2)}) collective-permute-start(f32[3,16,8,128]{3,2,1,0:T(8,128)S(1)} %collective-permute-done.16.refs_8_), channel_id=1, source_target_pairs={{0,8},{8,0},{1,9},{9,1},{2,10},{10,2},{3,11},{11,3},{4,12},{12,4},... | collective-permute-start | bytes 589832 | tf_op jit(solution)/shard_map/ppermute | solution.py:380
  91.6 3.1 %collective-permute-start.20 = (f32[3,16,8,128]{3,2,1,0:T(8,128)S(1)}, f32[3,16,8,128]{3,2,1,0:T(8,128)S(1)}, u32[]{:S(2)}, u32[]{:S(2)}) collective-permute-start(f32[3,16,8,128]{3,2,1,0:T(8,128)S(1)} %collective-permute-done.17.refs_9_), channel_id=1, source_target_pairs={{0,8},{8,0},{1,9},{9,1},{2,10},{10,2},{3,11},{11,3},{4,12},{12,4},... | collective-permute-start | bytes 589832 | tf_op jit(solution)/shard_map/ppermute | solution.py:380
  94.2 27.6 %collective-permute-start.26 = (f32[3,16,32,128]{3,2,1,0:T(8,128)S(1)}, f32[3,16,32,128]{3,2,1,0:T(8,128)S(1)}, u32[]{:S(2)}, u32[]{:S(2)}) collective-permute-start(f32[3,16,32,128]{3,2,1,0:T(8,128)S(1)} %get-tuple-element.22), channel_id=1, source_target_pairs={{0,8},{8,16},{16,24},{24,32},{32,40},{40,48},{48,56},{56,64},{64,7... | collective-permute-start | bytes 2359304 | tf_op jit(solution)/shard_map/ppermute | solution.py:375
  103.6 4.8 %collective-permute-start.22 = (f32[2,12,8,128]{3,2,1,0:T(8,128)S(1)}, f32[2,12,8,128]{3,2,1,0:T(8,128)S(1)}, u32[]{:S(2)}, u32[]{:S(2)}) collective-permute-start(f32[2,12,8,128]{3,2,1,0:T(8,128)S(1)} %get-tuple-element.19), channel_id=1, source_target_pairs={{0,1},{1,0},{2,3},{3,2},{4,5},{5,4},{6,7},{7,6},{8,9},{9,8},{10,11... | collective-permute-start | bytes 294920 | tf_op jit(solution)/shard_map/ppermute | solution.py:386
  103.7 7.8 %collective-permute-start.23 = (f32[2,12,8,128]{3,2,1,0:T(8,128)S(1)}, f32[2,12,8,128]{3,2,1,0:T(8,128)S(1)}, u32[]{:S(2)}, u32[]{:S(2)}) collective-permute-start(f32[2,12,8,128]{3,2,1,0:T(8,128)S(1)} %get-tuple-element.20), channel_id=1, source_target_pairs={{0,2},{1,3},{2,0},{3,1},{4,6},{5,7},{6,4},{7,5},{8,10},{9,11},{10,... | collective-permute-start | bytes 294920 | tf_op jit(solution)/shard_map/ppermute | solution.py:386
  107.8 5.8 %collective-permute-start.24 = (f32[2,12,8,128]{3,2,1,0:T(8,128)S(1)}, f32[2,12,8,128]{3,2,1,0:T(8,128)S(1)}, u32[]{:S(2)}, u32[]{:S(2)}) collective-permute-start(f32[2,12,8,128]{3,2,1,0:T(8,128)S(1)} %get-tuple-element.21), channel_id=1, source_target_pairs={{0,3},{1,2},{2,1},{3,0},{4,7},{5,6},{6,5},{7,4},{8,11},{9,10},{10,... | collective-permute-start | bytes 294920 | tf_op jit(solution)/shard_map/ppermute | solution.py:386
  113.7 8.1 %collective-permute-start.25 = (f32[12,8,128]{2,1,0:T(8,128)S(1)}, f32[12,8,128]{2,1,0:T(8,128)S(1)}, u32[]{:S(2)}, u32[]{:S(2)}) collective-permute-start(f32[12,8,128]{2,1,0:T(8,128)S(1)} %get-tuple-element.25), channel_id=1, source_target_pairs={{0,4},{4,0},{1,5},{5,1},{2,6},{6,2},{3,7},{7,3},{8,12},{12,8},{9,1... | collective-permute-start | bytes 147464 | tf_op jit(solution)/shard_map/ppermute | solution.py:387
  (8 other events, 43.2 us)

commit v9 on v8

--- a/solution.py
+++ b/solution.py
@@ -97,22 +97,31 @@
             mean[k, cell] = block_means(rows.at[cell % 2], cells)
 
 
-def strat_means_kernel(even, own, odd, means, rows):
-    for n, block in enumerate((even, own, odd)):
+def strat_means_kernel(even, own, means, rows):
+    for n, block in enumerate((own, even)):
         for cell in range(4):
             cells = [block[4 * cell + j] for j in range(4)]
             means[n, cell] = block_means(rows.at[cell % 2], cells)
 
 
-def columns_kernel(place, own, partner, columns):
+def columns_kernel(place, own, across, forwarded, columns):
     y = place[1]
-    for column, means in ((y, own), ((y + 2) % 4, partner)):
-        columns[column + 1 - 2 * (column % 2)] = means[0]
-        columns[column] = means[1]
-
-        @pl.when((column == 1) | (column == 2))
-        def _(column=column, means=means):
-            columns[3 - column] = means[2]
+    beside = y + 1 - 2 * (y % 2)
+    columns[y] = own[0]
+    columns[beside] = own[1]
+    inner = (y == 1) | (y == 2)
+    near = jnp.where(y < 2, 2, 1)
+    far = jnp.where(y < 2, 3, 0)
+
+    @pl.when(inner)
+    def _():
+        columns[near] = across[0]
+        columns[far] = across[1]
+
+    @pl.when(jnp.logical_not(inner))
+    def _():
+        columns[near] = forwarded[0]
+        columns[far] = forwarded[1]
 
 
 def fine_kernel(
@@ -255,7 +264,7 @@
         for x in range(32):
             ends[row, k, x] = end[k, x]
     for j in range(3):
-        plane = row ^ (j + 1)
+        plane = (row + 3 - j) % 4
         for k in range(3):
             ends[plane, k, pl.ds(16 * core, 16)] = here[j][k]
             ends[plane, k, pl.ds(16 * (1 - core), 16)] = there[j][k]
@@ -342,11 +351,14 @@
 
     spots = [lax.axis_index(name).astype(jnp.int32) for name in ("zl", "c", "x", "zh", "y")]
     where = jnp.stack(spots)
-    (three,) = call(strat_means_kernel, [(3, 4, 8, 128)], [((2, 32, 128), f32)])(
-        even_strat, stratification, odd_strat
+    (pair_means,) = call(strat_means_kernel, [(2, 4, 8, 128)], [((2, 32, 128), f32)])(
+        even_strat, stratification
     )
-    partner = lax.ppermute(three, "y", swapped(2))
-    (near,) = call(columns_kernel, [(4, 4, 8, 128)], [])(where[3:], three, partner)
+    across = lax.ppermute(pair_means, "y", [(1, 2), (2, 1)])
+    forwarded = lax.ppermute(across, "y", swapped(1))
+    (near,) = call(columns_kernel, [(4, 4, 8, 128)], [])(
+        where[3:], pair_means, across, forwarded
+    )
     far = lax.ppermute(near, "zh", ring(2, 1))
     half_spin = jnp.broadcast_to(0.5 * coriolis[:, None], (32, 128))
     coarse_spin = jnp.broadcast_to(4.0 * coriolis.reshape(8, 4).mean(axis=1)[:, None], (8, 128))
@@ -376,7 +388,7 @@
     pair = [state[0], (3, 16, 8, 128)]
     common = (where, coarse_spin, blocks, strat)
     end, part = call(plane_kernel, pair, [halves, increments])(*common, *mine, *other)
-    here = [lax.ppermute(part, "x", swapped(by)) for by in (1, 2, 3)]
+    here = [lax.ppermute(part, "x", ring(4, by)) for by in (1, 2, 3)]
     there = [lax.ppermute(part, "c", ring(2, 1)) for part in here]
     parts = call(
         chain_kernel, [(2, 12, 8, 128)] * 4, [((4, 3, 32, 8, 128), f32), state, halves, increments]

time: 123 us -> 117 us (0.951)
  waiting for transfers between devices: 34.7 us -> 24.2 us
  starting transfers between devices: 61.6 us -> 65 us
    ppermute x4 -> x5, starting transfers between devices: 19.6 us -> 28.7 us  [the longest x1 22.3 us: per_device(): forwarded = lax.ppermute(across, 'y', swapped(1))]
    ppermute x4 -> x5, waiting for transfers between devices: 15.1 us -> 9.54 us  [the longest x3 7.72 us: per_device(): here = [lax.ppermute(part, 'x', ring(4, by)) for by in (1, 2, 3)]]
    ppermute x1, starting transfers between devices: 5.13 us -> 0.09 us  [per_device(): far = lax.ppermute(near, 'zh', ring(2, 1))]
    ppermute x2, starting transfers between devices: 13 us -> 8.03 us  [per_device(): lax.ppermute(part, 'zl', swapped(2))]
    ppermute x1, starting transfers between devices: 2.35 us -> 6.03 us  [per_device(): sent = lax.ppermute(total[1], 'zh', ring(2, 1))]
    ppermute x1, waiting for transfers between devices: 5.74 us -> 2.31 us  [per_device(): sent = lax.ppermute(total[1], 'zh', ring(2, 1))]
  transfers between devices with their start and end apart: 27 -> 28, of which waited for: 11 -> 12; matrix products, arithmetic and copies ran while one was open for 1% -> 1% of each run, Pallas kernels for 16% -> 17%
where the time goes in v9:
time: 117 us; the launch traced here: 116 us
  starting transfers between devices  65 us (56%)
  waiting for transfers between devices  24.2 us (21%)
  Pallas kernels  23.9 us (20%)
  local copies, waits for them, and re-layouts  2.44 us (2%)
    pallas_call x8, Pallas kernels, run(): pl.pallas_call(kernel, out_shape=[jax.ShapeDtypeStruct(shape, f32) for sh...  23.9 us
    ppermute x1, starting transfers between devices, per_device(): forwarded = lax.ppermute(across, 'y', swapped(1))  22.3 us
    ppermute x2, starting transfers between devices, per_device(): lax.ppermute(part, 'zl', swapped(2))  8.03 us
    ppermute x3, waiting for transfers between devices, per_device(): here = [lax.ppermute(part, 'x', ring(4, by)) for by in (1, 2, 3)]  7.72 us
    ppermute x1, starting transfers between devices, per_device(): odd = lax.ppermute(start, SPACE, odd_edges)  7.68 us
    ppermute x1, starting transfers between devices, per_device(): sent = lax.ppermute(total[1], 'zh', ring(2, 1))  6.03 us
    ppermute x3, starting transfers between devices, per_device(): here = [lax.ppermute(part, 'x', ring(4, by)) for by in (1, 2, 3)]  5.73 us
    ppermute x3, starting transfers between devices, per_device(): total = total + lax.ppermute(parts[by], 'y', swapped(by))  4.78 us
  transfers between devices with their start and end apart: 28, of which 12 were waited for; matrix products, arithmetic and copies ran while one was open for 1% of the time, Pallas kernels for 17%

profile of v9, /device:TPU:24, one launch (start us, length us, event | category | flops | bytes accessed | tf_op | source)
XLA Modules:
  0.0 116.0 jit_solution(4882040400293271703)
XLA Ops:
  0.7 7.7 %collective-permute-start.4 = (f32[3,16,32,128]{3,2,1,0:T(8,128)}, f32[3,16,32,128]{3,2,1,0:T(8,128)S(1)}, u32[]{:S(2)}, u32[]{:S(2)}) collective-permute-start(f32[3,16,32,128]{3,2,1,0:T(8,128)} %bitcast.14), channel_id=1, source_target_pairs={{0,7},{1,2},{2,1},{3,4},{4,3},{5,6},{6,5},{7,0},{8,15},{9,10},{10,... | collective-permute-start | bytes 2359304 | tf_op jit(solution)/shard_map/ppermute | solution.py:343
  9.8 1.4 %collective-permute-start.2 = (f32[16,32,128]{2,1,0:T(8,128)S(1)}, f32[16,32,128]{2,1,0:T(8,128)}, u32[]{:S(2)}, u32[]{:S(2)}) collective-permute-start(f32[16,32,128]{2,1,0:T(8,128)S(1)} %collective-permute-done.even_strat.even), channel_id=1, source_target_pairs={{1,5},{5,1},{2,6},{6,2},{9,13},{13,9},{10,14},{14,10},{17,21},{21,... | collective-permute-start | bytes 786440 | tf_op jit(solution)/shard_map/ppermute | solution.py:347
  13.4 1.4 %collective-permute-start.3 = (f32[16,32,128]{2,1,0:T(8,128)}, f32[16,32,128]{2,1,0:T(8,128)}, u32[]{:S(2)}, u32[]{:S(2)}) collective-permute-start(f32[16,32,128]{2,1,0:T(8,128)} %collective-permute-done.2), channel_id=1, source_target_pairs={{1,3},{5,7},{2,0},{6,4},{9,11},{13,15},{10,8},{14,12},{17,19},{21,... | collective-permute-start | bytes 786440 | tf_op jit(solution)/shard_map/ppermute | solution.py:348
  15.6 22.3 %collective-permute-start.8 = (f32[2,4,8,128]{3,2,1,0:T(8,128)S(1)}, f32[2,4,8,128]{3,2,1,0:T(8,128)S(1)}, u32[]{:S(2)}, u32[]{:S(2)}) collective-permute-start(f32[2,4,8,128]{3,2,1,0:T(8,128)S(1)} %collective-permute-done.7.across), channel_id=1, source_target_pairs={{0,1},{1,0},{2,3},{3,2},{4,5},{5,4},{6,7},{7,6},{8,9},{9,8},{10,11... | collective-permute-start | bytes 98312 | tf_op jit(solution)/shard_map/ppermute | solution.py:358
  38.0 1.8 %collective-permute-done.8.forwarded = f32[2,4,8,128]{3,2,1,0:T(8,128)S(1)} collective-permute-done((f32[2,4,8,128]{3,2,1,0:T(8,128)S(1)}, f32[2,4,8,128]{3,2,1,0:T(8,128)S(1)}, u32[]{:S(2)}, u32[]{:S(2)}) %collective-permute-start.8) | collective-permute-done | bytes 32800 | tf_op jit(solution)/shard_map/ppermute | solution.py:358
  39.8 3.7 %collective-permute-start.6 = (f32[3,4,8,128]{3,2,1,0:T(8,128)S(1)}, f32[3,4,8,128]{3,2,1,0:T(8,128)S(1)}, u32[]{:S(2)}, u32[]{:S(2)}) collective-permute-start(f32[3,4,8,128]{3,2,1,0:T(8,128)S(1)} %shard_map.47.mean), channel_id=1, source_target_pairs={{0,248},{8,0},{16,8},{24,16},{32,24},{40,32},{48,40},{56,48},{64,5... | collective-permute-start | bytes 147464 | tf_op jit(solution)/shard_map/ppermute | solution.py:350
  44.2 3.6 %collective-permute-done.4.odd = f32[3,16,32,128]{3,2,1,0:T(8,128)S(1)} collective-permute-done((f32[3,16,32,128]{3,2,1,0:T(8,128)}, f32[3,16,32,128]{3,2,1,0:T(8,128)S(1)}, u32[]{:S(2)}, u32[]{:S(2)}) %collective-permute-start.4) | collective-permute-done | bytes 786464 | tf_op jit(solution)/shard_map/ppermute | solution.py:343
  47.9 10.9 %shard_map.46.fine = f32[3,16,32,128]{3,2,1,0:T(8,128)S(1)} custom-call(f32[32,128]{1,0:T(8,128)S(1)} %broadcast_in_dim.7.spin, bf16[3,256,256]{2,1,0:T(8,128)(2,1)S(1)} %maximum_maximum_fusion.blocks, s32[2]{0:T(128)S(1)} %pad_add_fusion.place, f32[16,32,128]{2,1,0:T(8,128)S(1)} %copy-done, f32[16,32,128]{2,1,0:T(8,128)S(1)} %collective-permute-done.even_strat.even, ...), custom_call_target="tpu_custom_call" | custom-call | flops 10000000000 | bytes 39062500 | tf_op jit(solution)/shard_map/pallas_call | solution.py:318
  59.6 3.9 %collective-permute-start.11 = (f32[12,8,128]{2,1,0:T(8,128)S(1)}, f32[12,8,128]{2,1,0:T(8,128)S(1)}, u32[]{:S(2)}, u32[]{:S(2)}) collective-permute-start(f32[12,8,128]{2,1,0:T(8,128)S(1)} %get-tuple-element.15.refs_0_), channel_id=1, source_target_pairs={{0,32},{16,48},{32,0},{48,16},{1,33},{17,49},{33,1},{49,17},{2,34}... | collective-permute-start | bytes 147464 | tf_op jit(solution)/shard_map/ppermute | solution.py:385
  63.7 4.1 %collective-permute-start.12 = (f32[12,8,128]{2,1,0:T(8,128)S(1)}, f32[12,8,128]{2,1,0:T(8,128)S(1)}, u32[]{:S(2)}, u32[]{:S(2)}) collective-permute-start(f32[12,8,128]{2,1,0:T(8,128)S(1)} %collective-permute-done.10.refs_1_), channel_id=1, source_target_pairs={{0,32},{16,48},{32,0},{48,16},{1,33},{17,49},{33,1},{49,17},{2,34}... | collective-permute-start | bytes 147464 | tf_op jit(solution)/shard_map/ppermute | solution.py:385
  68.3 2.1 %collective-permute-done.12.refs_3_ = f32[12,8,128]{2,1,0:T(8,128)S(1)} collective-permute-done((f32[12,8,128]{2,1,0:T(8,128)S(1)}, f32[12,8,128]{2,1,0:T(8,128)S(1)}, u32[]{:S(2)}, u32[]{:S(2)}) %collective-permute-start.12) | collective-permute-done | bytes 49184 | tf_op jit(solution)/shard_map/ppermute | solution.py:385
  71.7 2.7 %shard_map.51 = (f32[3,32,8,128]{3,2,1,0:T(8,128)S(1)}, f32[3,16,8,128]{3,2,1,0:T(8,128)S(1)}) custom-call(s32[5]{0:T(128)S(1)} %stack.25.where, f32[8,128]{1,0:T(8,128)S(1)} %broadcast_in_dim.6.spin, bf16[3,256,256]{2,1,0:T(8,128)(2,1)S(1)} %maximum_maximum_fusion.blocks, f32[32,8,128]{2,1,0:T(8,128)S(1)} %get-tuple-element.14.strat, ...), custom_call_target="tpu_custom_call" | custom-call | tf_op jit(solution)/shard_map/pallas_call | solution.py:318
  74.3 1.6 %collective-permute-start.17 = (f32[3,16,8,128]{3,2,1,0:T(8,128)S(1)}, f32[3,16,8,128]{3,2,1,0:T(8,128)S(1)}, u32[]{:S(2)}, u32[]{:S(2)}) collective-permute-start(f32[3,16,8,128]{3,2,1,0:T(8,128)S(1)} %get-tuple-element.17), channel_id=1, source_target_pairs={{0,64},{64,128},{128,192},{192,0},{1,65},{65,129},{129,193},{193,1... | collective-permute-start | bytes 589832 | tf_op jit(solution)/shard_map/ppermute | solution.py:391
  75.9 2.7 %collective-permute-start.18 = (f32[3,16,8,128]{3,2,1,0:T(8,128)S(1)}, f32[3,16,8,128]{3,2,1,0:T(8,128)S(1)}, u32[]{:S(2)}, u32[]{:S(2)}) collective-permute-start(f32[3,16,8,128]{3,2,1,0:T(8,128)S(1)} %get-tuple-element.17), channel_id=1, source_target_pairs={{0,128},{64,192},{128,0},{192,64},{1,129},{65,193},{129,1},{193,65... | collective-permute-start | bytes 589832 | tf_op jit(solution)/shard_map/ppermute | solution.py:391
  78.6 1.4 %collective-permute-start.19 = (f32[3,16,8,128]{3,2,1,0:T(8,128)S(1)}, f32[3,16,8,128]{3,2,1,0:T(8,128)S(1)}, u32[]{:S(2)}, u32[]{:S(2)}) collective-permute-start(f32[3,16,8,128]{3,2,1,0:T(8,128)S(1)} %get-tuple-element.17), channel_id=1, source_target_pairs={{0,192},{64,0},{128,64},{192,128},{1,193},{65,1},{129,65},{193,129... | collective-permute-start | bytes 589832 | tf_op jit(solution)/shard_map/ppermute | solution.py:391
  80.1 2.5 %collective-permute-done.17.refs_8_ = f32[3,16,8,128]{3,2,1,0:T(8,128)S(1)} collective-permute-done((f32[3,16,8,128]{3,2,1,0:T(8,128)S(1)}, f32[3,16,8,128]{3,2,1,0:T(8,128)S(1)}, u32[]{:S(2)}, u32[]{:S(2)}) %collective-permute-start.17) | collective-permute-done | bytes 196640 | tf_op jit(solution)/shard_map/ppermute | solution.py:391
  82.6 5.2 %collective-permute-done.18.refs_9_ = f32[3,16,8,128]{3,2,1,0:T(8,128)S(1)} collective-permute-done((f32[3,16,8,128]{3,2,1,0:T(8,128)S(1)}, f32[3,16,8,128]{3,2,1,0:T(8,128)S(1)}, u32[]{:S(2)}, u32[]{:S(2)}) %collective-permute-start.18) | collective-permute-done | bytes 196640 | tf_op jit(solution)/shard_map/ppermute | solution.py:391
  89.5 8.0 %shard_map.52 = (f32[2,12,8,128]{3,2,1,0:T(8,128)S(1)}, f32[2,12,8,128]{3,2,1,0:T(8,128)S(1)}, f32[2,12,8,128]{3,2,1,0:T(8,128)S(1)}, f32[2,12,8,128]{3,2,1,0:T(8,128)S(1)}) custom-call(s32[5]{0:T(128)S(1)} %stack.25.where, f32[8,128]{1,0:T(8,128)S(1)} %broadcast_in_dim.6.spin, bf16[3,256,256]{2,1,0:T(8,128)(2,1)S(1)} %maximum_maximum_fusion.blocks, ...), custom_call_target="tpu_custom_call" | custom-call | tf_op jit(solution)/shard_map/pallas_call | solution.py:318
  97.6 3.2 %collective-permute-start.24 = (f32[2,12,8,128]{3,2,1,0:T(8,128)S(1)}, f32[2,12,8,128]{3,2,1,0:T(8,128)S(1)}, u32[]{:S(2)}, u32[]{:S(2)}) collective-permute-start(f32[2,12,8,128]{3,2,1,0:T(8,128)S(1)} %get-tuple-element.20), channel_id=1, source_target_pairs={{0,2},{1,3},{2,0},{3,1},{4,6},{5,7},{6,4},{7,5},{8,10},{9,11},{10,... | collective-permute-start | bytes 294920 | tf_op jit(solution)/shard_map/ppermute | solution.py:398
  100.8 1.5 %collective-permute-start.25 = (f32[2,12,8,128]{3,2,1,0:T(8,128)S(1)}, f32[2,12,8,128]{3,2,1,0:T(8,128)S(1)}, u32[]{:S(2)}, u32[]{:S(2)}) collective-permute-start(f32[2,12,8,128]{3,2,1,0:T(8,128)S(1)} %get-tuple-element.21), channel_id=1, source_target_pairs={{0,3},{1,2},{2,1},{3,0},{4,7},{5,6},{6,5},{7,4},{8,11},{9,10},{10,... | collective-permute-start | bytes 294920 | tf_op jit(solution)/shard_map/ppermute | solution.py:398
  102.3 2.2 %collective-permute-done.24 = f32[2,12,8,128]{3,2,1,0:T(8,128)S(1)} collective-permute-done((f32[2,12,8,128]{3,2,1,0:T(8,128)S(1)}, f32[2,12,8,128]{3,2,1,0:T(8,128)S(1)}, u32[]{:S(2)}, u32[]{:S(2)}) %collective-permute-start.24) | collective-permute-done | bytes 98336 | tf_op jit(solution)/shard_map/ppermute | solution.py:398
  104.5 2.2 %collective-permute-done.25 = f32[2,12,8,128]{3,2,1,0:T(8,128)S(1)} collective-permute-done((f32[2,12,8,128]{3,2,1,0:T(8,128)S(1)}, f32[2,12,8,128]{3,2,1,0:T(8,128)S(1)}, u32[]{:S(2)}, u32[]{:S(2)}) %collective-permute-start.25) | collective-permute-done | bytes 98336 | tf_op jit(solution)/shard_map/ppermute | solution.py:398
  106.7 6.0 %collective-permute-start.26 = (f32[12,8,128]{2,1,0:T(8,128)S(1)}, f32[12,8,128]{2,1,0:T(8,128)S(1)}, u32[]{:S(2)}, u32[]{:S(2)}) collective-permute-start(f32[12,8,128]{2,1,0:T(8,128)S(1)} %get-tuple-element.25), channel_id=1, source_target_pairs={{0,4},{4,0},{1,5},{5,1},{2,6},{6,2},{3,7},{7,3},{8,12},{12,8},{9,1... | collective-permute-start | bytes 147464 | tf_op jit(solution)/shard_map/ppermute | solution.py:399
  112.7 2.3 %collective-permute-done.26.sent = f32[12,8,128]{2,1,0:T(8,128)S(1)} collective-permute-done((f32[12,8,128]{2,1,0:T(8,128)S(1)}, f32[12,8,128]{2,1,0:T(8,128)S(1)}, u32[]{:S(2)}, u32[]{:S(2)}) %collective-permute-start.26) | collective-permute-done | bytes 49184 | tf_op jit(solution)/shard_map/ppermute | solution.py:399
  (62 shorter events, 11.5 us)
Async XLA Ops:
  0.0 9.8 %collective-permute-start = (f32[16,32,128]{2,1,0:T(8,128)}, f32[16,32,128]{2,1,0:T(8,128)S(1)}, u32[]{:S(2)}, u32[]{:S(2)}) collective-permute-start(f32[16,32,128]{2,1,0:T(8,128)} %own.1), channel_id=1, source_target_pairs={{0,1},{1,0},{2,3},{3,2},{4,5},{5,4},{6,7},{7,6},{8,9},{9,8},{10,11... | collective-permute-start | bytes 786440 | tf_op jit(solution)/shard_map/ppermute | solution.py:345
  0.7 47.1 %collective-permute-start.4 = (f32[3,16,32,128]{3,2,1,0:T(8,128)}, f32[3,16,32,128]{3,2,1,0:T(8,128)S(1)}, u32[]{:S(2)}, u32[]{:S(2)}) collective-permute-start(f32[3,16,32,128]{3,2,1,0:T(8,128)} %bitcast.14), channel_id=1, source_target_pairs={{0,7},{1,2},{2,1},{3,4},{4,3},{5,6},{6,5},{7,0},{8,15},{9,10},{10,... | collective-permute-start | bytes 2359304 | tf_op jit(solution)/shard_map/ppermute | solution.py:343
  8.4 39.4 %collective-permute-start.5 = (f32[3,16,32,128]{3,2,1,0:T(8,128)}, f32[3,16,32,128]{3,2,1,0:T(8,128)S(1)}, u32[]{:S(2)}, u32[]{:S(2)}) collective-permute-start(f32[3,16,32,128]{3,2,1,0:T(8,128)} %bitcast.15), channel_id=1, source_target_pairs={{0,1},{1,0},{2,3},{3,2},{4,5},{5,4},{6,7},{7,6},{8,9},{9,8},{10,11... | collective-permute-start | bytes 2359304 | tf_op jit(solution)/shard_map/ppermute | solution.py:344
  8.4 35.7 %collective-permute-start.1 = (f32[16,32,128]{2,1,0:T(8,128)}, f32[16,32,128]{2,1,0:T(8,128)}, u32[]{:S(2)}, u32[]{:S(2)}) collective-permute-start(f32[16,32,128]{2,1,0:T(8,128)} %own.1), channel_id=1, source_target_pairs={{1,2},{2,1},{5,6},{6,5},{9,10},{10,9},{13,14},{14,13},{17,18},{18,... | collective-permute-start | bytes 786440 | tf_op jit(solution)/shard_map/ppermute | solution.py:346
  9.8 3.6 %collective-permute-start.2 = (f32[16,32,128]{2,1,0:T(8,128)S(1)}, f32[16,32,128]{2,1,0:T(8,128)}, u32[]{:S(2)}, u32[]{:S(2)}) collective-permute-start(f32[16,32,128]{2,1,0:T(8,128)S(1)} %collective-permute-done.even_strat.even), channel_id=1, source_target_pairs={{1,5},{5,1},{2,6},{6,2},{9,13},{13,9},{10,14},{14,10},{17,21},{21,... | collective-permute-start | bytes 786440 | tf_op jit(solution)/shard_map/ppermute | solution.py:347
  13.4 30.8 %collective-permute-start.3 = (f32[16,32,128]{2,1,0:T(8,128)}, f32[16,32,128]{2,1,0:T(8,128)}, u32[]{:S(2)}, u32[]{:S(2)}) collective-permute-start(f32[16,32,128]{2,1,0:T(8,128)} %collective-permute-done.2), channel_id=1, source_target_pairs={{1,3},{5,7},{2,0},{6,4},{9,11},{13,15},{10,8},{14,12},{17,19},{21,... | collective-permute-start | bytes 786440 | tf_op jit(solution)/shard_map/ppermute | solution.py:348
  15.6 24.2 %collective-permute-start.8 = (f32[2,4,8,128]{3,2,1,0:T(8,128)S(1)}, f32[2,4,8,128]{3,2,1,0:T(8,128)S(1)}, u32[]{:S(2)}, u32[]{:S(2)}) collective-permute-start(f32[2,4,8,128]{3,2,1,0:T(8,128)S(1)} %collective-permute-done.7.across), channel_id=1, source_target_pairs={{0,1},{1,0},{2,3},{3,2},{4,5},{5,4},{6,7},{7,6},{8,9},{9,8},{10,11... | collective-permute-start | bytes 98312 | tf_op jit(solution)/shard_map/ppermute | solution.py:358
  39.8 18.9 %collective-permute-start.6 = (f32[3,4,8,128]{3,2,1,0:T(8,128)S(1)}, f32[3,4,8,128]{3,2,1,0:T(8,128)S(1)}, u32[]{:S(2)}, u32[]{:S(2)}) collective-permute-start(f32[3,4,8,128]{3,2,1,0:T(8,128)S(1)} %shard_map.47.mean), channel_id=1, source_target_pairs={{0,248},{8,0},{16,8},{24,16},{32,24},{40,32},{48,40},{56,48},{64,5... | collective-permute-start | bytes 147464 | tf_op jit(solution)/shard_map/ppermute | solution.py:350
  44.1 14.7 %collective-permute-start.9 = (f32[4,4,8,128]{3,2,1,0:T(8,128)S(1)}, f32[4,4,8,128]{3,2,1,0:T(8,128)S(1)}, u32[]{:S(2)}, u32[]{:S(2)}) collective-permute-start(f32[4,4,8,128]{3,2,1,0:T(8,128)S(1)} %shard_map.49.strat_near), channel_id=1, source_target_pairs={{0,4},{4,0},{1,5},{5,1},{2,6},{6,2},{3,7},{7,3},{8,12},{12,8},{9,1... | collective-permute-start | bytes 196616 | tf_op jit(solution)/shard_map/ppermute | solution.py:362
  59.5 4.2 %collective-permute-start.10 = (f32[12,8,128]{2,1,0:T(8,128)S(1)}, f32[12,8,128]{2,1,0:T(8,128)S(1)}, u32[]{:S(2)}, u32[]{:S(2)}) collective-permute-start(f32[12,8,128]{2,1,0:T(8,128)S(1)} %get-tuple-element.15.refs_0_), channel_id=1, source_target_pairs={{0,16},{16,0},{32,48},{48,32},{1,17},{17,1},{33,49},{49,33},{2,18}... | collective-permute-start | bytes 147464 | tf_op jit(solution)/shard_map/ppermute | solution.py:383
  59.6 8.7 %collective-permute-start.11 = (f32[12,8,128]{2,1,0:T(8,128)S(1)}, f32[12,8,128]{2,1,0:T(8,128)S(1)}, u32[]{:S(2)}, u32[]{:S(2)}) collective-permute-start(f32[12,8,128]{2,1,0:T(8,128)S(1)} %get-tuple-element.15.refs_0_), channel_id=1, source_target_pairs={{0,32},{16,48},{32,0},{48,16},{1,33},{17,49},{33,1},{49,17},{2,34}... | collective-permute-start | bytes 147464 | tf_op jit(solution)/shard_map/ppermute | solution.py:385
  63.7 6.7 %collective-permute-start.12 = (f32[12,8,128]{2,1,0:T(8,128)S(1)}, f32[12,8,128]{2,1,0:T(8,128)S(1)}, u32[]{:S(2)}, u32[]{:S(2)}) collective-permute-start(f32[12,8,128]{2,1,0:T(8,128)S(1)} %collective-permute-done.10.refs_1_), channel_id=1, source_target_pairs={{0,32},{16,48},{32,0},{48,16},{1,33},{17,49},{33,1},{49,17},{2,34}... | collective-permute-start | bytes 147464 | tf_op jit(solution)/shard_map/ppermute | solution.py:385
  67.8 2.9 %collective-permute-start.13 = (f32[12,8,128]{2,1,0:T(8,128)S(1)}, f32[12,8,128]{2,1,0:T(8,128)S(1)}, u32[]{:S(2)}, u32[]{:S(2)}) collective-permute-start(f32[12,8,128]{2,1,0:T(8,128)S(1)} %get-tuple-element.15.refs_0_), channel_id=1, source_target_pairs={{0,8},{8,0},{1,9},{9,1},{2,10},{10,2},{3,11},{11,3},{4,12},{12,4},... | collective-permute-start | bytes 147464 | tf_op jit(solution)/shard_map/ppermute | solution.py:386
  67.8 2.9 %collective-permute-start.14 = (f32[12,8,128]{2,1,0:T(8,128)S(1)}, f32[12,8,128]{2,1,0:T(8,128)S(1)}, u32[]{:S(2)}, u32[]{:S(2)}) collective-permute-start(f32[12,8,128]{2,1,0:T(8,128)S(1)} %collective-permute-done.10.refs_1_), channel_id=1, source_target_pairs={{0,8},{8,0},{1,9},{9,1},{2,10},{10,2},{3,11},{11,3},{4,12},{12,4},... | collective-permute-start | bytes 147464 | tf_op jit(solution)/shard_map/ppermute | solution.py:386
  68.3 2.4 %collective-permute-start.15 = (f32[12,8,128]{2,1,0:T(8,128)S(1)}, f32[12,8,128]{2,1,0:T(8,128)S(1)}, u32[]{:S(2)}, u32[]{:S(2)}) collective-permute-start(f32[12,8,128]{2,1,0:T(8,128)S(1)} %collective-permute-done.11.refs_2_), channel_id=1, source_target_pairs={{0,8},{8,0},{1,9},{9,1},{2,10},{10,2},{3,11},{11,3},{4,12},{12,4},... | collective-permute-start | bytes 147464 | tf_op jit(solution)/shard_map/ppermute | solution.py:386
  74.3 8.3 %collective-permute-start.17 = (f32[3,16,8,128]{3,2,1,0:T(8,128)S(1)}, f32[3,16,8,128]{3,2,1,0:T(8,128)S(1)}, u32[]{:S(2)}, u32[]{:S(2)}) collective-permute-start(f32[3,16,8,128]{3,2,1,0:T(8,128)S(1)} %get-tuple-element.17), channel_id=1, source_target_pairs={{0,64},{64,128},{128,192},{192,0},{1,65},{65,129},{129,193},{193,1... | collective-permute-start | bytes 589832 | tf_op jit(solution)/shard_map/ppermute | solution.py:391
  75.9 11.9 %collective-permute-start.18 = (f32[3,16,8,128]{3,2,1,0:T(8,128)S(1)}, f32[3,16,8,128]{3,2,1,0:T(8,128)S(1)}, u32[]{:S(2)}, u32[]{:S(2)}) collective-permute-start(f32[3,16,8,128]{3,2,1,0:T(8,128)S(1)} %get-tuple-element.17), channel_id=1, source_target_pairs={{0,128},{64,192},{128,0},{192,64},{1,129},{65,193},{129,1},{193,65... | collective-permute-start | bytes 589832 | tf_op jit(solution)/shard_map/ppermute | solution.py:391
  78.6 9.2 %collective-permute-start.19 = (f32[3,16,8,128]{3,2,1,0:T(8,128)S(1)}, f32[3,16,8,128]{3,2,1,0:T(8,128)S(1)}, u32[]{:S(2)}, u32[]{:S(2)}) collective-permute-start(f32[3,16,8,128]{3,2,1,0:T(8,128)S(1)} %get-tuple-element.17), channel_id=1, source_target_pairs={{0,192},{64,0},{128,64},{192,128},{1,193},{65,1},{129,65},{193,129... | collective-permute-start | bytes 589832 | tf_op jit(solution)/shard_map/ppermute | solution.py:391
  82.6 5.7 %collective-permute-start.20 = (f32[3,16,8,128]{3,2,1,0:T(8,128)S(1)}, f32[3,16,8,128]{3,2,1,0:T(8,128)S(1)}, u32[]{:S(2)}, u32[]{:S(2)}) collective-permute-start(f32[3,16,8,128]{3,2,1,0:T(8,128)S(1)} %collective-permute-done.17.refs_8_), channel_id=1, source_target_pairs={{0,8},{8,0},{1,9},{9,1},{2,10},{10,2},{3,11},{11,3},{4,12},{12,4},... | collective-permute-start | bytes 589832 | tf_op jit(solution)/shard_map/ppermute | solution.py:392
  88.3 26.7 %collective-permute-start.27 = (f32[3,16,32,128]{3,2,1,0:T(8,128)S(1)}, f32[3,16,32,128]{3,2,1,0:T(8,128)S(1)}, u32[]{:S(2)}, u32[]{:S(2)}) collective-permute-start(f32[3,16,32,128]{3,2,1,0:T(8,128)S(1)} %get-tuple-element.22), channel_id=1, source_target_pairs={{0,8},{8,16},{16,24},{24,32},{32,40},{40,48},{48,56},{56,64},{64,7... | collective-permute-start | bytes 2359304 | tf_op jit(solution)/shard_map/ppermute | solution.py:387
  97.5 4.8 %collective-permute-start.23 = (f32[2,12,8,128]{3,2,1,0:T(8,128)S(1)}, f32[2,12,8,128]{3,2,1,0:T(8,128)S(1)}, u32[]{:S(2)}, u32[]{:S(2)}) collective-permute-start(f32[2,12,8,128]{3,2,1,0:T(8,128)S(1)} %get-tuple-element.19), channel_id=1, source_target_pairs={{0,1},{1,0},{2,3},{3,2},{4,5},{5,4},{6,7},{7,6},{8,9},{9,8},{10,11... | collective-permute-start | bytes 294920 | tf_op jit(solution)/shard_map/ppermute | solution.py:398
  97.6 6.9 %collective-permute-start.24 = (f32[2,12,8,128]{3,2,1,0:T(8,128)S(1)}, f32[2,12,8,128]{3,2,1,0:T(8,128)S(1)}, u32[]{:S(2)}, u32[]{:S(2)}) collective-permute-start(f32[2,12,8,128]{3,2,1,0:T(8,128)S(1)} %get-tuple-element.20), channel_id=1, source_target_pairs={{0,2},{1,3},{2,0},{3,1},{4,6},{5,7},{6,4},{7,5},{8,10},{9,11},{10,... | collective-permute-start | bytes 294920 | tf_op jit(solution)/shard_map/ppermute | solution.py:398
  100.8 5.8 %collective-permute-start.25 = (f32[2,12,8,128]{3,2,1,0:T(8,128)S(1)}, f32[2,12,8,128]{3,2,1,0:T(8,128)S(1)}, u32[]{:S(2)}, u32[]{:S(2)}) collective-permute-start(f32[2,12,8,128]{3,2,1,0:T(8,128)S(1)} %get-tuple-element.21), channel_id=1, source_target_pairs={{0,3},{1,2},{2,1},{3,0},{4,7},{5,6},{6,5},{7,4},{8,11},{9,10},{10,... | collective-permute-start | bytes 294920 | tf_op jit(solution)/shard_map/ppermute | solution.py:398
  106.7 8.3 %collective-permute-start.26 = (f32[12,8,128]{2,1,0:T(8,128)S(1)}, f32[12,8,128]{2,1,0:T(8,128)S(1)}, u32[]{:S(2)}, u32[]{:S(2)}) collective-permute-start(f32[12,8,128]{2,1,0:T(8,128)S(1)} %get-tuple-element.25), channel_id=1, source_target_pairs={{0,4},{4,0},{1,5},{5,1},{2,6},{6,2},{3,7},{7,3},{8,12},{12,8},{9,1... | collective-permute-start | bytes 147464 | tf_op jit(solution)/shard_map/ppermute | solution.py:399
  (9 other events, 44.9 us)

commit v10 on v9

--- a/solution.py
+++ b/solution.py
@@ -16,10 +16,8 @@
 PARAMS = pltpu.CompilerParams(vmem_limit_bytes=40 * 1024 * 1024)
 
 STEPS = 8
-HALO = 16
-WIDE = 16 + 2 * HALO
 COST = 10**10
-UNROLL = (11, 20, 18, 16, 14, 12, 10, 16)
+EVEN_UNROLL = (14, 12, 20, 16, 12, 8, 4)
 
 
 def ring(size, by):
@@ -34,54 +32,111 @@
     return pltpu.roll(q, 1, 0)
 
 
-def fine_steps(bufs, out, strat, half_spin, weights):
+def fine_step(src, dst, strat, half_spin, weights, sign, first, count, unroll, place=None):
     here_weight, up_weight, down_weight = weights
+    quarter = 0.25 * sign
+    place = place or (lambda x: x)
 
     def vertical(q):
         above, below = pltpu.roll(q, 127, 1), pltpu.roll(q, 1, 1)
         return here_weight[...] * q + (up_weight[...] * above + down_weight[...] * below)
 
-    for step in range(STEPS):
-        src, dst = bufs[step % 2], bufs[(step + 1) % 2]
-        reach = 2 * (STEPS - 1 - step)
-        first = HALO - reach
-        count = 16 + 2 * reach
-        back = 0
-        if reach == 0:
-            dst, back = out, HALO
-        unroll = UNROLL[step]
-
-        def zonal(x, src=src):
-            u = src[0, x]
-            sides = src[0, x + 1] + src[0, x - 1] + (y_next(u) + y_prev(u))
-            push = src[2, x + 1] - src[2, x - 1]
-            return vertical(u) + (half_spin[...] * src[1, x] - 0.25 * push) + 0.05 * sides
-
-        def chunk(i, carry, src=src, dst=dst, first=first, unroll=unroll, zonal=zonal, back=back):
-            before, here = carry
-            for k in range(unroll):
-                x = first + unroll * i + k
-                after = zonal(x + 1)
-                dst[0, x - back] = here
-                v = src[1, x]
-                b = src[2, x]
-                b_next, b_prev = y_next(b), y_prev(b)
-                v_new = (
-                    vertical(v)
-                    - (half_spin[...] * here + 0.25 * (b_next - b_prev))
-                    + 0.05 * (src[1, x + 1] + src[1, x - 1] + (y_next(v) + y_prev(v)))
-                )
-                dst[1, x - back] = v_new
-                flow = (after - before) + (y_next(v_new) - y_prev(v_new))
-                dst[2, x - back] = (
-                    vertical(b)
-                    - strat[x] * flow
-                    + 0.05 * (src[2, x + 1] + src[2, x - 1] + (b_next + b_prev))
-                )
-                before, here = here, after
-            return before, here
-
-        lax.fori_loop(0, count // unroll, chunk, (zonal(first - 1), zonal(first)))
+    def zonal(x):
+        u = src[0, x]
+        sides = src[0, x + 1] + src[0, x - 1] + (y_next(u) + y_prev(u))
+        push = src[2, x + 1] - src[2, x - 1]
+        return vertical(u) + (half_spin[...] * src[1, x] - quarter * push) + 0.05 * sides
+
+    def chunk(i, carry):
+        before, here = carry
+        for k in range(unroll):
+            x = first + unroll * i + k
+            after = zonal(x + 1)
+            dst[0, place(x)] = here
+            v = src[1, x]
+            b = src[2, x]
+            b_next, b_prev = y_next(b), y_prev(b)
+            v_new = (
+                vertical(v)
+                - (half_spin[...] * here + 0.25 * (b_next - b_prev))
+                + 0.05 * (src[1, x + 1] + src[1, x - 1] + (y_next(v) + y_prev(v)))
+            )
+            dst[1, place(x)] = v_new
+            flow = sign * (after - before) + (y_next(v_new) - y_prev(v_new))
+            dst[2, place(x)] = (
+                vertical(b)
+                - strat[x] * flow
+                + 0.05 * (src[2, x + 1] + src[2, x - 1] + (b_next + b_prev))
+            )
+            before, here = here, after
+        return before, here
+
+    lax.fori_loop(0, count // unroll, chunk, (zonal(first - 1), zonal(first)))
+
+
+def fill_weights(weights):
+    lane = lax.broadcasted_iota(jnp.int32, (32, 128), 1)
+    up = jnp.where(lane < 127, 0.15, 0.0).astype(jnp.float32)
+    down = jnp.where(lane > 0, 0.15, 0.0).astype(jnp.float32)
+    weights[0] = 0.8 - up - down
+    weights[1] = up
+    weights[2] = down
+    return [weights.at[n] for n in range(3)]
+
+
+def turned_round(place):
+    reverse = place[1] % 2
+
+    def cell(i):
+        return i * (1 - 2 * reverse) + 15 * reverse
+
+    return cell, (1 - 2 * reverse).astype(jnp.float32)
+
+
+def even_side_kernel(
+    spin, blocks, place, own_strat, even_strat, start, even, edges, one, two, strat, weights
+):
+    del blocks
+    cell, sign = turned_round(place)
+    for x in range(16):
+        strat[cell(x)] = 0.25 * own_strat[x]
+        strat[16 + cell(x)] = 0.25 * even_strat[x]
+        for k in range(3):
+            one[k, cell(x)] = start[k, x]
+            one[k, 16 + cell(x)] = even[k, x]
+    listed = fill_weights(weights)
+    bufs = (one, two)
+    for level in range(STEPS):
+        src = bufs[level % 2]
+        for k in range(3):
+            for x in range(4):
+                edges[level, k, x] = src[k, 2 * level + x]
+        if level < STEPS - 1:
+            fine_step(
+                src, bufs[(level + 1) % 2], strat, spin, listed, sign,
+                2 * level + 2, 28 - 4 * level, EVEN_UNROLL[level],
+            )
+
+
+def odd_side_kernel(
+    spin, place, own_strat, odd_strat, hopped_strat, edges, odd, out, one, two, strat, weights
+):
+    cell, sign = turned_round(place)
+    for x in range(16):
+        strat[cell(x)] = 0.25 * (odd_strat[x] + hopped_strat[x])
+        strat[16 + cell(x)] = 0.25 * own_strat[x]
+        for k in range(3):
+            one[k, cell(x)] = odd[k, x]
+    listed = fill_weights(weights)
+    bufs = (one, two)
+    for level in range(STEPS):
+        src, dst, where = bufs[level % 2], bufs[(level + 1) % 2], None
+        if level == STEPS - 1:
+            dst, where = out, lambda x: cell(x - 16)
+        for k in range(3):
+            for x in range(4):
+                src[k, 16 + 2 * level + x] = edges[level, k, x]
+        fine_step(src, dst, strat, spin, listed, sign, 2 * level + 2, 16, 16, where)
 
 
 def block_means(rows, cells):
@@ -122,31 +177,6 @@
     def _():
         columns[near] = forwarded[0]
         columns[far] = forwarded[1]
-
-
-def fine_kernel(
-    spin, blocks, place, own_strat, even_strat, odd_strat, hopped_strat, start, odd, even,
-    out, one, two, strat, weights,
-):
-    del blocks
-    at_odd = 32 * (place[1] % 2)
-    at_even = 32 - at_odd
-    for k in range(3):
-        for x in range(16):
-            one[k, 16 + x] = start[k, x]
-            one[k, at_even + x] = even[k, x]
-            one[k, at_odd + x] = odd[k, x]
-    for x in range(16):
-        strat[16 + x] = 0.25 * own_strat[x]
-        strat[at_even + x] = 0.25 * even_strat[x]
-        strat[at_odd + x] = 0.25 * (odd_strat[x] + hopped_strat[x])
-    lane = lax.broadcasted_iota(jnp.int32, (32, 128), 1)
-    up = jnp.where(lane < 127, 0.15, 0.0).astype(jnp.float32)
-    down = jnp.where(lane > 0, 0.15, 0.0).astype(jnp.float32)
-    weights[0] = 0.8 - up - down
-    weights[1] = up
-    weights[2] = down
-    fine_steps((one, two), out, strat, spin, [weights.at[n] for n in range(3)])
 
 
 def split_kernel(place, fine, next_mean, strat_near, strat_far, detail, increment, strat, rows):
@@ -367,15 +397,20 @@
     wide = jnp.concatenate([top, turned - top], axis=2).astype(bf16)
     blocks = jnp.concatenate([wide, wide], axis=1)
 
+    levels = ((3, 32, 32, 128), f32)
+    (edges,) = call(
+        even_side_kernel,
+        [(STEPS, 3, 4, 32, 128)],
+        [levels, levels, ((32, 32, 128), f32), ((3, 32, 128), f32)],
+
+    )(half_spin, blocks, where[3:], stratification, even_strat, start, even)
+    levels = ((3, 36, 32, 128), f32)
     (fine,) = call(
-        fine_kernel,
+        odd_side_kernel,
         [(3, 16, 32, 128)],
-        [((3, WIDE, 32, 128), f32)] * 2 + [((WIDE, 32, 128), f32), ((3, 32, 128), f32)],
+        [levels, levels, ((32, 32, 128), f32), ((3, 32, 128), f32)],
         COST,
-    )(
-        half_spin, blocks, where[3:], stratification, even_strat, odd_strat, hopped_strat,
-        start, odd, even,
-    )
+    )(half_spin, where[3:], stratification, odd_strat, hopped_strat, edges, odd)
     detail, increment, strat = call(
         split_kernel, [(3, 16, 32, 128), (12, 8, 128), (32, 8, 128)], [((4, 32, 128), f32)]
     )(where[3:], fine, next_mean, near, far)

time: 117 us -> 113 us (0.966)
  waiting for transfers between devices: 24.2 us -> 21.4 us
  starting transfers between devices: 65 us -> 63.3 us
    ppermute x1, starting transfers between devices: 0.09 us -> 6.36 us  [per_device(): far = lax.ppermute(near, 'zh', ring(2, 1))]
    ppermute x2, starting transfers between devices: 8.03 us -> 4.41 us  [per_device(): lax.ppermute(part, 'zl', swapped(2))]
    ppermute x1, waiting for transfers between devices: 3.61 us -> 0.01 us  [per_device(): odd = lax.ppermute(start, SPACE, odd_edges)]
    ppermute x1, starting transfers between devices: 3.69 us -> 0.42 us  [per_device(): next_mean = lax.ppermute(mean, TM, ring(32, -1))]
    ppermute x1, starting transfers between devices: 22.3 us -> 19.8 us  [per_device(): forwarded = lax.ppermute(across, 'y', swapped(1))]
    ppermute x1, starting transfers between devices: 0.09 us -> 1.46 us  [per_device(): beside = lax.ppermute(increment, 'zl', swapped(1))]
    ppermute x1, starting transfers between devices: 0.01 us -> 1.28 us  [per_device(): even = lax.ppermute(start, SPACE, even_edges)]
    pallas_call x8 -> x9, Pallas kernels: 23.9 us -> 23.9 us  [run(): pl.pallas_call(kernel, out_shape=[jax.ShapeDtypeStruct(shape, f32) for sh...]
  transfers between devices with their start and end apart: 28 -> 28, of which waited for: 12 -> 12; matrix products, arithmetic and copies ran while one was open for 1% -> 1% of each run, Pallas kernels for 17% -> 18%
where the time goes in v10:
time: 113 us; the launch traced here: 112 us
  starting transfers between devices  63.3 us (56%)
  Pallas kernels  23.9 us (21%)
  waiting for transfers between devices  21.4 us (19%)
  local copies, waits for them, and re-layouts  2.43 us (2%)
    pallas_call x9, Pallas kernels, run(): pl.pallas_call(kernel, out_shape=[jax.ShapeDtypeStruct(shape, f32) for sh...  23.9 us
    ppermute x1, starting transfers between devices, per_device(): forwarded = lax.ppermute(across, 'y', swapped(1))  19.8 us
    ppermute x3, waiting for transfers between devices, per_device(): here = [lax.ppermute(part, 'x', ring(4, by)) for by in (1, 2, 3)]  7.72 us
    ppermute x1, starting transfers between devices, per_device(): odd = lax.ppermute(start, SPACE, odd_edges)  6.85 us
    ppermute x1, starting transfers between devices, per_device(): far = lax.ppermute(near, 'zh', ring(2, 1))  6.36 us
    ppermute x3, starting transfers between devices, per_device(): here = [lax.ppermute(part, 'x', ring(4, by)) for by in (1, 2, 3)]  5.73 us
    ppermute x1, starting transfers between devices, per_device(): sent = lax.ppermute(total[1], 'zh', ring(2, 1))  5.57 us
    ppermute x3, starting transfers between devices, per_device(): total = total + lax.ppermute(parts[by], 'y', swapped(by))  4.88 us
  transfers between devices with their start and end apart: 28, of which 12 were waited for; matrix products, arithmetic and copies ran while one was open for 1% of the time, Pallas kernels for 18%

profile of v10, /device:TPU:24, one launch (start us, length us, event | category | flops | bytes accessed | tf_op | source)
XLA Modules:
  0.0 111.6 jit_solution(2159838103996528167)
XLA Ops:
  2.0 6.8 %collective-permute-start.5 = (f32[3,16,32,128]{3,2,1,0:T(8,128)}, f32[3,16,32,128]{3,2,1,0:T(8,128)S(1)}, u32[]{:S(2)}, u32[]{:S(2)}) collective-permute-start(f32[3,16,32,128]{3,2,1,0:T(8,128)} %bitcast.15), channel_id=1, source_target_pairs={{0,7},{1,2},{2,1},{3,4},{4,3},{5,6},{6,5},{7,0},{8,15},{9,10},{10,... | collective-permute-start | bytes 2359304 | tf_op jit(solution)/shard_map/ppermute | solution.py:373
  10.2 1.4 %collective-permute-start.2 = (f32[16,32,128]{2,1,0:T(8,128)S(1)}, f32[16,32,128]{2,1,0:T(8,128)}, u32[]{:S(2)}, u32[]{:S(2)}) collective-permute-start(f32[16,32,128]{2,1,0:T(8,128)S(1)} %collective-permute-done.1.even_strat.even), channel_id=1, source_target_pairs={{1,5},{5,1},{2,6},{6,2},{9,13},{13,9},{10,14},{14,10},{17,21},{21,... | collective-permute-start | bytes 786440 | tf_op jit(solution)/shard_map/ppermute | solution.py:377
  13.8 1.4 %collective-permute-start.3 = (f32[16,32,128]{2,1,0:T(8,128)}, f32[16,32,128]{2,1,0:T(8,128)}, u32[]{:S(2)}, u32[]{:S(2)}) collective-permute-start(f32[16,32,128]{2,1,0:T(8,128)} %collective-permute-done.2), channel_id=1, source_target_pairs={{1,3},{5,7},{2,0},{6,4},{9,11},{13,15},{10,8},{14,12},{17,19},{21,... | collective-permute-start | bytes 786440 | tf_op jit(solution)/shard_map/ppermute | solution.py:378
  16.1 19.8 %collective-permute-start.8 = (f32[2,4,8,128]{3,2,1,0:T(8,128)S(1)}, f32[2,4,8,128]{3,2,1,0:T(8,128)S(1)}, u32[]{:S(2)}, u32[]{:S(2)}) collective-permute-start(f32[2,4,8,128]{3,2,1,0:T(8,128)S(1)} %collective-permute-done.7.across), channel_id=1, source_target_pairs={{0,1},{1,0},{2,3},{3,2},{4,5},{5,4},{6,7},{7,6},{8,9},{9,8},{10,11... | collective-permute-start | bytes 98312 | tf_op jit(solution)/shard_map/ppermute | solution.py:388
  35.9 1.8 %collective-permute-done.8.forwarded = f32[2,4,8,128]{3,2,1,0:T(8,128)S(1)} collective-permute-done((f32[2,4,8,128]{3,2,1,0:T(8,128)S(1)}, f32[2,4,8,128]{3,2,1,0:T(8,128)S(1)}, u32[]{:S(2)}, u32[]{:S(2)}) %collective-permute-start.8) | collective-permute-done | bytes 32800 | tf_op jit(solution)/shard_map/ppermute | solution.py:388
  38.8 6.4 %collective-permute-start.9 = (f32[4,4,8,128]{3,2,1,0:T(8,128)S(1)}, f32[4,4,8,128]{3,2,1,0:T(8,128)S(1)}, u32[]{:S(2)}, u32[]{:S(2)}) collective-permute-start(f32[4,4,8,128]{3,2,1,0:T(8,128)S(1)} %shard_map.50.strat_near), channel_id=1, source_target_pairs={{0,4},{4,0},{1,5},{5,1},{2,6},{6,2},{3,7},{7,3},{8,12},{12,8},{9,1... | collective-permute-start | bytes 196616 | tf_op jit(solution)/shard_map/ppermute | solution.py:392
  45.2 5.2 %shard_map.46.edges = f32[8,3,4,32,128]{4,3,2,1,0:T(8,128)S(1)} custom-call(f32[32,128]{1,0:T(8,128)S(1)} %broadcast_in_dim.7.spin, bf16[3,256,256]{2,1,0:T(8,128)(2,1)S(1)} %maximum_maximum_fusion.blocks, s32[2]{0:T(128)S(1)} %pad_add_fusion.place, f32[16,32,128]{2,1,0:T(8,128)S(1)} %copy-done, f32[16,32,128]{2,1,0:T(8,128)S(1)} %collective-permute-done.1.even_strat.even, ...), custom_call_target="tpu_custom_call" | custom-call | tf_op jit(solution)/shard_map/pallas_call | solution.py:348
  50.4 5.7 %shard_map.47.fine = f32[3,16,32,128]{3,2,1,0:T(8,128)S(1)} custom-call(f32[32,128]{1,0:T(8,128)S(1)} %broadcast_in_dim.7.spin, s32[2]{0:T(128)S(1)} %pad_add_fusion.place, f32[16,32,128]{2,1,0:T(8,128)S(1)} %copy-done, f32[16,32,128]{2,1,0:T(8,128)} %collective-permute-done.odd_strat, f32[16,32,128]{2,1,0:T(8,128)} %collective-permute-done.3.hopped_strat, ...), custom_call_target="tpu_custom_call" | custom-call | flops 10000000000 | bytes 39062500 | tf_op jit(solution)/shard_map/pallas_call | solution.py:348
  56.9 1.5 %collective-permute-start.10 = (f32[12,8,128]{2,1,0:T(8,128)S(1)}, f32[12,8,128]{2,1,0:T(8,128)S(1)}, u32[]{:S(2)}, u32[]{:S(2)}) collective-permute-start(f32[12,8,128]{2,1,0:T(8,128)S(1)} %get-tuple-element.15.refs_0_), channel_id=1, source_target_pairs={{0,16},{16,0},{32,48},{48,32},{1,17},{17,1},{33,49},{49,33},{2,18}... | collective-permute-start | bytes 147464 | tf_op jit(solution)/shard_map/ppermute | solution.py:418
  58.3 2.1 %collective-permute-start.11 = (f32[12,8,128]{2,1,0:T(8,128)S(1)}, f32[12,8,128]{2,1,0:T(8,128)S(1)}, u32[]{:S(2)}, u32[]{:S(2)}) collective-permute-start(f32[12,8,128]{2,1,0:T(8,128)S(1)} %get-tuple-element.15.refs_0_), channel_id=1, source_target_pairs={{0,32},{16,48},{32,0},{48,16},{1,33},{17,49},{33,1},{49,17},{2,34}... | collective-permute-start | bytes 147464 | tf_op jit(solution)/shard_map/ppermute | solution.py:420
  61.1 2.4 %collective-permute-start.12 = (f32[12,8,128]{2,1,0:T(8,128)S(1)}, f32[12,8,128]{2,1,0:T(8,128)S(1)}, u32[]{:S(2)}, u32[]{:S(2)}) collective-permute-start(f32[12,8,128]{2,1,0:T(8,128)S(1)} %collective-permute-done.10.refs_1_), channel_id=1, source_target_pairs={{0,32},{16,48},{32,0},{48,16},{1,33},{17,49},{33,1},{49,17},{2,34}... | collective-permute-start | bytes 147464 | tf_op jit(solution)/shard_map/ppermute | solution.py:420
  64.2 1.8 %collective-permute-done.12.refs_3_ = f32[12,8,128]{2,1,0:T(8,128)S(1)} collective-permute-done((f32[12,8,128]{2,1,0:T(8,128)S(1)}, f32[12,8,128]{2,1,0:T(8,128)S(1)}, u32[]{:S(2)}, u32[]{:S(2)}) %collective-permute-start.12) | collective-permute-done | bytes 49184 | tf_op jit(solution)/shard_map/ppermute | solution.py:420
  67.4 2.7 %shard_map.52 = (f32[3,32,8,128]{3,2,1,0:T(8,128)S(1)}, f32[3,16,8,128]{3,2,1,0:T(8,128)S(1)}) custom-call(s32[5]{0:T(128)S(1)} %stack.25.where, f32[8,128]{1,0:T(8,128)S(1)} %broadcast_in_dim.6.spin, bf16[3,256,256]{2,1,0:T(8,128)(2,1)S(1)} %maximum_maximum_fusion.blocks, f32[32,8,128]{2,1,0:T(8,128)S(1)} %get-tuple-element.14.strat, ...), custom_call_target="tpu_custom_call" | custom-call | tf_op jit(solution)/shard_map/pallas_call | solution.py:348
  70.0 1.6 %collective-permute-start.17 = (f32[3,16,8,128]{3,2,1,0:T(8,128)S(1)}, f32[3,16,8,128]{3,2,1,0:T(8,128)S(1)}, u32[]{:S(2)}, u32[]{:S(2)}) collective-permute-start(f32[3,16,8,128]{3,2,1,0:T(8,128)S(1)} %get-tuple-element.17), channel_id=1, source_target_pairs={{0,64},{64,128},{128,192},{192,0},{1,65},{65,129},{129,193},{193,1... | collective-permute-start | bytes 589832 | tf_op jit(solution)/shard_map/ppermute | solution.py:426
  71.6 2.7 %collective-permute-start.18 = (f32[3,16,8,128]{3,2,1,0:T(8,128)S(1)}, f32[3,16,8,128]{3,2,1,0:T(8,128)S(1)}, u32[]{:S(2)}, u32[]{:S(2)}) collective-permute-start(f32[3,16,8,128]{3,2,1,0:T(8,128)S(1)} %get-tuple-element.17), channel_id=1, source_target_pairs={{0,128},{64,192},{128,0},{192,64},{1,129},{65,193},{129,1},{193,65... | collective-permute-start | bytes 589832 | tf_op jit(solution)/shard_map/ppermute | solution.py:426
  74.3 1.4 %collective-permute-start.19 = (f32[3,16,8,128]{3,2,1,0:T(8,128)S(1)}, f32[3,16,8,128]{3,2,1,0:T(8,128)S(1)}, u32[]{:S(2)}, u32[]{:S(2)}) collective-permute-start(f32[3,16,8,128]{3,2,1,0:T(8,128)S(1)} %get-tuple-element.17), channel_id=1, source_target_pairs={{0,192},{64,0},{128,64},{192,128},{1,193},{65,1},{129,65},{193,129... | collective-permute-start | bytes 589832 | tf_op jit(solution)/shard_map/ppermute | solution.py:426
  75.8 2.5 %collective-permute-done.17.refs_8_ = f32[3,16,8,128]{3,2,1,0:T(8,128)S(1)} collective-permute-done((f32[3,16,8,128]{3,2,1,0:T(8,128)S(1)}, f32[3,16,8,128]{3,2,1,0:T(8,128)S(1)}, u32[]{:S(2)}, u32[]{:S(2)}) %collective-permute-start.17) | collective-permute-done | bytes 196640 | tf_op jit(solution)/shard_map/ppermute | solution.py:426
  78.3 5.2 %collective-permute-done.18.refs_9_ = f32[3,16,8,128]{3,2,1,0:T(8,128)S(1)} collective-permute-done((f32[3,16,8,128]{3,2,1,0:T(8,128)S(1)}, f32[3,16,8,128]{3,2,1,0:T(8,128)S(1)}, u32[]{:S(2)}, u32[]{:S(2)}) %collective-permute-start.18) | collective-permute-done | bytes 196640 | tf_op jit(solution)/shard_map/ppermute | solution.py:426
  85.2 8.0 %shard_map.53 = (f32[2,12,8,128]{3,2,1,0:T(8,128)S(1)}, f32[2,12,8,128]{3,2,1,0:T(8,128)S(1)}, f32[2,12,8,128]{3,2,1,0:T(8,128)S(1)}, f32[2,12,8,128]{3,2,1,0:T(8,128)S(1)}) custom-call(s32[5]{0:T(128)S(1)} %stack.25.where, f32[8,128]{1,0:T(8,128)S(1)} %broadcast_in_dim.6.spin, bf16[3,256,256]{2,1,0:T(8,128)(2,1)S(1)} %maximum_maximum_fusion.blocks, ...), custom_call_target="tpu_custom_call" | custom-call | tf_op jit(solution)/shard_map/pallas_call | solution.py:348
  93.2 2.1 %collective-permute-start.23 = (f32[2,12,8,128]{3,2,1,0:T(8,128)S(1)}, f32[2,12,8,128]{3,2,1,0:T(8,128)S(1)}, u32[]{:S(2)}, u32[]{:S(2)}) collective-permute-start(f32[2,12,8,128]{3,2,1,0:T(8,128)S(1)} %get-tuple-element.19), channel_id=1, source_target_pairs={{0,1},{1,0},{2,3},{3,2},{4,5},{5,4},{6,7},{7,6},{8,9},{9,8},{10,11... | collective-permute-start | bytes 294920 | tf_op jit(solution)/shard_map/ppermute | solution.py:433
  95.9 2.2 %collective-permute-start.25 = (f32[2,12,8,128]{3,2,1,0:T(8,128)S(1)}, f32[2,12,8,128]{3,2,1,0:T(8,128)S(1)}, u32[]{:S(2)}, u32[]{:S(2)}) collective-permute-start(f32[2,12,8,128]{3,2,1,0:T(8,128)S(1)} %get-tuple-element.21), channel_id=1, source_target_pairs={{0,3},{1,2},{2,1},{3,0},{4,7},{5,6},{6,5},{7,4},{8,11},{9,10},{10,... | collective-permute-start | bytes 294920 | tf_op jit(solution)/shard_map/ppermute | solution.py:433
  98.1 3.4 %collective-permute-done.24 = f32[2,12,8,128]{3,2,1,0:T(8,128)S(1)} collective-permute-done((f32[2,12,8,128]{3,2,1,0:T(8,128)S(1)}, f32[2,12,8,128]{3,2,1,0:T(8,128)S(1)}, u32[]{:S(2)}, u32[]{:S(2)}) %collective-permute-start.24) | collective-permute-done | bytes 98336 | tf_op jit(solution)/shard_map/ppermute | solution.py:433
  102.5 5.6 %collective-permute-start.26 = (f32[12,8,128]{2,1,0:T(8,128)S(1)}, f32[12,8,128]{2,1,0:T(8,128)S(1)}, u32[]{:S(2)}, u32[]{:S(2)}) collective-permute-start(f32[12,8,128]{2,1,0:T(8,128)S(1)} %get-tuple-element.25), channel_id=1, source_target_pairs={{0,4},{4,0},{1,5},{5,1},{2,6},{6,2},{3,7},{7,3},{8,12},{12,8},{9,1... | collective-permute-start | bytes 147464 | tf_op jit(solution)/shard_map/ppermute | solution.py:434
  108.1 2.5 %collective-permute-done.26.sent = f32[12,8,128]{2,1,0:T(8,128)S(1)} collective-permute-done((f32[12,8,128]{2,1,0:T(8,128)S(1)}, f32[12,8,128]{2,1,0:T(8,128)S(1)}, u32[]{:S(2)}, u32[]{:S(2)}) %collective-permute-start.26) | collective-permute-done | bytes 49184 | tf_op jit(solution)/shard_map/ppermute | solution.py:434
  (63 shorter events, 15.2 us)
Async XLA Ops:
  0.0 10.2 %collective-permute-start.1 = (f32[16,32,128]{2,1,0:T(8,128)}, f32[16,32,128]{2,1,0:T(8,128)S(1)}, u32[]{:S(2)}, u32[]{:S(2)}) collective-permute-start(f32[16,32,128]{2,1,0:T(8,128)} %own.1), channel_id=1, source_target_pairs={{0,1},{1,0},{2,3},{3,2},{4,5},{5,4},{6,7},{7,6},{8,9},{9,8},{10,11... | collective-permute-start | bytes 786440 | tf_op jit(solution)/shard_map/ppermute | solution.py:375
  0.7 38.0 %collective-permute-start.4 = (f32[3,16,32,128]{3,2,1,0:T(8,128)}, f32[3,16,32,128]{3,2,1,0:T(8,128)S(1)}, u32[]{:S(2)}, u32[]{:S(2)}) collective-permute-start(f32[3,16,32,128]{3,2,1,0:T(8,128)} %bitcast.14), channel_id=1, source_target_pairs={{0,1},{1,0},{2,3},{3,2},{4,5},{5,4},{6,7},{7,6},{8,9},{9,8},{10,11... | collective-permute-start | bytes 2359304 | tf_op jit(solution)/shard_map/ppermute | solution.py:374
  2.0 48.4 %collective-permute-start.5 = (f32[3,16,32,128]{3,2,1,0:T(8,128)}, f32[3,16,32,128]{3,2,1,0:T(8,128)S(1)}, u32[]{:S(2)}, u32[]{:S(2)}) collective-permute-start(f32[3,16,32,128]{3,2,1,0:T(8,128)} %bitcast.15), channel_id=1, source_target_pairs={{0,7},{1,2},{2,1},{3,4},{4,3},{5,6},{6,5},{7,0},{8,15},{9,10},{10,... | collective-permute-start | bytes 2359304 | tf_op jit(solution)/shard_map/ppermute | solution.py:373
  8.9 41.5 %collective-permute-start = (f32[16,32,128]{2,1,0:T(8,128)}, f32[16,32,128]{2,1,0:T(8,128)}, u32[]{:S(2)}, u32[]{:S(2)}) collective-permute-start(f32[16,32,128]{2,1,0:T(8,128)} %own.1), channel_id=1, source_target_pairs={{1,2},{2,1},{5,6},{6,5},{9,10},{10,9},{13,14},{14,13},{17,18},{18,... | collective-permute-start | bytes 786440 | tf_op jit(solution)/shard_map/ppermute | solution.py:376
  10.2 3.6 %collective-permute-start.2 = (f32[16,32,128]{2,1,0:T(8,128)S(1)}, f32[16,32,128]{2,1,0:T(8,128)}, u32[]{:S(2)}, u32[]{:S(2)}) collective-permute-start(f32[16,32,128]{2,1,0:T(8,128)S(1)} %collective-permute-done.1.even_strat.even), channel_id=1, source_target_pairs={{1,5},{5,1},{2,6},{6,2},{9,13},{13,9},{10,14},{14,10},{17,21},{21,... | collective-permute-start | bytes 786440 | tf_op jit(solution)/shard_map/ppermute | solution.py:377
  13.8 36.6 %collective-permute-start.3 = (f32[16,32,128]{2,1,0:T(8,128)}, f32[16,32,128]{2,1,0:T(8,128)}, u32[]{:S(2)}, u32[]{:S(2)}) collective-permute-start(f32[16,32,128]{2,1,0:T(8,128)} %collective-permute-done.2), channel_id=1, source_target_pairs={{1,3},{5,7},{2,0},{6,4},{9,11},{13,15},{10,8},{14,12},{17,19},{21,... | collective-permute-start | bytes 786440 | tf_op jit(solution)/shard_map/ppermute | solution.py:378
  16.1 21.7 %collective-permute-start.8 = (f32[2,4,8,128]{3,2,1,0:T(8,128)S(1)}, f32[2,4,8,128]{3,2,1,0:T(8,128)S(1)}, u32[]{:S(2)}, u32[]{:S(2)}) collective-permute-start(f32[2,4,8,128]{3,2,1,0:T(8,128)S(1)} %collective-permute-done.7.across), channel_id=1, source_target_pairs={{0,1},{1,0},{2,3},{3,2},{4,5},{5,4},{6,7},{7,6},{8,9},{9,8},{10,11... | collective-permute-start | bytes 98312 | tf_op jit(solution)/shard_map/ppermute | solution.py:388
  37.8 18.4 %collective-permute-start.6 = (f32[3,4,8,128]{3,2,1,0:T(8,128)S(1)}, f32[3,4,8,128]{3,2,1,0:T(8,128)S(1)}, u32[]{:S(2)}, u32[]{:S(2)}) collective-permute-start(f32[3,4,8,128]{3,2,1,0:T(8,128)S(1)} %shard_map.48.mean), channel_id=1, source_target_pairs={{0,248},{8,0},{16,8},{24,16},{32,24},{40,32},{48,40},{56,48},{64,5... | collective-permute-start | bytes 147464 | tf_op jit(solution)/shard_map/ppermute | solution.py:380
  38.8 17.4 %collective-permute-start.9 = (f32[4,4,8,128]{3,2,1,0:T(8,128)S(1)}, f32[4,4,8,128]{3,2,1,0:T(8,128)S(1)}, u32[]{:S(2)}, u32[]{:S(2)}) collective-permute-start(f32[4,4,8,128]{3,2,1,0:T(8,128)S(1)} %shard_map.50.strat_near), channel_id=1, source_target_pairs={{0,4},{4,0},{1,5},{5,1},{2,6},{6,2},{3,7},{7,3},{8,12},{12,8},{9,1... | collective-permute-start | bytes 196616 | tf_op jit(solution)/shard_map/ppermute | solution.py:392
  56.9 4.2 %collective-permute-start.10 = (f32[12,8,128]{2,1,0:T(8,128)S(1)}, f32[12,8,128]{2,1,0:T(8,128)S(1)}, u32[]{:S(2)}, u32[]{:S(2)}) collective-permute-start(f32[12,8,128]{2,1,0:T(8,128)S(1)} %get-tuple-element.15.refs_0_), channel_id=1, source_target_pairs={{0,16},{16,0},{32,48},{48,32},{1,17},{17,1},{33,49},{49,33},{2,18}... | collective-permute-start | bytes 147464 | tf_op jit(solution)/shard_map/ppermute | solution.py:418
  58.3 5.9 %collective-permute-start.11 = (f32[12,8,128]{2,1,0:T(8,128)S(1)}, f32[12,8,128]{2,1,0:T(8,128)S(1)}, u32[]{:S(2)}, u32[]{:S(2)}) collective-permute-start(f32[12,8,128]{2,1,0:T(8,128)S(1)} %get-tuple-element.15.refs_0_), channel_id=1, source_target_pairs={{0,32},{16,48},{32,0},{48,16},{1,33},{17,49},{33,1},{49,17},{2,34}... | collective-permute-start | bytes 147464 | tf_op jit(solution)/shard_map/ppermute | solution.py:420
  61.1 5.0 %collective-permute-start.12 = (f32[12,8,128]{2,1,0:T(8,128)S(1)}, f32[12,8,128]{2,1,0:T(8,128)S(1)}, u32[]{:S(2)}, u32[]{:S(2)}) collective-permute-start(f32[12,8,128]{2,1,0:T(8,128)S(1)} %collective-permute-done.10.refs_1_), channel_id=1, source_target_pairs={{0,32},{16,48},{32,0},{48,16},{1,33},{17,49},{33,1},{49,17},{2,34}... | collective-permute-start | bytes 147464 | tf_op jit(solution)/shard_map/ppermute | solution.py:420
  63.4 2.9 %collective-permute-start.13 = (f32[12,8,128]{2,1,0:T(8,128)S(1)}, f32[12,8,128]{2,1,0:T(8,128)S(1)}, u32[]{:S(2)}, u32[]{:S(2)}) collective-permute-start(f32[12,8,128]{2,1,0:T(8,128)S(1)} %get-tuple-element.15.refs_0_), channel_id=1, source_target_pairs={{0,8},{8,0},{1,9},{9,1},{2,10},{10,2},{3,11},{11,3},{4,12},{12,4},... | collective-permute-start | bytes 147464 | tf_op jit(solution)/shard_map/ppermute | solution.py:421
  63.4 2.9 %collective-permute-start.14 = (f32[12,8,128]{2,1,0:T(8,128)S(1)}, f32[12,8,128]{2,1,0:T(8,128)S(1)}, u32[]{:S(2)}, u32[]{:S(2)}) collective-permute-start(f32[12,8,128]{2,1,0:T(8,128)S(1)} %collective-permute-done.10.refs_1_), channel_id=1, source_target_pairs={{0,8},{8,0},{1,9},{9,1},{2,10},{10,2},{3,11},{11,3},{4,12},{12,4},... | collective-permute-start | bytes 147464 | tf_op jit(solution)/shard_map/ppermute | solution.py:421
  64.2 2.1 %collective-permute-start.15 = (f32[12,8,128]{2,1,0:T(8,128)S(1)}, f32[12,8,128]{2,1,0:T(8,128)S(1)}, u32[]{:S(2)}, u32[]{:S(2)}) collective-permute-start(f32[12,8,128]{2,1,0:T(8,128)S(1)} %collective-permute-done.11.refs_2_), channel_id=1, source_target_pairs={{0,8},{8,0},{1,9},{9,1},{2,10},{10,2},{3,11},{11,3},{4,12},{12,4},... | collective-permute-start | bytes 147464 | tf_op jit(solution)/shard_map/ppermute | solution.py:421
  70.0 8.3 %collective-permute-start.17 = (f32[3,16,8,128]{3,2,1,0:T(8,128)S(1)}, f32[3,16,8,128]{3,2,1,0:T(8,128)S(1)}, u32[]{:S(2)}, u32[]{:S(2)}) collective-permute-start(f32[3,16,8,128]{3,2,1,0:T(8,128)S(1)} %get-tuple-element.17), channel_id=1, source_target_pairs={{0,64},{64,128},{128,192},{192,0},{1,65},{65,129},{129,193},{193,1... | collective-permute-start | bytes 589832 | tf_op jit(solution)/shard_map/ppermute | solution.py:426
  71.6 11.9 %collective-permute-start.18 = (f32[3,16,8,128]{3,2,1,0:T(8,128)S(1)}, f32[3,16,8,128]{3,2,1,0:T(8,128)S(1)}, u32[]{:S(2)}, u32[]{:S(2)}) collective-permute-start(f32[3,16,8,128]{3,2,1,0:T(8,128)S(1)} %get-tuple-element.17), channel_id=1, source_target_pairs={{0,128},{64,192},{128,0},{192,64},{1,129},{65,193},{129,1},{193,65... | collective-permute-start | bytes 589832 | tf_op jit(solution)/shard_map/ppermute | solution.py:426
  74.3 9.2 %collective-permute-start.19 = (f32[3,16,8,128]{3,2,1,0:T(8,128)S(1)}, f32[3,16,8,128]{3,2,1,0:T(8,128)S(1)}, u32[]{:S(2)}, u32[]{:S(2)}) collective-permute-start(f32[3,16,8,128]{3,2,1,0:T(8,128)S(1)} %get-tuple-element.17), channel_id=1, source_target_pairs={{0,192},{64,0},{128,64},{192,128},{1,193},{65,1},{129,65},{193,129... | collective-permute-start | bytes 589832 | tf_op jit(solution)/shard_map/ppermute | solution.py:426
  78.3 5.7 %collective-permute-start.20 = (f32[3,16,8,128]{3,2,1,0:T(8,128)S(1)}, f32[3,16,8,128]{3,2,1,0:T(8,128)S(1)}, u32[]{:S(2)}, u32[]{:S(2)}) collective-permute-start(f32[3,16,8,128]{3,2,1,0:T(8,128)S(1)} %collective-permute-done.17.refs_8_), channel_id=1, source_target_pairs={{0,8},{8,0},{1,9},{9,1},{2,10},{10,2},{3,11},{11,3},{4,12},{12,4},... | collective-permute-start | bytes 589832 | tf_op jit(solution)/shard_map/ppermute | solution.py:427
  84.0 26.6 %collective-permute-start.27 = (f32[3,16,32,128]{3,2,1,0:T(8,128)S(1)}, f32[3,16,32,128]{3,2,1,0:T(8,128)S(1)}, u32[]{:S(2)}, u32[]{:S(2)}) collective-permute-start(f32[3,16,32,128]{3,2,1,0:T(8,128)S(1)} %get-tuple-element.22), channel_id=1, source_target_pairs={{0,8},{8,16},{16,24},{24,32},{32,40},{40,48},{48,56},{56,64},{64,7... | collective-permute-start | bytes 2359304 | tf_op jit(solution)/shard_map/ppermute | solution.py:422
  93.2 4.9 %collective-permute-start.23 = (f32[2,12,8,128]{3,2,1,0:T(8,128)S(1)}, f32[2,12,8,128]{3,2,1,0:T(8,128)S(1)}, u32[]{:S(2)}, u32[]{:S(2)}) collective-permute-start(f32[2,12,8,128]{3,2,1,0:T(8,128)S(1)} %get-tuple-element.19), channel_id=1, source_target_pairs={{0,1},{1,0},{2,3},{3,2},{4,5},{5,4},{6,7},{7,6},{8,9},{9,8},{10,11... | collective-permute-start | bytes 294920 | tf_op jit(solution)/shard_map/ppermute | solution.py:433
  95.3 6.2 %collective-permute-start.24 = (f32[2,12,8,128]{3,2,1,0:T(8,128)S(1)}, f32[2,12,8,128]{3,2,1,0:T(8,128)S(1)}, u32[]{:S(2)}, u32[]{:S(2)}) collective-permute-start(f32[2,12,8,128]{3,2,1,0:T(8,128)S(1)} %get-tuple-element.20), channel_id=1, source_target_pairs={{0,2},{1,3},{2,0},{3,1},{4,6},{5,7},{6,4},{7,5},{8,10},{9,11},{10,... | collective-permute-start | bytes 294920 | tf_op jit(solution)/shard_map/ppermute | solution.py:433
  95.9 6.6 %collective-permute-start.25 = (f32[2,12,8,128]{3,2,1,0:T(8,128)S(1)}, f32[2,12,8,128]{3,2,1,0:T(8,128)S(1)}, u32[]{:S(2)}, u32[]{:S(2)}) collective-permute-start(f32[2,12,8,128]{3,2,1,0:T(8,128)S(1)} %get-tuple-element.21), channel_id=1, source_target_pairs={{0,3},{1,2},{2,1},{3,0},{4,7},{5,6},{6,5},{7,4},{8,11},{9,10},{10,... | collective-permute-start | bytes 294920 | tf_op jit(solution)/shard_map/ppermute | solution.py:433
  102.5 8.1 %collective-permute-start.26 = (f32[12,8,128]{2,1,0:T(8,128)S(1)}, f32[12,8,128]{2,1,0:T(8,128)S(1)}, u32[]{:S(2)}, u32[]{:S(2)}) collective-permute-start(f32[12,8,128]{2,1,0:T(8,128)S(1)} %get-tuple-element.25), channel_id=1, source_target_pairs={{0,4},{4,0},{1,5},{5,1},{2,6},{6,2},{3,7},{7,3},{8,12},{12,8},{9,1... | collective-permute-start | bytes 147464 | tf_op jit(solution)/shard_map/ppermute | solution.py:434
  (9 other events, 67.8 us)

commit v11 on v10

--- a/solution.py
+++ b/solution.py
@@ -283,34 +283,52 @@
         part[k] = state[k, pl.ds(16 * core, 16)]
 
 
-def chain_kernel(where, spin, blocks, strat, end, *refs):
-    mine, other, here, there = refs[:4], refs[4:8], refs[8:11], refs[11:14]
-    parts, (ends, state, halves, increments) = refs[14:18], refs[18:]
+def add_end(state, core, here, there):
+    for k in range(3):
+        for x in range(16):
+            near, far = 16 * core + x, 16 * (1 - core) + x
+            state[k, near] = state[k, near] + here[k, x]
+            state[k, far] = state[k, far] + there[k, x]
+
+
+def early_kernel(where, spin, blocks, strat, end, here, there, state, halves):
+    run, core, row = where[0], where[1], where[2]
+    closing = (row == 0) & (2 * run + core == 0)
+    clear(state)
+
+    @pl.when(closing)
+    def _():
+        for k in range(3):
+            for x in range(32):
+                state[k, x] = end[k, x]
+        steps(8, state, halves, blocks, spin, strat)
+
+    @pl.when(closing | (row == 3))
+    def _():
+        add_end(state, core, here, there)
+        steps(8, state, halves, blocks, spin, strat)
+
+
+def chain_kernel(where, spin, blocks, strat, early, *refs):
+    mine, other, (here_two, there_two, here_one, there_one) = refs[:4], refs[4:8], refs[8:12]
+    parts, (state, halves, increments) = refs[12:16], refs[16:]
     run, core, row, zh, y = where[0], where[1], where[2], where[3], where[4]
     turns = 2 * run + core
-    groups = jnp.where((row == 0) & (turns == 0), 4, row)
+    closing = (row == 0) & (turns == 0)
     table(where, increments, mine, other)
     for k in range(3):
         for x in range(32):
-            ends[row, k, x] = end[k, x]
-    for j in range(3):
-        plane = (row + 3 - j) % 4
-        for k in range(3):
-            ends[plane, k, pl.ds(16 * core, 16)] = here[j][k]
-            ends[plane, k, pl.ds(16 * (1 - core), 16)] = there[j][k]
-    clear(state)
-
-    def group(g, carry):
-        @pl.when(g > 0)
-        def _():
-            steps(8, state, halves, blocks, spin, strat)
-
-        for k in range(3):
-            for x in range(32):
-                state[k, x] = state[k, x] + ends[g, k, x]
-        return carry
-
-    lax.fori_loop(0, groups, group, 0)
+            state[k, x] = early[k, x]
+
+    @pl.when(closing | (row >= 2))
+    def _():
+        add_end(state, core, here_two, there_two)
+        steps(8, state, halves, blocks, spin, strat)
+
+    @pl.when(closing | (row >= 1))
+    def _():
+        add_end(state, core, here_one, there_one)
+
     block = 4 * zh + y
 
     def turn(i, carry):
@@ -371,9 +389,12 @@
     even_edges = [(s, s ^ 1) for s in range(8)]
     odd_edges = [(s, (s + 1 if s % 2 else s - 1) % 8) for s in range(8)]
     odd = lax.ppermute(start, SPACE, odd_edges)
-    even = lax.ppermute(start, SPACE, even_edges)
     even_strat = lax.ppermute(stratification, SPACE, even_edges)
-    odd_strat = lax.ppermute(stratification, SPACE, [(1, 2), (2, 1), (5, 6), (6, 5)])
+    even_strat, later, strat_later = lax.optimization_barrier(
+        (even_strat, start, stratification)
+    )
+    even = lax.ppermute(later, SPACE, even_edges)
+    odd_strat = lax.ppermute(strat_later, SPACE, [(1, 2), (2, 1), (5, 6), (6, 5)])
     relayed = lax.ppermute(even_strat, SPACE, [(1, 5), (5, 1), (2, 6), (6, 2)])
     hopped_strat = lax.ppermute(relayed, SPACE, [(1, 3), (5, 7), (2, 0), (6, 4)])
     (mean,) = call(means_kernel, [(3, 4, 8, 128)], [((2, 32, 128), f32)], COST)(start)
@@ -402,7 +423,6 @@
         even_side_kernel,
         [(STEPS, 3, 4, 32, 128)],
         [levels, levels, ((32, 32, 128), f32), ((3, 32, 128), f32)],
-
     )(half_spin, blocks, where[3:], stratification, even_strat, start, even)
     levels = ((3, 36, 32, 128), f32)
     (fine,) = call(
@@ -423,11 +443,14 @@
     pair = [state[0], (3, 16, 8, 128)]
     common = (where, coarse_spin, blocks, strat)
     end, part = call(plane_kernel, pair, [halves, increments])(*common, *mine, *other)
-    here = [lax.ppermute(part, "x", ring(4, by)) for by in (1, 2, 3)]
-    there = [lax.ppermute(part, "c", ring(2, 1)) for part in here]
-    parts = call(
-        chain_kernel, [(2, 12, 8, 128)] * 4, [((4, 3, 32, 8, 128), f32), state, halves, increments]
-    )(*common, end, *mine, *other, *here, *there)
+    here = [lax.ppermute(part, "x", ring(4, by)) for by in (3, 2, 1)]
+    there = [lax.ppermute(here[0], "c", ring(2, 1))]
+    there[0], here[1], here[2] = lax.optimization_barrier((there[0], here[1], here[2]))
+    (early,) = call(early_kernel, [state[0]], [halves])(*common, end, here[0], there[0])
+    there += [lax.ppermute(part, "c", ring(2, 1)) for part in here[1:]]
+    parts = call(chain_kernel, [(2, 12, 8, 128)] * 4, [state, halves, increments])(
+        *common, early, *mine, *other, here[1], there[1], here[2], there[2]
+    )
     total = parts[0]
     for by in (1, 2, 3):
         total = total + lax.ppermute(parts[by], "y", swapped(by))

time: 113 us -> 117 us (1.035)
  waiting for transfers between devices: 21.4 us -> 29.4 us
  starting transfers between devices: 63.3 us -> 59.3 us
    ppermute x1, starting transfers between devices: 19.8 us -> 8.56 us  [per_device(): forwarded = lax.ppermute(across, 'y', swapped(1))]
    ppermute x8, starting transfers between devices: 8.88 us -> 15.5 us  [the longest x1 8.4 us: per_device(): even = lax.ppermute(later, SPACE, even_edges)]
    ppermute x1, waiting for transfers between devices: 1.82 us -> 8.43 us  [per_device(): forwarded = lax.ppermute(across, 'y', swapped(1))]
    ppermute x2, starting transfers between devices: 4.41 us -> 9.11 us  [per_device(): lax.ppermute(part, 'zl', swapped(2))]
    ppermute x1, starting transfers between devices: 6.36 us -> 2.81 us  [per_device(): far = lax.ppermute(near, 'zh', ring(2, 1))]
    ppermute x1, starting transfers between devices: 0.42 us -> 2.52 us  [per_device(): next_mean = lax.ppermute(mean, TM, ring(32, -1))]
    ppermute x1, starting transfers between devices: 5.57 us -> 3.57 us  [per_device(): sent = lax.ppermute(total[1], 'zh', ring(2, 1))]
    ppermute x1, waiting for transfers between devices: 2.52 us -> 4.51 us  [per_device(): sent = lax.ppermute(total[1], 'zh', ring(2, 1))]
  transfers between devices with their start and end apart: 28 -> 28, of which waited for: 12 -> 8; matrix products, arithmetic and copies ran while one was open for 1% -> 1% of each run, Pallas kernels for 18% -> 17%
where the time goes in v11:
time: 117 us
  starting transfers between devices  59.3 us (51%)
  waiting for transfers between devices  29.4 us (25%)
  Pallas kernels  24.9 us (21%)
  local copies, waits for them, and re-layouts  2.47 us (2%)
    pallas_call x10, Pallas kernels, run(): pl.pallas_call(kernel, out_shape=[jax.ShapeDtypeStruct(shape, f32) for sh...  24.9 us
    ppermute x3, waiting for transfers between devices, per_device(): here = [lax.ppermute(part, 'x', ring(4, by)) for by in (3, 2, 1)]  9.82 us
    ppermute x2, starting transfers between devices, per_device(): lax.ppermute(part, 'zl', swapped(2))  9.11 us
    ppermute x1, starting transfers between devices, per_device(): forwarded = lax.ppermute(across, 'y', swapped(1))  8.56 us
    ppermute x1, waiting for transfers between devices, per_device(): forwarded = lax.ppermute(across, 'y', swapped(1))  8.43 us
    ppermute x1, starting transfers between devices, per_device(): even = lax.ppermute(later, SPACE, even_edges)  8.4 us
    ppermute x1, starting transfers between devices, per_device(): odd = lax.ppermute(start, SPACE, odd_edges)  7.68 us
    ppermute x3, starting transfers between devices, per_device(): here = [lax.ppermute(part, 'x', ring(4, by)) for by in (3, 2, 1)]  5.13 us
  transfers between devices with their start and end apart: 28, of which 8 were waited for; matrix products, arithmetic and copies ran while one was open for 1% of the time, Pallas kernels for 17%

profile of v11, /device:TPU:24, one launch (start us, length us, event | category | flops | bytes accessed | tf_op | source)
XLA Modules:
  0.0 116.6 jit_solution(821764322328959725)
XLA Ops:
  0.7 7.7 %collective-permute-start.5 = (f32[3,16,32,128]{3,2,1,0:T(8,128)}, f32[3,16,32,128]{3,2,1,0:T(8,128)S(1)}, u32[]{:S(2)}, u32[]{:S(2)}) collective-permute-start(f32[3,16,32,128]{3,2,1,0:T(8,128)} %bitcast.14), channel_id=1, source_target_pairs={{0,7},{1,2},{2,1},{3,4},{4,3},{5,6},{6,5},{7,0},{8,15},{9,10},{10,... | collective-permute-start | bytes 2359304 | tf_op jit(solution)/shard_map/ppermute | solution.py:391
  9.8 8.4 %collective-permute-start.4 = (f32[3,16,32,128]{3,2,1,0:T(8,128)}, f32[3,16,32,128]{3,2,1,0:T(8,128)S(1)}, u32[]{:S(2)}, u32[]{:S(2)}) collective-permute-start(f32[3,16,32,128]{3,2,1,0:T(8,128)} %bitcast.15), channel_id=1, source_target_pairs={{0,1},{1,0},{2,3},{3,2},{4,5},{5,4},{6,7},{7,6},{8,9},{9,8},{10,11... | collective-permute-start | bytes 2359304 | tf_op jit(solution)/shard_map/ppermute | solution.py:396
  24.0 8.6 %collective-permute-start.8 = (f32[2,4,8,128]{3,2,1,0:T(8,128)S(1)}, f32[2,4,8,128]{3,2,1,0:T(8,128)S(1)}, u32[]{:S(2)}, u32[]{:S(2)}) collective-permute-start(f32[2,4,8,128]{3,2,1,0:T(8,128)S(1)} %collective-permute-done.7.across), channel_id=1, source_target_pairs={{0,1},{1,0},{2,3},{3,2},{4,5},{5,4},{6,7},{7,6},{8,9},{9,8},{10,11... | collective-permute-start | bytes 98312 | tf_op jit(solution)/shard_map/ppermute | solution.py:409
  32.7 8.4 %collective-permute-done.8.forwarded = f32[2,4,8,128]{3,2,1,0:T(8,128)S(1)} collective-permute-done((f32[2,4,8,128]{3,2,1,0:T(8,128)S(1)}, f32[2,4,8,128]{3,2,1,0:T(8,128)S(1)}, u32[]{:S(2)}, u32[]{:S(2)}) %collective-permute-start.8) | collective-permute-done | bytes 32800 | tf_op jit(solution)/shard_map/ppermute | solution.py:409
  41.1 2.5 %collective-permute-start.6 = (f32[3,4,8,128]{3,2,1,0:T(8,128)S(1)}, f32[3,4,8,128]{3,2,1,0:T(8,128)S(1)}, u32[]{:S(2)}, u32[]{:S(2)}) collective-permute-start(f32[3,4,8,128]{3,2,1,0:T(8,128)S(1)} %shard_map.48.mean), channel_id=1, source_target_pairs={{0,248},{8,0},{16,8},{24,16},{32,24},{40,32},{48,40},{56,48},{64,5... | collective-permute-start | bytes 147464 | tf_op jit(solution)/shard_map/ppermute | solution.py:401
  44.2 2.8 %collective-permute-start.9 = (f32[4,4,8,128]{3,2,1,0:T(8,128)S(1)}, f32[4,4,8,128]{3,2,1,0:T(8,128)S(1)}, u32[]{:S(2)}, u32[]{:S(2)}) collective-permute-start(f32[4,4,8,128]{3,2,1,0:T(8,128)S(1)} %shard_map.50.strat_near), channel_id=1, source_target_pairs={{0,4},{4,0},{1,5},{5,1},{2,6},{6,2},{3,7},{7,3},{8,12},{12,8},{9,1... | collective-permute-start | bytes 196616 | tf_op jit(solution)/shard_map/ppermute | solution.py:413
  47.1 5.2 %shard_map.46.edges = f32[8,3,4,32,128]{4,3,2,1,0:T(8,128)S(1)} custom-call(f32[32,128]{1,0:T(8,128)S(1)} %broadcast_in_dim.7.spin, bf16[3,256,256]{2,1,0:T(8,128)(2,1)S(1)} %maximum_maximum_fusion.blocks, s32[2]{0:T(128)S(1)} %pad_add_fusion.place, f32[16,32,128]{2,1,0:T(8,128)S(1)} %copy-done, f32[16,32,128]{2,1,0:T(8,128)S(1)} %collective-permute-done.even_strat.even, ...), custom_call_target="tpu_custom_call" | custom-call | tf_op jit(solution)/shard_map/pallas_call | solution.py:366
  52.3 5.7 %shard_map.47.fine = f32[3,16,32,128]{3,2,1,0:T(8,128)S(1)} custom-call(f32[32,128]{1,0:T(8,128)S(1)} %broadcast_in_dim.7.spin, s32[2]{0:T(128)S(1)} %pad_add_fusion.place, f32[16,32,128]{2,1,0:T(8,128)S(1)} %copy-done, f32[16,32,128]{2,1,0:T(8,128)} %collective-permute-done.1.odd_strat, f32[16,32,128]{2,1,0:T(8,128)} %collective-permute-done.3.hopped_strat, ...), custom_call_target="tpu_custom_call" | custom-call | flops 10000000000 | bytes 39062500 | tf_op jit(solution)/shard_map/pallas_call | solution.py:366
  58.9 4.8 %collective-permute-start.11 = (f32[12,8,128]{2,1,0:T(8,128)S(1)}, f32[12,8,128]{2,1,0:T(8,128)S(1)}, u32[]{:S(2)}, u32[]{:S(2)}) collective-permute-start(f32[12,8,128]{2,1,0:T(8,128)S(1)} %get-tuple-element.24.refs_0_), channel_id=1, source_target_pairs={{0,32},{16,48},{32,0},{48,16},{1,33},{17,49},{33,1},{49,17},{2,34}... | collective-permute-start | bytes 147464 | tf_op jit(solution)/shard_map/ppermute | solution.py:440
  63.7 4.3 %collective-permute-start.12 = (f32[12,8,128]{2,1,0:T(8,128)S(1)}, f32[12,8,128]{2,1,0:T(8,128)S(1)}, u32[]{:S(2)}, u32[]{:S(2)}) collective-permute-start(f32[12,8,128]{2,1,0:T(8,128)S(1)} %collective-permute-done.10.refs_1_), channel_id=1, source_target_pairs={{0,32},{16,48},{32,0},{48,16},{1,33},{17,49},{33,1},{49,17},{2,34}... | collective-permute-start | bytes 147464 | tf_op jit(solution)/shard_map/ppermute | solution.py:440
  68.5 2.1 %collective-permute-done.12.refs_3_ = f32[12,8,128]{2,1,0:T(8,128)S(1)} collective-permute-done((f32[12,8,128]{2,1,0:T(8,128)S(1)}, f32[12,8,128]{2,1,0:T(8,128)S(1)}, u32[]{:S(2)}, u32[]{:S(2)}) %collective-permute-start.12) | collective-permute-done | bytes 49184 | tf_op jit(solution)/shard_map/ppermute | solution.py:440
  71.9 2.8 %shard_map.52 = (f32[3,32,8,128]{3,2,1,0:T(8,128)S(1)}, f32[3,16,8,128]{3,2,1,0:T(8,128)S(1)}) custom-call(s32[5]{0:T(128)S(1)} %stack.25.where, f32[8,128]{1,0:T(8,128)S(1)} %broadcast_in_dim.6.spin, bf16[3,256,256]{2,1,0:T(8,128)(2,1)S(1)} %maximum_maximum_fusion.blocks, f32[32,8,128]{2,1,0:T(8,128)S(1)} %get-tuple-element.23.strat, ...), custom_call_target="tpu_custom_call" | custom-call | tf_op jit(solution)/shard_map/pallas_call | solution.py:366
  74.7 2.8 %collective-permute-start.17 = (f32[3,16,8,128]{3,2,1,0:T(8,128)S(1)}, f32[3,16,8,128]{3,2,1,0:T(8,128)S(1)}, u32[]{:S(2)}, u32[]{:S(2)}) collective-permute-start(f32[3,16,8,128]{3,2,1,0:T(8,128)S(1)} %get-tuple-element.26), channel_id=1, source_target_pairs={{0,192},{64,0},{128,64},{192,128},{1,193},{65,1},{129,65},{193,129... | collective-permute-start | bytes 589832 | tf_op jit(solution)/shard_map/ppermute | solution.py:446
  77.6 2.3 %collective-permute-start.19 = (f32[3,16,8,128]{3,2,1,0:T(8,128)S(1)}, f32[3,16,8,128]{3,2,1,0:T(8,128)S(1)}, u32[]{:S(2)}, u32[]{:S(2)}) collective-permute-start(f32[3,16,8,128]{3,2,1,0:T(8,128)S(1)} %get-tuple-element.26), channel_id=1, source_target_pairs={{0,128},{64,192},{128,0},{192,64},{1,129},{65,193},{129,1},{193,65... | collective-permute-start | bytes 589832 | tf_op jit(solution)/shard_map/ppermute | solution.py:446
  79.8 6.4 %collective-permute-done.17.here = f32[3,16,8,128]{3,2,1,0:T(8,128)S(1)} collective-permute-done((f32[3,16,8,128]{3,2,1,0:T(8,128)S(1)}, f32[3,16,8,128]{3,2,1,0:T(8,128)S(1)}, u32[]{:S(2)}, u32[]{:S(2)}) %collective-permute-start.17) | collective-permute-done | bytes 196640 | tf_op jit(solution)/shard_map/ppermute | solution.py:446
  86.3 3.4 %collective-permute-done.20.refs_10_ = f32[3,16,8,128]{3,2,1,0:T(8,128)S(1)} collective-permute-done((f32[3,16,8,128]{3,2,1,0:T(8,128)S(1)}, f32[3,16,8,128]{3,2,1,0:T(8,128)S(1)}, u32[]{:S(2)}, u32[]{:S(2)}) %collective-permute-start.20) | collective-permute-done | bytes 196640 | tf_op jit(solution)/shard_map/ppermute | solution.py:446
  90.3 5.4 %shard_map.53.early = f32[3,32,8,128]{3,2,1,0:T(8,128)S(1)} custom-call(s32[5]{0:T(128)S(1)} %stack.25.where, f32[8,128]{1,0:T(8,128)S(1)} %broadcast_in_dim.6.spin, bf16[3,256,256]{2,1,0:T(8,128)(2,1)S(1)} %maximum_maximum_fusion.blocks, f32[32,8,128]{2,1,0:T(8,128)S(1)} %get-tuple-element.23.strat, f32[3,32,8,128]{3,2,1,0:T(8,128)S(1)} %get-tuple-element.25.end, ...), custom_call_target="tpu_custom_call" | custom-call | tf_op jit(solution)/shard_map/pallas_call | solution.py:366
  95.7 3.4 %shard_map.54 = (f32[2,12,8,128]{3,2,1,0:T(8,128)S(1)}, f32[2,12,8,128]{3,2,1,0:T(8,128)S(1)}, f32[2,12,8,128]{3,2,1,0:T(8,128)S(1)}, f32[2,12,8,128]{3,2,1,0:T(8,128)S(1)}) custom-call(s32[5]{0:T(128)S(1)} %stack.25.where, f32[8,128]{1,0:T(8,128)S(1)} %broadcast_in_dim.6.spin, bf16[3,256,256]{2,1,0:T(8,128)(2,1)S(1)} %maximum_maximum_fusion.blocks, ...), custom_call_target="tpu_custom_call" | custom-call | tf_op jit(solution)/shard_map/pallas_call | solution.py:366
  99.2 2.5 %collective-permute-start.24 = (f32[2,12,8,128]{3,2,1,0:T(8,128)S(1)}, f32[2,12,8,128]{3,2,1,0:T(8,128)S(1)}, u32[]{:S(2)}, u32[]{:S(2)}) collective-permute-start(f32[2,12,8,128]{3,2,1,0:T(8,128)S(1)} %get-tuple-element.32), channel_id=1, source_target_pairs={{0,2},{1,3},{2,0},{3,1},{4,6},{5,7},{6,4},{7,5},{8,10},{9,11},{10,... | collective-permute-start | bytes 294920 | tf_op jit(solution)/shard_map/ppermute | solution.py:456
  101.7 2.2 %collective-permute-start.25 = (f32[2,12,8,128]{3,2,1,0:T(8,128)S(1)}, f32[2,12,8,128]{3,2,1,0:T(8,128)S(1)}, u32[]{:S(2)}, u32[]{:S(2)}) collective-permute-start(f32[2,12,8,128]{3,2,1,0:T(8,128)S(1)} %get-tuple-element.33), channel_id=1, source_target_pairs={{0,3},{1,2},{2,1},{3,0},{4,7},{5,6},{6,5},{7,4},{8,11},{9,10},{10,... | collective-permute-start | bytes 294920 | tf_op jit(solution)/shard_map/ppermute | solution.py:456
  103.9 1.5 %collective-permute-done.24 = f32[2,12,8,128]{3,2,1,0:T(8,128)S(1)} collective-permute-done((f32[2,12,8,128]{3,2,1,0:T(8,128)S(1)}, f32[2,12,8,128]{3,2,1,0:T(8,128)S(1)}, u32[]{:S(2)}, u32[]{:S(2)}) %collective-permute-start.24) | collective-permute-done | bytes 98336 | tf_op jit(solution)/shard_map/ppermute | solution.py:456
  105.4 2.1 %collective-permute-done.25 = f32[2,12,8,128]{3,2,1,0:T(8,128)S(1)} collective-permute-done((f32[2,12,8,128]{3,2,1,0:T(8,128)S(1)}, f32[2,12,8,128]{3,2,1,0:T(8,128)S(1)}, u32[]{:S(2)}, u32[]{:S(2)}) %collective-permute-start.25) | collective-permute-done | bytes 98336 | tf_op jit(solution)/shard_map/ppermute | solution.py:456
  107.6 3.6 %collective-permute-start.26 = (f32[12,8,128]{2,1,0:T(8,128)S(1)}, f32[12,8,128]{2,1,0:T(8,128)S(1)}, u32[]{:S(2)}, u32[]{:S(2)}) collective-permute-start(f32[12,8,128]{2,1,0:T(8,128)S(1)} %get-tuple-element.37), channel_id=1, source_target_pairs={{0,4},{4,0},{1,5},{5,1},{2,6},{6,2},{3,7},{7,3},{8,12},{12,8},{9,1... | collective-permute-start | bytes 147464 | tf_op jit(solution)/shard_map/ppermute | solution.py:457
  111.1 4.5 %collective-permute-done.26.sent = f32[12,8,128]{2,1,0:T(8,128)S(1)} collective-permute-done((f32[12,8,128]{2,1,0:T(8,128)S(1)}, f32[12,8,128]{2,1,0:T(8,128)S(1)}, u32[]{:S(2)}, u32[]{:S(2)}) %collective-permute-start.26) | collective-permute-done | bytes 49184 | tf_op jit(solution)/shard_map/ppermute | solution.py:457
  (64 shorter events, 12.9 us)
Async XLA Ops:
  0.0 8.4 %collective-permute-start = (f32[16,32,128]{2,1,0:T(8,128)}, f32[16,32,128]{2,1,0:T(8,128)S(1)}, u32[]{:S(2)}, u32[]{:S(2)}) collective-permute-start(f32[16,32,128]{2,1,0:T(8,128)} %own.1), channel_id=1, source_target_pairs={{0,1},{1,0},{2,3},{3,2},{4,5},{5,4},{6,7},{7,6},{8,9},{9,8},{10,11... | collective-permute-start | bytes 786440 | tf_op jit(solution)/shard_map/ppermute | solution.py:392
  0.7 51.6 %collective-permute-start.5 = (f32[3,16,32,128]{3,2,1,0:T(8,128)}, f32[3,16,32,128]{3,2,1,0:T(8,128)S(1)}, u32[]{:S(2)}, u32[]{:S(2)}) collective-permute-start(f32[3,16,32,128]{3,2,1,0:T(8,128)} %bitcast.14), channel_id=1, source_target_pairs={{0,7},{1,2},{2,1},{3,4},{4,3},{5,6},{6,5},{7,0},{8,15},{9,10},{10,... | collective-permute-start | bytes 2359304 | tf_op jit(solution)/shard_map/ppermute | solution.py:391
  8.4 13.5 %collective-permute-start.2 = (f32[16,32,128]{2,1,0:T(8,128)S(1)}, f32[16,32,128]{2,1,0:T(8,128)}, u32[]{:S(2)}, u32[]{:S(2)}) collective-permute-start(f32[16,32,128]{2,1,0:T(8,128)S(1)} %collective-permute-done.even_strat.even), channel_id=1, source_target_pairs={{1,5},{5,1},{2,6},{6,2},{9,13},{13,9},{10,14},{14,10},{17,21},{21,... | collective-permute-start | bytes 786440 | tf_op jit(solution)/shard_map/ppermute | solution.py:398
  9.8 34.4 %collective-permute-start.4 = (f32[3,16,32,128]{3,2,1,0:T(8,128)}, f32[3,16,32,128]{3,2,1,0:T(8,128)S(1)}, u32[]{:S(2)}, u32[]{:S(2)}) collective-permute-start(f32[3,16,32,128]{3,2,1,0:T(8,128)} %bitcast.15), channel_id=1, source_target_pairs={{0,1},{1,0},{2,3},{3,2},{4,5},{5,4},{6,7},{7,6},{8,9},{9,8},{10,11... | collective-permute-start | bytes 2359304 | tf_op jit(solution)/shard_map/ppermute | solution.py:396
  20.5 31.8 %collective-permute-start.1 = (f32[16,32,128]{2,1,0:T(8,128)S(1)}, f32[16,32,128]{2,1,0:T(8,128)}, u32[]{:S(2)}, u32[]{:S(2)}) collective-permute-start(f32[16,32,128]{2,1,0:T(8,128)S(1)} %copy-done), channel_id=1, source_target_pairs={{1,2},{2,1},{5,6},{6,5},{9,10},{10,9},{13,14},{14,13},{17,18},{18,... | collective-permute-start | bytes 786440 | tf_op jit(solution)/shard_map/ppermute | solution.py:397
  22.0 30.3 %collective-permute-start.3 = (f32[16,32,128]{2,1,0:T(8,128)}, f32[16,32,128]{2,1,0:T(8,128)}, u32[]{:S(2)}, u32[]{:S(2)}) collective-permute-start(f32[16,32,128]{2,1,0:T(8,128)} %collective-permute-done.2), channel_id=1, source_target_pairs={{1,3},{5,7},{2,0},{6,4},{9,11},{13,15},{10,8},{14,12},{17,19},{21,... | collective-permute-start | bytes 786440 | tf_op jit(solution)/shard_map/ppermute | solution.py:399
  24.0 17.1 %collective-permute-start.8 = (f32[2,4,8,128]{3,2,1,0:T(8,128)S(1)}, f32[2,4,8,128]{3,2,1,0:T(8,128)S(1)}, u32[]{:S(2)}, u32[]{:S(2)}) collective-permute-start(f32[2,4,8,128]{3,2,1,0:T(8,128)S(1)} %collective-permute-done.7.across), channel_id=1, source_target_pairs={{0,1},{1,0},{2,3},{3,2},{4,5},{5,4},{6,7},{7,6},{8,9},{9,8},{10,11... | collective-permute-start | bytes 98312 | tf_op jit(solution)/shard_map/ppermute | solution.py:409
  41.1 17.0 %collective-permute-start.6 = (f32[3,4,8,128]{3,2,1,0:T(8,128)S(1)}, f32[3,4,8,128]{3,2,1,0:T(8,128)S(1)}, u32[]{:S(2)}, u32[]{:S(2)}) collective-permute-start(f32[3,4,8,128]{3,2,1,0:T(8,128)S(1)} %shard_map.48.mean), channel_id=1, source_target_pairs={{0,248},{8,0},{16,8},{24,16},{32,24},{40,32},{48,40},{56,48},{64,5... | collective-permute-start | bytes 147464 | tf_op jit(solution)/shard_map/ppermute | solution.py:401
  44.2 13.9 %collective-permute-start.9 = (f32[4,4,8,128]{3,2,1,0:T(8,128)S(1)}, f32[4,4,8,128]{3,2,1,0:T(8,128)S(1)}, u32[]{:S(2)}, u32[]{:S(2)}) collective-permute-start(f32[4,4,8,128]{3,2,1,0:T(8,128)S(1)} %shard_map.50.strat_near), channel_id=1, source_target_pairs={{0,4},{4,0},{1,5},{5,1},{2,6},{6,2},{3,7},{7,3},{8,12},{12,8},{9,1... | collective-permute-start | bytes 196616 | tf_op jit(solution)/shard_map/ppermute | solution.py:413
  58.8 4.9 %collective-permute-start.10 = (f32[12,8,128]{2,1,0:T(8,128)S(1)}, f32[12,8,128]{2,1,0:T(8,128)S(1)}, u32[]{:S(2)}, u32[]{:S(2)}) collective-permute-start(f32[12,8,128]{2,1,0:T(8,128)S(1)} %get-tuple-element.24.refs_0_), channel_id=1, source_target_pairs={{0,16},{16,0},{32,48},{48,32},{1,17},{17,1},{33,49},{49,33},{2,18}... | collective-permute-start | bytes 147464 | tf_op jit(solution)/shard_map/ppermute | solution.py:438
  58.9 9.6 %collective-permute-start.11 = (f32[12,8,128]{2,1,0:T(8,128)S(1)}, f32[12,8,128]{2,1,0:T(8,128)S(1)}, u32[]{:S(2)}, u32[]{:S(2)}) collective-permute-start(f32[12,8,128]{2,1,0:T(8,128)S(1)} %get-tuple-element.24.refs_0_), channel_id=1, source_target_pairs={{0,32},{16,48},{32,0},{48,16},{1,33},{17,49},{33,1},{49,17},{2,34}... | collective-permute-start | bytes 147464 | tf_op jit(solution)/shard_map/ppermute | solution.py:440
  63.7 6.9 %collective-permute-start.12 = (f32[12,8,128]{2,1,0:T(8,128)S(1)}, f32[12,8,128]{2,1,0:T(8,128)S(1)}, u32[]{:S(2)}, u32[]{:S(2)}) collective-permute-start(f32[12,8,128]{2,1,0:T(8,128)S(1)} %collective-permute-done.10.refs_1_), channel_id=1, source_target_pairs={{0,32},{16,48},{32,0},{48,16},{1,33},{17,49},{33,1},{49,17},{2,34}... | collective-permute-start | bytes 147464 | tf_op jit(solution)/shard_map/ppermute | solution.py:440
  68.0 2.9 %collective-permute-start.14 = (f32[12,8,128]{2,1,0:T(8,128)S(1)}, f32[12,8,128]{2,1,0:T(8,128)S(1)}, u32[]{:S(2)}, u32[]{:S(2)}) collective-permute-start(f32[12,8,128]{2,1,0:T(8,128)S(1)} %collective-permute-done.10.refs_1_), channel_id=1, source_target_pairs={{0,8},{8,0},{1,9},{9,1},{2,10},{10,2},{3,11},{11,3},{4,12},{12,4},... | collective-permute-start | bytes 147464 | tf_op jit(solution)/shard_map/ppermute | solution.py:441
  74.7 11.6 %collective-permute-start.17 = (f32[3,16,8,128]{3,2,1,0:T(8,128)S(1)}, f32[3,16,8,128]{3,2,1,0:T(8,128)S(1)}, u32[]{:S(2)}, u32[]{:S(2)}) collective-permute-start(f32[3,16,8,128]{3,2,1,0:T(8,128)S(1)} %get-tuple-element.26), channel_id=1, source_target_pairs={{0,192},{64,0},{128,64},{192,128},{1,193},{65,1},{129,65},{193,129... | collective-permute-start | bytes 589832 | tf_op jit(solution)/shard_map/ppermute | solution.py:446
  77.6 12.1 %collective-permute-start.20 = (f32[3,16,8,128]{3,2,1,0:T(8,128)S(1)}, f32[3,16,8,128]{3,2,1,0:T(8,128)S(1)}, u32[]{:S(2)}, u32[]{:S(2)}) collective-permute-start(f32[3,16,8,128]{3,2,1,0:T(8,128)S(1)} %get-tuple-element.26), channel_id=1, source_target_pairs={{0,64},{64,128},{128,192},{192,0},{1,65},{65,129},{129,193},{193,1... | collective-permute-start | bytes 589832 | tf_op jit(solution)/shard_map/ppermute | solution.py:446
  77.6 12.1 %collective-permute-start.19 = (f32[3,16,8,128]{3,2,1,0:T(8,128)S(1)}, f32[3,16,8,128]{3,2,1,0:T(8,128)S(1)}, u32[]{:S(2)}, u32[]{:S(2)}) collective-permute-start(f32[3,16,8,128]{3,2,1,0:T(8,128)S(1)} %get-tuple-element.26), channel_id=1, source_target_pairs={{0,128},{64,192},{128,0},{192,64},{1,129},{65,193},{129,1},{193,65... | collective-permute-start | bytes 589832 | tf_op jit(solution)/shard_map/ppermute | solution.py:446
  86.3 3.4 %collective-permute-start.18 = (f32[3,16,8,128]{3,2,1,0:T(8,128)S(1)}, f32[3,16,8,128]{3,2,1,0:T(8,128)S(1)}, u32[]{:S(2)}, u32[]{:S(2)}) collective-permute-start(f32[3,16,8,128]{3,2,1,0:T(8,128)S(1)} %collective-permute-done.17.here), channel_id=1, source_target_pairs={{0,8},{8,0},{1,9},{9,1},{2,10},{10,2},{3,11},{11,3},{4,12},{12,4},... | collective-permute-start | bytes 589832 | tf_op jit(solution)/shard_map/ppermute | solution.py:447
  89.7 6.0 %collective-permute-start.21 = (f32[3,16,8,128]{3,2,1,0:T(8,128)S(1)}, f32[3,16,8,128]{3,2,1,0:T(8,128)S(1)}, u32[]{:S(2)}, u32[]{:S(2)}) collective-permute-start(f32[3,16,8,128]{3,2,1,0:T(8,128)S(1)} %collective-permute-done.19.refs_8_), channel_id=1, source_target_pairs={{0,8},{8,0},{1,9},{9,1},{2,10},{10,2},{3,11},{11,3},{4,12},{12,4},... | collective-permute-start | bytes 589832 | tf_op jit(solution)/shard_map/ppermute | solution.py:450
  89.7 6.0 %collective-permute-start.22 = (f32[3,16,8,128]{3,2,1,0:T(8,128)S(1)}, f32[3,16,8,128]{3,2,1,0:T(8,128)S(1)}, u32[]{:S(2)}, u32[]{:S(2)}) collective-permute-start(f32[3,16,8,128]{3,2,1,0:T(8,128)S(1)} %collective-permute-done.20.refs_10_), channel_id=1, source_target_pairs={{0,8},{8,0},{1,9},{9,1},{2,10},{10,2},{3,11},{11,3},{4,12},{12,4},... | collective-permute-start | bytes 589832 | tf_op jit(solution)/shard_map/ppermute | solution.py:450
  90.2 21.0 %collective-permute-start.27 = (f32[3,16,32,128]{3,2,1,0:T(8,128)S(1)}, f32[3,16,32,128]{3,2,1,0:T(8,128)S(1)}, u32[]{:S(2)}, u32[]{:S(2)}) collective-permute-start(f32[3,16,32,128]{3,2,1,0:T(8,128)S(1)} %get-tuple-element.34), channel_id=1, source_target_pairs={{0,8},{8,16},{16,24},{24,32},{32,40},{40,48},{48,56},{56,64},{64,7... | collective-permute-start | bytes 2359304 | tf_op jit(solution)/shard_map/ppermute | solution.py:442
  99.1 4.8 %collective-permute-start.23 = (f32[2,12,8,128]{3,2,1,0:T(8,128)S(1)}, f32[2,12,8,128]{3,2,1,0:T(8,128)S(1)}, u32[]{:S(2)}, u32[]{:S(2)}) collective-permute-start(f32[2,12,8,128]{3,2,1,0:T(8,128)S(1)} %get-tuple-element.31), channel_id=1, source_target_pairs={{0,1},{1,0},{2,3},{3,2},{4,5},{5,4},{6,7},{7,6},{8,9},{9,8},{10,11... | collective-permute-start | bytes 294920 | tf_op jit(solution)/shard_map/ppermute | solution.py:456
  99.2 6.2 %collective-permute-start.24 = (f32[2,12,8,128]{3,2,1,0:T(8,128)S(1)}, f32[2,12,8,128]{3,2,1,0:T(8,128)S(1)}, u32[]{:S(2)}, u32[]{:S(2)}) collective-permute-start(f32[2,12,8,128]{3,2,1,0:T(8,128)S(1)} %get-tuple-element.32), channel_id=1, source_target_pairs={{0,2},{1,3},{2,0},{3,1},{4,6},{5,7},{6,4},{7,5},{8,10},{9,11},{10,... | collective-permute-start | bytes 294920 | tf_op jit(solution)/shard_map/ppermute | solution.py:456
  101.7 5.8 %collective-permute-start.25 = (f32[2,12,8,128]{3,2,1,0:T(8,128)S(1)}, f32[2,12,8,128]{3,2,1,0:T(8,128)S(1)}, u32[]{:S(2)}, u32[]{:S(2)}) collective-permute-start(f32[2,12,8,128]{3,2,1,0:T(8,128)S(1)} %get-tuple-element.33), channel_id=1, source_target_pairs={{0,3},{1,2},{2,1},{3,0},{4,7},{5,6},{6,5},{7,4},{8,11},{9,10},{10,... | collective-permute-start | bytes 294920 | tf_op jit(solution)/shard_map/ppermute | solution.py:456
  107.6 8.1 %collective-permute-start.26 = (f32[12,8,128]{2,1,0:T(8,128)S(1)}, f32[12,8,128]{2,1,0:T(8,128)S(1)}, u32[]{:S(2)}, u32[]{:S(2)}) collective-permute-start(f32[12,8,128]{2,1,0:T(8,128)S(1)} %get-tuple-element.37), channel_id=1, source_target_pairs={{0,4},{4,0},{1,5},{5,1},{2,6},{6,2},{3,7},{7,3},{8,12},{12,8},{9,1... | collective-permute-start | bytes 147464 | tf_op jit(solution)/shard_map/ppermute | solution.py:457
  (9 other events, 78.3 us)

commit v12 on v10

--- a/solution.py
+++ b/solution.py
@@ -159,7 +159,7 @@
             means[n, cell] = block_means(rows.at[cell % 2], cells)
 
 
-def columns_kernel(place, own, across, forwarded, columns):
+def columns_kernel(place, own, relayed, across, forwarded, columns, far_columns):
     y = place[1]
     beside = y + 1 - 2 * (y % 2)
     columns[y] = own[0]
@@ -172,11 +172,19 @@
     def _():
         columns[near] = across[0]
         columns[far] = across[1]
+        far_columns[near] = across[2]
+        far_columns[far] = across[3]
+        far_columns[y] = relayed[0]
+        far_columns[beside] = relayed[1]
 
     @pl.when(jnp.logical_not(inner))
     def _():
         columns[near] = forwarded[0]
         columns[far] = forwarded[1]
+        far_columns[near] = forwarded[2]
+        far_columns[far] = forwarded[3]
+        far_columns[beside] = forwarded[4]
+        far_columns[y] = forwarded[5]
 
 
 def split_kernel(place, fine, next_mean, strat_near, strat_far, detail, increment, strat, rows):
@@ -374,22 +382,25 @@
     even = lax.ppermute(start, SPACE, even_edges)
     even_strat = lax.ppermute(stratification, SPACE, even_edges)
     odd_strat = lax.ppermute(stratification, SPACE, [(1, 2), (2, 1), (5, 6), (6, 5)])
-    relayed = lax.ppermute(even_strat, SPACE, [(1, 5), (5, 1), (2, 6), (6, 2)])
-    hopped_strat = lax.ppermute(relayed, SPACE, [(1, 3), (5, 7), (2, 0), (6, 4)])
-    (mean,) = call(means_kernel, [(3, 4, 8, 128)], [((2, 32, 128), f32)], COST)(start)
-    next_mean = lax.ppermute(mean, TM, ring(32, -1))
-
-    spots = [lax.axis_index(name).astype(jnp.int32) for name in ("zl", "c", "x", "zh", "y")]
-    where = jnp.stack(spots)
     (pair_means,) = call(strat_means_kernel, [(2, 4, 8, 128)], [((2, 32, 128), f32)])(
         even_strat, stratification
     )
-    across = lax.ppermute(pair_means, "y", [(1, 2), (2, 1)])
-    forwarded = lax.ppermute(across, "y", swapped(1))
-    (near,) = call(columns_kernel, [(4, 4, 8, 128)], [])(
-        where[3:], pair_means, across, forwarded
+    load = jnp.concatenate([even_strat, pair_means.reshape(2, 32, 128)])
+    relayed = lax.ppermute(load, SPACE, [(1, 5), (5, 1), (2, 6), (6, 2)])
+    hopped_strat = lax.ppermute(relayed[:16], SPACE, [(1, 3), (5, 7), (2, 0), (6, 4)])
+    (mean,) = call(means_kernel, [(3, 4, 8, 128)], [((2, 32, 128), f32)])(start)
+    next_mean = lax.ppermute(mean, TM, ring(32, -1))
+
+    spots = [lax.axis_index(name).astype(jnp.int32) for name in ("zl", "c", "x", "zh", "y")]
+    where = jnp.stack(spots)
+    relayed_means = relayed[16:].reshape(2, 4, 8, 128)
+    across = lax.ppermute(
+        jnp.concatenate([pair_means, relayed_means]), "y", [(1, 2), (2, 1)]
     )
-    far = lax.ppermute(near, "zh", ring(2, 1))
+    forwarded = lax.ppermute(jnp.concatenate([across, relayed_means]), "y", swapped(1))
+    near, far = call(columns_kernel, [(4, 4, 8, 128)] * 2, [])(
+        where[3:], pair_means, relayed_means, across, forwarded
+    )
     half_spin = jnp.broadcast_to(0.5 * coriolis[:, None], (32, 128))
     coarse_spin = jnp.broadcast_to(4.0 * coriolis.reshape(8, 4).mean(axis=1)[:, None], (8, 128))
     turned = jnp.swapaxes(inverse_blocks, 1, 2)

time: 113 us -> 117 us (1.035); the launches traced: 112 us -> 117 us
  waiting for transfers between devices: 21.4 us -> 24.2 us
  starting transfers between devices: 63.3 us -> 65 us
    ppermute x5 -> x4, starting transfers between devices: 29.6 us -> 19.5 us  [the longest x1 16.7 us: per_device(): lax.ppermute(jnp.concatenate([across, relayed_means]), 'y', swapped(1))]
    ppermute x2, starting transfers between devices: 4.41 us -> 12.3 us  [per_device(): lax.ppermute(part, 'zl', swapped(2))]
    ppermute x1, starting transfers between devices: 0.42 us -> 4.77 us  [per_device(): next_mean = lax.ppermute(mean, TM, ring(32, -1))]
    ppermute x5 -> x4, waiting for transfers between devices: 1.83 us -> 4.22 us  [the longest x1 4.21 us: per_device(): lax.ppermute(jnp.concatenate([across, relayed_means]), 'y', swapped(1))]
  transfers between devices with their start and end apart: 28 -> 27, of which waited for: 12 -> 10; matrix products, arithmetic and copies ran while one was open for 1% -> 2% of each run, Pallas kernels for 18% -> 17%
where the time goes in v12:
time: 117 us
  starting transfers between devices  65 us (56%)
  waiting for transfers between devices  24.2 us (21%)
  Pallas kernels  24 us (21%)
  local copies, waits for them, and re-layouts  3.04 us (3%)
    pallas_call x9, Pallas kernels, run(): pl.pallas_call(kernel, out_shape=[jax.ShapeDtypeStruct(shape, f32) for sh...  24 us
    ppermute x1, starting transfers between devices, per_device(): lax.ppermute(jnp.concatenate([across, relayed_means]), 'y', swapped(1))  16.7 us
    ppermute x2, starting transfers between devices, per_device(): lax.ppermute(part, 'zl', swapped(2))  12.3 us
    ppermute x3, waiting for transfers between devices, per_device(): here = [lax.ppermute(part, 'x', ring(4, by)) for by in (1, 2, 3)]  7.72 us
    ppermute x1, starting transfers between devices, per_device(): odd = lax.ppermute(start, SPACE, odd_edges)  6.85 us
    ppermute x3, starting transfers between devices, per_device(): here = [lax.ppermute(part, 'x', ring(4, by)) for by in (1, 2, 3)]  5.73 us
    ppermute x3, starting transfers between devices, per_device(): total = total + lax.ppermute(parts[by], 'y', swapped(by))  4.78 us
    ppermute x1, starting transfers between devices, per_device(): next_mean = lax.ppermute(mean, TM, ring(32, -1))  4.77 us
  transfers between devices with their start and end apart: 27, of which 10 were waited for; matrix products, arithmetic and copies ran while one was open for 2% of the time, Pallas kernels for 17%

profile of v12, /device:TPU:24, one launch (start us, length us, event | category | flops | bytes accessed | tf_op | source)
XLA Modules:
  0.0 116.9 jit_solution(1995979327708281252)
XLA Ops:
  2.0 6.8 %collective-permute-start.5 = (f32[3,16,32,128]{3,2,1,0:T(8,128)}, f32[3,16,32,128]{3,2,1,0:T(8,128)S(1)}, u32[]{:S(2)}, u32[]{:S(2)}) collective-permute-start(f32[3,16,32,128]{3,2,1,0:T(8,128)} %bitcast.18), channel_id=1, source_target_pairs={{0,7},{1,2},{2,1},{3,4},{4,3},{5,6},{6,5},{7,0},{8,15},{9,10},{10,... | collective-permute-start | bytes 2359304 | tf_op jit(solution)/shard_map/ppermute | solution.py:381
  8.9 1.4 %collective-permute-start = (f32[16,32,128]{2,1,0:T(8,128)}, f32[16,32,128]{2,1,0:T(8,128)}, u32[]{:S(2)}, u32[]{:S(2)}) collective-permute-start(f32[16,32,128]{2,1,0:T(8,128)} %own_strat.3), channel_id=1, source_target_pairs={{1,2},{2,1},{5,6},{6,5},{9,10},{10,9},{13,14},{14,13},{17,18},{18,... | collective-permute-start | bytes 786440 | tf_op jit(solution)/shard_map/ppermute | solution.py:384
  16.1 16.7 %collective-permute-start.8 = (f32[6,4,8,128]{3,2,1,0:T(8,128)S(1)}, f32[6,4,8,128]{3,2,1,0:T(8,128)S(1)}, u32[]{:S(2)}, u32[]{:S(2)}) collective-permute-start(f32[6,4,8,128]{3,2,1,0:T(8,128)S(1)} %pad_maximum_fusion.1), channel_id=1, source_target_pairs={{0,1},{1,0},{2,3},{3,2},{4,5},{5,4},{6,7},{7,6},{8,9},{9,8},{10,11... | collective-permute-start | bytes 294920 | tf_op jit(solution)/shard_map/ppermute | solution.py:400
  32.9 4.2 %collective-permute-done.8.forwarded = f32[6,4,8,128]{3,2,1,0:T(8,128)S(1)} collective-permute-done((f32[6,4,8,128]{3,2,1,0:T(8,128)S(1)}, f32[6,4,8,128]{3,2,1,0:T(8,128)S(1)}, u32[]{:S(2)}, u32[]{:S(2)}) %collective-permute-start.8) | collective-permute-done | bytes 98336 | tf_op jit(solution)/shard_map/ppermute | solution.py:400
  37.1 4.8 %collective-permute-start.6 = (f32[3,4,8,128]{3,2,1,0:T(8,128)S(1)}, f32[3,4,8,128]{3,2,1,0:T(8,128)S(1)}, u32[]{:S(2)}, u32[]{:S(2)}) collective-permute-start(f32[3,4,8,128]{3,2,1,0:T(8,128)S(1)} %shard_map.49.mean), channel_id=1, source_target_pairs={{0,248},{8,0},{16,8},{24,16},{32,24},{40,32},{48,40},{56,48},{64,5... | collective-permute-start | bytes 147464 | tf_op jit(solution)/shard_map/ppermute | solution.py:392
  42.7 5.1 %shard_map.47.edges = f32[8,3,4,32,128]{4,3,2,1,0:T(8,128)S(1)} custom-call(f32[32,128]{1,0:T(8,128)S(1)} %broadcast_in_dim.7.spin, bf16[3,256,256]{2,1,0:T(8,128)(2,1)S(1)} %maximum_maximum_fusion.blocks, s32[2]{0:T(128)S(1)} %pad_add_fusion.place, f32[16,32,128]{2,1,0:T(8,128)S(1)} %copy-done.2, f32[16,32,128]{2,1,0:T(8,128)S(1)} %collective-permute-done.1.even.even_strat, ...), custom_call_target="tpu_custom_call" | custom-call | tf_op jit(solution)/shard_map/pallas_call | solution.py:356
  47.9 5.7 %shard_map.48.fine = f32[3,16,32,128]{3,2,1,0:T(8,128)S(1)} custom-call(f32[32,128]{1,0:T(8,128)S(1)} %broadcast_in_dim.7.spin, s32[2]{0:T(128)S(1)} %pad_add_fusion.place, f32[16,32,128]{2,1,0:T(8,128)S(1)} %copy-done.2, f32[16,32,128]{2,1,0:T(8,128)} %collective-permute-done.odd_strat, f32[16,32,128]{2,1,0:T(8,128)} %collective-permute-done.3.hopped_strat, ...), custom_call_target="tpu_custom_call" | custom-call | flops 10000000000 | bytes 39062500 | tf_op jit(solution)/shard_map/pallas_call | solution.py:356
  54.3 2.1 %collective-permute-start.9 = (f32[12,8,128]{2,1,0:T(8,128)S(1)}, f32[12,8,128]{2,1,0:T(8,128)S(1)}, u32[]{:S(2)}, u32[]{:S(2)}) collective-permute-start(f32[12,8,128]{2,1,0:T(8,128)S(1)} %get-tuple-element.19.refs_0_), channel_id=1, source_target_pairs={{0,16},{16,0},{32,48},{48,32},{1,17},{17,1},{33,49},{49,33},{2,18}... | collective-permute-start | bytes 147464 | tf_op jit(solution)/shard_map/ppermute | solution.py:429
  56.4 7.9 %collective-permute-start.10 = (f32[12,8,128]{2,1,0:T(8,128)S(1)}, f32[12,8,128]{2,1,0:T(8,128)S(1)}, u32[]{:S(2)}, u32[]{:S(2)}) collective-permute-start(f32[12,8,128]{2,1,0:T(8,128)S(1)} %get-tuple-element.19.refs_0_), channel_id=1, source_target_pairs={{0,32},{16,48},{32,0},{48,16},{1,33},{17,49},{33,1},{49,17},{2,34}... | collective-permute-start | bytes 147464 | tf_op jit(solution)/shard_map/ppermute | solution.py:431
  64.3 4.3 %collective-permute-start.11 = (f32[12,8,128]{2,1,0:T(8,128)S(1)}, f32[12,8,128]{2,1,0:T(8,128)S(1)}, u32[]{:S(2)}, u32[]{:S(2)}) collective-permute-start(f32[12,8,128]{2,1,0:T(8,128)S(1)} %collective-permute-done.9.refs_1_), channel_id=1, source_target_pairs={{0,32},{16,48},{32,0},{48,16},{1,33},{17,49},{33,1},{49,17},{2,34}... | collective-permute-start | bytes 147464 | tf_op jit(solution)/shard_map/ppermute | solution.py:431
  69.1 1.9 %collective-permute-done.11.refs_3_ = f32[12,8,128]{2,1,0:T(8,128)S(1)} collective-permute-done((f32[12,8,128]{2,1,0:T(8,128)S(1)}, f32[12,8,128]{2,1,0:T(8,128)S(1)}, u32[]{:S(2)}, u32[]{:S(2)}) %collective-permute-start.11) | collective-permute-done | bytes 49184 | tf_op jit(solution)/shard_map/ppermute | solution.py:431
  72.4 2.7 %shard_map.52 = (f32[3,32,8,128]{3,2,1,0:T(8,128)S(1)}, f32[3,16,8,128]{3,2,1,0:T(8,128)S(1)}) custom-call(s32[5]{0:T(128)S(1)} %stack.25.where, f32[8,128]{1,0:T(8,128)S(1)} %broadcast_in_dim.6.spin, bf16[3,256,256]{2,1,0:T(8,128)(2,1)S(1)} %maximum_maximum_fusion.blocks, f32[32,8,128]{2,1,0:T(8,128)S(1)} %get-tuple-element.18.strat, ...), custom_call_target="tpu_custom_call" | custom-call | tf_op jit(solution)/shard_map/pallas_call | solution.py:356
  75.0 1.6 %collective-permute-start.16 = (f32[3,16,8,128]{3,2,1,0:T(8,128)S(1)}, f32[3,16,8,128]{3,2,1,0:T(8,128)S(1)}, u32[]{:S(2)}, u32[]{:S(2)}) collective-permute-start(f32[3,16,8,128]{3,2,1,0:T(8,128)S(1)} %get-tuple-element.21), channel_id=1, source_target_pairs={{0,64},{64,128},{128,192},{192,0},{1,65},{65,129},{129,193},{193,1... | collective-permute-start | bytes 589832 | tf_op jit(solution)/shard_map/ppermute | solution.py:437
  76.6 2.7 %collective-permute-start.17 = (f32[3,16,8,128]{3,2,1,0:T(8,128)S(1)}, f32[3,16,8,128]{3,2,1,0:T(8,128)S(1)}, u32[]{:S(2)}, u32[]{:S(2)}) collective-permute-start(f32[3,16,8,128]{3,2,1,0:T(8,128)S(1)} %get-tuple-element.21), channel_id=1, source_target_pairs={{0,128},{64,192},{128,0},{192,64},{1,129},{65,193},{129,1},{193,65... | collective-permute-start | bytes 589832 | tf_op jit(solution)/shard_map/ppermute | solution.py:437
  79.3 1.4 %collective-permute-start.18 = (f32[3,16,8,128]{3,2,1,0:T(8,128)S(1)}, f32[3,16,8,128]{3,2,1,0:T(8,128)S(1)}, u32[]{:S(2)}, u32[]{:S(2)}) collective-permute-start(f32[3,16,8,128]{3,2,1,0:T(8,128)S(1)} %get-tuple-element.21), channel_id=1, source_target_pairs={{0,192},{64,0},{128,64},{192,128},{1,193},{65,1},{129,65},{193,129... | collective-permute-start | bytes 589832 | tf_op jit(solution)/shard_map/ppermute | solution.py:437
  80.8 2.5 %collective-permute-done.16.refs_8_ = f32[3,16,8,128]{3,2,1,0:T(8,128)S(1)} collective-permute-done((f32[3,16,8,128]{3,2,1,0:T(8,128)S(1)}, f32[3,16,8,128]{3,2,1,0:T(8,128)S(1)}, u32[]{:S(2)}, u32[]{:S(2)}) %collective-permute-start.16) | collective-permute-done | bytes 196640 | tf_op jit(solution)/shard_map/ppermute | solution.py:437
  83.3 5.2 %collective-permute-done.17.refs_9_ = f32[3,16,8,128]{3,2,1,0:T(8,128)S(1)} collective-permute-done((f32[3,16,8,128]{3,2,1,0:T(8,128)S(1)}, f32[3,16,8,128]{3,2,1,0:T(8,128)S(1)}, u32[]{:S(2)}, u32[]{:S(2)}) %collective-permute-start.17) | collective-permute-done | bytes 196640 | tf_op jit(solution)/shard_map/ppermute | solution.py:437
  90.2 8.0 %shard_map.53 = (f32[2,12,8,128]{3,2,1,0:T(8,128)S(1)}, f32[2,12,8,128]{3,2,1,0:T(8,128)S(1)}, f32[2,12,8,128]{3,2,1,0:T(8,128)S(1)}, f32[2,12,8,128]{3,2,1,0:T(8,128)S(1)}) custom-call(s32[5]{0:T(128)S(1)} %stack.25.where, f32[8,128]{1,0:T(8,128)S(1)} %broadcast_in_dim.6.spin, bf16[3,256,256]{2,1,0:T(8,128)(2,1)S(1)} %maximum_maximum_fusion.blocks, ...), custom_call_target="tpu_custom_call" | custom-call | tf_op jit(solution)/shard_map/pallas_call | solution.py:356
  98.3 3.4 %collective-permute-start.23 = (f32[2,12,8,128]{3,2,1,0:T(8,128)S(1)}, f32[2,12,8,128]{3,2,1,0:T(8,128)S(1)}, u32[]{:S(2)}, u32[]{:S(2)}) collective-permute-start(f32[2,12,8,128]{3,2,1,0:T(8,128)S(1)} %get-tuple-element.24), channel_id=1, source_target_pairs={{0,2},{1,3},{2,0},{3,1},{4,6},{5,7},{6,4},{7,5},{8,10},{9,11},{10,... | collective-permute-start | bytes 294920 | tf_op jit(solution)/shard_map/ppermute | solution.py:444
  101.7 1.3 %collective-permute-start.24 = (f32[2,12,8,128]{3,2,1,0:T(8,128)S(1)}, f32[2,12,8,128]{3,2,1,0:T(8,128)S(1)}, u32[]{:S(2)}, u32[]{:S(2)}) collective-permute-start(f32[2,12,8,128]{3,2,1,0:T(8,128)S(1)} %get-tuple-element.25), channel_id=1, source_target_pairs={{0,3},{1,2},{2,1},{3,0},{4,7},{5,6},{6,5},{7,4},{8,11},{9,10},{10,... | collective-permute-start | bytes 294920 | tf_op jit(solution)/shard_map/ppermute | solution.py:444
  103.0 2.3 %collective-permute-done.23 = f32[2,12,8,128]{3,2,1,0:T(8,128)S(1)} collective-permute-done((f32[2,12,8,128]{3,2,1,0:T(8,128)S(1)}, f32[2,12,8,128]{3,2,1,0:T(8,128)S(1)}, u32[]{:S(2)}, u32[]{:S(2)}) %collective-permute-start.23) | collective-permute-done | bytes 98336 | tf_op jit(solution)/shard_map/ppermute | solution.py:444
  105.3 2.2 %collective-permute-done.24 = f32[2,12,8,128]{3,2,1,0:T(8,128)S(1)} collective-permute-done((f32[2,12,8,128]{3,2,1,0:T(8,128)S(1)}, f32[2,12,8,128]{3,2,1,0:T(8,128)S(1)}, u32[]{:S(2)}, u32[]{:S(2)}) %collective-permute-start.24) | collective-permute-done | bytes 98336 | tf_op jit(solution)/shard_map/ppermute | solution.py:444
  107.6 4.7 %collective-permute-start.25 = (f32[12,8,128]{2,1,0:T(8,128)S(1)}, f32[12,8,128]{2,1,0:T(8,128)S(1)}, u32[]{:S(2)}, u32[]{:S(2)}) collective-permute-start(f32[12,8,128]{2,1,0:T(8,128)S(1)} %get-tuple-element.29), channel_id=1, source_target_pairs={{0,4},{4,0},{1,5},{5,1},{2,6},{6,2},{3,7},{7,3},{8,12},{12,8},{9,1... | collective-permute-start | bytes 147464 | tf_op jit(solution)/shard_map/ppermute | solution.py:445
  112.2 3.7 %collective-permute-done.25.sent = f32[12,8,128]{2,1,0:T(8,128)S(1)} collective-permute-done((f32[12,8,128]{2,1,0:T(8,128)S(1)}, f32[12,8,128]{2,1,0:T(8,128)S(1)}, u32[]{:S(2)}, u32[]{:S(2)}) %collective-permute-start.25) | collective-permute-done | bytes 49184 | tf_op jit(solution)/shard_map/ppermute | solution.py:445
  (64 shorter events, 14.0 us)
Async XLA Ops:
  0.0 11.3 %collective-permute-start.1 = (f32[16,32,128]{2,1,0:T(8,128)}, f32[16,32,128]{2,1,0:T(8,128)S(1)}, u32[]{:S(2)}, u32[]{:S(2)}) collective-permute-start(f32[16,32,128]{2,1,0:T(8,128)} %own_strat.3), channel_id=1, source_target_pairs={{0,1},{1,0},{2,3},{3,2},{4,5},{5,4},{6,7},{7,6},{8,9},{9,8},{10,11... | collective-permute-start | bytes 786440 | tf_op jit(solution)/shard_map/ppermute | solution.py:383
  0.7 41.9 %collective-permute-start.4 = (f32[3,16,32,128]{3,2,1,0:T(8,128)}, f32[3,16,32,128]{3,2,1,0:T(8,128)S(1)}, u32[]{:S(2)}, u32[]{:S(2)}) collective-permute-start(f32[3,16,32,128]{3,2,1,0:T(8,128)} %bitcast.17), channel_id=1, source_target_pairs={{0,1},{1,0},{2,3},{3,2},{4,5},{5,4},{6,7},{7,6},{8,9},{9,8},{10,11... | collective-permute-start | bytes 2359304 | tf_op jit(solution)/shard_map/ppermute | solution.py:382
  2.0 45.8 %collective-permute-start.5 = (f32[3,16,32,128]{3,2,1,0:T(8,128)}, f32[3,16,32,128]{3,2,1,0:T(8,128)S(1)}, u32[]{:S(2)}, u32[]{:S(2)}) collective-permute-start(f32[3,16,32,128]{3,2,1,0:T(8,128)} %bitcast.18), channel_id=1, source_target_pairs={{0,7},{1,2},{2,1},{3,4},{4,3},{5,6},{6,5},{7,0},{8,15},{9,10},{10,... | collective-permute-start | bytes 2359304 | tf_op jit(solution)/shard_map/ppermute | solution.py:381
  8.9 38.9 %collective-permute-start = (f32[16,32,128]{2,1,0:T(8,128)}, f32[16,32,128]{2,1,0:T(8,128)}, u32[]{:S(2)}, u32[]{:S(2)}) collective-permute-start(f32[16,32,128]{2,1,0:T(8,128)} %own_strat.3), channel_id=1, source_target_pairs={{1,2},{2,1},{5,6},{6,5},{9,10},{10,9},{13,14},{14,13},{17,18},{18,... | collective-permute-start | bytes 786440 | tf_op jit(solution)/shard_map/ppermute | solution.py:384
  13.3 2.8 %collective-permute-start.7 = (f32[4,4,8,128]{3,2,1,0:T(8,128)S(1)}, f32[4,4,8,128]{3,2,1,0:T(8,128)S(1)}, u32[]{:S(2)}, u32[]{:S(2)}) collective-permute-start(f32[4,4,8,128]{3,2,1,0:T(8,128)S(1)} %pad_maximum_fusion.2), channel_id=1, source_target_pairs={{1,2},{2,1},{5,6},{6,5},{9,10},{10,9},{13,14},{14,13},{17,18},{18,... | collective-permute-start | bytes 196616 | tf_op jit(solution)/shard_map/ppermute | solution.py:397
  14.7 33.2 %collective-permute-start.3 = (f32[16,32,128]{2,1,0:T(8,128)}, f32[16,32,128]{2,1,0:T(8,128)}, u32[]{:S(2)}, u32[]{:S(2)}) collective-permute-start(f32[16,32,128]{2,1,0:T(8,128)} %slice.21), channel_id=1, source_target_pairs={{1,3},{5,7},{2,0},{6,4},{9,11},{13,15},{10,8},{14,12},{17,19},{21,... | collective-permute-start | bytes 786440 | tf_op jit(solution)/shard_map/ppermute | solution.py:390
  16.1 21.0 %collective-permute-start.8 = (f32[6,4,8,128]{3,2,1,0:T(8,128)S(1)}, f32[6,4,8,128]{3,2,1,0:T(8,128)S(1)}, u32[]{:S(2)}, u32[]{:S(2)}) collective-permute-start(f32[6,4,8,128]{3,2,1,0:T(8,128)S(1)} %pad_maximum_fusion.1), channel_id=1, source_target_pairs={{0,1},{1,0},{2,3},{3,2},{4,5},{5,4},{6,7},{7,6},{8,9},{9,8},{10,11... | collective-permute-start | bytes 294920 | tf_op jit(solution)/shard_map/ppermute | solution.py:400
  37.1 16.5 %collective-permute-start.6 = (f32[3,4,8,128]{3,2,1,0:T(8,128)S(1)}, f32[3,4,8,128]{3,2,1,0:T(8,128)S(1)}, u32[]{:S(2)}, u32[]{:S(2)}) collective-permute-start(f32[3,4,8,128]{3,2,1,0:T(8,128)S(1)} %shard_map.49.mean), channel_id=1, source_target_pairs={{0,248},{8,0},{16,8},{24,16},{32,24},{40,32},{48,40},{56,48},{64,5... | collective-permute-start | bytes 147464 | tf_op jit(solution)/shard_map/ppermute | solution.py:392
  54.3 10.0 %collective-permute-start.9 = (f32[12,8,128]{2,1,0:T(8,128)S(1)}, f32[12,8,128]{2,1,0:T(8,128)S(1)}, u32[]{:S(2)}, u32[]{:S(2)}) collective-permute-start(f32[12,8,128]{2,1,0:T(8,128)S(1)} %get-tuple-element.19.refs_0_), channel_id=1, source_target_pairs={{0,16},{16,0},{32,48},{48,32},{1,17},{17,1},{33,49},{49,33},{2,18}... | collective-permute-start | bytes 147464 | tf_op jit(solution)/shard_map/ppermute | solution.py:429
  56.4 12.8 %collective-permute-start.10 = (f32[12,8,128]{2,1,0:T(8,128)S(1)}, f32[12,8,128]{2,1,0:T(8,128)S(1)}, u32[]{:S(2)}, u32[]{:S(2)}) collective-permute-start(f32[12,8,128]{2,1,0:T(8,128)S(1)} %get-tuple-element.19.refs_0_), channel_id=1, source_target_pairs={{0,32},{16,48},{32,0},{48,16},{1,33},{17,49},{33,1},{49,17},{2,34}... | collective-permute-start | bytes 147464 | tf_op jit(solution)/shard_map/ppermute | solution.py:431
  64.3 6.8 %collective-permute-start.11 = (f32[12,8,128]{2,1,0:T(8,128)S(1)}, f32[12,8,128]{2,1,0:T(8,128)S(1)}, u32[]{:S(2)}, u32[]{:S(2)}) collective-permute-start(f32[12,8,128]{2,1,0:T(8,128)S(1)} %collective-permute-done.9.refs_1_), channel_id=1, source_target_pairs={{0,32},{16,48},{32,0},{48,16},{1,33},{17,49},{33,1},{49,17},{2,34}... | collective-permute-start | bytes 147464 | tf_op jit(solution)/shard_map/ppermute | solution.py:431
  68.6 2.7 %collective-permute-start.12 = (f32[12,8,128]{2,1,0:T(8,128)S(1)}, f32[12,8,128]{2,1,0:T(8,128)S(1)}, u32[]{:S(2)}, u32[]{:S(2)}) collective-permute-start(f32[12,8,128]{2,1,0:T(8,128)S(1)} %get-tuple-element.19.refs_0_), channel_id=1, source_target_pairs={{0,8},{8,0},{1,9},{9,1},{2,10},{10,2},{3,11},{11,3},{4,12},{12,4},... | collective-permute-start | bytes 147464 | tf_op jit(solution)/shard_map/ppermute | solution.py:432
  68.6 2.7 %collective-permute-start.13 = (f32[12,8,128]{2,1,0:T(8,128)S(1)}, f32[12,8,128]{2,1,0:T(8,128)S(1)}, u32[]{:S(2)}, u32[]{:S(2)}) collective-permute-start(f32[12,8,128]{2,1,0:T(8,128)S(1)} %collective-permute-done.9.refs_1_), channel_id=1, source_target_pairs={{0,8},{8,0},{1,9},{9,1},{2,10},{10,2},{3,11},{11,3},{4,12},{12,4},... | collective-permute-start | bytes 147464 | tf_op jit(solution)/shard_map/ppermute | solution.py:432
  69.1 2.2 %collective-permute-start.14 = (f32[12,8,128]{2,1,0:T(8,128)S(1)}, f32[12,8,128]{2,1,0:T(8,128)S(1)}, u32[]{:S(2)}, u32[]{:S(2)}) collective-permute-start(f32[12,8,128]{2,1,0:T(8,128)S(1)} %collective-permute-done.10.refs_2_), channel_id=1, source_target_pairs={{0,8},{8,0},{1,9},{9,1},{2,10},{10,2},{3,11},{11,3},{4,12},{12,4},... | collective-permute-start | bytes 147464 | tf_op jit(solution)/shard_map/ppermute | solution.py:432
  75.0 8.3 %collective-permute-start.16 = (f32[3,16,8,128]{3,2,1,0:T(8,128)S(1)}, f32[3,16,8,128]{3,2,1,0:T(8,128)S(1)}, u32[]{:S(2)}, u32[]{:S(2)}) collective-permute-start(f32[3,16,8,128]{3,2,1,0:T(8,128)S(1)} %get-tuple-element.21), channel_id=1, source_target_pairs={{0,64},{64,128},{128,192},{192,0},{1,65},{65,129},{129,193},{193,1... | collective-permute-start | bytes 589832 | tf_op jit(solution)/shard_map/ppermute | solution.py:437
  76.6 11.9 %collective-permute-start.17 = (f32[3,16,8,128]{3,2,1,0:T(8,128)S(1)}, f32[3,16,8,128]{3,2,1,0:T(8,128)S(1)}, u32[]{:S(2)}, u32[]{:S(2)}) collective-permute-start(f32[3,16,8,128]{3,2,1,0:T(8,128)S(1)} %get-tuple-element.21), channel_id=1, source_target_pairs={{0,128},{64,192},{128,0},{192,64},{1,129},{65,193},{129,1},{193,65... | collective-permute-start | bytes 589832 | tf_op jit(solution)/shard_map/ppermute | solution.py:437
  79.3 9.2 %collective-permute-start.18 = (f32[3,16,8,128]{3,2,1,0:T(8,128)S(1)}, f32[3,16,8,128]{3,2,1,0:T(8,128)S(1)}, u32[]{:S(2)}, u32[]{:S(2)}) collective-permute-start(f32[3,16,8,128]{3,2,1,0:T(8,128)S(1)} %get-tuple-element.21), channel_id=1, source_target_pairs={{0,192},{64,0},{128,64},{192,128},{1,193},{65,1},{129,65},{193,129... | collective-permute-start | bytes 589832 | tf_op jit(solution)/shard_map/ppermute | solution.py:437
  83.3 5.7 %collective-permute-start.19 = (f32[3,16,8,128]{3,2,1,0:T(8,128)S(1)}, f32[3,16,8,128]{3,2,1,0:T(8,128)S(1)}, u32[]{:S(2)}, u32[]{:S(2)}) collective-permute-start(f32[3,16,8,128]{3,2,1,0:T(8,128)S(1)} %collective-permute-done.16.refs_8_), channel_id=1, source_target_pairs={{0,8},{8,0},{1,9},{9,1},{2,10},{10,2},{3,11},{11,3},{4,12},{12,4},... | collective-permute-start | bytes 589832 | tf_op jit(solution)/shard_map/ppermute | solution.py:438
  88.5 1.7 %collective-permute-start.21 = (f32[3,16,8,128]{3,2,1,0:T(8,128)S(1)}, f32[3,16,8,128]{3,2,1,0:T(8,128)S(1)}, u32[]{:S(2)}, u32[]{:S(2)}) collective-permute-start(f32[3,16,8,128]{3,2,1,0:T(8,128)S(1)} %collective-permute-done.18.refs_10_), channel_id=1, source_target_pairs={{0,8},{8,0},{1,9},{9,1},{2,10},{10,2},{3,11},{11,3},{4,12},{12,4},... | collective-permute-start | bytes 589832 | tf_op jit(solution)/shard_map/ppermute | solution.py:438
  89.0 26.9 %collective-permute-start.26 = (f32[3,16,32,128]{3,2,1,0:T(8,128)S(1)}, f32[3,16,32,128]{3,2,1,0:T(8,128)S(1)}, u32[]{:S(2)}, u32[]{:S(2)}) collective-permute-start(f32[3,16,32,128]{3,2,1,0:T(8,128)S(1)} %get-tuple-element.26), channel_id=1, source_target_pairs={{0,8},{8,16},{16,24},{24,32},{32,40},{40,48},{48,56},{56,64},{64,7... | collective-permute-start | bytes 2359304 | tf_op jit(solution)/shard_map/ppermute | solution.py:433
  98.2 4.8 %collective-permute-start.22 = (f32[2,12,8,128]{3,2,1,0:T(8,128)S(1)}, f32[2,12,8,128]{3,2,1,0:T(8,128)S(1)}, u32[]{:S(2)}, u32[]{:S(2)}) collective-permute-start(f32[2,12,8,128]{3,2,1,0:T(8,128)S(1)} %get-tuple-element.23), channel_id=1, source_target_pairs={{0,1},{1,0},{2,3},{3,2},{4,5},{5,4},{6,7},{7,6},{8,9},{9,8},{10,11... | collective-permute-start | bytes 294920 | tf_op jit(solution)/shard_map/ppermute | solution.py:444
  98.3 7.0 %collective-permute-start.23 = (f32[2,12,8,128]{3,2,1,0:T(8,128)S(1)}, f32[2,12,8,128]{3,2,1,0:T(8,128)S(1)}, u32[]{:S(2)}, u32[]{:S(2)}) collective-permute-start(f32[2,12,8,128]{3,2,1,0:T(8,128)S(1)} %get-tuple-element.24), channel_id=1, source_target_pairs={{0,2},{1,3},{2,0},{3,1},{4,6},{5,7},{6,4},{7,5},{8,10},{9,11},{10,... | collective-permute-start | bytes 294920 | tf_op jit(solution)/shard_map/ppermute | solution.py:444
  101.7 5.8 %collective-permute-start.24 = (f32[2,12,8,128]{3,2,1,0:T(8,128)S(1)}, f32[2,12,8,128]{3,2,1,0:T(8,128)S(1)}, u32[]{:S(2)}, u32[]{:S(2)}) collective-permute-start(f32[2,12,8,128]{3,2,1,0:T(8,128)S(1)} %get-tuple-element.25), channel_id=1, source_target_pairs={{0,3},{1,2},{2,1},{3,0},{4,7},{5,6},{6,5},{7,4},{8,11},{9,10},{10,... | collective-permute-start | bytes 294920 | tf_op jit(solution)/shard_map/ppermute | solution.py:444
  107.6 8.3 %collective-permute-start.25 = (f32[12,8,128]{2,1,0:T(8,128)S(1)}, f32[12,8,128]{2,1,0:T(8,128)S(1)}, u32[]{:S(2)}, u32[]{:S(2)}) collective-permute-start(f32[12,8,128]{2,1,0:T(8,128)S(1)} %get-tuple-element.29), channel_id=1, source_target_pairs={{0,4},{4,0},{1,5},{5,1},{2,6},{6,2},{3,7},{7,3},{8,12},{12,8},{9,1... | collective-permute-start | bytes 147464 | tf_op jit(solution)/shard_map/ppermute | solution.py:445
  (7 other events, 63.3 us)
